TPU v7x, 128 devices: a whole 4x4x4 slice. The times are simulated.
128 devices in a mesh: shot: 8 (over x_hi, y), rcv: 16 (over x_lo, z, core).
Axes of the slice: x: 4 (x_hi: 2, x_lo: 2; x = x_hi * 2 + x_lo), y: 4, z: 4, core: 2. Of those that a mesh axis runs over, the one named last changes fastest.
Arguments:
- surface_data: bfloat16 [4, 2, 512, 8192], P(None, None, 'rcv', 'shot'), may hold values from -6 to 6
- source_traces: bfloat16 [4, 2, 512, 8192], P(None, None, 'shot', 'rcv'), may hold values from -0.21875 to 0.21875
- block_ids: int32 [12], replicated, may hold values from 0 to 15
Outputs:
- multiples: bfloat16 [4, 2, 8192, 8192], P(None, None, 'shot', 'rcv')
All inputs are finite; a program needn't handle non-finite values.
Results may differ from a plain program's by a relative error of at most 0.001.
Values may be sent and summed in bfloat16 or wider, within the bound.
No kernel may reach another device: no remote copies, remote signals or barrier semaphores. Data moves between devices by JAX's collectives and lax.ppermute only.
A program may use at most 128 MiB of HBM per device.

v0:
```python
import jax
import jax.numpy as jnp
from jax import lax
from jax.sharding import PartitionSpec as P

BLK = 32
STEPS = 12


def from_root(value, axis, root):
    mine = lax.axis_index(axis) == root
    return lax.psum(jnp.where(mine, value, jnp.zeros_like(value)), axis)


def complex_product(left, right):
    freqs = left.shape[0]
    points = left.shape[2]
    shots = left.shape[3]
    stacked_left = left.reshape(freqs, 2 * points, shots)
    upper = jnp.concatenate([right[:, 0], right[:, 1]], axis=2)
    lower = jnp.concatenate([-right[:, 1], right[:, 0]], axis=2)
    stacked_right = jnp.concatenate([upper, lower], axis=1)
    return jnp.einsum(
        "fks,fkc->fsc", stacked_left, stacked_right, preferred_element_type=jnp.float32
    )


def per_device(surface_data, source_traces, block_ids):
    freqs = surface_data.shape[0]
    shots = surface_data.shape[3]
    rcvs = source_traces.shape[3]
    src_rows = source_traces.shape[2]
    my_shot = lax.axis_index("shot")
    whole_surface = lax.all_gather(surface_data, "rcv", axis=2, tiled=True)

    def fetch(step):
        block = block_ids[step]
        first = block * BLK
        left = lax.dynamic_slice_in_dim(whole_surface, first, BLK, 2)
        owner = first // src_rows
        offset = jnp.clip(first - my_shot * src_rows, 0, src_rows - BLK)
        piece = lax.dynamic_slice_in_dim(source_traces, offset, BLK, 2)
        right = from_root(piece, "shot", owner)
        return (left, right)

    def add_step(step, total):
        left, right = fetch(step)
        return total + complex_product(left, right)

    start_total = jnp.zeros((freqs, shots, 2 * rcvs), jnp.float32)
    total = lax.fori_loop(0, STEPS, add_step, start_total)
    result = total.reshape(freqs, shots, 2, rcvs).transpose(0, 2, 1, 3)
    return result.astype(jnp.bfloat16)


def solution(mesh):
    in_specs = (P(None, None, "rcv", "shot"), P(None, None, "shot", "rcv"), P())
    out_specs = P(None, None, "shot", "rcv")
    return jax.shard_map(
        per_device, mesh=mesh, in_specs=in_specs, out_specs=out_specs, check_vma=False
    )
```

profile of v0, /device:TPU:1, one launch (start us, length us, event | category | flops | bytes accessed | tf_op | source)
XLA Modules:
  0.0 1313.3 jit_solution(1475360233014813595)
XLA Ops:
  7.3 57.6 %all-gather.2.cloned.1.call-done = bf16[4,2,512,1024]{3,2,1,0:T(8,128)(2,1)} async-done(((bf16[4,2,32,1024]{3,2,1,0:T(8,128)(2,1)}), bf16[4,2,512,1024]{3,2,1,0:T(8,128)(2,1)}) %all-gather.2.cloned.1.call-update) | async-done | bytes 8388624 | tf_op jit(solution)/shard_map/all_gather | solution.py:34
  64.8 1216.9 %while.16 = (s32[]{:T(128)}, f32[4,1024,1024]{2,1,0:T(8,128)}, s32[12]{0:T(128)}, bf16[4,2,512,1024]{3,2,1,0:T(8,128)(2,1)}, s32[]{:T(128)}, /*index=5*/bf16[4,2...) while((s32[]{:T(128)}, f32[4,1024,1024]{2,1,0:T(8,128)}, ...), condition=%wide.region_2.3_spmd.clone, body=%wide.region_0.2_spmd.clone.sunk | while | flops 547684352 | bytes 38404584 | solution.py:51
  64.8 1.2 dynamic_slice.41
  66.8 1.7 copy_select_fusion.2
  69.7 78.6 %all-reduce.2.cloned.1.call-done = bf16[4,2,32,512]{3,2,0,1:T(8,128)(2,1)} async-done(((bf16[4,2,32,512]{3,2,0,1:T(8,128)(2,1)}), bf16[4,2,32,512]{3,2,0,1:T(8,128)(2,1)}) %all-reduce.2.cloned.1.call-update) | async-done | bytes 262160 | tf_op jit(solution)/shard_map/while/body/eval_jaxpr/psum | solution.py:12
  150.2 8.1 select_add_fusion.2
  158.3 1.2 dynamic_slice.41
  160.2 1.7 copy_select_fusion.2
  163.1 81.5 %all-reduce.2.cloned.1.call-done = bf16[4,2,32,512]{3,2,0,1:T(8,128)(2,1)} async-done(((bf16[4,2,32,512]{3,2,0,1:T(8,128)(2,1)}), bf16[4,2,32,512]{3,2,0,1:T(8,128)(2,1)}) %all-reduce.2.cloned.1.call-update) | async-done | bytes 262160 | tf_op jit(solution)/shard_map/while/body/eval_jaxpr/psum | solution.py:12
  246.5 13.9 %select_add_fusion.2 = f32[4,1024,1024]{2,1,0:T(8,128)} fusion(f32[4,1024,1024]{2,1,0:T(8,128)} %get-tuple-element.268, bf16[4,64,1024]{2,1,0:T(8,128)(2,1)S(1)} %bitcast.22, pred[]{:T(512)S(6)} %compare.11, bf16[4,32,512]{2,1,0:T(8,128)(2,1)S(1)} %get-tuple-element.249, bf16[4,32,512]{2,1,0:T(8,128)(2,1)S(1)} %fusion.15, ...), kind=kOutput, calls=%fused_computation.clone.1 | convolution fusion | flops 547356672 | bytes 34471936 | tf_op jit(solution)/shard_map/while/body/eval_jaxpr/fks,fkc->fsc/dot_general | solution.py:23
  260.4 1.2 dynamic_slice.41
  262.3 1.7 copy_select_fusion.2
  265.2 81.5 %all-reduce.2.cloned.1.call-done = bf16[4,2,32,512]{3,2,0,1:T(8,128)(2,1)} async-done(((bf16[4,2,32,512]{3,2,0,1:T(8,128)(2,1)}), bf16[4,2,32,512]{3,2,0,1:T(8,128)(2,1)}) %all-reduce.2.cloned.1.call-update) | async-done | bytes 262160 | tf_op jit(solution)/shard_map/while/body/eval_jaxpr/psum | solution.py:12
  348.7 13.9 %select_add_fusion.2 = f32[4,1024,1024]{2,1,0:T(8,128)} fusion(f32[4,1024,1024]{2,1,0:T(8,128)} %get-tuple-element.268, bf16[4,64,1024]{2,1,0:T(8,128)(2,1)S(1)} %bitcast.22, pred[]{:T(512)S(6)} %compare.11, bf16[4,32,512]{2,1,0:T(8,128)(2,1)S(1)} %get-tuple-element.249, bf16[4,32,512]{2,1,0:T(8,128)(2,1)S(1)} %fusion.15, ...), kind=kOutput, calls=%fused_computation.clone.1 | convolution fusion | flops 547356672 | bytes 34471936 | tf_op jit(solution)/shard_map/while/body/eval_jaxpr/fks,fkc->fsc/dot_general | solution.py:23
  362.5 1.2 dynamic_slice.41
  364.5 1.7 copy_select_fusion.2
  367.3 81.5 %all-reduce.2.cloned.1.call-done = bf16[4,2,32,512]{3,2,0,1:T(8,128)(2,1)} async-done(((bf16[4,2,32,512]{3,2,0,1:T(8,128)(2,1)}), bf16[4,2,32,512]{3,2,0,1:T(8,128)(2,1)}) %all-reduce.2.cloned.1.call-update) | async-done | bytes 262160 | tf_op jit(solution)/shard_map/while/body/eval_jaxpr/psum | solution.py:12
  450.8 13.9 %select_add_fusion.2 = f32[4,1024,1024]{2,1,0:T(8,128)} fusion(f32[4,1024,1024]{2,1,0:T(8,128)} %get-tuple-element.268, bf16[4,64,1024]{2,1,0:T(8,128)(2,1)S(1)} %bitcast.22, pred[]{:T(512)S(6)} %compare.11, bf16[4,32,512]{2,1,0:T(8,128)(2,1)S(1)} %get-tuple-element.249, bf16[4,32,512]{2,1,0:T(8,128)(2,1)S(1)} %fusion.15, ...), kind=kOutput, calls=%fused_computation.clone.1 | convolution fusion | flops 547356672 | bytes 34471936 | tf_op jit(solution)/shard_map/while/body/eval_jaxpr/fks,fkc->fsc/dot_general | solution.py:23
  464.7 1.2 dynamic_slice.41
  466.6 1.7 copy_select_fusion.2
  469.5 81.5 %all-reduce.2.cloned.1.call-done = bf16[4,2,32,512]{3,2,0,1:T(8,128)(2,1)} async-done(((bf16[4,2,32,512]{3,2,0,1:T(8,128)(2,1)}), bf16[4,2,32,512]{3,2,0,1:T(8,128)(2,1)}) %all-reduce.2.cloned.1.call-update) | async-done | bytes 262160 | tf_op jit(solution)/shard_map/while/body/eval_jaxpr/psum | solution.py:12
  552.9 13.9 %select_add_fusion.2 = f32[4,1024,1024]{2,1,0:T(8,128)} fusion(f32[4,1024,1024]{2,1,0:T(8,128)} %get-tuple-element.268, bf16[4,64,1024]{2,1,0:T(8,128)(2,1)S(1)} %bitcast.22, pred[]{:T(512)S(6)} %compare.11, bf16[4,32,512]{2,1,0:T(8,128)(2,1)S(1)} %get-tuple-element.249, bf16[4,32,512]{2,1,0:T(8,128)(2,1)S(1)} %fusion.15, ...), kind=kOutput, calls=%fused_computation.clone.1 | convolution fusion | flops 547356672 | bytes 34471936 | tf_op jit(solution)/shard_map/while/body/eval_jaxpr/fks,fkc->fsc/dot_general | solution.py:23
  566.8 1.2 dynamic_slice.41
  568.7 1.8 copy_select_fusion.2
  571.6 81.5 %all-reduce.2.cloned.1.call-done = bf16[4,2,32,512]{3,2,0,1:T(8,128)(2,1)} async-done(((bf16[4,2,32,512]{3,2,0,1:T(8,128)(2,1)}), bf16[4,2,32,512]{3,2,0,1:T(8,128)(2,1)}) %all-reduce.2.cloned.1.call-update) | async-done | bytes 262160 | tf_op jit(solution)/shard_map/while/body/eval_jaxpr/psum | solution.py:12
  655.0 13.9 %select_add_fusion.2 = f32[4,1024,1024]{2,1,0:T(8,128)} fusion(f32[4,1024,1024]{2,1,0:T(8,128)} %get-tuple-element.268, bf16[4,64,1024]{2,1,0:T(8,128)(2,1)S(1)} %bitcast.22, pred[]{:T(512)S(6)} %compare.11, bf16[4,32,512]{2,1,0:T(8,128)(2,1)S(1)} %get-tuple-element.249, bf16[4,32,512]{2,1,0:T(8,128)(2,1)S(1)} %fusion.15, ...), kind=kOutput, calls=%fused_computation.clone.1 | convolution fusion | flops 547356672 | bytes 34471936 | tf_op jit(solution)/shard_map/while/body/eval_jaxpr/fks,fkc->fsc/dot_general | solution.py:23
  668.9 1.2 dynamic_slice.41
  670.9 1.7 copy_select_fusion.2
  673.7 81.6 %all-reduce.2.cloned.1.call-done = bf16[4,2,32,512]{3,2,0,1:T(8,128)(2,1)} async-done(((bf16[4,2,32,512]{3,2,0,1:T(8,128)(2,1)}), bf16[4,2,32,512]{3,2,0,1:T(8,128)(2,1)}) %all-reduce.2.cloned.1.call-update) | async-done | bytes 262160 | tf_op jit(solution)/shard_map/while/body/eval_jaxpr/psum | solution.py:12
  757.2 13.9 %select_add_fusion.2 = f32[4,1024,1024]{2,1,0:T(8,128)} fusion(f32[4,1024,1024]{2,1,0:T(8,128)} %get-tuple-element.268, bf16[4,64,1024]{2,1,0:T(8,128)(2,1)S(1)} %bitcast.22, pred[]{:T(512)S(6)} %compare.11, bf16[4,32,512]{2,1,0:T(8,128)(2,1)S(1)} %get-tuple-element.249, bf16[4,32,512]{2,1,0:T(8,128)(2,1)S(1)} %fusion.15, ...), kind=kOutput, calls=%fused_computation.clone.1 | convolution fusion | flops 547356672 | bytes 34471936 | tf_op jit(solution)/shard_map/while/body/eval_jaxpr/fks,fkc->fsc/dot_general | solution.py:23
  771.1 1.2 dynamic_slice.41
  773.0 1.7 copy_select_fusion.2
  775.9 81.5 %all-reduce.2.cloned.1.call-done = bf16[4,2,32,512]{3,2,0,1:T(8,128)(2,1)} async-done(((bf16[4,2,32,512]{3,2,0,1:T(8,128)(2,1)}), bf16[4,2,32,512]{3,2,0,1:T(8,128)(2,1)}) %all-reduce.2.cloned.1.call-update) | async-done | bytes 262160 | tf_op jit(solution)/shard_map/while/body/eval_jaxpr/psum | solution.py:12
  859.4 13.9 %select_add_fusion.2 = f32[4,1024,1024]{2,1,0:T(8,128)} fusion(f32[4,1024,1024]{2,1,0:T(8,128)} %get-tuple-element.268, bf16[4,64,1024]{2,1,0:T(8,128)(2,1)S(1)} %bitcast.22, pred[]{:T(512)S(6)} %compare.11, bf16[4,32,512]{2,1,0:T(8,128)(2,1)S(1)} %get-tuple-element.249, bf16[4,32,512]{2,1,0:T(8,128)(2,1)S(1)} %fusion.15, ...), kind=kOutput, calls=%fused_computation.clone.1 | convolution fusion | flops 547356672 | bytes 34471936 | tf_op jit(solution)/shard_map/while/body/eval_jaxpr/fks,fkc->fsc/dot_general | solution.py:23
  875.2 1.7 copy_select_fusion.2
  878.1 81.5 %all-reduce.2.cloned.1.call-done = bf16[4,2,32,512]{3,2,0,1:T(8,128)(2,1)} async-done(((bf16[4,2,32,512]{3,2,0,1:T(8,128)(2,1)}), bf16[4,2,32,512]{3,2,0,1:T(8,128)(2,1)}) %all-reduce.2.cloned.1.call-update) | async-done | bytes 262160 | tf_op jit(solution)/shard_map/while/body/eval_jaxpr/psum | solution.py:12
  961.5 13.9 %select_add_fusion.2 = f32[4,1024,1024]{2,1,0:T(8,128)} fusion(f32[4,1024,1024]{2,1,0:T(8,128)} %get-tuple-element.268, bf16[4,64,1024]{2,1,0:T(8,128)(2,1)S(1)} %bitcast.22, pred[]{:T(512)S(6)} %compare.11, bf16[4,32,512]{2,1,0:T(8,128)(2,1)S(1)} %get-tuple-element.249, bf16[4,32,512]{2,1,0:T(8,128)(2,1)S(1)} %fusion.15, ...), kind=kOutput, calls=%fused_computation.clone.1 | convolution fusion | flops 547356672 | bytes 34471936 | tf_op jit(solution)/shard_map/while/body/eval_jaxpr/fks,fkc->fsc/dot_general | solution.py:23
  977.3 1.8 copy_select_fusion.2
  980.2 81.5 %all-reduce.2.cloned.1.call-done = bf16[4,2,32,512]{3,2,0,1:T(8,128)(2,1)} async-done(((bf16[4,2,32,512]{3,2,0,1:T(8,128)(2,1)}), bf16[4,2,32,512]{3,2,0,1:T(8,128)(2,1)}) %all-reduce.2.cloned.1.call-update) | async-done | bytes 262160 | tf_op jit(solution)/shard_map/while/body/eval_jaxpr/psum | solution.py:12
  1063.6 13.9 %select_add_fusion.2 = f32[4,1024,1024]{2,1,0:T(8,128)} fusion(f32[4,1024,1024]{2,1,0:T(8,128)} %get-tuple-element.268, bf16[4,64,1024]{2,1,0:T(8,128)(2,1)S(1)} %bitcast.22, pred[]{:T(512)S(6)} %compare.11, bf16[4,32,512]{2,1,0:T(8,128)(2,1)S(1)} %get-tuple-element.249, bf16[4,32,512]{2,1,0:T(8,128)(2,1)S(1)} %fusion.15, ...), kind=kOutput, calls=%fused_computation.clone.1 | convolution fusion | flops 547356672 | bytes 34471936 | tf_op jit(solution)/shard_map/while/body/eval_jaxpr/fks,fkc->fsc/dot_general | solution.py:23
  1079.4 1.7 copy_select_fusion.2
  1082.3 81.5 %all-reduce.2.cloned.1.call-done = bf16[4,2,32,512]{3,2,0,1:T(8,128)(2,1)} async-done(((bf16[4,2,32,512]{3,2,0,1:T(8,128)(2,1)}), bf16[4,2,32,512]{3,2,0,1:T(8,128)(2,1)}) %all-reduce.2.cloned.1.call-update) | async-done | bytes 262160 | tf_op jit(solution)/shard_map/while/body/eval_jaxpr/psum | solution.py:12
  1165.8 13.9 %select_add_fusion.2 = f32[4,1024,1024]{2,1,0:T(8,128)} fusion(f32[4,1024,1024]{2,1,0:T(8,128)} %get-tuple-element.268, bf16[4,64,1024]{2,1,0:T(8,128)(2,1)S(1)} %bitcast.22, pred[]{:T(512)S(6)} %compare.11, bf16[4,32,512]{2,1,0:T(8,128)(2,1)S(1)} %get-tuple-element.249, bf16[4,32,512]{2,1,0:T(8,128)(2,1)S(1)} %fusion.15, ...), kind=kOutput, calls=%fused_computation.clone.1 | convolution fusion | flops 547356672 | bytes 34471936 | tf_op jit(solution)/shard_map/while/body/eval_jaxpr/fks,fkc->fsc/dot_general | solution.py:23
  1181.6 1.7 copy_select_fusion.2
  1184.5 81.5 %all-reduce.2.cloned.1.call-done = bf16[4,2,32,512]{3,2,0,1:T(8,128)(2,1)} async-done(((bf16[4,2,32,512]{3,2,0,1:T(8,128)(2,1)}), bf16[4,2,32,512]{3,2,0,1:T(8,128)(2,1)}) %all-reduce.2.cloned.1.call-update) | async-done | bytes 262160 | tf_op jit(solution)/shard_map/while/body/eval_jaxpr/psum | solution.py:12
  1267.9 13.9 %select_add_fusion.2 = f32[4,1024,1024]{2,1,0:T(8,128)} fusion(f32[4,1024,1024]{2,1,0:T(8,128)} %get-tuple-element.268, bf16[4,64,1024]{2,1,0:T(8,128)(2,1)S(1)} %bitcast.22, pred[]{:T(512)S(6)} %compare.11, bf16[4,32,512]{2,1,0:T(8,128)(2,1)S(1)} %get-tuple-element.249, bf16[4,32,512]{2,1,0:T(8,128)(2,1)S(1)} %fusion.15, ...), kind=kOutput, calls=%fused_computation.clone.1 | convolution fusion | flops 547356672 | bytes 34471936 | tf_op jit(solution)/shard_map/while/body/eval_jaxpr/fks,fkc->fsc/dot_general | solution.py:23
  1281.8 13.6 %copy.6 = bf16[4,1024,1024]{1,2,0:T(8,128)(2,1)} copy(f32[4,1024,1024]{2,1,0:T(8,128)} %get-tuple-element.162) | data formatting | bytes 25165824 | tf_op jit(solution)/shard_map/while | solution.py:51
  1295.4 11.4 copy.7
  (67 shorter events, 41.8 us)
Async XLA Ops:
  6.5 58.3 %all-gather.2.cloned.1.call-start = ((), (), s32[]{:S(2)}) async-start(), calls=%async_computation | async-start | bytes 8912896 | tf_op jit(solution)/shard_map/all_gather | solution.py:34
  64.8 83.4 %all-reduce.2.cloned.1.call-start = ((), (), s32[]{:S(2)}) async-start(), calls=%async_computation.1 | async-start | bytes 524288 | tf_op jit(solution)/shard_map/while/body/eval_jaxpr/psum | solution.py:12
  158.3 86.3 %all-reduce.2.cloned.1.call-start = ((), (), s32[]{:S(2)}) async-start(), calls=%async_computation.1 | async-start | bytes 524288 | tf_op jit(solution)/shard_map/while/body/eval_jaxpr/psum | solution.py:12
  260.4 86.3 %all-reduce.2.cloned.1.call-start = ((), (), s32[]{:S(2)}) async-start(), calls=%async_computation.1 | async-start | bytes 524288 | tf_op jit(solution)/shard_map/while/body/eval_jaxpr/psum | solution.py:12
  362.5 86.3 %all-reduce.2.cloned.1.call-start = ((), (), s32[]{:S(2)}) async-start(), calls=%async_computation.1 | async-start | bytes 524288 | tf_op jit(solution)/shard_map/while/body/eval_jaxpr/psum | solution.py:12
  464.7 86.3 %all-reduce.2.cloned.1.call-start = ((), (), s32[]{:S(2)}) async-start(), calls=%async_computation.1 | async-start | bytes 524288 | tf_op jit(solution)/shard_map/while/body/eval_jaxpr/psum | solution.py:12
  566.8 86.3 %all-reduce.2.cloned.1.call-start = ((), (), s32[]{:S(2)}) async-start(), calls=%async_computation.1 | async-start | bytes 524288 | tf_op jit(solution)/shard_map/while/body/eval_jaxpr/psum | solution.py:12
  668.9 86.4 %all-reduce.2.cloned.1.call-start = ((), (), s32[]{:S(2)}) async-start(), calls=%async_computation.1 | async-start | bytes 524288 | tf_op jit(solution)/shard_map/while/body/eval_jaxpr/psum | solution.py:12
  771.1 86.3 %all-reduce.2.cloned.1.call-start = ((), (), s32[]{:S(2)}) async-start(), calls=%async_computation.1 | async-start | bytes 524288 | tf_op jit(solution)/shard_map/while/body/eval_jaxpr/psum | solution.py:12
  873.2 86.3 %all-reduce.2.cloned.1.call-start = ((), (), s32[]{:S(2)}) async-start(), calls=%async_computation.1 | async-start | bytes 524288 | tf_op jit(solution)/shard_map/while/body/eval_jaxpr/psum | solution.py:12
  975.4 86.3 %all-reduce.2.cloned.1.call-start = ((), (), s32[]{:S(2)}) async-start(), calls=%async_computation.1 | async-start | bytes 524288 | tf_op jit(solution)/shard_map/while/body/eval_jaxpr/psum | solution.py:12
  1077.5 86.3 %all-reduce.2.cloned.1.call-start = ((), (), s32[]{:S(2)}) async-start(), calls=%async_computation.1 | async-start | bytes 524288 | tf_op jit(solution)/shard_map/while/body/eval_jaxpr/psum | solution.py:12
  1179.6 86.3 %all-reduce.2.cloned.1.call-start = ((), (), s32[]{:S(2)}) async-start(), calls=%async_computation.1 | async-start | bytes 524288 | tf_op jit(solution)/shard_map/while/body/eval_jaxpr/psum | solution.py:12
Sparse Core Ops, SparseCore 0:
  9.0 55.7 all-gather.1
  68.7 79.5 all-reduce.1
  162.1 82.4 all-reduce.1
  264.2 82.4 all-reduce.1
  366.4 82.4 all-reduce.1
  468.5 82.4 all-reduce.1
  570.6 82.4 all-reduce.1
  672.7 82.5 all-reduce.1
  774.9 82.4 all-reduce.1
  877.1 82.4 all-reduce.1
  979.2 82.4 all-reduce.1
  1081.3 82.4 all-reduce.1
  1183.5 82.4 all-reduce.1
where the time goes:
time: 1320 us; the launch traced here: 1310 us
  waiting for transfers between devices  1030 us (78%)
  matrix products  161 us (12%)
  local copies, waits for them, and re-layouts  64.8 us (5%)
  other arithmetic  32 us (2%)
    psum x12, waiting for transfers between devices, from_root(): return lax.psum(jnp.where(mine, value, jnp.zeros_like(value)), axis)  975 us
    dot_general x12, matrix products, complex_product(): jnp.einsum('fks,fkc->fsc', stacked_left, stacked_right, preferred_element...  161 us
    all_gather x1, waiting for transfers between devices, per_device(): whole_surface = lax.all_gather(surface_data, 'rcv', axis=2, tiled=True)  57.6 us
  transfers between devices with their start and end apart: 13, of which 13 were waited for; matrix products, arithmetic and copies ran while one was open for 1% of the time, Pallas kernels for 0%

commit v1 on v0

v1 whole, which is shorter than its diff:
```python
import jax
import jax.numpy as jnp
from jax import lax
from jax.experimental import pallas as pl
from jax.experimental.pallas import tpu as pltpu
from jax.sharding import PartitionSpec as P

BLK = 32
STEPS = 12
ROWS = 256
AXES = ("shot", "rcv")
X, Y, Z, CORES = 4, 4, 4, 2


def moved(value, dx=0, dy=0, dz=0, flip_x=False, flip_core=False):
    def index(x, y, z, core):
        x_hi, x_lo = divmod(x, 2)
        return (((x_hi * Y + y) * 2 + x_lo) * Z + z) * CORES + core

    pairs = []
    for x in range(X):
        for y in range(Y):
            for z in range(Z):
                for core in range(CORES):
                    way = 1 - 2 * core
                    to_x = x ^ 1 if flip_x else (x + way * dx) % X
                    to_core = core ^ 1 if flip_core else core
                    target = index(to_x, (y + way * dy) % Y, (z + way * dz) % Z, to_core)
                    pairs.append((index(x, y, z, core), target))
    return lax.ppermute(value, AXES, pairs)


def choose(refs, which, act):
    if len(refs) == 1:
        act(refs[0])
        return
    half = len(refs) // 2

    @pl.when(which < half)
    def _():
        choose(refs[:half], which, act)

    @pl.when(which >= half)
    def _():
        choose(refs[half:], which - half, act)


def multiply_kernel(a_where, b_where, b_row, *refs):
    a_refs, b_refs = refs[:16], refs[16:24]
    out, a_buf, b_buf, lhs, rhs, a_sem, b_sem = refs[24:]
    freqs = a_buf.shape[1]
    f = pl.program_id(0)
    rcvs = b_buf.shape[4]

    def fetch(first_freq, count, slot):
        these = pl.ds(first_freq, count)
        for step in range(STEPS):

            def from_surface(ref):
                pltpu.make_async_copy(
                    ref.at[these], a_buf.at[step, these], a_sem.at[slot]
                ).start()

            choose(a_refs, a_where[step], from_surface)

            def from_traces(ref):
                first = pl.multiple_of(b_row[step], BLK)
                pltpu.make_async_copy(
                    ref.at[these, :, pl.ds(first, BLK)], b_buf.at[step, these], b_sem.at[slot]
                ).start()

            choose(b_refs, b_where[step], from_traces)

    def arrive(first_freq, count, slot):
        these = pl.ds(first_freq, count)
        for buf, sem in ((a_buf, a_sem), (b_buf, b_sem)):
            part = buf.at[:, these]
            pltpu.make_async_copy(part, part, sem.at[slot]).wait()

    @pl.when(f == 0)
    def _():
        fetch(0, 1, 0)
        fetch(1, freqs - 1, 1)
        arrive(0, 1, 0)

    @pl.when(f == 1)
    def _():
        arrive(1, freqs - 1, 1)

    for step in range(STEPS):
        real = b_buf[step, f, 0]
        imag = b_buf[step, f, 1]
        rhs[0, step, 0] = real
        rhs[0, step, 1] = -imag
        rhs[1, step, 0] = imag
        rhs[1, step, 1] = real

    depth = STEPS * 2 * BLK
    for first in range(0, lhs.shape[0], ROWS):
        block = a_buf[:, f, :, :, first : first + ROWS].reshape(depth, ROWS)
        lhs[first : first + ROWS, :] = block.T

    for part in range(2):
        out[0, part] = jnp.dot(
            lhs[...], rhs[part].reshape(depth, rcvs), preferred_element_type=jnp.float32
        ).astype(out.dtype)


def multiply(a_parts, b_parts, a_where, b_where, b_row):
    freqs, _, _, shots = a_parts[0].shape
    rcvs = b_parts[0].shape[3]
    depth = STEPS * 2 * BLK
    return pl.pallas_call(
        multiply_kernel,
        out_shape=jax.ShapeDtypeStruct((freqs, 2, shots, rcvs), jnp.bfloat16),
        grid_spec=pltpu.PrefetchScalarGridSpec(
            num_scalar_prefetch=3,
            grid=(freqs,),
            in_specs=[pl.BlockSpec(memory_space=pl.ANY)] * (len(a_parts) + len(b_parts)),
            out_specs=pl.BlockSpec((1, 2, shots, rcvs), lambda f, *_: (f, 0, 0, 0)),
            scratch_shapes=[
                pltpu.VMEM((STEPS, freqs, 2, BLK, shots), jnp.bfloat16),
                pltpu.VMEM((STEPS, freqs, 2, BLK, rcvs), jnp.bfloat16),
                pltpu.VMEM((shots, depth), jnp.bfloat16),
                pltpu.VMEM((2, STEPS, 2, BLK, rcvs), jnp.bfloat16),
                pltpu.SemaphoreType.DMA((2,)),
                pltpu.SemaphoreType.DMA((2,)),
            ],
        ),
        compiler_params=pltpu.CompilerParams(vmem_limit_bytes=56 * 1024 * 1024),
        cost_estimate=pl.CostEstimate(
            flops=2 * freqs * shots * 2 * rcvs * depth,
            bytes_accessed=20 * 1024 * 1024,
            transcendentals=0,
        ),
    )(a_where, b_where, b_row, *a_parts, *b_parts)


def places(block_ids):
    shot, rcv = lax.axis_index("shot"), lax.axis_index("rcv")
    core, z, x_lo = rcv % CORES, rcv // CORES % Z, rcv // (CORES * Z)
    of_core, of_z, of_x = block_ids % CORES, block_ids // CORES % Z, block_ids // (CORES * Z)
    distance = jnp.where(of_core == 0, z - of_z, of_z - z) % Z
    a_where = ((of_core != core) * 2 + (of_x != x_lo)) * Z + distance
    owner = block_ids // 2
    y, of_y = shot % Y, owner % Y
    distance = jnp.where(core == 0, y - of_y, of_y - y) % Y
    b_where = (shot // Y != owner // Y) * Y + distance
    return a_where.astype(jnp.int32), b_where.astype(jnp.int32), block_ids % 2 * BLK


def after(value, *earlier):
    return lax.optimization_barrier((value, *earlier))[0]


def per_device(surface_data, source_traces, block_ids):
    a, b = surface_data, source_traces

    def send(name, value, **way):
        with jax.named_scope(name):
            return moved(value, **way)

    def swap(name, value):
        return send(name, value, flip_core=True)

    b_hop = send("b_hop", b, dx=1)
    b_1 = send("b_1", b, dy=1)
    a_1 = send("a_1", a, dz=1)
    b_x = send("b_x", b_hop, dx=1)
    a_x = send("a_x", after(a, b_x), flip_x=True)
    a_2 = send("a_2", a_1, dz=1)
    a_3 = send("a_3", after(a, a_2), dz=-1)
    b_x1 = send("b_x1", b_x, dy=1)
    b_x2 = send("b_x2", b_x1, dy=1)
    a_x1 = send("a_x1", a_x, dz=1)
    a_x3 = send("a_x3", after(a_x, a_2), dz=-1)
    a_x2 = send("a_x2", a_2, flip_x=True)
    other = swap("other", a)
    b_3 = send("b_3", after(b, other), dy=-1)
    b_2 = send("b_2", after(b_1, b_3, a_2), dy=1)
    b_x3 = send("b_x3", after(b_x, b_2), dy=-1)
    other_1 = swap("other_1", after(a_1, a_2))
    other_2 = swap("other_2", after(a_2, a_3))
    other_3 = swap("other_3", after(a_3, b_2))
    other_x = swap("other_x", after(a_x, a_x3, b_x2, b_2))
    other_x1 = swap("other_x1", after(a_x1, b_1))
    other_x2 = swap("other_x2", after(a_x2, b_1))
    other_x3 = swap("other_x3", after(a_x3, other_3))

    a_parts = [a, a_1, a_2, a_3, a_x, a_x1, a_x2, a_x3]
    a_parts += [other, other_1, other_2, other_3, other_x, other_x1, other_x2, other_x3]
    b_parts = [b, b_1, b_2, b_3, b_x, b_x1, b_x2, b_x3]
    return multiply(a_parts, b_parts, *places(block_ids))


def solution(mesh):
    in_specs = (P(None, None, "rcv", "shot"), P(None, None, "shot", "rcv"), P())
    out_specs = P(None, None, "shot", "rcv")
    return jax.shard_map(
        per_device, mesh=mesh, in_specs=in_specs, out_specs=out_specs, check_vma=False
    )
```

time: 1320 us -> 74.1 us (0.06)
  waiting for transfers between devices: 1030 us -> 24.7 us
  matrix products: 161 us -> 0 us
  local copies, waits for them, and re-layouts: 64.8 us -> 0.46 us
  starting transfers between devices: 0.03 us -> 34.1 us
  other arithmetic: 32 us -> 2.52 us
    psum x12 -> x0, waiting for transfers between devices: 975 us -> none  [from_root(): return lax.psum(jnp.where(mine, value, jnp.zeros_like(value)), axis)]
    dot_general x12 -> x0, matrix products: 161 us -> none  [complex_product(): jnp.einsum('fks,fkc->fsc', stacked_left, stacked_right, preferred_element...]
    all_gather x1 -> x0, waiting for transfers between devices: 57.6 us -> none  [per_device(): whole_surface = lax.all_gather(surface_data, 'rcv', axis=2, tiled=True)]
    ppermute x0 -> x23, starting transfers between devices: none -> 34.1 us  [moved(): return lax.ppermute(value, AXES, pairs)]
    dynamic_slice x24 -> x0, local copies, waits for them, and re-layouts: 28 us -> none  [the longest x12 14.8 us: fetch(): block = block_ids[step]]
    ppermute x0 -> x23, waiting for transfers between devices: none -> 24.7 us  [moved(): return lax.ppermute(value, AXES, pairs)]
    select_n x12 -> x0, other arithmetic: 21 us -> none  [from_root(): return lax.psum(jnp.where(mine, value, jnp.zeros_like(value)), axis)]
    while x1 -> x0, local copies, waits for them, and re-layouts: 13.6 us -> none  [per_device(): total = lax.fori_loop(0, STEPS, add_step, start_total)]
  transfers between devices with their start and end apart: 13 -> 23, of which waited for: 13 -> 9; matrix products, arithmetic and copies ran while one was open for 1% -> 3% of each run, Pallas kernels for 0% -> 0%
where the time goes in v1:
time: 74.1 us; the launch traced here: 73.8 us
  starting transfers between devices  34.1 us (46%)
  waiting for transfers between devices  24.7 us (33%)
  Pallas kernels  11.8 us (16%)
  other arithmetic  2.52 us (3%)
    ppermute x23, starting transfers between devices, moved(): return lax.ppermute(value, AXES, pairs)  34.1 us
    ppermute x23, waiting for transfers between devices, moved(): return lax.ppermute(value, AXES, pairs)  24.7 us
    pallas_call x1, Pallas kernels, multiply(): pl.pallas_call(multiply_kernel, out_shape=jax.ShapeDtypeStruct((freqs, 2,...  11.8 us
  transfers between devices with their start and end apart: 23, of which 9 were waited for; matrix products, arithmetic and copies ran while one was open for 3% of the time, Pallas kernels for 0%

profile of v1, /device:TPU:1, one launch (start us, length us, event | category | flops | bytes accessed | tf_op | source)
XLA Modules:
  0.0 73.8 jit_solution(11848268633161079120)
XLA Ops:
  0.0 3.3 %collective-permute-start.3 = (bf16[4,2,64,512]{3,2,1,0:T(8,128)(2,1)}, bf16[4,2,64,512]{3,2,1,0:T(8,128)(2,1)S(1)}, u32[]{:S(2)}, u32[]{:S(2)}) collective-permute-start(bf16[4,2,64,512]{3,2,1,0:T(8,128)(2,1)} %refs_16_.1), channel_id=1, source_target_pairs={{0,8},{1,73},{2,10},{3,75},{4,12},{5,77},{6,14},{7,79},{16,24},{17... | collective-permute-start | bytes 1572872 | tf_op jit(solution)/shard_map/b_hop/ppermute | solution.py:30
  3.3 3.8 %collective-permute-start = (bf16[4,2,32,1024]{3,2,1,0:T(8,128)(2,1)}, bf16[4,2,32,1024]{3,2,1,0:T(8,128)(2,1)S(1)}, u32[]{:S(2)}, u32[]{:S(2)}) collective-permute-start(bf16[4,2,32,1024]{3,2,1,0:T(8,128)(2,1)} %refs_0_.1), channel_id=1, source_target_pairs={{0,2},{1,7},{2,4},{3,1},{4,6},{5,3},{6,0},{7,5},{16,18},{17,23},{1... | collective-permute-start | bytes 1572872 | tf_op jit(solution)/shard_map/a_1/ppermute | solution.py:30
  7.1 0.0 collective-permute-start.9
  7.1 2.7 %collective-permute-done.3 = bf16[4,2,64,512]{3,2,1,0:T(8,128)(2,1)S(1)} collective-permute-done((bf16[4,2,64,512]{3,2,1,0:T(8,128)(2,1)}, bf16[4,2,64,512]{3,2,1,0:T(8,128)(2,1)S(1)}, u32[]{:S(2)}, u32[]{:S(2)}) %collective-permute-start.3) | collective-permute-done | bytes 524320 | tf_op jit(solution)/shard_map/b_hop/ppermute | solution.py:30
  9.8 3.3 %collective-permute-start.4 = (bf16[4,2,64,512]{3,2,1,0:T(8,128)(2,1)S(1)}, bf16[4,2,64,512]{3,2,1,0:T(8,128)(2,1)S(1)}, u32[]{:S(2)}, u32[]{:S(2)}) collective-permute-start(bf16[4,2,64,512]{3,2,1,0:T(8,128)(2,1)S(1)} %collective-permute-done.3), channel_id=1, source_target_pairs={{0,8},{1,73},{2,10},{3,75},{4,12},{5,77},{6,14},{7,79},{16,24},{17... | collective-permute-start | bytes 1572872 | tf_op jit(solution)/shard_map/b_x/ppermute | solution.py:30
  13.1 0.5 collective-permute-done.refs_1_
  13.5 3.0 %collective-permute-start.1 = (bf16[4,2,32,1024]{3,2,1,0:T(8,128)(2,1)S(1)}, bf16[4,2,32,1024]{3,2,1,0:T(8,128)(2,1)S(1)}, u32[]{:S(2)}, u32[]{:S(2)}) collective-permute-start(bf16[4,2,32,1024]{3,2,1,0:T(8,128)(2,1)S(1)} %collective-permute-done.refs_1_), channel_id=1, source_target_pairs={{0,2},{1,7},{2,4},{3,1},{4,6},{5,3},{6,0},{7,5},{16,18},{17,23},{1... | collective-permute-start | bytes 1572872 | tf_op jit(solution)/shard_map/a_2/ppermute | solution.py:30
  16.5 2.7 %collective-permute-start.12 = (bf16[4,2,64,512]{3,2,1,0:T(8,128)(2,1)}, bf16[4,2,64,512]{3,2,1,0:T(8,128)(2,1)S(1)}, u32[]{:S(2)}, u32[]{:S(2)}) collective-permute-start(bf16[4,2,64,512]{3,2,1,0:T(8,128)(2,1)} %refs_16_.1), channel_id=1, source_target_pairs={{0,16},{1,49},{2,18},{3,51},{4,20},{5,53},{6,22},{7,55},{16,32},{1... | collective-permute-start | bytes 1572872 | tf_op jit(solution)/shard_map/b_1/ppermute | solution.py:30
  19.3 0.0 collective-permute-done.9.refs_8_
  19.3 0.0 collective-permute-start.13
  19.3 0.0 collective-permute-done.4.refs_20_
  19.3 0.1 collective-permute-start.5
  19.4 3.3 %collective-permute-done.1.refs_2_ = bf16[4,2,32,1024]{3,2,1,0:T(8,128)(2,1)S(1)} collective-permute-done((bf16[4,2,32,1024]{3,2,1,0:T(8,128)(2,1)S(1)}, bf16[4,2,32,1024]{3,2,1,0:T(8,128)(2,1)S(1)}, u32[]{:S(2)}, u32[]{:S(2)}) %collective-permute-start.1) | collective-permute-done | bytes 524320 | tf_op jit(solution)/shard_map/a_2/ppermute | solution.py:30
  22.7 0.3 collective-permute-start.2
  22.9 2.7 %collective-permute-start.16 = (bf16[4,2,64,512]{3,2,1,0:T(8,128)(2,1)S(1)}, bf16[4,2,64,512]{3,2,1,0:T(8,128)(2,1)S(1)}, u32[]{:S(2)}, u32[]{:S(2)}) collective-permute-start(bf16[4,2,64,512]{3,2,1,0:T(8,128)(2,1)S(1)} %collective-permute-done.4.refs_20_), channel_id=1, source_target_pairs={{0,16},{1,49},{2,18},{3,51},{4,20},{5,53},{6,22},{7,55},{16,32},{1... | collective-permute-start | bytes 1572872 | tf_op jit(solution)/shard_map/b_x1/ppermute | solution.py:30
  25.6 5.1 %collective-permute-done.12.refs_17_ = bf16[4,2,64,512]{3,2,1,0:T(8,128)(2,1)S(1)} collective-permute-done((bf16[4,2,64,512]{3,2,1,0:T(8,128)(2,1)}, bf16[4,2,64,512]{3,2,1,0:T(8,128)(2,1)S(1)}, u32[]{:S(2)}, u32[]{:S(2)}) %collective-permute-start.12) | collective-permute-done | bytes 524320 | tf_op jit(solution)/shard_map/b_1/ppermute | solution.py:30
  30.7 0.0 collective-permute-done.13.refs_19_
  30.7 2.3 %collective-permute-start.14 = (bf16[4,2,64,512]{3,2,1,0:T(8,128)(2,1)S(1)}, bf16[4,2,64,512]{3,2,1,0:T(8,128)(2,1)S(1)}, u32[]{:S(2)}, u32[]{:S(2)}) collective-permute-start(bf16[4,2,64,512]{3,2,1,0:T(8,128)(2,1)S(1)} %collective-permute-done.12.refs_17_), channel_id=1, source_target_pairs={{0,16},{1,49},{2,18},{3,51},{4,20},{5,53},{6,22},{7,55},{16,32},{1... | collective-permute-start | bytes 1572872 | tf_op jit(solution)/shard_map/b_2/ppermute | solution.py:30
  33.0 0.0 collective-permute-start.7
  33.0 0.0 collective-permute-done.5.refs_4_
  33.0 1.9 %collective-permute-start.6 = (bf16[4,2,32,1024]{3,2,1,0:T(8,128)(2,1)}, bf16[4,2,32,1024]{3,2,1,0:T(8,128)(2,1)}, u32[]{:S(2)}, u32[]{:S(2)}) collective-permute-start(bf16[4,2,32,1024]{3,2,1,0:T(8,128)(2,1)} %collective-permute-done.5.refs_4_), channel_id=1, source_target_pairs={{0,2},{1,7},{2,4},{3,1},{4,6},{5,3},{6,0},{7,5},{16,18},{17,23},{1... | collective-permute-start | bytes 1572872 | tf_op jit(solution)/shard_map/a_x1/ppermute | solution.py:30
  34.9 1.4 %collective-permute-done.16.refs_21_ = bf16[4,2,64,512]{3,2,1,0:T(8,128)(2,1)S(1)} collective-permute-done((bf16[4,2,64,512]{3,2,1,0:T(8,128)(2,1)S(1)}, bf16[4,2,64,512]{3,2,1,0:T(8,128)(2,1)S(1)}, u32[]{:S(2)}, u32[]{:S(2)}) %collective-permute-start.16) | collective-permute-done | bytes 524320 | tf_op jit(solution)/shard_map/b_x1/ppermute | solution.py:30
  36.3 2.2 %collective-permute-start.17 = (bf16[4,2,64,512]{3,2,1,0:T(8,128)(2,1)S(1)}, bf16[4,2,64,512]{3,2,1,0:T(8,128)(2,1)S(1)}, u32[]{:S(2)}, u32[]{:S(2)}) collective-permute-start(bf16[4,2,64,512]{3,2,1,0:T(8,128)(2,1)S(1)} %collective-permute-done.16.refs_21_), channel_id=1, source_target_pairs={{0,16},{1,49},{2,18},{3,51},{4,20},{5,53},{6,22},{7,55},{16,32},{1... | collective-permute-start | bytes 1572872 | tf_op jit(solution)/shard_map/b_x2/ppermute | solution.py:30
  38.5 0.0 collective-permute-done.2.refs_3_
  38.5 0.0 collective-permute-start.8
  38.5 3.4 %collective-permute-done.14.refs_18_ = bf16[4,2,64,512]{3,2,1,0:T(8,128)(2,1)S(1)} collective-permute-done((bf16[4,2,64,512]{3,2,1,0:T(8,128)(2,1)S(1)}, bf16[4,2,64,512]{3,2,1,0:T(8,128)(2,1)S(1)}, u32[]{:S(2)}, u32[]{:S(2)}) %collective-permute-start.14) | collective-permute-done | bytes 524320 | tf_op jit(solution)/shard_map/b_2/ppermute | solution.py:30
  41.9 0.7 collective-permute-start.15
  42.6 4.4 %collective-permute-done.7.refs_6_ = bf16[4,2,32,1024]{3,2,1,0:T(8,128)(2,1)} collective-permute-done((bf16[4,2,32,1024]{3,2,1,0:T(8,128)(2,1)S(1)}, bf16[4,2,32,1024]{3,2,1,0:T(8,128)(2,1)}, u32[]{:S(2)}, u32[]{:S(2)}) %collective-permute-start.7) | collective-permute-done | bytes 524320 | tf_op jit(solution)/shard_map/a_x2/ppermute | solution.py:30
  47.0 0.4 collective-permute-start.10
  47.4 0.0 collective-permute-done.6.refs_5_
  47.4 0.1 collective-permute-start.11
  47.5 0.0 collective-permute-done.17.refs_22_
  47.5 0.8 %collective-permute-start.20 = (bf16[4,2,32,1024]{3,2,1,0:T(8,128)(2,1)}, bf16[4,2,32,1024]{3,2,1,0:T(8,128)(2,1)}, u32[]{:S(2)}, u32[]{:S(2)}) collective-permute-start(bf16[4,2,32,1024]{3,2,1,0:T(8,128)(2,1)} %collective-permute-done.7.refs_6_), channel_id=1, source_target_pairs={{0,1},{1,0},{2,3},{3,2},{4,5},{5,4},{6,7},{7,6},{16,17},{17,16},{1... | collective-permute-start | bytes 1572872 | tf_op jit(solution)/shard_map/other_x2/ppermute | solution.py:30
  48.4 1.6 %collective-permute-done.8.refs_7_ = bf16[4,2,32,1024]{3,2,1,0:T(8,128)(2,1)} collective-permute-done((bf16[4,2,32,1024]{3,2,1,0:T(8,128)(2,1)}, bf16[4,2,32,1024]{3,2,1,0:T(8,128)(2,1)}, u32[]{:S(2)}, u32[]{:S(2)}) %collective-permute-start.8) | collective-permute-done | bytes 524320 | tf_op jit(solution)/shard_map/a_x3/ppermute | solution.py:30
  50.0 1.3 %collective-permute-start.22 = (bf16[4,2,64,512]{3,2,1,0:T(8,128)(2,1)S(1)}, bf16[4,2,64,512]{3,2,1,0:T(8,128)(2,1)}, u32[]{:S(2)}, u32[]{:S(2)}) collective-permute-start(bf16[4,2,64,512]{3,2,1,0:T(8,128)(2,1)S(1)} %collective-permute-done.4.refs_20_), channel_id=1, source_target_pairs={{0,48},{1,17},{2,50},{3,19},{4,52},{5,21},{6,54},{7,23},{16,0},{17... | collective-permute-start | bytes 1572872 | tf_op jit(solution)/shard_map/b_x3/ppermute | solution.py:30
  51.3 0.0 collective-permute-done.15.refs_11_
  51.3 4.6 %collective-permute-start.19 = (bf16[4,2,32,1024]{3,2,1,0:T(8,128)(2,1)}, bf16[4,2,32,1024]{3,2,1,0:T(8,128)(2,1)}, u32[]{:S(2)}, u32[]{:S(2)}) collective-permute-start(bf16[4,2,32,1024]{3,2,1,0:T(8,128)(2,1)} %collective-permute-done.6.refs_5_), channel_id=1, source_target_pairs={{0,1},{1,0},{2,3},{3,2},{4,5},{5,4},{6,7},{7,6},{16,17},{17,16},{1... | collective-permute-start | bytes 1572872 | tf_op jit(solution)/shard_map/other_x1/ppermute | solution.py:30
  55.9 0.0 collective-permute-done.10.refs_9_
  55.9 0.1 collective-permute-start.21
  56.0 0.0 collective-permute-done.11.refs_10_
  56.0 0.5 collective-permute-start.18
  56.5 0.2 copy-done.11
  56.7 0.2 copy-done.12
  56.9 1.3 %fusion.1 = (s32[12]{0:T(128)}, s32[12]{0:T(128)S(1)}) fusion(pred[]{:T(512)S(6)} %eq.18, s32[]{:T(128)S(6)} %select_n.83, s32[]{:T(128)S(6)} %select_n.80, s32[12]{0:T(128)} %param.5), kind=kLoop, calls=%fused_computation.25 | loop fusion | flops 612 | bytes 153 | tf_op jit(solution)/shard_map/add | solution.py:148
  58.2 1.2 %broadcast_multiply_fusion = (s32[12]{0:T(128)}, s32[12]{0:T(128)}) fusion(s32[12]{0:T(128)} %param.5, s32[12]{0:T(128)S(1)} %get-tuple-element.32, s32[]{:T(128)S(6)} %select_n.75, s32[]{:T(128)S(6)} %select_n.73, s32[]{:T(128)S(6)} %select_n.71), kind=kLoop, calls=%fused_computation.29 | loop fusion | flops 684 | bytes 204 | tf_op jit(solution)/shard_map/mul | solution.py:149
  59.5 0.0 collective-permute-done.20.refs_14_
  59.5 2.4 %collective-permute-done.22.refs_23_ = bf16[4,2,64,512]{3,2,1,0:T(8,128)(2,1)} collective-permute-done((bf16[4,2,64,512]{3,2,1,0:T(8,128)(2,1)S(1)}, bf16[4,2,64,512]{3,2,1,0:T(8,128)(2,1)}, u32[]{:S(2)}, u32[]{:S(2)}) %collective-permute-start.22) | collective-permute-done | bytes 524320 | tf_op jit(solution)/shard_map/b_x3/ppermute | solution.py:30
  61.9 11.8 %shard_map.37 = bf16[4,2,1024,512]{3,2,1,0:T(8,128)(2,1)} custom-call(s32[12]{0:T(128)} %get-tuple-element.34.a_where, s32[12]{0:T(128)} %get-tuple-element.31.b_where, s32[12]{0:T(128)} %get-tuple-element.33.b_row, bf16[4,2,32,1024]{3,2,1,0:T(8,128)(2,1)} %refs_0_.1, bf16[4,2,32,1024]{3,2,1,0:T(8,128)(2,1)} %copy-done, bf16[4,2,32,1024]{3,2,1,0:T(8,128)(2,1)} %copy-done.3, ...), custom_call_target="tpu_custom_call" | custom-call | flops 6442450944 | bytes 20971520 | tf_op jit(solution)/shard_map/pallas_call | solution.py:113
  (27 shorter events, 0.1 us)
Async XLA Ops:
  0.0 9.8 %collective-permute-start.3 = (bf16[4,2,64,512]{3,2,1,0:T(8,128)(2,1)}, bf16[4,2,64,512]{3,2,1,0:T(8,128)(2,1)S(1)}, u32[]{:S(2)}, u32[]{:S(2)}) collective-permute-start(bf16[4,2,64,512]{3,2,1,0:T(8,128)(2,1)} %refs_16_.1), channel_id=1, source_target_pairs={{0,8},{1,73},{2,10},{3,75},{4,12},{5,77},{6,14},{7,79},{16,24},{17... | collective-permute-start | bytes 1572872 | tf_op jit(solution)/shard_map/b_hop/ppermute | solution.py:30
  3.3 10.2 %collective-permute-start = (bf16[4,2,32,1024]{3,2,1,0:T(8,128)(2,1)}, bf16[4,2,32,1024]{3,2,1,0:T(8,128)(2,1)S(1)}, u32[]{:S(2)}, u32[]{:S(2)}) collective-permute-start(bf16[4,2,32,1024]{3,2,1,0:T(8,128)(2,1)} %refs_0_.1), channel_id=1, source_target_pairs={{0,2},{1,7},{2,4},{3,1},{4,6},{5,3},{6,0},{7,5},{16,18},{17,23},{1... | collective-permute-start | bytes 1572872 | tf_op jit(solution)/shard_map/a_1/ppermute | solution.py:30
  7.1 12.2 %collective-permute-start.9 = (bf16[4,2,32,1024]{3,2,1,0:T(8,128)(2,1)}, bf16[4,2,32,1024]{3,2,1,0:T(8,128)(2,1)S(1)}, u32[]{:S(2)}, u32[]{:S(2)}) collective-permute-start(bf16[4,2,32,1024]{3,2,1,0:T(8,128)(2,1)} %refs_0_.1), channel_id=1, source_target_pairs={{0,1},{1,0},{2,3},{3,2},{4,5},{5,4},{6,7},{7,6},{16,17},{17,16},{1... | collective-permute-start | bytes 1572872 | tf_op jit(solution)/shard_map/other/ppermute | solution.py:30
  9.8 9.5 %collective-permute-start.4 = (bf16[4,2,64,512]{3,2,1,0:T(8,128)(2,1)S(1)}, bf16[4,2,64,512]{3,2,1,0:T(8,128)(2,1)S(1)}, u32[]{:S(2)}, u32[]{:S(2)}) collective-permute-start(bf16[4,2,64,512]{3,2,1,0:T(8,128)(2,1)S(1)} %collective-permute-done.3), channel_id=1, source_target_pairs={{0,8},{1,73},{2,10},{3,75},{4,12},{5,77},{6,14},{7,79},{16,24},{17... | collective-permute-start | bytes 1572872 | tf_op jit(solution)/shard_map/b_x/ppermute | solution.py:30
  13.5 48.4 %copy-start = (bf16[4,2,32,1024]{3,2,1,0:T(8,128)(2,1)}, bf16[4,2,32,1024]{3,2,1,0:T(8,128)(2,1)S(1)}, u32[]{:S(2)}) copy-start(bf16[4,2,32,1024]{3,2,1,0:T(8,128)(2,1)S(1)} %collective-permute-done.refs_1_) | copy-start | bytes 1572868
  13.5 9.1 %collective-permute-start.1 = (bf16[4,2,32,1024]{3,2,1,0:T(8,128)(2,1)S(1)}, bf16[4,2,32,1024]{3,2,1,0:T(8,128)(2,1)S(1)}, u32[]{:S(2)}, u32[]{:S(2)}) collective-permute-start(bf16[4,2,32,1024]{3,2,1,0:T(8,128)(2,1)S(1)} %collective-permute-done.refs_1_), channel_id=1, source_target_pairs={{0,2},{1,7},{2,4},{3,1},{4,6},{5,3},{6,0},{7,5},{16,18},{17,23},{1... | collective-permute-start | bytes 1572872 | tf_op jit(solution)/shard_map/a_2/ppermute | solution.py:30
  16.5 14.2 %collective-permute-start.12 = (bf16[4,2,64,512]{3,2,1,0:T(8,128)(2,1)}, bf16[4,2,64,512]{3,2,1,0:T(8,128)(2,1)S(1)}, u32[]{:S(2)}, u32[]{:S(2)}) collective-permute-start(bf16[4,2,64,512]{3,2,1,0:T(8,128)(2,1)} %refs_16_.1), channel_id=1, source_target_pairs={{0,16},{1,49},{2,18},{3,51},{4,20},{5,53},{6,22},{7,55},{16,32},{1... | collective-permute-start | bytes 1572872 | tf_op jit(solution)/shard_map/b_1/ppermute | solution.py:30
  19.3 42.6 %copy-start.1 = (bf16[4,2,32,1024]{3,2,1,0:T(8,128)(2,1)}, bf16[4,2,32,1024]{3,2,1,0:T(8,128)(2,1)S(1)}, u32[]{:S(2)}) copy-start(bf16[4,2,32,1024]{3,2,1,0:T(8,128)(2,1)S(1)} %collective-permute-done.9.refs_8_) | copy-start | bytes 1572868
  19.3 11.5 %collective-permute-start.13 = (bf16[4,2,64,512]{3,2,1,0:T(8,128)(2,1)}, bf16[4,2,64,512]{3,2,1,0:T(8,128)(2,1)S(1)}, u32[]{:S(2)}, u32[]{:S(2)}) collective-permute-start(bf16[4,2,64,512]{3,2,1,0:T(8,128)(2,1)} %refs_16_.1), channel_id=1, source_target_pairs={{0,48},{1,17},{2,50},{3,19},{4,52},{5,21},{6,54},{7,23},{16,0},{17... | collective-permute-start | bytes 1572872 | tf_op jit(solution)/shard_map/b_3/ppermute | solution.py:30
  19.3 42.6 %copy-start.2 = (bf16[4,2,64,512]{3,2,1,0:T(8,128)(2,1)}, bf16[4,2,64,512]{3,2,1,0:T(8,128)(2,1)S(1)}, u32[]{:S(2)}) copy-start(bf16[4,2,64,512]{3,2,1,0:T(8,128)(2,1)S(1)} %collective-permute-done.4.refs_20_) | copy-start | bytes 1572868
  19.3 13.7 %collective-permute-start.5 = (bf16[4,2,32,1024]{3,2,1,0:T(8,128)(2,1)}, bf16[4,2,32,1024]{3,2,1,0:T(8,128)(2,1)}, u32[]{:S(2)}, u32[]{:S(2)}) collective-permute-start(bf16[4,2,32,1024]{3,2,1,0:T(8,128)(2,1)} %refs_0_.1), channel_id=1, source_target_pairs={{0,8},{1,9},{2,10},{3,11},{4,12},{5,13},{6,14},{7,15},{16,24},{17,... | collective-permute-start | bytes 1572872 | tf_op jit(solution)/shard_map/a_x/ppermute | solution.py:30
  22.7 39.3 %copy-start.3 = (bf16[4,2,32,1024]{3,2,1,0:T(8,128)(2,1)}, bf16[4,2,32,1024]{3,2,1,0:T(8,128)(2,1)S(1)}, u32[]{:S(2)}) copy-start(bf16[4,2,32,1024]{3,2,1,0:T(8,128)(2,1)S(1)} %collective-permute-done.1.refs_2_) | copy-start | bytes 1572868
  22.7 15.9 %collective-permute-start.2 = (bf16[4,2,32,1024]{3,2,1,0:T(8,128)(2,1)}, bf16[4,2,32,1024]{3,2,1,0:T(8,128)(2,1)S(1)}, u32[]{:S(2)}, u32[]{:S(2)}) collective-permute-start(bf16[4,2,32,1024]{3,2,1,0:T(8,128)(2,1)} %refs_0_.1), channel_id=1, source_target_pairs={{0,6},{1,3},{2,0},{3,5},{4,2},{5,7},{6,4},{7,1},{16,22},{17,19},{1... | collective-permute-start | bytes 1572872 | tf_op jit(solution)/shard_map/a_3/ppermute | solution.py:30
  22.9 13.4 %collective-permute-start.16 = (bf16[4,2,64,512]{3,2,1,0:T(8,128)(2,1)S(1)}, bf16[4,2,64,512]{3,2,1,0:T(8,128)(2,1)S(1)}, u32[]{:S(2)}, u32[]{:S(2)}) collective-permute-start(bf16[4,2,64,512]{3,2,1,0:T(8,128)(2,1)S(1)} %collective-permute-done.4.refs_20_), channel_id=1, source_target_pairs={{0,16},{1,49},{2,18},{3,51},{4,20},{5,53},{6,22},{7,55},{16,32},{1... | collective-permute-start | bytes 1572872 | tf_op jit(solution)/shard_map/b_x1/ppermute | solution.py:30
  30.7 31.2 %copy-start.4 = (bf16[4,2,64,512]{3,2,1,0:T(8,128)(2,1)}, bf16[4,2,64,512]{3,2,1,0:T(8,128)(2,1)S(1)}, u32[]{:S(2)}) copy-start(bf16[4,2,64,512]{3,2,1,0:T(8,128)(2,1)S(1)} %collective-permute-done.12.refs_17_) | copy-start | bytes 1572868
  30.7 31.2 %copy-start.5 = (bf16[4,2,64,512]{3,2,1,0:T(8,128)(2,1)}, bf16[4,2,64,512]{3,2,1,0:T(8,128)(2,1)S(1)}, u32[]{:S(2)}) copy-start(bf16[4,2,64,512]{3,2,1,0:T(8,128)(2,1)S(1)} %collective-permute-done.13.refs_19_) | copy-start | bytes 1572868
  30.7 11.2 %collective-permute-start.14 = (bf16[4,2,64,512]{3,2,1,0:T(8,128)(2,1)S(1)}, bf16[4,2,64,512]{3,2,1,0:T(8,128)(2,1)S(1)}, u32[]{:S(2)}, u32[]{:S(2)}) collective-permute-start(bf16[4,2,64,512]{3,2,1,0:T(8,128)(2,1)S(1)} %collective-permute-done.12.refs_17_), channel_id=1, source_target_pairs={{0,16},{1,49},{2,18},{3,51},{4,20},{5,53},{6,22},{7,55},{16,32},{1... | collective-permute-start | bytes 1572872 | tf_op jit(solution)/shard_map/b_2/ppermute | solution.py:30
  33.0 14.0 %collective-permute-start.7 = (bf16[4,2,32,1024]{3,2,1,0:T(8,128)(2,1)S(1)}, bf16[4,2,32,1024]{3,2,1,0:T(8,128)(2,1)}, u32[]{:S(2)}, u32[]{:S(2)}) collective-permute-start(bf16[4,2,32,1024]{3,2,1,0:T(8,128)(2,1)S(1)} %collective-permute-done.1.refs_2_), channel_id=1, source_target_pairs={{0,8},{1,9},{2,10},{3,11},{4,12},{5,13},{6,14},{7,15},{16,24},{17,... | collective-permute-start | bytes 1572872 | tf_op jit(solution)/shard_map/a_x2/ppermute | solution.py:30
  33.0 14.4 %collective-permute-start.6 = (bf16[4,2,32,1024]{3,2,1,0:T(8,128)(2,1)}, bf16[4,2,32,1024]{3,2,1,0:T(8,128)(2,1)}, u32[]{:S(2)}, u32[]{:S(2)}) collective-permute-start(bf16[4,2,32,1024]{3,2,1,0:T(8,128)(2,1)} %collective-permute-done.5.refs_4_), channel_id=1, source_target_pairs={{0,2},{1,7},{2,4},{3,1},{4,6},{5,3},{6,0},{7,5},{16,18},{17,23},{1... | collective-permute-start | bytes 1572872 | tf_op jit(solution)/shard_map/a_x1/ppermute | solution.py:30
  36.3 20.2 %copy-start.7 = (bf16[4,2,64,512]{3,2,1,0:T(8,128)(2,1)}, bf16[4,2,64,512]{3,2,1,0:T(8,128)(2,1)S(1)}, u32[]{:S(2)}) copy-start(bf16[4,2,64,512]{3,2,1,0:T(8,128)(2,1)S(1)} %collective-permute-done.16.refs_21_) | copy-start | bytes 1572868
  36.3 11.2 %collective-permute-start.17 = (bf16[4,2,64,512]{3,2,1,0:T(8,128)(2,1)S(1)}, bf16[4,2,64,512]{3,2,1,0:T(8,128)(2,1)S(1)}, u32[]{:S(2)}, u32[]{:S(2)}) collective-permute-start(bf16[4,2,64,512]{3,2,1,0:T(8,128)(2,1)S(1)} %collective-permute-done.16.refs_21_), channel_id=1, source_target_pairs={{0,16},{1,49},{2,18},{3,51},{4,20},{5,53},{6,22},{7,55},{16,32},{1... | collective-permute-start | bytes 1572872 | tf_op jit(solution)/shard_map/b_x2/ppermute | solution.py:30
  38.5 17.5 %copy-start.6 = (bf16[4,2,32,1024]{3,2,1,0:T(8,128)(2,1)}, bf16[4,2,32,1024]{3,2,1,0:T(8,128)(2,1)S(1)}, u32[]{:S(2)}) copy-start(bf16[4,2,32,1024]{3,2,1,0:T(8,128)(2,1)S(1)} %collective-permute-done.2.refs_3_) | copy-start | bytes 1572868
  38.5 11.5 %collective-permute-start.8 = (bf16[4,2,32,1024]{3,2,1,0:T(8,128)(2,1)}, bf16[4,2,32,1024]{3,2,1,0:T(8,128)(2,1)}, u32[]{:S(2)}, u32[]{:S(2)}) collective-permute-start(bf16[4,2,32,1024]{3,2,1,0:T(8,128)(2,1)} %collective-permute-done.5.refs_4_), channel_id=1, source_target_pairs={{0,6},{1,3},{2,0},{3,5},{4,2},{5,7},{6,4},{7,1},{16,22},{17,19},{1... | collective-permute-start | bytes 1572872 | tf_op jit(solution)/shard_map/a_x3/ppermute | solution.py:30
  41.9 14.6 %copy-start.8 = (bf16[4,2,64,512]{3,2,1,0:T(8,128)(2,1)}, bf16[4,2,64,512]{3,2,1,0:T(8,128)(2,1)S(1)}, u32[]{:S(2)}) copy-start(bf16[4,2,64,512]{3,2,1,0:T(8,128)(2,1)S(1)} %collective-permute-done.14.refs_18_) | copy-start | bytes 1572868
  41.9 9.3 %collective-permute-start.15 = (bf16[4,2,32,1024]{3,2,1,0:T(8,128)(2,1)S(1)}, bf16[4,2,32,1024]{3,2,1,0:T(8,128)(2,1)S(1)}, u32[]{:S(2)}, u32[]{:S(2)}) collective-permute-start(bf16[4,2,32,1024]{3,2,1,0:T(8,128)(2,1)S(1)} %collective-permute-done.2.refs_3_), channel_id=1, source_target_pairs={{0,1},{1,0},{2,3},{3,2},{4,5},{5,4},{6,7},{7,6},{16,17},{17,16},{1... | collective-permute-start | bytes 1572872 | tf_op jit(solution)/shard_map/other_3/ppermute | solution.py:30
  47.0 8.9 %collective-permute-start.10 = (bf16[4,2,32,1024]{3,2,1,0:T(8,128)(2,1)S(1)}, bf16[4,2,32,1024]{3,2,1,0:T(8,128)(2,1)S(1)}, u32[]{:S(2)}, u32[]{:S(2)}) collective-permute-start(bf16[4,2,32,1024]{3,2,1,0:T(8,128)(2,1)S(1)} %collective-permute-done.refs_1_), channel_id=1, source_target_pairs={{0,1},{1,0},{2,3},{3,2},{4,5},{5,4},{6,7},{7,6},{16,17},{17,16},{1... | collective-permute-start | bytes 1572872 | tf_op jit(solution)/shard_map/other_1/ppermute | solution.py:30
  47.4 8.6 %collective-permute-start.11 = (bf16[4,2,32,1024]{3,2,1,0:T(8,128)(2,1)S(1)}, bf16[4,2,32,1024]{3,2,1,0:T(8,128)(2,1)S(1)}, u32[]{:S(2)}, u32[]{:S(2)}) collective-permute-start(bf16[4,2,32,1024]{3,2,1,0:T(8,128)(2,1)S(1)} %collective-permute-done.1.refs_2_), channel_id=1, source_target_pairs={{0,1},{1,0},{2,3},{3,2},{4,5},{5,4},{6,7},{7,6},{16,17},{17,16},{1... | collective-permute-start | bytes 1572872 | tf_op jit(solution)/shard_map/other_2/ppermute | solution.py:30
  47.5 9.0 %copy-start.9 = (bf16[4,2,64,512]{3,2,1,0:T(8,128)(2,1)}, bf16[4,2,64,512]{3,2,1,0:T(8,128)(2,1)S(1)}, u32[]{:S(2)}) copy-start(bf16[4,2,64,512]{3,2,1,0:T(8,128)(2,1)S(1)} %collective-permute-done.17.refs_22_) | copy-start | bytes 1572868
  47.5 11.9 %collective-permute-start.20 = (bf16[4,2,32,1024]{3,2,1,0:T(8,128)(2,1)}, bf16[4,2,32,1024]{3,2,1,0:T(8,128)(2,1)}, u32[]{:S(2)}, u32[]{:S(2)}) collective-permute-start(bf16[4,2,32,1024]{3,2,1,0:T(8,128)(2,1)} %collective-permute-done.7.refs_6_), channel_id=1, source_target_pairs={{0,1},{1,0},{2,3},{3,2},{4,5},{5,4},{6,7},{7,6},{16,17},{17,16},{1... | collective-permute-start | bytes 1572872 | tf_op jit(solution)/shard_map/other_x2/ppermute | solution.py:30
  50.0 11.9 %collective-permute-start.22 = (bf16[4,2,64,512]{3,2,1,0:T(8,128)(2,1)S(1)}, bf16[4,2,64,512]{3,2,1,0:T(8,128)(2,1)}, u32[]{:S(2)}, u32[]{:S(2)}) collective-permute-start(bf16[4,2,64,512]{3,2,1,0:T(8,128)(2,1)S(1)} %collective-permute-done.4.refs_20_), channel_id=1, source_target_pairs={{0,48},{1,17},{2,50},{3,19},{4,52},{5,21},{6,54},{7,23},{16,0},{17... | collective-permute-start | bytes 1572872 | tf_op jit(solution)/shard_map/b_x3/ppermute | solution.py:30
  51.3 5.2 %copy-start.10 = (bf16[4,2,32,1024]{3,2,1,0:T(8,128)(2,1)}, bf16[4,2,32,1024]{3,2,1,0:T(8,128)(2,1)S(1)}, u32[]{:S(2)}) copy-start(bf16[4,2,32,1024]{3,2,1,0:T(8,128)(2,1)S(1)} %collective-permute-done.15.refs_11_) | copy-start | bytes 1572868
  51.3 10.6 %collective-permute-start.19 = (bf16[4,2,32,1024]{3,2,1,0:T(8,128)(2,1)}, bf16[4,2,32,1024]{3,2,1,0:T(8,128)(2,1)}, u32[]{:S(2)}, u32[]{:S(2)}) collective-permute-start(bf16[4,2,32,1024]{3,2,1,0:T(8,128)(2,1)} %collective-permute-done.6.refs_5_), channel_id=1, source_target_pairs={{0,1},{1,0},{2,3},{3,2},{4,5},{5,4},{6,7},{7,6},{16,17},{17,16},{1... | collective-permute-start | bytes 1572872 | tf_op jit(solution)/shard_map/other_x1/ppermute | solution.py:30
  55.9 0.8 %copy-start.11 = (bf16[4,2,32,1024]{3,2,1,0:T(8,128)(2,1)}, bf16[4,2,32,1024]{3,2,1,0:T(8,128)(2,1)S(1)}, u32[]{:S(2)}) copy-start(bf16[4,2,32,1024]{3,2,1,0:T(8,128)(2,1)S(1)} %collective-permute-done.10.refs_9_) | copy-start | bytes 1572868
  55.9 6.0 %collective-permute-start.21 = (bf16[4,2,32,1024]{3,2,1,0:T(8,128)(2,1)}, bf16[4,2,32,1024]{3,2,1,0:T(8,128)(2,1)}, u32[]{:S(2)}, u32[]{:S(2)}) collective-permute-start(bf16[4,2,32,1024]{3,2,1,0:T(8,128)(2,1)} %collective-permute-done.8.refs_7_), channel_id=1, source_target_pairs={{0,1},{1,0},{2,3},{3,2},{4,5},{5,4},{6,7},{7,6},{16,17},{17,16},{1... | collective-permute-start | bytes 1572872 | tf_op jit(solution)/shard_map/other_x3/ppermute | solution.py:30
  56.0 0.9 %copy-start.12 = (bf16[4,2,32,1024]{3,2,1,0:T(8,128)(2,1)}, bf16[4,2,32,1024]{3,2,1,0:T(8,128)(2,1)S(1)}, u32[]{:S(2)}) copy-start(bf16[4,2,32,1024]{3,2,1,0:T(8,128)(2,1)S(1)} %collective-permute-done.11.refs_10_) | copy-start | bytes 1572868
  56.0 5.9 %collective-permute-start.18 = (bf16[4,2,32,1024]{3,2,1,0:T(8,128)(2,1)}, bf16[4,2,32,1024]{3,2,1,0:T(8,128)(2,1)}, u32[]{:S(2)}, u32[]{:S(2)}) collective-permute-start(bf16[4,2,32,1024]{3,2,1,0:T(8,128)(2,1)} %collective-permute-done.5.refs_4_), channel_id=1, source_target_pairs={{0,1},{1,0},{2,3},{3,2},{4,5},{5,4},{6,7},{7,6},{16,17},{17,16},{1... | collective-permute-start | bytes 1572872 | tf_op jit(solution)/shard_map/other_x/ppermute | solution.py:30

commit v2 on v1

--- a/solution.py
+++ b/solution.py
@@ -165,27 +165,27 @@
 
     b_hop = send("b_hop", b, dx=1)
     b_1 = send("b_1", b, dy=1)
+    b_3 = send("b_3", b, dy=-1)
     a_1 = send("a_1", a, dz=1)
     b_x = send("b_x", b_hop, dx=1)
-    a_x = send("a_x", after(a, b_x), flip_x=True)
+    b_2 = send("b_2", b_1, dy=1)
     a_2 = send("a_2", a_1, dz=1)
-    a_3 = send("a_3", after(a, a_2), dz=-1)
     b_x1 = send("b_x1", b_x, dy=1)
     b_x2 = send("b_x2", b_x1, dy=1)
-    a_x1 = send("a_x1", a_x, dz=1)
-    a_x3 = send("a_x3", after(a_x, a_2), dz=-1)
-    a_x2 = send("a_x2", a_2, flip_x=True)
+    a_x2 = send("a_x2", after(a_2, b_2), flip_x=True)
     other = swap("other", a)
-    b_3 = send("b_3", after(b, other), dy=-1)
-    b_2 = send("b_2", after(b_1, b_3, a_2), dy=1)
-    b_x3 = send("b_x3", after(b_x, b_2), dy=-1)
-    other_1 = swap("other_1", after(a_1, a_2))
-    other_2 = swap("other_2", after(a_2, a_3))
-    other_3 = swap("other_3", after(a_3, b_2))
-    other_x = swap("other_x", after(a_x, a_x3, b_x2, b_2))
-    other_x1 = swap("other_x1", after(a_x1, b_1))
+    a_x = send("a_x", after(a, other), flip_x=True)
+    other_1 = swap("other_1", after(a_1, b_3))
+    a_3 = send("a_3", after(a, other_1), dz=-1)
+    b_x3 = send("b_x3", after(b_x, a_3), dy=-1)
+    other_2 = swap("other_2", a_2)
+    a_x3 = send("a_x3", after(a_x, other_2), dz=-1)
+    other_3 = swap("other_3", a_3)
+    other_x = swap("other_x", a_x)
+    a_x1 = send("a_x1", after(a_x, other_x), dz=1)
+    other_x1 = swap("other_x1", after(a_x1, a_x2))
     other_x2 = swap("other_x2", after(a_x2, b_1))
-    other_x3 = swap("other_x3", after(a_x3, other_3))
+    other_x3 = swap("other_x3", a_x3)
 
     a_parts = [a, a_1, a_2, a_3, a_x, a_x1, a_x2, a_x3]
     a_parts += [other, other_1, other_2, other_3, other_x, other_x1, other_x2, other_x3]

time: 74.1 us -> 67.8 us (0.915)
  waiting for transfers between devices: 24.7 us -> 15.2 us
  starting transfers between devices: 34.1 us -> 37.8 us
    ppermute x23, waiting for transfers between devices: 24.7 us -> 15.2 us  [moved(): return lax.ppermute(value, AXES, pairs)]
    ppermute x23, starting transfers between devices: 34.1 us -> 37.8 us  [moved(): return lax.ppermute(value, AXES, pairs)]
  transfers between devices with their start and end apart: 23 -> 23, of which waited for: 9 -> 5; matrix products, arithmetic and copies ran while one was open for 3% -> 4% of each run, Pallas kernels for 0% -> 0%
where the time goes in v2:
time: 67.8 us; the launch traced here: 67.7 us
  starting transfers between devices  37.8 us (56%)
  waiting for transfers between devices  15.2 us (22%)
  Pallas kernels  12 us (18%)
  other arithmetic  2.52 us (4%)
    ppermute x23, starting transfers between devices, moved(): return lax.ppermute(value, AXES, pairs)  37.8 us
    ppermute x23, waiting for transfers between devices, moved(): return lax.ppermute(value, AXES, pairs)  15.2 us
    pallas_call x1, Pallas kernels, multiply(): pl.pallas_call(multiply_kernel, out_shape=jax.ShapeDtypeStruct((freqs, 2,...  12 us
  transfers between devices with their start and end apart: 23, of which 5 were waited for; matrix products, arithmetic and copies ran while one was open for 4% of the time, Pallas kernels for 0%

profile of v2, /device:TPU:1, one launch (start us, length us, event | category | flops | bytes accessed | tf_op | source)
XLA Modules:
  0.0 67.7 jit_solution(15431856678585314523)
XLA Ops:
  0.0 1.4 %collective-permute-start.5 = (bf16[4,2,32,1024]{3,2,1,0:T(8,128)(2,1)}, bf16[4,2,32,1024]{3,2,1,0:T(8,128)(2,1)S(1)}, u32[]{:S(2)}, u32[]{:S(2)}) collective-permute-start(bf16[4,2,32,1024]{3,2,1,0:T(8,128)(2,1)} %refs_0_.1), channel_id=1, source_target_pairs={{0,1},{1,0},{2,3},{3,2},{4,5},{5,4},{6,7},{7,6},{16,17},{17,16},{1... | collective-permute-start | bytes 1572872 | tf_op jit(solution)/shard_map/other/ppermute | solution.py:30
  1.4 2.6 %collective-permute-start.18 = (bf16[4,2,64,512]{3,2,1,0:T(8,128)(2,1)}, bf16[4,2,64,512]{3,2,1,0:T(8,128)(2,1)S(1)}, u32[]{:S(2)}, u32[]{:S(2)}) collective-permute-start(bf16[4,2,64,512]{3,2,1,0:T(8,128)(2,1)} %refs_16_.1), channel_id=1, source_target_pairs={{0,8},{1,73},{2,10},{3,75},{4,12},{5,77},{6,14},{7,79},{16,24},{17... | collective-permute-start | bytes 1572872 | tf_op jit(solution)/shard_map/b_hop/ppermute | solution.py:30
  4.0 3.8 %collective-permute-start = (bf16[4,2,32,1024]{3,2,1,0:T(8,128)(2,1)}, bf16[4,2,32,1024]{3,2,1,0:T(8,128)(2,1)S(1)}, u32[]{:S(2)}, u32[]{:S(2)}) collective-permute-start(bf16[4,2,32,1024]{3,2,1,0:T(8,128)(2,1)} %refs_0_.1), channel_id=1, source_target_pairs={{0,2},{1,7},{2,4},{3,1},{4,6},{5,3},{6,0},{7,5},{16,18},{17,23},{1... | collective-permute-start | bytes 1572872 | tf_op jit(solution)/shard_map/a_1/ppermute | solution.py:30
  7.7 1.3 %collective-permute-start.2 = (bf16[4,2,64,512]{3,2,1,0:T(8,128)(2,1)}, bf16[4,2,64,512]{3,2,1,0:T(8,128)(2,1)S(1)}, u32[]{:S(2)}, u32[]{:S(2)}) collective-permute-start(bf16[4,2,64,512]{3,2,1,0:T(8,128)(2,1)} %refs_16_.1), channel_id=1, source_target_pairs={{0,48},{1,17},{2,50},{3,19},{4,52},{5,21},{6,54},{7,23},{16,0},{17... | collective-permute-start | bytes 1572872 | tf_op jit(solution)/shard_map/b_3/ppermute | solution.py:30
  9.0 1.4 %collective-permute-start.9 = (bf16[4,2,64,512]{3,2,1,0:T(8,128)(2,1)}, bf16[4,2,64,512]{3,2,1,0:T(8,128)(2,1)S(1)}, u32[]{:S(2)}, u32[]{:S(2)}) collective-permute-start(bf16[4,2,64,512]{3,2,1,0:T(8,128)(2,1)} %refs_16_.1), channel_id=1, source_target_pairs={{0,16},{1,49},{2,18},{3,51},{4,20},{5,53},{6,22},{7,55},{16,32},{1... | collective-permute-start | bytes 1572872 | tf_op jit(solution)/shard_map/b_1/ppermute | solution.py:30
  10.5 0.0 collective-permute-done.5.refs_8_
  10.5 0.0 collective-permute-start.6
  10.5 0.0 collective-permute-done.18
  10.5 3.2 %collective-permute-start.19 = (bf16[4,2,64,512]{3,2,1,0:T(8,128)(2,1)S(1)}, bf16[4,2,64,512]{3,2,1,0:T(8,128)(2,1)S(1)}, u32[]{:S(2)}, u32[]{:S(2)}) collective-permute-start(bf16[4,2,64,512]{3,2,1,0:T(8,128)(2,1)S(1)} %collective-permute-done.18), channel_id=1, source_target_pairs={{0,8},{1,73},{2,10},{3,75},{4,12},{5,77},{6,14},{7,79},{16,24},{17... | collective-permute-start | bytes 1572872 | tf_op jit(solution)/shard_map/b_x/ppermute | solution.py:30
  13.7 0.5 collective-permute-done.refs_1_
  14.2 3.3 %collective-permute-start.1 = (bf16[4,2,32,1024]{3,2,1,0:T(8,128)(2,1)S(1)}, bf16[4,2,32,1024]{3,2,1,0:T(8,128)(2,1)S(1)}, u32[]{:S(2)}, u32[]{:S(2)}) collective-permute-start(bf16[4,2,32,1024]{3,2,1,0:T(8,128)(2,1)S(1)} %collective-permute-done.refs_1_), channel_id=1, source_target_pairs={{0,2},{1,7},{2,4},{3,1},{4,6},{5,3},{6,0},{7,5},{16,18},{17,23},{1... | collective-permute-start | bytes 1572872 | tf_op jit(solution)/shard_map/a_2/ppermute | solution.py:30
  17.5 5.1 %collective-permute-done.2.refs_19_ = bf16[4,2,64,512]{3,2,1,0:T(8,128)(2,1)S(1)} collective-permute-done((bf16[4,2,64,512]{3,2,1,0:T(8,128)(2,1)}, bf16[4,2,64,512]{3,2,1,0:T(8,128)(2,1)S(1)}, u32[]{:S(2)}, u32[]{:S(2)}) %collective-permute-start.2) | collective-permute-done | bytes 524320 | tf_op jit(solution)/shard_map/b_3/ppermute | solution.py:30
  22.6 0.0 collective-permute-start.3
  22.6 0.0 collective-permute-done.9.refs_17_
  22.7 0.8 %collective-permute-start.10 = (bf16[4,2,64,512]{3,2,1,0:T(8,128)(2,1)S(1)}, bf16[4,2,64,512]{3,2,1,0:T(8,128)(2,1)S(1)}, u32[]{:S(2)}, u32[]{:S(2)}) collective-permute-start(bf16[4,2,64,512]{3,2,1,0:T(8,128)(2,1)S(1)} %collective-permute-done.9.refs_17_), channel_id=1, source_target_pairs={{0,16},{1,49},{2,18},{3,51},{4,20},{5,53},{6,22},{7,55},{16,32},{1... | collective-permute-start | bytes 1572872 | tf_op jit(solution)/shard_map/b_2/ppermute | solution.py:30
  23.5 0.0 collective-permute-done.6.refs_4_
  23.5 0.2 collective-permute-start.7
  23.7 4.6 %collective-permute-done.19.refs_20_ = bf16[4,2,64,512]{3,2,1,0:T(8,128)(2,1)S(1)} collective-permute-done((bf16[4,2,64,512]{3,2,1,0:T(8,128)(2,1)S(1)}, bf16[4,2,64,512]{3,2,1,0:T(8,128)(2,1)S(1)}, u32[]{:S(2)}, u32[]{:S(2)}) %collective-permute-start.19) | collective-permute-done | bytes 524320 | tf_op jit(solution)/shard_map/b_x/ppermute | solution.py:30
  28.3 2.9 %collective-permute-start.20 = (bf16[4,2,64,512]{3,2,1,0:T(8,128)(2,1)S(1)}, bf16[4,2,64,512]{3,2,1,0:T(8,128)(2,1)S(1)}, u32[]{:S(2)}, u32[]{:S(2)}) collective-permute-start(bf16[4,2,64,512]{3,2,1,0:T(8,128)(2,1)S(1)} %collective-permute-done.19.refs_20_), channel_id=1, source_target_pairs={{0,16},{1,49},{2,18},{3,51},{4,20},{5,53},{6,22},{7,55},{16,32},{1... | collective-permute-start | bytes 1572872 | tf_op jit(solution)/shard_map/b_x1/ppermute | solution.py:30
  31.1 0.0 collective-permute-done.1.refs_2_
  31.1 0.0 collective-permute-start.12
  31.1 0.0 collective-permute-done.3.refs_9_
  31.2 0.2 collective-permute-start.4
  31.4 0.0 collective-permute-done.10.refs_18_
  31.4 0.8 %collective-permute-start.11 = (bf16[4,2,32,1024]{3,2,1,0:T(8,128)(2,1)S(1)}, bf16[4,2,32,1024]{3,2,1,0:T(8,128)(2,1)}, u32[]{:S(2)}, u32[]{:S(2)}) collective-permute-start(bf16[4,2,32,1024]{3,2,1,0:T(8,128)(2,1)S(1)} %collective-permute-done.1.refs_2_), channel_id=1, source_target_pairs={{0,8},{1,9},{2,10},{3,11},{4,12},{5,13},{6,14},{7,15},{16,24},{17,... | collective-permute-start | bytes 1572872 | tf_op jit(solution)/shard_map/a_x2/ppermute | solution.py:30
  32.2 0.0 collective-permute-done.7.refs_12_
  32.2 2.2 %collective-permute-start.8 = (bf16[4,2,32,1024]{3,2,1,0:T(8,128)(2,1)S(1)}, bf16[4,2,32,1024]{3,2,1,0:T(8,128)(2,1)}, u32[]{:S(2)}, u32[]{:S(2)}) collective-permute-start(bf16[4,2,32,1024]{3,2,1,0:T(8,128)(2,1)S(1)} %collective-permute-done.6.refs_4_), channel_id=1, source_target_pairs={{0,2},{1,7},{2,4},{3,1},{4,6},{5,3},{6,0},{7,5},{16,18},{17,23},{1... | collective-permute-start | bytes 1572872 | tf_op jit(solution)/shard_map/a_x1/ppermute | solution.py:30
  34.4 2.8 %collective-permute-done.20.refs_21_ = bf16[4,2,64,512]{3,2,1,0:T(8,128)(2,1)S(1)} collective-permute-done((bf16[4,2,64,512]{3,2,1,0:T(8,128)(2,1)S(1)}, bf16[4,2,64,512]{3,2,1,0:T(8,128)(2,1)S(1)}, u32[]{:S(2)}, u32[]{:S(2)}) %collective-permute-start.20) | collective-permute-done | bytes 524320 | tf_op jit(solution)/shard_map/b_x1/ppermute | solution.py:30
  37.3 3.1 %collective-permute-start.21 = (bf16[4,2,64,512]{3,2,1,0:T(8,128)(2,1)S(1)}, bf16[4,2,64,512]{3,2,1,0:T(8,128)(2,1)S(1)}, u32[]{:S(2)}, u32[]{:S(2)}) collective-permute-start(bf16[4,2,64,512]{3,2,1,0:T(8,128)(2,1)S(1)} %collective-permute-done.20.refs_21_), channel_id=1, source_target_pairs={{0,16},{1,49},{2,18},{3,51},{4,20},{5,53},{6,22},{7,55},{16,32},{1... | collective-permute-start | bytes 1572872 | tf_op jit(solution)/shard_map/b_x2/ppermute | solution.py:30
  40.4 0.0 collective-permute-done.12.refs_10_
  40.4 0.1 collective-permute-start.13
  40.5 2.1 %collective-permute-done.4.refs_3_ = bf16[4,2,32,1024]{3,2,1,0:T(8,128)(2,1)} collective-permute-done((bf16[4,2,32,1024]{3,2,1,0:T(8,128)(2,1)}, bf16[4,2,32,1024]{3,2,1,0:T(8,128)(2,1)}, u32[]{:S(2)}, u32[]{:S(2)}) %collective-permute-start.4) | collective-permute-done | bytes 524320 | tf_op jit(solution)/shard_map/a_3/ppermute | solution.py:30
  42.6 0.0 collective-permute-start.22
  42.6 0.0 collective-permute-done.11.refs_6_
  42.6 4.2 %collective-permute-start.16 = (bf16[4,2,32,1024]{3,2,1,0:T(8,128)(2,1)}, bf16[4,2,32,1024]{3,2,1,0:T(8,128)(2,1)}, u32[]{:S(2)}, u32[]{:S(2)}) collective-permute-start(bf16[4,2,32,1024]{3,2,1,0:T(8,128)(2,1)} %collective-permute-done.11.refs_6_), channel_id=1, source_target_pairs={{0,1},{1,0},{2,3},{3,2},{4,5},{5,4},{6,7},{7,6},{16,17},{17,16},{1... | collective-permute-start | bytes 1572872 | tf_op jit(solution)/shard_map/other_x2/ppermute | solution.py:30
  46.9 0.0 collective-permute-done.8.refs_5_
  46.9 2.5 %collective-permute-start.14 = (bf16[4,2,32,1024]{3,2,1,0:T(8,128)(2,1)}, bf16[4,2,32,1024]{3,2,1,0:T(8,128)(2,1)}, u32[]{:S(2)}, u32[]{:S(2)}) collective-permute-start(bf16[4,2,32,1024]{3,2,1,0:T(8,128)(2,1)} %collective-permute-done.4.refs_3_), channel_id=1, source_target_pairs={{0,1},{1,0},{2,3},{3,2},{4,5},{5,4},{6,7},{7,6},{16,17},{17,16},{1... | collective-permute-start | bytes 1572872 | tf_op jit(solution)/shard_map/other_3/ppermute | solution.py:30
  49.3 0.0 collective-permute-done.21.refs_22_
  49.3 3.6 %collective-permute-start.15 = (bf16[4,2,32,1024]{3,2,1,0:T(8,128)(2,1)}, bf16[4,2,32,1024]{3,2,1,0:T(8,128)(2,1)}, u32[]{:S(2)}, u32[]{:S(2)}) collective-permute-start(bf16[4,2,32,1024]{3,2,1,0:T(8,128)(2,1)} %collective-permute-done.8.refs_5_), channel_id=1, source_target_pairs={{0,1},{1,0},{2,3},{3,2},{4,5},{5,4},{6,7},{7,6},{16,17},{17,16},{1... | collective-permute-start | bytes 1572872 | tf_op jit(solution)/shard_map/other_x1/ppermute | solution.py:30
  52.9 0.0 collective-permute-done.13.refs_7_
  52.9 0.1 collective-permute-start.17
  53.1 1.3 %fusion.1 = (s32[12]{0:T(128)}, s32[12]{0:T(128)S(1)}) fusion(pred[]{:T(512)S(6)} %eq.18, s32[]{:T(128)S(6)} %select_n.83, s32[]{:T(128)S(6)} %select_n.80, s32[12]{0:T(128)} %param.5), kind=kLoop, calls=%fused_computation.25 | loop fusion | flops 612 | bytes 153 | tf_op jit(solution)/shard_map/add | solution.py:148
  54.4 1.2 %broadcast_multiply_fusion = (s32[12]{0:T(128)}, s32[12]{0:T(128)}) fusion(s32[12]{0:T(128)} %param.5, s32[12]{0:T(128)S(1)} %get-tuple-element.24, s32[]{:T(128)S(6)} %select_n.75, s32[]{:T(128)S(6)} %select_n.73, s32[]{:T(128)S(6)} %select_n.71), kind=kLoop, calls=%fused_computation.29 | loop fusion | flops 684 | bytes 204 | tf_op jit(solution)/shard_map/mul | solution.py:149
  55.6 0.0 collective-permute-done.22.refs_23_
  55.6 0.0 collective-permute-done.14.refs_11_
  55.7 0.0 collective-permute-done.15.refs_13_
  55.7 0.0 collective-permute-done.17.refs_15_
  55.7 12.0 %shard_map.37 = bf16[4,2,1024,512]{3,2,1,0:T(8,128)(2,1)} custom-call(s32[12]{0:T(128)} %get-tuple-element.26.a_where, s32[12]{0:T(128)} %get-tuple-element.23.b_where, s32[12]{0:T(128)} %get-tuple-element.25.b_row, bf16[4,2,32,1024]{3,2,1,0:T(8,128)(2,1)} %refs_0_.1, bf16[4,2,32,1024]{3,2,1,0:T(8,128)(2,1)} %copy-done.1, ...), custom_call_target="tpu_custom_call" | custom-call | flops 6442450944 | bytes 20971520 | tf_op jit(solution)/shard_map/pallas_call | solution.py:113
  (27 shorter events, 0.1 us)
Async XLA Ops:
  0.0 10.5 %collective-permute-start.5 = (bf16[4,2,32,1024]{3,2,1,0:T(8,128)(2,1)}, bf16[4,2,32,1024]{3,2,1,0:T(8,128)(2,1)S(1)}, u32[]{:S(2)}, u32[]{:S(2)}) collective-permute-start(bf16[4,2,32,1024]{3,2,1,0:T(8,128)(2,1)} %refs_0_.1), channel_id=1, source_target_pairs={{0,1},{1,0},{2,3},{3,2},{4,5},{5,4},{6,7},{7,6},{16,17},{17,16},{1... | collective-permute-start | bytes 1572872 | tf_op jit(solution)/shard_map/other/ppermute | solution.py:30
  1.4 9.1 %collective-permute-start.18 = (bf16[4,2,64,512]{3,2,1,0:T(8,128)(2,1)}, bf16[4,2,64,512]{3,2,1,0:T(8,128)(2,1)S(1)}, u32[]{:S(2)}, u32[]{:S(2)}) collective-permute-start(bf16[4,2,64,512]{3,2,1,0:T(8,128)(2,1)} %refs_16_.1), channel_id=1, source_target_pairs={{0,8},{1,73},{2,10},{3,75},{4,12},{5,77},{6,14},{7,79},{16,24},{17... | collective-permute-start | bytes 1572872 | tf_op jit(solution)/shard_map/b_hop/ppermute | solution.py:30
  4.0 10.2 %collective-permute-start = (bf16[4,2,32,1024]{3,2,1,0:T(8,128)(2,1)}, bf16[4,2,32,1024]{3,2,1,0:T(8,128)(2,1)S(1)}, u32[]{:S(2)}, u32[]{:S(2)}) collective-permute-start(bf16[4,2,32,1024]{3,2,1,0:T(8,128)(2,1)} %refs_0_.1), channel_id=1, source_target_pairs={{0,2},{1,7},{2,4},{3,1},{4,6},{5,3},{6,0},{7,5},{16,18},{17,23},{1... | collective-permute-start | bytes 1572872 | tf_op jit(solution)/shard_map/a_1/ppermute | solution.py:30
  7.7 14.9 %collective-permute-start.2 = (bf16[4,2,64,512]{3,2,1,0:T(8,128)(2,1)}, bf16[4,2,64,512]{3,2,1,0:T(8,128)(2,1)S(1)}, u32[]{:S(2)}, u32[]{:S(2)}) collective-permute-start(bf16[4,2,64,512]{3,2,1,0:T(8,128)(2,1)} %refs_16_.1), channel_id=1, source_target_pairs={{0,48},{1,17},{2,50},{3,19},{4,52},{5,21},{6,54},{7,23},{16,0},{17... | collective-permute-start | bytes 1572872 | tf_op jit(solution)/shard_map/b_3/ppermute | solution.py:30
  9.0 13.6 %collective-permute-start.9 = (bf16[4,2,64,512]{3,2,1,0:T(8,128)(2,1)}, bf16[4,2,64,512]{3,2,1,0:T(8,128)(2,1)S(1)}, u32[]{:S(2)}, u32[]{:S(2)}) collective-permute-start(bf16[4,2,64,512]{3,2,1,0:T(8,128)(2,1)} %refs_16_.1), channel_id=1, source_target_pairs={{0,16},{1,49},{2,18},{3,51},{4,20},{5,53},{6,22},{7,55},{16,32},{1... | collective-permute-start | bytes 1572872 | tf_op jit(solution)/shard_map/b_1/ppermute | solution.py:30
  10.5 45.2 %copy-start = (bf16[4,2,32,1024]{3,2,1,0:T(8,128)(2,1)}, bf16[4,2,32,1024]{3,2,1,0:T(8,128)(2,1)S(1)}, u32[]{:S(2)}) copy-start(bf16[4,2,32,1024]{3,2,1,0:T(8,128)(2,1)S(1)} %collective-permute-done.5.refs_8_) | copy-start | bytes 1572868
  10.5 13.0 %collective-permute-start.6 = (bf16[4,2,32,1024]{3,2,1,0:T(8,128)(2,1)}, bf16[4,2,32,1024]{3,2,1,0:T(8,128)(2,1)S(1)}, u32[]{:S(2)}, u32[]{:S(2)}) collective-permute-start(bf16[4,2,32,1024]{3,2,1,0:T(8,128)(2,1)} %refs_0_.1), channel_id=1, source_target_pairs={{0,8},{1,9},{2,10},{3,11},{4,12},{5,13},{6,14},{7,15},{16,24},{17,... | collective-permute-start | bytes 1572872 | tf_op jit(solution)/shard_map/a_x/ppermute | solution.py:30
  10.5 17.8 %collective-permute-start.19 = (bf16[4,2,64,512]{3,2,1,0:T(8,128)(2,1)S(1)}, bf16[4,2,64,512]{3,2,1,0:T(8,128)(2,1)S(1)}, u32[]{:S(2)}, u32[]{:S(2)}) collective-permute-start(bf16[4,2,64,512]{3,2,1,0:T(8,128)(2,1)S(1)} %collective-permute-done.18), channel_id=1, source_target_pairs={{0,8},{1,73},{2,10},{3,75},{4,12},{5,77},{6,14},{7,79},{16,24},{17... | collective-permute-start | bytes 1572872 | tf_op jit(solution)/shard_map/b_x/ppermute | solution.py:30
  14.2 41.5 %copy-start.1 = (bf16[4,2,32,1024]{3,2,1,0:T(8,128)(2,1)}, bf16[4,2,32,1024]{3,2,1,0:T(8,128)(2,1)S(1)}, u32[]{:S(2)}) copy-start(bf16[4,2,32,1024]{3,2,1,0:T(8,128)(2,1)S(1)} %collective-permute-done.refs_1_) | copy-start | bytes 1572868
  14.2 16.9 %collective-permute-start.1 = (bf16[4,2,32,1024]{3,2,1,0:T(8,128)(2,1)S(1)}, bf16[4,2,32,1024]{3,2,1,0:T(8,128)(2,1)S(1)}, u32[]{:S(2)}, u32[]{:S(2)}) collective-permute-start(bf16[4,2,32,1024]{3,2,1,0:T(8,128)(2,1)S(1)} %collective-permute-done.refs_1_), channel_id=1, source_target_pairs={{0,2},{1,7},{2,4},{3,1},{4,6},{5,3},{6,0},{7,5},{16,18},{17,23},{1... | collective-permute-start | bytes 1572872 | tf_op jit(solution)/shard_map/a_2/ppermute | solution.py:30
  22.6 33.1 %copy-start.2 = (bf16[4,2,64,512]{3,2,1,0:T(8,128)(2,1)}, bf16[4,2,64,512]{3,2,1,0:T(8,128)(2,1)S(1)}, u32[]{:S(2)}) copy-start(bf16[4,2,64,512]{3,2,1,0:T(8,128)(2,1)S(1)} %collective-permute-done.2.refs_19_) | copy-start | bytes 1572868
  22.6 8.5 %collective-permute-start.3 = (bf16[4,2,32,1024]{3,2,1,0:T(8,128)(2,1)S(1)}, bf16[4,2,32,1024]{3,2,1,0:T(8,128)(2,1)S(1)}, u32[]{:S(2)}, u32[]{:S(2)}) collective-permute-start(bf16[4,2,32,1024]{3,2,1,0:T(8,128)(2,1)S(1)} %collective-permute-done.refs_1_), channel_id=1, source_target_pairs={{0,1},{1,0},{2,3},{3,2},{4,5},{5,4},{6,7},{7,6},{16,17},{17,16},{1... | collective-permute-start | bytes 1572872 | tf_op jit(solution)/shard_map/other_1/ppermute | solution.py:30
  22.6 33.1 %copy-start.3 = (bf16[4,2,64,512]{3,2,1,0:T(8,128)(2,1)}, bf16[4,2,64,512]{3,2,1,0:T(8,128)(2,1)S(1)}, u32[]{:S(2)}) copy-start(bf16[4,2,64,512]{3,2,1,0:T(8,128)(2,1)S(1)} %collective-permute-done.9.refs_17_) | copy-start | bytes 1572868
  22.7 8.7 %collective-permute-start.10 = (bf16[4,2,64,512]{3,2,1,0:T(8,128)(2,1)S(1)}, bf16[4,2,64,512]{3,2,1,0:T(8,128)(2,1)S(1)}, u32[]{:S(2)}, u32[]{:S(2)}) collective-permute-start(bf16[4,2,64,512]{3,2,1,0:T(8,128)(2,1)S(1)} %collective-permute-done.9.refs_17_), channel_id=1, source_target_pairs={{0,16},{1,49},{2,18},{3,51},{4,20},{5,53},{6,22},{7,55},{16,32},{1... | collective-permute-start | bytes 1572872 | tf_op jit(solution)/shard_map/b_2/ppermute | solution.py:30
  23.5 32.2 %copy-start.4 = (bf16[4,2,32,1024]{3,2,1,0:T(8,128)(2,1)}, bf16[4,2,32,1024]{3,2,1,0:T(8,128)(2,1)S(1)}, u32[]{:S(2)}) copy-start(bf16[4,2,32,1024]{3,2,1,0:T(8,128)(2,1)S(1)} %collective-permute-done.6.refs_4_) | copy-start | bytes 1572868
  23.5 8.7 %collective-permute-start.7 = (bf16[4,2,32,1024]{3,2,1,0:T(8,128)(2,1)S(1)}, bf16[4,2,32,1024]{3,2,1,0:T(8,128)(2,1)S(1)}, u32[]{:S(2)}, u32[]{:S(2)}) collective-permute-start(bf16[4,2,32,1024]{3,2,1,0:T(8,128)(2,1)S(1)} %collective-permute-done.6.refs_4_), channel_id=1, source_target_pairs={{0,1},{1,0},{2,3},{3,2},{4,5},{5,4},{6,7},{7,6},{16,17},{17,16},{1... | collective-permute-start | bytes 1572872 | tf_op jit(solution)/shard_map/other_x/ppermute | solution.py:30
  28.3 27.5 %copy-start.5 = (bf16[4,2,64,512]{3,2,1,0:T(8,128)(2,1)}, bf16[4,2,64,512]{3,2,1,0:T(8,128)(2,1)S(1)}, u32[]{:S(2)}) copy-start(bf16[4,2,64,512]{3,2,1,0:T(8,128)(2,1)S(1)} %collective-permute-done.19.refs_20_) | copy-start | bytes 1572868
  28.3 9.0 %collective-permute-start.20 = (bf16[4,2,64,512]{3,2,1,0:T(8,128)(2,1)S(1)}, bf16[4,2,64,512]{3,2,1,0:T(8,128)(2,1)S(1)}, u32[]{:S(2)}, u32[]{:S(2)}) collective-permute-start(bf16[4,2,64,512]{3,2,1,0:T(8,128)(2,1)S(1)} %collective-permute-done.19.refs_20_), channel_id=1, source_target_pairs={{0,16},{1,49},{2,18},{3,51},{4,20},{5,53},{6,22},{7,55},{16,32},{1... | collective-permute-start | bytes 1572872 | tf_op jit(solution)/shard_map/b_x1/ppermute | solution.py:30
  31.1 21.8 %copy-start.6 = (bf16[4,2,32,1024]{3,2,1,0:T(8,128)(2,1)}, bf16[4,2,32,1024]{3,2,1,0:T(8,128)(2,1)S(1)}, u32[]{:S(2)}) copy-start(bf16[4,2,32,1024]{3,2,1,0:T(8,128)(2,1)S(1)} %collective-permute-done.1.refs_2_) | copy-start | bytes 1572868
  31.1 9.2 %collective-permute-start.12 = (bf16[4,2,32,1024]{3,2,1,0:T(8,128)(2,1)S(1)}, bf16[4,2,32,1024]{3,2,1,0:T(8,128)(2,1)S(1)}, u32[]{:S(2)}, u32[]{:S(2)}) collective-permute-start(bf16[4,2,32,1024]{3,2,1,0:T(8,128)(2,1)S(1)} %collective-permute-done.1.refs_2_), channel_id=1, source_target_pairs={{0,1},{1,0},{2,3},{3,2},{4,5},{5,4},{6,7},{7,6},{16,17},{17,16},{1... | collective-permute-start | bytes 1572872 | tf_op jit(solution)/shard_map/other_2/ppermute | solution.py:30
  31.2 21.9 %copy-start.7 = (bf16[4,2,32,1024]{3,2,1,0:T(8,128)(2,1)}, bf16[4,2,32,1024]{3,2,1,0:T(8,128)(2,1)S(1)}, u32[]{:S(2)}) copy-start(bf16[4,2,32,1024]{3,2,1,0:T(8,128)(2,1)S(1)} %collective-permute-done.3.refs_9_) | copy-start | bytes 1572868
  31.2 11.5 %collective-permute-start.4 = (bf16[4,2,32,1024]{3,2,1,0:T(8,128)(2,1)}, bf16[4,2,32,1024]{3,2,1,0:T(8,128)(2,1)}, u32[]{:S(2)}, u32[]{:S(2)}) collective-permute-start(bf16[4,2,32,1024]{3,2,1,0:T(8,128)(2,1)} %refs_0_.1), channel_id=1, source_target_pairs={{0,6},{1,3},{2,0},{3,5},{4,2},{5,7},{6,4},{7,1},{16,22},{17,19},{1... | collective-permute-start | bytes 1572872 | tf_op jit(solution)/shard_map/a_3/ppermute | solution.py:30
  31.4 21.6 %copy-start.8 = (bf16[4,2,64,512]{3,2,1,0:T(8,128)(2,1)}, bf16[4,2,64,512]{3,2,1,0:T(8,128)(2,1)S(1)}, u32[]{:S(2)}) copy-start(bf16[4,2,64,512]{3,2,1,0:T(8,128)(2,1)S(1)} %collective-permute-done.10.refs_18_) | copy-start | bytes 1572868
  31.4 11.3 %collective-permute-start.11 = (bf16[4,2,32,1024]{3,2,1,0:T(8,128)(2,1)S(1)}, bf16[4,2,32,1024]{3,2,1,0:T(8,128)(2,1)}, u32[]{:S(2)}, u32[]{:S(2)}) collective-permute-start(bf16[4,2,32,1024]{3,2,1,0:T(8,128)(2,1)S(1)} %collective-permute-done.1.refs_2_), channel_id=1, source_target_pairs={{0,8},{1,9},{2,10},{3,11},{4,12},{5,13},{6,14},{7,15},{16,24},{17,... | collective-permute-start | bytes 1572872 | tf_op jit(solution)/shard_map/a_x2/ppermute | solution.py:30
  32.2 20.8 %copy-start.9 = (bf16[4,2,32,1024]{3,2,1,0:T(8,128)(2,1)}, bf16[4,2,32,1024]{3,2,1,0:T(8,128)(2,1)S(1)}, u32[]{:S(2)}) copy-start(bf16[4,2,32,1024]{3,2,1,0:T(8,128)(2,1)S(1)} %collective-permute-done.7.refs_12_) | copy-start | bytes 1572868
  32.2 14.6 %collective-permute-start.8 = (bf16[4,2,32,1024]{3,2,1,0:T(8,128)(2,1)S(1)}, bf16[4,2,32,1024]{3,2,1,0:T(8,128)(2,1)}, u32[]{:S(2)}, u32[]{:S(2)}) collective-permute-start(bf16[4,2,32,1024]{3,2,1,0:T(8,128)(2,1)S(1)} %collective-permute-done.6.refs_4_), channel_id=1, source_target_pairs={{0,2},{1,7},{2,4},{3,1},{4,6},{5,3},{6,0},{7,5},{16,18},{17,23},{1... | collective-permute-start | bytes 1572872 | tf_op jit(solution)/shard_map/a_x1/ppermute | solution.py:30
  37.3 15.8 %copy-start.10 = (bf16[4,2,64,512]{3,2,1,0:T(8,128)(2,1)}, bf16[4,2,64,512]{3,2,1,0:T(8,128)(2,1)S(1)}, u32[]{:S(2)}) copy-start(bf16[4,2,64,512]{3,2,1,0:T(8,128)(2,1)S(1)} %collective-permute-done.20.refs_21_) | copy-start | bytes 1572868
  37.3 12.1 %collective-permute-start.21 = (bf16[4,2,64,512]{3,2,1,0:T(8,128)(2,1)S(1)}, bf16[4,2,64,512]{3,2,1,0:T(8,128)(2,1)S(1)}, u32[]{:S(2)}, u32[]{:S(2)}) collective-permute-start(bf16[4,2,64,512]{3,2,1,0:T(8,128)(2,1)S(1)} %collective-permute-done.20.refs_21_), channel_id=1, source_target_pairs={{0,16},{1,49},{2,18},{3,51},{4,20},{5,53},{6,22},{7,55},{16,32},{1... | collective-permute-start | bytes 1572872 | tf_op jit(solution)/shard_map/b_x2/ppermute | solution.py:30
  40.4 12.7 %copy-start.11 = (bf16[4,2,32,1024]{3,2,1,0:T(8,128)(2,1)}, bf16[4,2,32,1024]{3,2,1,0:T(8,128)(2,1)S(1)}, u32[]{:S(2)}) copy-start(bf16[4,2,32,1024]{3,2,1,0:T(8,128)(2,1)S(1)} %collective-permute-done.12.refs_10_) | copy-start | bytes 1572868
  40.4 12.5 %collective-permute-start.13 = (bf16[4,2,32,1024]{3,2,1,0:T(8,128)(2,1)S(1)}, bf16[4,2,32,1024]{3,2,1,0:T(8,128)(2,1)}, u32[]{:S(2)}, u32[]{:S(2)}) collective-permute-start(bf16[4,2,32,1024]{3,2,1,0:T(8,128)(2,1)S(1)} %collective-permute-done.6.refs_4_), channel_id=1, source_target_pairs={{0,6},{1,3},{2,0},{3,5},{4,2},{5,7},{6,4},{7,1},{16,22},{17,19},{1... | collective-permute-start | bytes 1572872 | tf_op jit(solution)/shard_map/a_x3/ppermute | solution.py:30
  42.6 13.0 %collective-permute-start.22 = (bf16[4,2,64,512]{3,2,1,0:T(8,128)(2,1)S(1)}, bf16[4,2,64,512]{3,2,1,0:T(8,128)(2,1)}, u32[]{:S(2)}, u32[]{:S(2)}) collective-permute-start(bf16[4,2,64,512]{3,2,1,0:T(8,128)(2,1)S(1)} %collective-permute-done.19.refs_20_), channel_id=1, source_target_pairs={{0,48},{1,17},{2,50},{3,19},{4,52},{5,21},{6,54},{7,23},{16,0},{17... | collective-permute-start | bytes 1572872 | tf_op jit(solution)/shard_map/b_x3/ppermute | solution.py:30
  42.6 13.0 %collective-permute-start.16 = (bf16[4,2,32,1024]{3,2,1,0:T(8,128)(2,1)}, bf16[4,2,32,1024]{3,2,1,0:T(8,128)(2,1)}, u32[]{:S(2)}, u32[]{:S(2)}) collective-permute-start(bf16[4,2,32,1024]{3,2,1,0:T(8,128)(2,1)} %collective-permute-done.11.refs_6_), channel_id=1, source_target_pairs={{0,1},{1,0},{2,3},{3,2},{4,5},{5,4},{6,7},{7,6},{16,17},{17,16},{1... | collective-permute-start | bytes 1572872 | tf_op jit(solution)/shard_map/other_x2/ppermute | solution.py:30
  46.9 8.8 %collective-permute-start.14 = (bf16[4,2,32,1024]{3,2,1,0:T(8,128)(2,1)}, bf16[4,2,32,1024]{3,2,1,0:T(8,128)(2,1)}, u32[]{:S(2)}, u32[]{:S(2)}) collective-permute-start(bf16[4,2,32,1024]{3,2,1,0:T(8,128)(2,1)} %collective-permute-done.4.refs_3_), channel_id=1, source_target_pairs={{0,1},{1,0},{2,3},{3,2},{4,5},{5,4},{6,7},{7,6},{16,17},{17,16},{1... | collective-permute-start | bytes 1572872 | tf_op jit(solution)/shard_map/other_3/ppermute | solution.py:30
  49.3 3.7 %copy-start.12 = (bf16[4,2,64,512]{3,2,1,0:T(8,128)(2,1)}, bf16[4,2,64,512]{3,2,1,0:T(8,128)(2,1)S(1)}, u32[]{:S(2)}) copy-start(bf16[4,2,64,512]{3,2,1,0:T(8,128)(2,1)S(1)} %collective-permute-done.21.refs_22_) | copy-start | bytes 1572868
  49.3 6.3 %collective-permute-start.15 = (bf16[4,2,32,1024]{3,2,1,0:T(8,128)(2,1)}, bf16[4,2,32,1024]{3,2,1,0:T(8,128)(2,1)}, u32[]{:S(2)}, u32[]{:S(2)}) collective-permute-start(bf16[4,2,32,1024]{3,2,1,0:T(8,128)(2,1)} %collective-permute-done.8.refs_5_), channel_id=1, source_target_pairs={{0,1},{1,0},{2,3},{3,2},{4,5},{5,4},{6,7},{7,6},{16,17},{17,16},{1... | collective-permute-start | bytes 1572872 | tf_op jit(solution)/shard_map/other_x1/ppermute | solution.py:30
  52.9 2.7 %collective-permute-start.17 = (bf16[4,2,32,1024]{3,2,1,0:T(8,128)(2,1)}, bf16[4,2,32,1024]{3,2,1,0:T(8,128)(2,1)}, u32[]{:S(2)}, u32[]{:S(2)}) collective-permute-start(bf16[4,2,32,1024]{3,2,1,0:T(8,128)(2,1)} %collective-permute-done.13.refs_7_), channel_id=1, source_target_pairs={{0,1},{1,0},{2,3},{3,2},{4,5},{5,4},{6,7},{7,6},{16,17},{17,16},{1... | collective-permute-start | bytes 1572872 | tf_op jit(solution)/shard_map/other_x3/ppermute | solution.py:30

commit v3 on v1

--- a/solution.py
+++ b/solution.py
@@ -163,29 +163,28 @@
     def swap(name, value):
         return send(name, value, flip_core=True)
 
-    b_hop = send("b_hop", b, dx=1)
+    a_1 = send("a_1", a, dz=1)
+    b_x = send("b_x", b, dx=2)
+    a_3 = send("a_3", a, dz=-1)
+    b_3 = send("b_3", b, dy=-1)
     b_1 = send("b_1", b, dy=1)
-    a_1 = send("a_1", a, dz=1)
-    b_x = send("b_x", b_hop, dx=1)
-    a_x = send("a_x", after(a, b_x), flip_x=True)
-    a_2 = send("a_2", a_1, dz=1)
-    a_3 = send("a_3", after(a, a_2), dz=-1)
+    a_x = send("a_x", after(a, a_1), flip_x=True)
     b_x1 = send("b_x1", b_x, dy=1)
-    b_x2 = send("b_x2", b_x1, dy=1)
-    a_x1 = send("a_x1", a_x, dz=1)
-    a_x3 = send("a_x3", after(a_x, a_2), dz=-1)
+    other = swap("other", after(a, a_3))
+    a_2 = send("a_2", after(a_1, b_3), dz=1)
+    b_2 = send("b_2", b_1, dy=1)
+    other_3 = swap("other_3", after(a_3, a_x))
+    other_x = swap("other_x", after(a_x, b_x1))
+    a_x1 = send("a_x1", after(a_x, other), dz=1)
     a_x2 = send("a_x2", a_2, flip_x=True)
-    other = swap("other", a)
-    b_3 = send("b_3", after(b, other), dy=-1)
-    b_2 = send("b_2", after(b_1, b_3, a_2), dy=1)
     b_x3 = send("b_x3", after(b_x, b_2), dy=-1)
-    other_1 = swap("other_1", after(a_1, a_2))
-    other_2 = swap("other_2", after(a_2, a_3))
-    other_3 = swap("other_3", after(a_3, b_2))
-    other_x = swap("other_x", after(a_x, a_x3, b_x2, b_2))
-    other_x1 = swap("other_x1", after(a_x1, b_1))
-    other_x2 = swap("other_x2", after(a_x2, b_1))
-    other_x3 = swap("other_x3", after(a_x3, other_3))
+    a_x3 = send("a_x3", after(a_x, other_3), dz=-1)
+    b_x2 = send("b_x2", after(b_x1, other_x), dy=1)
+    other_x1 = swap("other_x1", a_x1)
+    other_1 = swap("other_1", after(a_1, a_x2))
+    other_2 = swap("other_2", after(a_2, b_x3))
+    other_x3 = swap("other_x3", a_x3)
+    other_x2 = swap("other_x2", after(a_x2, b_x2))
 
     a_parts = [a, a_1, a_2, a_3, a_x, a_x1, a_x2, a_x3]
     a_parts += [other, other_1, other_2, other_3, other_x, other_x1, other_x2, other_x3]

time: 74.1 us -> 68.5 us (0.924)
  starting transfers between devices: 34.1 us -> 27.9 us
  waiting for transfers between devices: 24.7 us -> 25.8 us
    ppermute x23 -> x22, starting transfers between devices: 34.1 us -> 27.9 us  [moved(): return lax.ppermute(value, AXES, pairs)]
    ppermute x23 -> x22, waiting for transfers between devices: 24.7 us -> 25.8 us  [moved(): return lax.ppermute(value, AXES, pairs)]
  transfers between devices with their start and end apart: 23 -> 22, of which waited for: 9 -> 8; matrix products, arithmetic and copies ran while one was open for 3% -> 4% of each run, Pallas kernels for 0% -> 0%
where the time goes in v3:
time: 68.5 us; the launch traced here: 68.4 us
  starting transfers between devices  27.9 us (41%)
  waiting for transfers between devices  25.8 us (38%)
  Pallas kernels  12 us (18%)
  other arithmetic  2.48 us (4%)
    ppermute x22, starting transfers between devices, moved(): return lax.ppermute(value, AXES, pairs)  27.9 us
    ppermute x22, waiting for transfers between devices, moved(): return lax.ppermute(value, AXES, pairs)  25.8 us
    pallas_call x1, Pallas kernels, multiply(): pl.pallas_call(multiply_kernel, out_shape=jax.ShapeDtypeStruct((freqs, 2,...  12 us
  transfers between devices with their start and end apart: 22, of which 8 were waited for; matrix products, arithmetic and copies ran while one was open for 4% of the time, Pallas kernels for 0%

profile of v3, /device:TPU:1, one launch (start us, length us, event | category | flops | bytes accessed | tf_op | source)
XLA Modules:
  0.0 68.4 jit_solution(6203414556030775879)
XLA Ops:
  0.0 4.6 %collective-permute-start = (bf16[4,2,32,1024]{3,2,1,0:T(8,128)(2,1)}, bf16[4,2,32,1024]{3,2,1,0:T(8,128)(2,1)S(1)}, u32[]{:S(2)}, u32[]{:S(2)}) collective-permute-start(bf16[4,2,32,1024]{3,2,1,0:T(8,128)(2,1)} %refs_0_.1), channel_id=1, source_target_pairs={{0,2},{1,7},{2,4},{3,1},{4,6},{5,3},{6,0},{7,5},{16,18},{17,23},{1... | collective-permute-start | bytes 1572872 | tf_op jit(solution)/shard_map/a_1/ppermute | solution.py:30
  4.6 2.7 %collective-permute-start.11 = (bf16[4,2,64,512]{3,2,1,0:T(8,128)(2,1)}, bf16[4,2,64,512]{3,2,1,0:T(8,128)(2,1)S(1)}, u32[]{:S(2)}, u32[]{:S(2)}) collective-permute-start(bf16[4,2,64,512]{3,2,1,0:T(8,128)(2,1)} %refs_16_.1), channel_id=1, source_target_pairs={{0,64},{1,65},{2,66},{3,67},{4,68},{5,69},{6,70},{7,71},{16,80},{1... | collective-permute-start | bytes 1572872 | tf_op jit(solution)/shard_map/b_x/ppermute | solution.py:30
  7.3 0.0 collective-permute-start.3
  7.3 2.7 %collective-permute-start.12 = (bf16[4,2,64,512]{3,2,1,0:T(8,128)(2,1)}, bf16[4,2,64,512]{3,2,1,0:T(8,128)(2,1)S(1)}, u32[]{:S(2)}, u32[]{:S(2)}) collective-permute-start(bf16[4,2,64,512]{3,2,1,0:T(8,128)(2,1)} %refs_16_.1), channel_id=1, source_target_pairs={{0,16},{1,49},{2,18},{3,51},{4,20},{5,53},{6,22},{7,55},{16,32},{1... | collective-permute-start | bytes 1572872 | tf_op jit(solution)/shard_map/b_1/ppermute | solution.py:30
  10.1 0.0 collective-permute-start.1
  10.1 2.3 %collective-permute-done.refs_1_ = bf16[4,2,32,1024]{3,2,1,0:T(8,128)(2,1)S(1)} collective-permute-done((bf16[4,2,32,1024]{3,2,1,0:T(8,128)(2,1)}, bf16[4,2,32,1024]{3,2,1,0:T(8,128)(2,1)S(1)}, u32[]{:S(2)}, u32[]{:S(2)}) %collective-permute-start) | collective-permute-done | bytes 524320 | tf_op jit(solution)/shard_map/a_1/ppermute | solution.py:30
  12.4 6.8 %collective-permute-done.11.refs_20_ = bf16[4,2,64,512]{3,2,1,0:T(8,128)(2,1)S(1)} collective-permute-done((bf16[4,2,64,512]{3,2,1,0:T(8,128)(2,1)}, bf16[4,2,64,512]{3,2,1,0:T(8,128)(2,1)S(1)}, u32[]{:S(2)}, u32[]{:S(2)}) %collective-permute-start.11) | collective-permute-done | bytes 524320 | tf_op jit(solution)/shard_map/b_x/ppermute | solution.py:30
  19.2 2.7 %collective-permute-start.16 = (bf16[4,2,64,512]{3,2,1,0:T(8,128)(2,1)S(1)}, bf16[4,2,64,512]{3,2,1,0:T(8,128)(2,1)S(1)}, u32[]{:S(2)}, u32[]{:S(2)}) collective-permute-start(bf16[4,2,64,512]{3,2,1,0:T(8,128)(2,1)S(1)} %collective-permute-done.11.refs_20_), channel_id=1, source_target_pairs={{0,16},{1,49},{2,18},{3,51},{4,20},{5,53},{6,22},{7,55},{16,32},{1... | collective-permute-start | bytes 1572872 | tf_op jit(solution)/shard_map/b_x1/ppermute | solution.py:30
  22.0 1.5 %collective-permute-start.4 = (bf16[4,2,32,1024]{3,2,1,0:T(8,128)(2,1)}, bf16[4,2,32,1024]{3,2,1,0:T(8,128)(2,1)S(1)}, u32[]{:S(2)}, u32[]{:S(2)}) collective-permute-start(bf16[4,2,32,1024]{3,2,1,0:T(8,128)(2,1)} %refs_0_.1), channel_id=1, source_target_pairs={{0,8},{1,9},{2,10},{3,11},{4,12},{5,13},{6,14},{7,15},{16,24},{17,... | collective-permute-start | bytes 1572872 | tf_op jit(solution)/shard_map/a_x/ppermute | solution.py:30
  23.5 0.0 collective-permute-done.3.refs_3_
  23.5 0.0 collective-permute-done.12.refs_17_
  23.5 0.0 copy-start.3
  23.5 0.2 collective-permute-start.13
  23.8 1.2 %collective-permute-start.5 = (bf16[4,2,32,1024]{3,2,1,0:T(8,128)(2,1)}, bf16[4,2,32,1024]{3,2,1,0:T(8,128)(2,1)S(1)}, u32[]{:S(2)}, u32[]{:S(2)}) collective-permute-start(bf16[4,2,32,1024]{3,2,1,0:T(8,128)(2,1)} %refs_0_.1), channel_id=1, source_target_pairs={{0,1},{1,0},{2,3},{3,2},{4,5},{5,4},{6,7},{7,6},{16,17},{17,16},{1... | collective-permute-start | bytes 1572872 | tf_op jit(solution)/shard_map/other/ppermute | solution.py:30
  24.9 0.1 collective-permute-done.1.refs_19_
  25.1 2.1 %collective-permute-start.2 = (bf16[4,2,32,1024]{3,2,1,0:T(8,128)(2,1)S(1)}, bf16[4,2,32,1024]{3,2,1,0:T(8,128)(2,1)}, u32[]{:S(2)}, u32[]{:S(2)}) collective-permute-start(bf16[4,2,32,1024]{3,2,1,0:T(8,128)(2,1)S(1)} %collective-permute-done.refs_1_), channel_id=1, source_target_pairs={{0,2},{1,7},{2,4},{3,1},{4,6},{5,3},{6,0},{7,5},{16,18},{17,23},{1... | collective-permute-start | bytes 1572872 | tf_op jit(solution)/shard_map/a_2/ppermute | solution.py:30
  27.2 0.9 %collective-permute-done.16.refs_21_ = bf16[4,2,64,512]{3,2,1,0:T(8,128)(2,1)S(1)} collective-permute-done((bf16[4,2,64,512]{3,2,1,0:T(8,128)(2,1)S(1)}, bf16[4,2,64,512]{3,2,1,0:T(8,128)(2,1)S(1)}, u32[]{:S(2)}, u32[]{:S(2)}) %collective-permute-start.16) | collective-permute-done | bytes 524320 | tf_op jit(solution)/shard_map/b_x1/ppermute | solution.py:30
  28.1 7.4 %collective-permute-done.4.refs_4_ = bf16[4,2,32,1024]{3,2,1,0:T(8,128)(2,1)S(1)} collective-permute-done((bf16[4,2,32,1024]{3,2,1,0:T(8,128)(2,1)}, bf16[4,2,32,1024]{3,2,1,0:T(8,128)(2,1)S(1)}, u32[]{:S(2)}, u32[]{:S(2)}) %collective-permute-start.4) | collective-permute-done | bytes 524320 | tf_op jit(solution)/shard_map/a_x/ppermute | solution.py:30
  35.5 0.0 collective-permute-start.17
  35.5 0.5 collective-permute-start.8
  36.0 0.0 collective-permute-done.13.refs_18_
  36.0 0.0 collective-permute-start.14
  36.0 0.0 collective-permute-done.5.refs_8_
  36.0 0.8 %collective-permute-start.6 = (bf16[4,2,32,1024]{3,2,1,0:T(8,128)(2,1)S(1)}, bf16[4,2,32,1024]{3,2,1,0:T(8,128)(2,1)}, u32[]{:S(2)}, u32[]{:S(2)}) collective-permute-start(bf16[4,2,32,1024]{3,2,1,0:T(8,128)(2,1)S(1)} %collective-permute-done.4.refs_4_), channel_id=1, source_target_pairs={{0,2},{1,7},{2,4},{3,1},{4,6},{5,3},{6,0},{7,5},{16,18},{17,23},{1... | collective-permute-start | bytes 1572872 | tf_op jit(solution)/shard_map/a_x1/ppermute | solution.py:30
  36.8 0.0 collective-permute-done.2.refs_2_
  36.8 1.2 %collective-permute-start.7 = (bf16[4,2,32,1024]{3,2,1,0:T(8,128)(2,1)}, bf16[4,2,32,1024]{3,2,1,0:T(8,128)(2,1)}, u32[]{:S(2)}, u32[]{:S(2)}) collective-permute-start(bf16[4,2,32,1024]{3,2,1,0:T(8,128)(2,1)} %collective-permute-done.2.refs_2_), channel_id=1, source_target_pairs={{0,8},{1,9},{2,10},{3,11},{4,12},{5,13},{6,14},{7,15},{16,24},{17,... | collective-permute-start | bytes 1572872 | tf_op jit(solution)/shard_map/a_x2/ppermute | solution.py:30
  38.0 0.0 collective-permute-done.17.refs_12_
  38.0 2.6 %collective-permute-start.19 = (bf16[4,2,64,512]{3,2,1,0:T(8,128)(2,1)S(1)}, bf16[4,2,64,512]{3,2,1,0:T(8,128)(2,1)S(1)}, u32[]{:S(2)}, u32[]{:S(2)}) collective-permute-start(bf16[4,2,64,512]{3,2,1,0:T(8,128)(2,1)S(1)} %collective-permute-done.16.refs_21_), channel_id=1, source_target_pairs={{0,16},{1,49},{2,18},{3,51},{4,20},{5,53},{6,22},{7,55},{16,32},{1... | collective-permute-start | bytes 1572872 | tf_op jit(solution)/shard_map/b_x2/ppermute | solution.py:30
  40.6 0.0 collective-permute-done.8.refs_11_
  40.6 0.4 collective-permute-start.9
  41.1 6.2 %collective-permute-done.14.refs_23_ = bf16[4,2,64,512]{3,2,1,0:T(8,128)(2,1)S(1)} collective-permute-done((bf16[4,2,64,512]{3,2,1,0:T(8,128)(2,1)S(1)}, bf16[4,2,64,512]{3,2,1,0:T(8,128)(2,1)S(1)}, u32[]{:S(2)}, u32[]{:S(2)}) %collective-permute-start.14) | collective-permute-done | bytes 524320 | tf_op jit(solution)/shard_map/b_x3/ppermute | solution.py:30
  47.3 2.0 %collective-permute-start.15 = (bf16[4,2,32,1024]{3,2,1,0:T(8,128)(2,1)}, bf16[4,2,32,1024]{3,2,1,0:T(8,128)(2,1)}, u32[]{:S(2)}, u32[]{:S(2)}) collective-permute-start(bf16[4,2,32,1024]{3,2,1,0:T(8,128)(2,1)} %collective-permute-done.2.refs_2_), channel_id=1, source_target_pairs={{0,1},{1,0},{2,3},{3,2},{4,5},{5,4},{6,7},{7,6},{16,17},{17,16},{1... | collective-permute-start | bytes 1572872 | tf_op jit(solution)/shard_map/other_2/ppermute | solution.py:30
  49.3 0.2 collective-permute-done.7.refs_6_
  49.5 2.0 %collective-permute-start.10 = (bf16[4,2,32,1024]{3,2,1,0:T(8,128)(2,1)S(1)}, bf16[4,2,32,1024]{3,2,1,0:T(8,128)(2,1)}, u32[]{:S(2)}, u32[]{:S(2)}) collective-permute-start(bf16[4,2,32,1024]{3,2,1,0:T(8,128)(2,1)S(1)} %collective-permute-done.refs_1_), channel_id=1, source_target_pairs={{0,1},{1,0},{2,3},{3,2},{4,5},{5,4},{6,7},{7,6},{16,17},{17,16},{1... | collective-permute-start | bytes 1572872 | tf_op jit(solution)/shard_map/other_1/ppermute | solution.py:30
  51.5 0.0 collective-permute-done.6.refs_5_
  51.5 0.0 collective-permute-start.18
  51.5 0.0 collective-permute-done.19.refs_22_
  51.5 1.7 %collective-permute-done.9.refs_7_ = bf16[4,2,32,1024]{3,2,1,0:T(8,128)(2,1)} collective-permute-done((bf16[4,2,32,1024]{3,2,1,0:T(8,128)(2,1)S(1)}, bf16[4,2,32,1024]{3,2,1,0:T(8,128)(2,1)}, u32[]{:S(2)}, u32[]{:S(2)}) %collective-permute-start.9) | collective-permute-done | bytes 524320 | tf_op jit(solution)/shard_map/a_x3/ppermute | solution.py:30
  53.2 0.0 collective-permute-start.21
  53.2 0.5 collective-permute-start.20
  53.8 1.2 %fusion.1 = (s32[12]{0:T(128)}, s32[12]{0:T(128)S(1)}) fusion(pred[]{:T(512)S(6)} %eq.18, s32[]{:T(128)S(6)} %select_n.83, s32[]{:T(128)S(6)} %select_n.80, s32[12]{0:T(128)} %param.5), kind=kLoop, calls=%fused_computation.25 | loop fusion | flops 612 | bytes 153 | tf_op jit(solution)/shard_map/add | solution.py:148
  55.0 1.3 %broadcast_multiply_fusion = (s32[12]{0:T(128)}, s32[12]{0:T(128)}) fusion(s32[12]{0:T(128)} %param.5, s32[12]{0:T(128)S(1)} %get-tuple-element.30, s32[]{:T(128)S(6)} %select_n.75, s32[]{:T(128)S(6)} %select_n.73, s32[]{:T(128)S(6)} %select_n.71), kind=kLoop, calls=%fused_computation.29 | loop fusion | flops 684 | bytes 204 | tf_op jit(solution)/shard_map/mul | solution.py:149
  56.3 0.0 collective-permute-done.15.refs_10_
  56.3 0.0 collective-permute-done.10.refs_9_
  56.3 0.0 collective-permute-done.18.refs_13_
  56.3 0.0 collective-permute-done.21.refs_15_
  56.3 0.0 collective-permute-done.20.refs_14_
  56.4 12.0 %shard_map.37 = bf16[4,2,1024,512]{3,2,1,0:T(8,128)(2,1)} custom-call(s32[12]{0:T(128)} %get-tuple-element.32.a_where, s32[12]{0:T(128)} %get-tuple-element.29.b_where, s32[12]{0:T(128)} %get-tuple-element.31.b_row, bf16[4,2,32,1024]{3,2,1,0:T(8,128)(2,1)} %refs_0_.1, bf16[4,2,32,1024]{3,2,1,0:T(8,128)(2,1)} %copy-done, ...), custom_call_target="tpu_custom_call" | custom-call | flops 6442450944 | bytes 20971520 | tf_op jit(solution)/shard_map/pallas_call | solution.py:113
  (25 shorter events, 0.0 us)
Async XLA Ops:
  0.0 12.4 %collective-permute-start = (bf16[4,2,32,1024]{3,2,1,0:T(8,128)(2,1)}, bf16[4,2,32,1024]{3,2,1,0:T(8,128)(2,1)S(1)}, u32[]{:S(2)}, u32[]{:S(2)}) collective-permute-start(bf16[4,2,32,1024]{3,2,1,0:T(8,128)(2,1)} %refs_0_.1), channel_id=1, source_target_pairs={{0,2},{1,7},{2,4},{3,1},{4,6},{5,3},{6,0},{7,5},{16,18},{17,23},{1... | collective-permute-start | bytes 1572872 | tf_op jit(solution)/shard_map/a_1/ppermute | solution.py:30
  4.6 14.7 %collective-permute-start.11 = (bf16[4,2,64,512]{3,2,1,0:T(8,128)(2,1)}, bf16[4,2,64,512]{3,2,1,0:T(8,128)(2,1)S(1)}, u32[]{:S(2)}, u32[]{:S(2)}) collective-permute-start(bf16[4,2,64,512]{3,2,1,0:T(8,128)(2,1)} %refs_16_.1), channel_id=1, source_target_pairs={{0,64},{1,65},{2,66},{3,67},{4,68},{5,69},{6,70},{7,71},{16,80},{1... | collective-permute-start | bytes 1572872 | tf_op jit(solution)/shard_map/b_x/ppermute | solution.py:30
  7.3 16.2 %collective-permute-start.3 = (bf16[4,2,32,1024]{3,2,1,0:T(8,128)(2,1)}, bf16[4,2,32,1024]{3,2,1,0:T(8,128)(2,1)S(1)}, u32[]{:S(2)}, u32[]{:S(2)}) collective-permute-start(bf16[4,2,32,1024]{3,2,1,0:T(8,128)(2,1)} %refs_0_.1), channel_id=1, source_target_pairs={{0,6},{1,3},{2,0},{3,5},{4,2},{5,7},{6,4},{7,1},{16,22},{17,19},{1... | collective-permute-start | bytes 1572872 | tf_op jit(solution)/shard_map/a_3/ppermute | solution.py:30
  7.3 16.2 %collective-permute-start.12 = (bf16[4,2,64,512]{3,2,1,0:T(8,128)(2,1)}, bf16[4,2,64,512]{3,2,1,0:T(8,128)(2,1)S(1)}, u32[]{:S(2)}, u32[]{:S(2)}) collective-permute-start(bf16[4,2,64,512]{3,2,1,0:T(8,128)(2,1)} %refs_16_.1), channel_id=1, source_target_pairs={{0,16},{1,49},{2,18},{3,51},{4,20},{5,53},{6,22},{7,55},{16,32},{1... | collective-permute-start | bytes 1572872 | tf_op jit(solution)/shard_map/b_1/ppermute | solution.py:30
  10.1 15.0 %collective-permute-start.1 = (bf16[4,2,64,512]{3,2,1,0:T(8,128)(2,1)}, bf16[4,2,64,512]{3,2,1,0:T(8,128)(2,1)S(1)}, u32[]{:S(2)}, u32[]{:S(2)}) collective-permute-start(bf16[4,2,64,512]{3,2,1,0:T(8,128)(2,1)} %refs_16_.1), channel_id=1, source_target_pairs={{0,48},{1,17},{2,50},{3,19},{4,52},{5,21},{6,54},{7,23},{16,0},{17... | collective-permute-start | bytes 1572872 | tf_op jit(solution)/shard_map/b_3/ppermute | solution.py:30
  12.4 43.9 %copy-start = (bf16[4,2,32,1024]{3,2,1,0:T(8,128)(2,1)}, bf16[4,2,32,1024]{3,2,1,0:T(8,128)(2,1)S(1)}, u32[]{:S(2)}) copy-start(bf16[4,2,32,1024]{3,2,1,0:T(8,128)(2,1)S(1)} %collective-permute-done.refs_1_) | copy-start | bytes 1572868
  19.2 37.1 %copy-start.1 = (bf16[4,2,64,512]{3,2,1,0:T(8,128)(2,1)}, bf16[4,2,64,512]{3,2,1,0:T(8,128)(2,1)S(1)}, u32[]{:S(2)}) copy-start(bf16[4,2,64,512]{3,2,1,0:T(8,128)(2,1)S(1)} %collective-permute-done.11.refs_20_) | copy-start | bytes 1572868
  19.2 8.9 %collective-permute-start.16 = (bf16[4,2,64,512]{3,2,1,0:T(8,128)(2,1)S(1)}, bf16[4,2,64,512]{3,2,1,0:T(8,128)(2,1)S(1)}, u32[]{:S(2)}, u32[]{:S(2)}) collective-permute-start(bf16[4,2,64,512]{3,2,1,0:T(8,128)(2,1)S(1)} %collective-permute-done.11.refs_20_), channel_id=1, source_target_pairs={{0,16},{1,49},{2,18},{3,51},{4,20},{5,53},{6,22},{7,55},{16,32},{1... | collective-permute-start | bytes 1572872 | tf_op jit(solution)/shard_map/b_x1/ppermute | solution.py:30
  22.0 13.5 %collective-permute-start.4 = (bf16[4,2,32,1024]{3,2,1,0:T(8,128)(2,1)}, bf16[4,2,32,1024]{3,2,1,0:T(8,128)(2,1)S(1)}, u32[]{:S(2)}, u32[]{:S(2)}) collective-permute-start(bf16[4,2,32,1024]{3,2,1,0:T(8,128)(2,1)} %refs_0_.1), channel_id=1, source_target_pairs={{0,8},{1,9},{2,10},{3,11},{4,12},{5,13},{6,14},{7,15},{16,24},{17,... | collective-permute-start | bytes 1572872 | tf_op jit(solution)/shard_map/a_x/ppermute | solution.py:30
  23.5 32.9 %copy-start.2 = (bf16[4,2,32,1024]{3,2,1,0:T(8,128)(2,1)}, bf16[4,2,32,1024]{3,2,1,0:T(8,128)(2,1)S(1)}, u32[]{:S(2)}) copy-start(bf16[4,2,32,1024]{3,2,1,0:T(8,128)(2,1)S(1)} %collective-permute-done.3.refs_3_) | copy-start | bytes 1572868
  23.5 32.9 %copy-start.3 = (bf16[4,2,64,512]{3,2,1,0:T(8,128)(2,1)}, bf16[4,2,64,512]{3,2,1,0:T(8,128)(2,1)S(1)}, u32[]{:S(2)}) copy-start(bf16[4,2,64,512]{3,2,1,0:T(8,128)(2,1)S(1)} %collective-permute-done.12.refs_17_) | copy-start | bytes 1572868
  23.5 12.5 %collective-permute-start.13 = (bf16[4,2,64,512]{3,2,1,0:T(8,128)(2,1)S(1)}, bf16[4,2,64,512]{3,2,1,0:T(8,128)(2,1)S(1)}, u32[]{:S(2)}, u32[]{:S(2)}) collective-permute-start(bf16[4,2,64,512]{3,2,1,0:T(8,128)(2,1)S(1)} %collective-permute-done.12.refs_17_), channel_id=1, source_target_pairs={{0,16},{1,49},{2,18},{3,51},{4,20},{5,53},{6,22},{7,55},{16,32},{1... | collective-permute-start | bytes 1572872 | tf_op jit(solution)/shard_map/b_2/ppermute | solution.py:30
  23.8 12.2 %collective-permute-start.5 = (bf16[4,2,32,1024]{3,2,1,0:T(8,128)(2,1)}, bf16[4,2,32,1024]{3,2,1,0:T(8,128)(2,1)S(1)}, u32[]{:S(2)}, u32[]{:S(2)}) collective-permute-start(bf16[4,2,32,1024]{3,2,1,0:T(8,128)(2,1)} %refs_0_.1), channel_id=1, source_target_pairs={{0,1},{1,0},{2,3},{3,2},{4,5},{5,4},{6,7},{7,6},{16,17},{17,16},{1... | collective-permute-start | bytes 1572872 | tf_op jit(solution)/shard_map/other/ppermute | solution.py:30
  25.1 31.3 %copy-start.4 = (bf16[4,2,64,512]{3,2,1,0:T(8,128)(2,1)}, bf16[4,2,64,512]{3,2,1,0:T(8,128)(2,1)S(1)}, u32[]{:S(2)}) copy-start(bf16[4,2,64,512]{3,2,1,0:T(8,128)(2,1)S(1)} %collective-permute-done.1.refs_19_) | copy-start | bytes 1572868
  25.1 11.8 %collective-permute-start.2 = (bf16[4,2,32,1024]{3,2,1,0:T(8,128)(2,1)S(1)}, bf16[4,2,32,1024]{3,2,1,0:T(8,128)(2,1)}, u32[]{:S(2)}, u32[]{:S(2)}) collective-permute-start(bf16[4,2,32,1024]{3,2,1,0:T(8,128)(2,1)S(1)} %collective-permute-done.refs_1_), channel_id=1, source_target_pairs={{0,2},{1,7},{2,4},{3,1},{4,6},{5,3},{6,0},{7,5},{16,18},{17,23},{1... | collective-permute-start | bytes 1572872 | tf_op jit(solution)/shard_map/a_2/ppermute | solution.py:30
  28.1 28.3 %copy-start.5 = (bf16[4,2,64,512]{3,2,1,0:T(8,128)(2,1)}, bf16[4,2,64,512]{3,2,1,0:T(8,128)(2,1)S(1)}, u32[]{:S(2)}) copy-start(bf16[4,2,64,512]{3,2,1,0:T(8,128)(2,1)S(1)} %collective-permute-done.16.refs_21_) | copy-start | bytes 1572868
  35.5 16.0 %copy-start.6 = (bf16[4,2,32,1024]{3,2,1,0:T(8,128)(2,1)}, bf16[4,2,32,1024]{3,2,1,0:T(8,128)(2,1)S(1)}, u32[]{:S(2)}) copy-start(bf16[4,2,32,1024]{3,2,1,0:T(8,128)(2,1)S(1)} %collective-permute-done.4.refs_4_) | copy-start | bytes 1572868
  35.5 2.6 %collective-permute-start.17 = (bf16[4,2,32,1024]{3,2,1,0:T(8,128)(2,1)S(1)}, bf16[4,2,32,1024]{3,2,1,0:T(8,128)(2,1)S(1)}, u32[]{:S(2)}, u32[]{:S(2)}) collective-permute-start(bf16[4,2,32,1024]{3,2,1,0:T(8,128)(2,1)S(1)} %collective-permute-done.4.refs_4_), channel_id=1, source_target_pairs={{0,1},{1,0},{2,3},{3,2},{4,5},{5,4},{6,7},{7,6},{16,17},{17,16},{1... | collective-permute-start | bytes 1572872 | tf_op jit(solution)/shard_map/other_x/ppermute | solution.py:30
  35.5 5.2 %collective-permute-start.8 = (bf16[4,2,32,1024]{3,2,1,0:T(8,128)(2,1)S(1)}, bf16[4,2,32,1024]{3,2,1,0:T(8,128)(2,1)S(1)}, u32[]{:S(2)}, u32[]{:S(2)}) collective-permute-start(bf16[4,2,32,1024]{3,2,1,0:T(8,128)(2,1)S(1)} %collective-permute-done.3.refs_3_), channel_id=1, source_target_pairs={{0,1},{1,0},{2,3},{3,2},{4,5},{5,4},{6,7},{7,6},{16,17},{17,16},{1... | collective-permute-start | bytes 1572872 | tf_op jit(solution)/shard_map/other_3/ppermute | solution.py:30
  36.0 17.2 %copy-start.7 = (bf16[4,2,64,512]{3,2,1,0:T(8,128)(2,1)}, bf16[4,2,64,512]{3,2,1,0:T(8,128)(2,1)S(1)}, u32[]{:S(2)}) copy-start(bf16[4,2,64,512]{3,2,1,0:T(8,128)(2,1)S(1)} %collective-permute-done.13.refs_18_) | copy-start | bytes 1572868
  36.0 11.3 %collective-permute-start.14 = (bf16[4,2,64,512]{3,2,1,0:T(8,128)(2,1)S(1)}, bf16[4,2,64,512]{3,2,1,0:T(8,128)(2,1)S(1)}, u32[]{:S(2)}, u32[]{:S(2)}) collective-permute-start(bf16[4,2,64,512]{3,2,1,0:T(8,128)(2,1)S(1)} %collective-permute-done.11.refs_20_), channel_id=1, source_target_pairs={{0,48},{1,17},{2,50},{3,19},{4,52},{5,21},{6,54},{7,23},{16,0},{17... | collective-permute-start | bytes 1572872 | tf_op jit(solution)/shard_map/b_x3/ppermute | solution.py:30
  36.0 17.2 %copy-start.8 = (bf16[4,2,32,1024]{3,2,1,0:T(8,128)(2,1)}, bf16[4,2,32,1024]{3,2,1,0:T(8,128)(2,1)S(1)}, u32[]{:S(2)}) copy-start(bf16[4,2,32,1024]{3,2,1,0:T(8,128)(2,1)S(1)} %collective-permute-done.5.refs_8_) | copy-start | bytes 1572868
  36.0 15.5 %collective-permute-start.6 = (bf16[4,2,32,1024]{3,2,1,0:T(8,128)(2,1)S(1)}, bf16[4,2,32,1024]{3,2,1,0:T(8,128)(2,1)}, u32[]{:S(2)}, u32[]{:S(2)}) collective-permute-start(bf16[4,2,32,1024]{3,2,1,0:T(8,128)(2,1)S(1)} %collective-permute-done.4.refs_4_), channel_id=1, source_target_pairs={{0,2},{1,7},{2,4},{3,1},{4,6},{5,3},{6,0},{7,5},{16,18},{17,23},{1... | collective-permute-start | bytes 1572872 | tf_op jit(solution)/shard_map/a_x1/ppermute | solution.py:30
  36.8 12.7 %collective-permute-start.7 = (bf16[4,2,32,1024]{3,2,1,0:T(8,128)(2,1)}, bf16[4,2,32,1024]{3,2,1,0:T(8,128)(2,1)}, u32[]{:S(2)}, u32[]{:S(2)}) collective-permute-start(bf16[4,2,32,1024]{3,2,1,0:T(8,128)(2,1)} %collective-permute-done.2.refs_2_), channel_id=1, source_target_pairs={{0,8},{1,9},{2,10},{3,11},{4,12},{5,13},{6,14},{7,15},{16,24},{17,... | collective-permute-start | bytes 1572872 | tf_op jit(solution)/shard_map/a_x2/ppermute | solution.py:30
  38.0 15.7 %copy-start.9 = (bf16[4,2,32,1024]{3,2,1,0:T(8,128)(2,1)}, bf16[4,2,32,1024]{3,2,1,0:T(8,128)(2,1)S(1)}, u32[]{:S(2)}) copy-start(bf16[4,2,32,1024]{3,2,1,0:T(8,128)(2,1)S(1)} %collective-permute-done.17.refs_12_) | copy-start | bytes 1572868
  38.0 13.4 %collective-permute-start.19 = (bf16[4,2,64,512]{3,2,1,0:T(8,128)(2,1)S(1)}, bf16[4,2,64,512]{3,2,1,0:T(8,128)(2,1)S(1)}, u32[]{:S(2)}, u32[]{:S(2)}) collective-permute-start(bf16[4,2,64,512]{3,2,1,0:T(8,128)(2,1)S(1)} %collective-permute-done.16.refs_21_), channel_id=1, source_target_pairs={{0,16},{1,49},{2,18},{3,51},{4,20},{5,53},{6,22},{7,55},{16,32},{1... | collective-permute-start | bytes 1572872 | tf_op jit(solution)/shard_map/b_x2/ppermute | solution.py:30
  40.6 13.1 %copy-start.10 = (bf16[4,2,32,1024]{3,2,1,0:T(8,128)(2,1)}, bf16[4,2,32,1024]{3,2,1,0:T(8,128)(2,1)S(1)}, u32[]{:S(2)}) copy-start(bf16[4,2,32,1024]{3,2,1,0:T(8,128)(2,1)S(1)} %collective-permute-done.8.refs_11_) | copy-start | bytes 1572868
  40.6 12.6 %collective-permute-start.9 = (bf16[4,2,32,1024]{3,2,1,0:T(8,128)(2,1)S(1)}, bf16[4,2,32,1024]{3,2,1,0:T(8,128)(2,1)}, u32[]{:S(2)}, u32[]{:S(2)}) collective-permute-start(bf16[4,2,32,1024]{3,2,1,0:T(8,128)(2,1)S(1)} %collective-permute-done.4.refs_4_), channel_id=1, source_target_pairs={{0,6},{1,3},{2,0},{3,5},{4,2},{5,7},{6,4},{7,1},{16,22},{17,19},{1... | collective-permute-start | bytes 1572872 | tf_op jit(solution)/shard_map/a_x3/ppermute | solution.py:30
  47.3 6.4 %copy-start.11 = (bf16[4,2,64,512]{3,2,1,0:T(8,128)(2,1)}, bf16[4,2,64,512]{3,2,1,0:T(8,128)(2,1)S(1)}, u32[]{:S(2)}) copy-start(bf16[4,2,64,512]{3,2,1,0:T(8,128)(2,1)S(1)} %collective-permute-done.14.refs_23_) | copy-start | bytes 1572868
  47.3 9.0 %collective-permute-start.15 = (bf16[4,2,32,1024]{3,2,1,0:T(8,128)(2,1)}, bf16[4,2,32,1024]{3,2,1,0:T(8,128)(2,1)}, u32[]{:S(2)}, u32[]{:S(2)}) collective-permute-start(bf16[4,2,32,1024]{3,2,1,0:T(8,128)(2,1)} %collective-permute-done.2.refs_2_), channel_id=1, source_target_pairs={{0,1},{1,0},{2,3},{3,2},{4,5},{5,4},{6,7},{7,6},{16,17},{17,16},{1... | collective-permute-start | bytes 1572872 | tf_op jit(solution)/shard_map/other_2/ppermute | solution.py:30
  49.5 6.8 %collective-permute-start.10 = (bf16[4,2,32,1024]{3,2,1,0:T(8,128)(2,1)S(1)}, bf16[4,2,32,1024]{3,2,1,0:T(8,128)(2,1)}, u32[]{:S(2)}, u32[]{:S(2)}) collective-permute-start(bf16[4,2,32,1024]{3,2,1,0:T(8,128)(2,1)S(1)} %collective-permute-done.refs_1_), channel_id=1, source_target_pairs={{0,1},{1,0},{2,3},{3,2},{4,5},{5,4},{6,7},{7,6},{16,17},{17,16},{1... | collective-permute-start | bytes 1572872 | tf_op jit(solution)/shard_map/other_1/ppermute | solution.py:30
  51.5 4.8 %collective-permute-start.18 = (bf16[4,2,32,1024]{3,2,1,0:T(8,128)(2,1)}, bf16[4,2,32,1024]{3,2,1,0:T(8,128)(2,1)}, u32[]{:S(2)}, u32[]{:S(2)}) collective-permute-start(bf16[4,2,32,1024]{3,2,1,0:T(8,128)(2,1)} %collective-permute-done.6.refs_5_), channel_id=1, source_target_pairs={{0,1},{1,0},{2,3},{3,2},{4,5},{5,4},{6,7},{7,6},{16,17},{17,16},{1... | collective-permute-start | bytes 1572872 | tf_op jit(solution)/shard_map/other_x1/ppermute | solution.py:30
  51.5 2.3 %copy-start.12 = (bf16[4,2,64,512]{3,2,1,0:T(8,128)(2,1)}, bf16[4,2,64,512]{3,2,1,0:T(8,128)(2,1)S(1)}, u32[]{:S(2)}) copy-start(bf16[4,2,64,512]{3,2,1,0:T(8,128)(2,1)S(1)} %collective-permute-done.19.refs_22_) | copy-start | bytes 1572868
  53.2 3.1 %collective-permute-start.21 = (bf16[4,2,32,1024]{3,2,1,0:T(8,128)(2,1)}, bf16[4,2,32,1024]{3,2,1,0:T(8,128)(2,1)}, u32[]{:S(2)}, u32[]{:S(2)}) collective-permute-start(bf16[4,2,32,1024]{3,2,1,0:T(8,128)(2,1)} %collective-permute-done.9.refs_7_), channel_id=1, source_target_pairs={{0,1},{1,0},{2,3},{3,2},{4,5},{5,4},{6,7},{7,6},{16,17},{17,16},{1... | collective-permute-start | bytes 1572872 | tf_op jit(solution)/shard_map/other_x3/ppermute | solution.py:30
  53.2 3.1 %collective-permute-start.20 = (bf16[4,2,32,1024]{3,2,1,0:T(8,128)(2,1)}, bf16[4,2,32,1024]{3,2,1,0:T(8,128)(2,1)}, u32[]{:S(2)}, u32[]{:S(2)}) collective-permute-start(bf16[4,2,32,1024]{3,2,1,0:T(8,128)(2,1)} %collective-permute-done.7.refs_6_), channel_id=1, source_target_pairs={{0,1},{1,0},{2,3},{3,2},{4,5},{5,4},{6,7},{7,6},{16,17},{17,16},{1... | collective-permute-start | bytes 1572872 | tf_op jit(solution)/shard_map/other_x2/ppermute | solution.py:30

commit v4 on v3

--- a/solution.py
+++ b/solution.py
@@ -47,10 +47,11 @@
 
 def multiply_kernel(a_where, b_where, b_row, *refs):
     a_refs, b_refs = refs[:16], refs[16:24]
-    out, a_buf, b_buf, lhs, rhs, a_sem, b_sem = refs[24:]
+    out, a_buf, b_buf, lhs_even, lhs_odd, rhs_even, rhs_odd, a_sem, b_sem = refs[24:]
     freqs = a_buf.shape[1]
     f = pl.program_id(0)
     rcvs = b_buf.shape[4]
+    depth = STEPS * 2 * BLK
 
     def fetch(first_freq, count, slot):
         these = pl.ds(first_freq, count)
@@ -77,33 +78,49 @@
             part = buf.at[:, these]
             pltpu.make_async_copy(part, part, sem.at[slot]).wait()
 
+    def prepare(freq, quarter, lhs, rhs):
+        first = quarter * ROWS
+        block = a_buf[:, freq, :, :, first : first + ROWS].reshape(depth, ROWS)
+        lhs[first : first + ROWS, :] = block.T
+        for step in range(quarter * STEPS // 4, (quarter + 1) * STEPS // 4):
+            real = b_buf[step, freq, 0]
+            imag = b_buf[step, freq, 1]
+            rhs[0, step, 0] = real
+            rhs[0, step, 1] = -imag
+            rhs[1, step, 0] = imag
+            rhs[1, step, 1] = real
+
+    def work(lhs, rhs, next_lhs=None, next_rhs=None):
+        width = rcvs // 2
+        for quarter in range(4):
+            part, first = quarter // 2, quarter % 2 * width
+            right = rhs[part, :, :, :, first : first + width].reshape(depth, width)
+            out[0, part, :, first : first + width] = jnp.dot(
+                lhs[...], right, preferred_element_type=jnp.float32
+            ).astype(out.dtype)
+            if next_lhs is not None:
+                prepare(f + 1, quarter, next_lhs, next_rhs)
+
     @pl.when(f == 0)
     def _():
         fetch(0, 1, 0)
         fetch(1, freqs - 1, 1)
         arrive(0, 1, 0)
-
-    @pl.when(f == 1)
-    def _():
+        for quarter in range(4):
+            prepare(0, quarter, lhs_even, rhs_even)
         arrive(1, freqs - 1, 1)
 
-    for step in range(STEPS):
-        real = b_buf[step, f, 0]
-        imag = b_buf[step, f, 1]
-        rhs[0, step, 0] = real
-        rhs[0, step, 1] = -imag
-        rhs[1, step, 0] = imag
-        rhs[1, step, 1] = real
-
-    depth = STEPS * 2 * BLK
-    for first in range(0, lhs.shape[0], ROWS):
-        block = a_buf[:, f, :, :, first : first + ROWS].reshape(depth, ROWS)
-        lhs[first : first + ROWS, :] = block.T
-
-    for part in range(2):
-        out[0, part] = jnp.dot(
-            lhs[...], rhs[part].reshape(depth, rcvs), preferred_element_type=jnp.float32
-        ).astype(out.dtype)
+    @pl.when(f % 2 == 0)
+    def _():
+        work(lhs_even, rhs_even, lhs_odd, rhs_odd)
+
+    @pl.when((f % 2 == 1) & (f < freqs - 1))
+    def _():
+        work(lhs_odd, rhs_odd, lhs_even, rhs_even)
+
+    @pl.when(f == freqs - 1)
+    def _():
+        work(lhs_odd, rhs_odd)
 
 
 def multiply(a_parts, b_parts, a_where, b_where, b_row):
@@ -122,6 +139,8 @@
                 pltpu.VMEM((STEPS, freqs, 2, BLK, shots), jnp.bfloat16),
                 pltpu.VMEM((STEPS, freqs, 2, BLK, rcvs), jnp.bfloat16),
                 pltpu.VMEM((shots, depth), jnp.bfloat16),
+                pltpu.VMEM((shots, depth), jnp.bfloat16),
+                pltpu.VMEM((2, STEPS, 2, BLK, rcvs), jnp.bfloat16),
                 pltpu.VMEM((2, STEPS, 2, BLK, rcvs), jnp.bfloat16),
                 pltpu.SemaphoreType.DMA((2,)),
                 pltpu.SemaphoreType.DMA((2,)),

time: 68.5 us -> 70.2 us (1.025)
  Pallas kernels: 12 us -> 13.5 us
    pallas_call x1, Pallas kernels: 12 us -> 13.5 us  [multiply(): pl.pallas_call(multiply_kernel, out_shape=jax.ShapeDtypeStruct((freqs, 2,...]
where the time goes in v4:
time: 70.2 us; the launch traced here: 70.1 us
  starting transfers between devices  27.9 us (40%)
  waiting for transfers between devices  25.8 us (37%)
  Pallas kernels  13.5 us (19%)
  other arithmetic  2.48 us (4%)
    ppermute x22, starting transfers between devices, moved(): return lax.ppermute(value, AXES, pairs)  27.9 us
    ppermute x22, waiting for transfers between devices, moved(): return lax.ppermute(value, AXES, pairs)  25.8 us
    pallas_call x1, Pallas kernels, multiply(): pl.pallas_call(multiply_kernel, out_shape=jax.ShapeDtypeStruct((freqs, 2,...  13.5 us
  transfers between devices with their start and end apart: 22, of which 8 were waited for; matrix products, arithmetic and copies ran while one was open for 4% of the time, Pallas kernels for 0%

profile of v4, /device:TPU:1, one launch (start us, length us, event | category | flops | bytes accessed | tf_op | source)
XLA Modules:
  0.0 70.1 jit_solution(15388556112547601820)
XLA Ops:
  0.0 4.6 %collective-permute-start = (bf16[4,2,32,1024]{3,2,1,0:T(8,128)(2,1)}, bf16[4,2,32,1024]{3,2,1,0:T(8,128)(2,1)S(1)}, u32[]{:S(2)}, u32[]{:S(2)}) collective-permute-start(bf16[4,2,32,1024]{3,2,1,0:T(8,128)(2,1)} %refs_0_.1), channel_id=1, source_target_pairs={{0,2},{1,7},{2,4},{3,1},{4,6},{5,3},{6,0},{7,5},{16,18},{17,23},{1... | collective-permute-start | bytes 1572872 | tf_op jit(solution)/shard_map/a_1/ppermute | solution.py:30
  4.6 2.7 %collective-permute-start.11 = (bf16[4,2,64,512]{3,2,1,0:T(8,128)(2,1)}, bf16[4,2,64,512]{3,2,1,0:T(8,128)(2,1)S(1)}, u32[]{:S(2)}, u32[]{:S(2)}) collective-permute-start(bf16[4,2,64,512]{3,2,1,0:T(8,128)(2,1)} %refs_16_.1), channel_id=1, source_target_pairs={{0,64},{1,65},{2,66},{3,67},{4,68},{5,69},{6,70},{7,71},{16,80},{1... | collective-permute-start | bytes 1572872 | tf_op jit(solution)/shard_map/b_x/ppermute | solution.py:30
  7.3 0.0 collective-permute-start.3
  7.3 2.7 %collective-permute-start.12 = (bf16[4,2,64,512]{3,2,1,0:T(8,128)(2,1)}, bf16[4,2,64,512]{3,2,1,0:T(8,128)(2,1)S(1)}, u32[]{:S(2)}, u32[]{:S(2)}) collective-permute-start(bf16[4,2,64,512]{3,2,1,0:T(8,128)(2,1)} %refs_16_.1), channel_id=1, source_target_pairs={{0,16},{1,49},{2,18},{3,51},{4,20},{5,53},{6,22},{7,55},{16,32},{1... | collective-permute-start | bytes 1572872 | tf_op jit(solution)/shard_map/b_1/ppermute | solution.py:30
  10.1 0.0 collective-permute-start.1
  10.1 2.3 %collective-permute-done.refs_1_ = bf16[4,2,32,1024]{3,2,1,0:T(8,128)(2,1)S(1)} collective-permute-done((bf16[4,2,32,1024]{3,2,1,0:T(8,128)(2,1)}, bf16[4,2,32,1024]{3,2,1,0:T(8,128)(2,1)S(1)}, u32[]{:S(2)}, u32[]{:S(2)}) %collective-permute-start) | collective-permute-done | bytes 524320 | tf_op jit(solution)/shard_map/a_1/ppermute | solution.py:30
  12.4 6.8 %collective-permute-done.11.refs_20_ = bf16[4,2,64,512]{3,2,1,0:T(8,128)(2,1)S(1)} collective-permute-done((bf16[4,2,64,512]{3,2,1,0:T(8,128)(2,1)}, bf16[4,2,64,512]{3,2,1,0:T(8,128)(2,1)S(1)}, u32[]{:S(2)}, u32[]{:S(2)}) %collective-permute-start.11) | collective-permute-done | bytes 524320 | tf_op jit(solution)/shard_map/b_x/ppermute | solution.py:30
  19.2 2.7 %collective-permute-start.16 = (bf16[4,2,64,512]{3,2,1,0:T(8,128)(2,1)S(1)}, bf16[4,2,64,512]{3,2,1,0:T(8,128)(2,1)S(1)}, u32[]{:S(2)}, u32[]{:S(2)}) collective-permute-start(bf16[4,2,64,512]{3,2,1,0:T(8,128)(2,1)S(1)} %collective-permute-done.11.refs_20_), channel_id=1, source_target_pairs={{0,16},{1,49},{2,18},{3,51},{4,20},{5,53},{6,22},{7,55},{16,32},{1... | collective-permute-start | bytes 1572872 | tf_op jit(solution)/shard_map/b_x1/ppermute | solution.py:30
  22.0 1.5 %collective-permute-start.4 = (bf16[4,2,32,1024]{3,2,1,0:T(8,128)(2,1)}, bf16[4,2,32,1024]{3,2,1,0:T(8,128)(2,1)S(1)}, u32[]{:S(2)}, u32[]{:S(2)}) collective-permute-start(bf16[4,2,32,1024]{3,2,1,0:T(8,128)(2,1)} %refs_0_.1), channel_id=1, source_target_pairs={{0,8},{1,9},{2,10},{3,11},{4,12},{5,13},{6,14},{7,15},{16,24},{17,... | collective-permute-start | bytes 1572872 | tf_op jit(solution)/shard_map/a_x/ppermute | solution.py:30
  23.5 0.0 collective-permute-done.3.refs_3_
  23.5 0.0 collective-permute-done.12.refs_17_
  23.5 0.2 collective-permute-start.13
  23.8 1.2 %collective-permute-start.5 = (bf16[4,2,32,1024]{3,2,1,0:T(8,128)(2,1)}, bf16[4,2,32,1024]{3,2,1,0:T(8,128)(2,1)S(1)}, u32[]{:S(2)}, u32[]{:S(2)}) collective-permute-start(bf16[4,2,32,1024]{3,2,1,0:T(8,128)(2,1)} %refs_0_.1), channel_id=1, source_target_pairs={{0,1},{1,0},{2,3},{3,2},{4,5},{5,4},{6,7},{7,6},{16,17},{17,16},{1... | collective-permute-start | bytes 1572872 | tf_op jit(solution)/shard_map/other/ppermute | solution.py:30
  24.9 0.1 collective-permute-done.1.refs_19_
  25.1 2.1 %collective-permute-start.2 = (bf16[4,2,32,1024]{3,2,1,0:T(8,128)(2,1)S(1)}, bf16[4,2,32,1024]{3,2,1,0:T(8,128)(2,1)}, u32[]{:S(2)}, u32[]{:S(2)}) collective-permute-start(bf16[4,2,32,1024]{3,2,1,0:T(8,128)(2,1)S(1)} %collective-permute-done.refs_1_), channel_id=1, source_target_pairs={{0,2},{1,7},{2,4},{3,1},{4,6},{5,3},{6,0},{7,5},{16,18},{17,23},{1... | collective-permute-start | bytes 1572872 | tf_op jit(solution)/shard_map/a_2/ppermute | solution.py:30
  27.2 0.9 %collective-permute-done.16.refs_21_ = bf16[4,2,64,512]{3,2,1,0:T(8,128)(2,1)S(1)} collective-permute-done((bf16[4,2,64,512]{3,2,1,0:T(8,128)(2,1)S(1)}, bf16[4,2,64,512]{3,2,1,0:T(8,128)(2,1)S(1)}, u32[]{:S(2)}, u32[]{:S(2)}) %collective-permute-start.16) | collective-permute-done | bytes 524320 | tf_op jit(solution)/shard_map/b_x1/ppermute | solution.py:30
  28.1 7.4 %collective-permute-done.4.refs_4_ = bf16[4,2,32,1024]{3,2,1,0:T(8,128)(2,1)S(1)} collective-permute-done((bf16[4,2,32,1024]{3,2,1,0:T(8,128)(2,1)}, bf16[4,2,32,1024]{3,2,1,0:T(8,128)(2,1)S(1)}, u32[]{:S(2)}, u32[]{:S(2)}) %collective-permute-start.4) | collective-permute-done | bytes 524320 | tf_op jit(solution)/shard_map/a_x/ppermute | solution.py:30
  35.5 0.0 collective-permute-start.17
  35.5 0.5 collective-permute-start.8
  36.0 0.0 collective-permute-done.13.refs_18_
  36.0 0.0 collective-permute-start.14
  36.0 0.0 collective-permute-done.5.refs_8_
  36.0 0.8 %collective-permute-start.6 = (bf16[4,2,32,1024]{3,2,1,0:T(8,128)(2,1)S(1)}, bf16[4,2,32,1024]{3,2,1,0:T(8,128)(2,1)}, u32[]{:S(2)}, u32[]{:S(2)}) collective-permute-start(bf16[4,2,32,1024]{3,2,1,0:T(8,128)(2,1)S(1)} %collective-permute-done.4.refs_4_), channel_id=1, source_target_pairs={{0,2},{1,7},{2,4},{3,1},{4,6},{5,3},{6,0},{7,5},{16,18},{17,23},{1... | collective-permute-start | bytes 1572872 | tf_op jit(solution)/shard_map/a_x1/ppermute | solution.py:30
  36.8 0.0 collective-permute-done.2.refs_2_
  36.8 1.2 %collective-permute-start.7 = (bf16[4,2,32,1024]{3,2,1,0:T(8,128)(2,1)}, bf16[4,2,32,1024]{3,2,1,0:T(8,128)(2,1)}, u32[]{:S(2)}, u32[]{:S(2)}) collective-permute-start(bf16[4,2,32,1024]{3,2,1,0:T(8,128)(2,1)} %collective-permute-done.2.refs_2_), channel_id=1, source_target_pairs={{0,8},{1,9},{2,10},{3,11},{4,12},{5,13},{6,14},{7,15},{16,24},{17,... | collective-permute-start | bytes 1572872 | tf_op jit(solution)/shard_map/a_x2/ppermute | solution.py:30
  38.0 0.0 collective-permute-done.17.refs_12_
  38.0 2.6 %collective-permute-start.19 = (bf16[4,2,64,512]{3,2,1,0:T(8,128)(2,1)S(1)}, bf16[4,2,64,512]{3,2,1,0:T(8,128)(2,1)S(1)}, u32[]{:S(2)}, u32[]{:S(2)}) collective-permute-start(bf16[4,2,64,512]{3,2,1,0:T(8,128)(2,1)S(1)} %collective-permute-done.16.refs_21_), channel_id=1, source_target_pairs={{0,16},{1,49},{2,18},{3,51},{4,20},{5,53},{6,22},{7,55},{16,32},{1... | collective-permute-start | bytes 1572872 | tf_op jit(solution)/shard_map/b_x2/ppermute | solution.py:30
  40.6 0.0 collective-permute-done.8.refs_11_
  40.6 0.4 collective-permute-start.9
  41.1 6.2 %collective-permute-done.14.refs_23_ = bf16[4,2,64,512]{3,2,1,0:T(8,128)(2,1)S(1)} collective-permute-done((bf16[4,2,64,512]{3,2,1,0:T(8,128)(2,1)S(1)}, bf16[4,2,64,512]{3,2,1,0:T(8,128)(2,1)S(1)}, u32[]{:S(2)}, u32[]{:S(2)}) %collective-permute-start.14) | collective-permute-done | bytes 524320 | tf_op jit(solution)/shard_map/b_x3/ppermute | solution.py:30
  47.3 2.0 %collective-permute-start.15 = (bf16[4,2,32,1024]{3,2,1,0:T(8,128)(2,1)}, bf16[4,2,32,1024]{3,2,1,0:T(8,128)(2,1)}, u32[]{:S(2)}, u32[]{:S(2)}) collective-permute-start(bf16[4,2,32,1024]{3,2,1,0:T(8,128)(2,1)} %collective-permute-done.2.refs_2_), channel_id=1, source_target_pairs={{0,1},{1,0},{2,3},{3,2},{4,5},{5,4},{6,7},{7,6},{16,17},{17,16},{1... | collective-permute-start | bytes 1572872 | tf_op jit(solution)/shard_map/other_2/ppermute | solution.py:30
  49.3 0.2 collective-permute-done.7.refs_6_
  49.5 2.0 %collective-permute-start.10 = (bf16[4,2,32,1024]{3,2,1,0:T(8,128)(2,1)S(1)}, bf16[4,2,32,1024]{3,2,1,0:T(8,128)(2,1)}, u32[]{:S(2)}, u32[]{:S(2)}) collective-permute-start(bf16[4,2,32,1024]{3,2,1,0:T(8,128)(2,1)S(1)} %collective-permute-done.refs_1_), channel_id=1, source_target_pairs={{0,1},{1,0},{2,3},{3,2},{4,5},{5,4},{6,7},{7,6},{16,17},{17,16},{1... | collective-permute-start | bytes 1572872 | tf_op jit(solution)/shard_map/other_1/ppermute | solution.py:30
  51.5 0.0 collective-permute-done.6.refs_5_
  51.5 0.0 collective-permute-start.18
  51.5 0.0 collective-permute-done.19.refs_22_
  51.5 1.7 %collective-permute-done.9.refs_7_ = bf16[4,2,32,1024]{3,2,1,0:T(8,128)(2,1)} collective-permute-done((bf16[4,2,32,1024]{3,2,1,0:T(8,128)(2,1)S(1)}, bf16[4,2,32,1024]{3,2,1,0:T(8,128)(2,1)}, u32[]{:S(2)}, u32[]{:S(2)}) %collective-permute-start.9) | collective-permute-done | bytes 524320 | tf_op jit(solution)/shard_map/a_x3/ppermute | solution.py:30
  53.2 0.0 copy-done.7
  53.2 0.0 collective-permute-start.21
  53.2 0.5 collective-permute-start.20
  53.8 1.2 %fusion.1 = (s32[12]{0:T(128)}, s32[12]{0:T(128)S(1)}) fusion(pred[]{:T(512)S(6)} %eq.18, s32[]{:T(128)S(6)} %select_n.83, s32[]{:T(128)S(6)} %select_n.80, s32[12]{0:T(128)} %param.5), kind=kLoop, calls=%fused_computation.25 | loop fusion | flops 612 | bytes 153 | tf_op jit(solution)/shard_map/add | solution.py:167
  55.0 1.3 %broadcast_multiply_fusion = (s32[12]{0:T(128)}, s32[12]{0:T(128)}) fusion(s32[12]{0:T(128)} %param.5, s32[12]{0:T(128)S(1)} %get-tuple-element.30, s32[]{:T(128)S(6)} %select_n.75, s32[]{:T(128)S(6)} %select_n.73, s32[]{:T(128)S(6)} %select_n.71), kind=kLoop, calls=%fused_computation.29 | loop fusion | flops 684 | bytes 204 | tf_op jit(solution)/shard_map/mul | solution.py:168
  56.3 0.0 collective-permute-done.15.refs_10_
  56.3 0.0 collective-permute-done.10.refs_9_
  56.3 0.0 collective-permute-done.18.refs_13_
  56.3 0.0 collective-permute-done.21.refs_15_
  56.3 0.0 collective-permute-done.20.refs_14_
  56.4 13.5 %shard_map.37 = bf16[4,2,1024,512]{3,2,1,0:T(8,128)(2,1)} custom-call(s32[12]{0:T(128)} %get-tuple-element.32.a_where, s32[12]{0:T(128)} %get-tuple-element.29.b_where, s32[12]{0:T(128)} %get-tuple-element.31.b_row, bf16[4,2,32,1024]{3,2,1,0:T(8,128)(2,1)} %refs_0_.1, bf16[4,2,32,1024]{3,2,1,0:T(8,128)(2,1)} %copy-done, ...), custom_call_target="tpu_custom_call" | custom-call | flops 6442450944 | bytes 20971520 | tf_op jit(solution)/shard_map/pallas_call | solution.py:130
  (25 shorter events, 0.0 us)
Async XLA Ops:
  0.0 12.4 %collective-permute-start = (bf16[4,2,32,1024]{3,2,1,0:T(8,128)(2,1)}, bf16[4,2,32,1024]{3,2,1,0:T(8,128)(2,1)S(1)}, u32[]{:S(2)}, u32[]{:S(2)}) collective-permute-start(bf16[4,2,32,1024]{3,2,1,0:T(8,128)(2,1)} %refs_0_.1), channel_id=1, source_target_pairs={{0,2},{1,7},{2,4},{3,1},{4,6},{5,3},{6,0},{7,5},{16,18},{17,23},{1... | collective-permute-start | bytes 1572872 | tf_op jit(solution)/shard_map/a_1/ppermute | solution.py:30
  4.6 14.7 %collective-permute-start.11 = (bf16[4,2,64,512]{3,2,1,0:T(8,128)(2,1)}, bf16[4,2,64,512]{3,2,1,0:T(8,128)(2,1)S(1)}, u32[]{:S(2)}, u32[]{:S(2)}) collective-permute-start(bf16[4,2,64,512]{3,2,1,0:T(8,128)(2,1)} %refs_16_.1), channel_id=1, source_target_pairs={{0,64},{1,65},{2,66},{3,67},{4,68},{5,69},{6,70},{7,71},{16,80},{1... | collective-permute-start | bytes 1572872 | tf_op jit(solution)/shard_map/b_x/ppermute | solution.py:30
  7.3 16.2 %collective-permute-start.3 = (bf16[4,2,32,1024]{3,2,1,0:T(8,128)(2,1)}, bf16[4,2,32,1024]{3,2,1,0:T(8,128)(2,1)S(1)}, u32[]{:S(2)}, u32[]{:S(2)}) collective-permute-start(bf16[4,2,32,1024]{3,2,1,0:T(8,128)(2,1)} %refs_0_.1), channel_id=1, source_target_pairs={{0,6},{1,3},{2,0},{3,5},{4,2},{5,7},{6,4},{7,1},{16,22},{17,19},{1... | collective-permute-start | bytes 1572872 | tf_op jit(solution)/shard_map/a_3/ppermute | solution.py:30
  7.3 16.2 %collective-permute-start.12 = (bf16[4,2,64,512]{3,2,1,0:T(8,128)(2,1)}, bf16[4,2,64,512]{3,2,1,0:T(8,128)(2,1)S(1)}, u32[]{:S(2)}, u32[]{:S(2)}) collective-permute-start(bf16[4,2,64,512]{3,2,1,0:T(8,128)(2,1)} %refs_16_.1), channel_id=1, source_target_pairs={{0,16},{1,49},{2,18},{3,51},{4,20},{5,53},{6,22},{7,55},{16,32},{1... | collective-permute-start | bytes 1572872 | tf_op jit(solution)/shard_map/b_1/ppermute | solution.py:30
  10.1 15.0 %collective-permute-start.1 = (bf16[4,2,64,512]{3,2,1,0:T(8,128)(2,1)}, bf16[4,2,64,512]{3,2,1,0:T(8,128)(2,1)S(1)}, u32[]{:S(2)}, u32[]{:S(2)}) collective-permute-start(bf16[4,2,64,512]{3,2,1,0:T(8,128)(2,1)} %refs_16_.1), channel_id=1, source_target_pairs={{0,48},{1,17},{2,50},{3,19},{4,52},{5,21},{6,54},{7,23},{16,0},{17... | collective-permute-start | bytes 1572872 | tf_op jit(solution)/shard_map/b_3/ppermute | solution.py:30
  12.4 43.9 %copy-start = (bf16[4,2,32,1024]{3,2,1,0:T(8,128)(2,1)}, bf16[4,2,32,1024]{3,2,1,0:T(8,128)(2,1)S(1)}, u32[]{:S(2)}) copy-start(bf16[4,2,32,1024]{3,2,1,0:T(8,128)(2,1)S(1)} %collective-permute-done.refs_1_) | copy-start | bytes 1572868
  19.2 37.1 %copy-start.1 = (bf16[4,2,64,512]{3,2,1,0:T(8,128)(2,1)}, bf16[4,2,64,512]{3,2,1,0:T(8,128)(2,1)S(1)}, u32[]{:S(2)}) copy-start(bf16[4,2,64,512]{3,2,1,0:T(8,128)(2,1)S(1)} %collective-permute-done.11.refs_20_) | copy-start | bytes 1572868
  19.2 8.9 %collective-permute-start.16 = (bf16[4,2,64,512]{3,2,1,0:T(8,128)(2,1)S(1)}, bf16[4,2,64,512]{3,2,1,0:T(8,128)(2,1)S(1)}, u32[]{:S(2)}, u32[]{:S(2)}) collective-permute-start(bf16[4,2,64,512]{3,2,1,0:T(8,128)(2,1)S(1)} %collective-permute-done.11.refs_20_), channel_id=1, source_target_pairs={{0,16},{1,49},{2,18},{3,51},{4,20},{5,53},{6,22},{7,55},{16,32},{1... | collective-permute-start | bytes 1572872 | tf_op jit(solution)/shard_map/b_x1/ppermute | solution.py:30
  22.0 13.5 %collective-permute-start.4 = (bf16[4,2,32,1024]{3,2,1,0:T(8,128)(2,1)}, bf16[4,2,32,1024]{3,2,1,0:T(8,128)(2,1)S(1)}, u32[]{:S(2)}, u32[]{:S(2)}) collective-permute-start(bf16[4,2,32,1024]{3,2,1,0:T(8,128)(2,1)} %refs_0_.1), channel_id=1, source_target_pairs={{0,8},{1,9},{2,10},{3,11},{4,12},{5,13},{6,14},{7,15},{16,24},{17,... | collective-permute-start | bytes 1572872 | tf_op jit(solution)/shard_map/a_x/ppermute | solution.py:30
  23.5 32.9 %copy-start.2 = (bf16[4,2,32,1024]{3,2,1,0:T(8,128)(2,1)}, bf16[4,2,32,1024]{3,2,1,0:T(8,128)(2,1)S(1)}, u32[]{:S(2)}) copy-start(bf16[4,2,32,1024]{3,2,1,0:T(8,128)(2,1)S(1)} %collective-permute-done.3.refs_3_) | copy-start | bytes 1572868
  23.5 32.9 %copy-start.3 = (bf16[4,2,64,512]{3,2,1,0:T(8,128)(2,1)}, bf16[4,2,64,512]{3,2,1,0:T(8,128)(2,1)S(1)}, u32[]{:S(2)}) copy-start(bf16[4,2,64,512]{3,2,1,0:T(8,128)(2,1)S(1)} %collective-permute-done.12.refs_17_) | copy-start | bytes 1572868
  23.5 12.5 %collective-permute-start.13 = (bf16[4,2,64,512]{3,2,1,0:T(8,128)(2,1)S(1)}, bf16[4,2,64,512]{3,2,1,0:T(8,128)(2,1)S(1)}, u32[]{:S(2)}, u32[]{:S(2)}) collective-permute-start(bf16[4,2,64,512]{3,2,1,0:T(8,128)(2,1)S(1)} %collective-permute-done.12.refs_17_), channel_id=1, source_target_pairs={{0,16},{1,49},{2,18},{3,51},{4,20},{5,53},{6,22},{7,55},{16,32},{1... | collective-permute-start | bytes 1572872 | tf_op jit(solution)/shard_map/b_2/ppermute | solution.py:30
  23.8 12.2 %collective-permute-start.5 = (bf16[4,2,32,1024]{3,2,1,0:T(8,128)(2,1)}, bf16[4,2,32,1024]{3,2,1,0:T(8,128)(2,1)S(1)}, u32[]{:S(2)}, u32[]{:S(2)}) collective-permute-start(bf16[4,2,32,1024]{3,2,1,0:T(8,128)(2,1)} %refs_0_.1), channel_id=1, source_target_pairs={{0,1},{1,0},{2,3},{3,2},{4,5},{5,4},{6,7},{7,6},{16,17},{17,16},{1... | collective-permute-start | bytes 1572872 | tf_op jit(solution)/shard_map/other/ppermute | solution.py:30
  25.1 31.3 %copy-start.4 = (bf16[4,2,64,512]{3,2,1,0:T(8,128)(2,1)}, bf16[4,2,64,512]{3,2,1,0:T(8,128)(2,1)S(1)}, u32[]{:S(2)}) copy-start(bf16[4,2,64,512]{3,2,1,0:T(8,128)(2,1)S(1)} %collective-permute-done.1.refs_19_) | copy-start | bytes 1572868
  25.1 11.8 %collective-permute-start.2 = (bf16[4,2,32,1024]{3,2,1,0:T(8,128)(2,1)S(1)}, bf16[4,2,32,1024]{3,2,1,0:T(8,128)(2,1)}, u32[]{:S(2)}, u32[]{:S(2)}) collective-permute-start(bf16[4,2,32,1024]{3,2,1,0:T(8,128)(2,1)S(1)} %collective-permute-done.refs_1_), channel_id=1, source_target_pairs={{0,2},{1,7},{2,4},{3,1},{4,6},{5,3},{6,0},{7,5},{16,18},{17,23},{1... | collective-permute-start | bytes 1572872 | tf_op jit(solution)/shard_map/a_2/ppermute | solution.py:30
  28.1 28.3 %copy-start.5 = (bf16[4,2,64,512]{3,2,1,0:T(8,128)(2,1)}, bf16[4,2,64,512]{3,2,1,0:T(8,128)(2,1)S(1)}, u32[]{:S(2)}) copy-start(bf16[4,2,64,512]{3,2,1,0:T(8,128)(2,1)S(1)} %collective-permute-done.16.refs_21_) | copy-start | bytes 1572868
  35.5 16.0 %copy-start.6 = (bf16[4,2,32,1024]{3,2,1,0:T(8,128)(2,1)}, bf16[4,2,32,1024]{3,2,1,0:T(8,128)(2,1)S(1)}, u32[]{:S(2)}) copy-start(bf16[4,2,32,1024]{3,2,1,0:T(8,128)(2,1)S(1)} %collective-permute-done.4.refs_4_) | copy-start | bytes 1572868
  35.5 2.6 %collective-permute-start.17 = (bf16[4,2,32,1024]{3,2,1,0:T(8,128)(2,1)S(1)}, bf16[4,2,32,1024]{3,2,1,0:T(8,128)(2,1)S(1)}, u32[]{:S(2)}, u32[]{:S(2)}) collective-permute-start(bf16[4,2,32,1024]{3,2,1,0:T(8,128)(2,1)S(1)} %collective-permute-done.4.refs_4_), channel_id=1, source_target_pairs={{0,1},{1,0},{2,3},{3,2},{4,5},{5,4},{6,7},{7,6},{16,17},{17,16},{1... | collective-permute-start | bytes 1572872 | tf_op jit(solution)/shard_map/other_x/ppermute | solution.py:30
  35.5 5.2 %collective-permute-start.8 = (bf16[4,2,32,1024]{3,2,1,0:T(8,128)(2,1)S(1)}, bf16[4,2,32,1024]{3,2,1,0:T(8,128)(2,1)S(1)}, u32[]{:S(2)}, u32[]{:S(2)}) collective-permute-start(bf16[4,2,32,1024]{3,2,1,0:T(8,128)(2,1)S(1)} %collective-permute-done.3.refs_3_), channel_id=1, source_target_pairs={{0,1},{1,0},{2,3},{3,2},{4,5},{5,4},{6,7},{7,6},{16,17},{17,16},{1... | collective-permute-start | bytes 1572872 | tf_op jit(solution)/shard_map/other_3/ppermute | solution.py:30
  36.0 17.2 %copy-start.7 = (bf16[4,2,64,512]{3,2,1,0:T(8,128)(2,1)}, bf16[4,2,64,512]{3,2,1,0:T(8,128)(2,1)S(1)}, u32[]{:S(2)}) copy-start(bf16[4,2,64,512]{3,2,1,0:T(8,128)(2,1)S(1)} %collective-permute-done.13.refs_18_) | copy-start | bytes 1572868
  36.0 11.3 %collective-permute-start.14 = (bf16[4,2,64,512]{3,2,1,0:T(8,128)(2,1)S(1)}, bf16[4,2,64,512]{3,2,1,0:T(8,128)(2,1)S(1)}, u32[]{:S(2)}, u32[]{:S(2)}) collective-permute-start(bf16[4,2,64,512]{3,2,1,0:T(8,128)(2,1)S(1)} %collective-permute-done.11.refs_20_), channel_id=1, source_target_pairs={{0,48},{1,17},{2,50},{3,19},{4,52},{5,21},{6,54},{7,23},{16,0},{17... | collective-permute-start | bytes 1572872 | tf_op jit(solution)/shard_map/b_x3/ppermute | solution.py:30
  36.0 17.2 %copy-start.8 = (bf16[4,2,32,1024]{3,2,1,0:T(8,128)(2,1)}, bf16[4,2,32,1024]{3,2,1,0:T(8,128)(2,1)S(1)}, u32[]{:S(2)}) copy-start(bf16[4,2,32,1024]{3,2,1,0:T(8,128)(2,1)S(1)} %collective-permute-done.5.refs_8_) | copy-start | bytes 1572868
  36.0 15.5 %collective-permute-start.6 = (bf16[4,2,32,1024]{3,2,1,0:T(8,128)(2,1)S(1)}, bf16[4,2,32,1024]{3,2,1,0:T(8,128)(2,1)}, u32[]{:S(2)}, u32[]{:S(2)}) collective-permute-start(bf16[4,2,32,1024]{3,2,1,0:T(8,128)(2,1)S(1)} %collective-permute-done.4.refs_4_), channel_id=1, source_target_pairs={{0,2},{1,7},{2,4},{3,1},{4,6},{5,3},{6,0},{7,5},{16,18},{17,23},{1... | collective-permute-start | bytes 1572872 | tf_op jit(solution)/shard_map/a_x1/ppermute | solution.py:30
  36.8 12.7 %collective-permute-start.7 = (bf16[4,2,32,1024]{3,2,1,0:T(8,128)(2,1)}, bf16[4,2,32,1024]{3,2,1,0:T(8,128)(2,1)}, u32[]{:S(2)}, u32[]{:S(2)}) collective-permute-start(bf16[4,2,32,1024]{3,2,1,0:T(8,128)(2,1)} %collective-permute-done.2.refs_2_), channel_id=1, source_target_pairs={{0,8},{1,9},{2,10},{3,11},{4,12},{5,13},{6,14},{7,15},{16,24},{17,... | collective-permute-start | bytes 1572872 | tf_op jit(solution)/shard_map/a_x2/ppermute | solution.py:30
  38.0 15.7 %copy-start.9 = (bf16[4,2,32,1024]{3,2,1,0:T(8,128)(2,1)}, bf16[4,2,32,1024]{3,2,1,0:T(8,128)(2,1)S(1)}, u32[]{:S(2)}) copy-start(bf16[4,2,32,1024]{3,2,1,0:T(8,128)(2,1)S(1)} %collective-permute-done.17.refs_12_) | copy-start | bytes 1572868
  38.0 13.4 %collective-permute-start.19 = (bf16[4,2,64,512]{3,2,1,0:T(8,128)(2,1)S(1)}, bf16[4,2,64,512]{3,2,1,0:T(8,128)(2,1)S(1)}, u32[]{:S(2)}, u32[]{:S(2)}) collective-permute-start(bf16[4,2,64,512]{3,2,1,0:T(8,128)(2,1)S(1)} %collective-permute-done.16.refs_21_), channel_id=1, source_target_pairs={{0,16},{1,49},{2,18},{3,51},{4,20},{5,53},{6,22},{7,55},{16,32},{1... | collective-permute-start | bytes 1572872 | tf_op jit(solution)/shard_map/b_x2/ppermute | solution.py:30
  40.6 13.1 %copy-start.10 = (bf16[4,2,32,1024]{3,2,1,0:T(8,128)(2,1)}, bf16[4,2,32,1024]{3,2,1,0:T(8,128)(2,1)S(1)}, u32[]{:S(2)}) copy-start(bf16[4,2,32,1024]{3,2,1,0:T(8,128)(2,1)S(1)} %collective-permute-done.8.refs_11_) | copy-start | bytes 1572868
  40.6 12.6 %collective-permute-start.9 = (bf16[4,2,32,1024]{3,2,1,0:T(8,128)(2,1)S(1)}, bf16[4,2,32,1024]{3,2,1,0:T(8,128)(2,1)}, u32[]{:S(2)}, u32[]{:S(2)}) collective-permute-start(bf16[4,2,32,1024]{3,2,1,0:T(8,128)(2,1)S(1)} %collective-permute-done.4.refs_4_), channel_id=1, source_target_pairs={{0,6},{1,3},{2,0},{3,5},{4,2},{5,7},{6,4},{7,1},{16,22},{17,19},{1... | collective-permute-start | bytes 1572872 | tf_op jit(solution)/shard_map/a_x3/ppermute | solution.py:30
  47.3 6.4 %copy-start.11 = (bf16[4,2,64,512]{3,2,1,0:T(8,128)(2,1)}, bf16[4,2,64,512]{3,2,1,0:T(8,128)(2,1)S(1)}, u32[]{:S(2)}) copy-start(bf16[4,2,64,512]{3,2,1,0:T(8,128)(2,1)S(1)} %collective-permute-done.14.refs_23_) | copy-start | bytes 1572868
  47.3 9.0 %collective-permute-start.15 = (bf16[4,2,32,1024]{3,2,1,0:T(8,128)(2,1)}, bf16[4,2,32,1024]{3,2,1,0:T(8,128)(2,1)}, u32[]{:S(2)}, u32[]{:S(2)}) collective-permute-start(bf16[4,2,32,1024]{3,2,1,0:T(8,128)(2,1)} %collective-permute-done.2.refs_2_), channel_id=1, source_target_pairs={{0,1},{1,0},{2,3},{3,2},{4,5},{5,4},{6,7},{7,6},{16,17},{17,16},{1... | collective-permute-start | bytes 1572872 | tf_op jit(solution)/shard_map/other_2/ppermute | solution.py:30
  49.5 6.8 %collective-permute-start.10 = (bf16[4,2,32,1024]{3,2,1,0:T(8,128)(2,1)S(1)}, bf16[4,2,32,1024]{3,2,1,0:T(8,128)(2,1)}, u32[]{:S(2)}, u32[]{:S(2)}) collective-permute-start(bf16[4,2,32,1024]{3,2,1,0:T(8,128)(2,1)S(1)} %collective-permute-done.refs_1_), channel_id=1, source_target_pairs={{0,1},{1,0},{2,3},{3,2},{4,5},{5,4},{6,7},{7,6},{16,17},{17,16},{1... | collective-permute-start | bytes 1572872 | tf_op jit(solution)/shard_map/other_1/ppermute | solution.py:30
  51.5 4.8 %collective-permute-start.18 = (bf16[4,2,32,1024]{3,2,1,0:T(8,128)(2,1)}, bf16[4,2,32,1024]{3,2,1,0:T(8,128)(2,1)}, u32[]{:S(2)}, u32[]{:S(2)}) collective-permute-start(bf16[4,2,32,1024]{3,2,1,0:T(8,128)(2,1)} %collective-permute-done.6.refs_5_), channel_id=1, source_target_pairs={{0,1},{1,0},{2,3},{3,2},{4,5},{5,4},{6,7},{7,6},{16,17},{17,16},{1... | collective-permute-start | bytes 1572872 | tf_op jit(solution)/shard_map/other_x1/ppermute | solution.py:30
  51.5 2.3 %copy-start.12 = (bf16[4,2,64,512]{3,2,1,0:T(8,128)(2,1)}, bf16[4,2,64,512]{3,2,1,0:T(8,128)(2,1)S(1)}, u32[]{:S(2)}) copy-start(bf16[4,2,64,512]{3,2,1,0:T(8,128)(2,1)S(1)} %collective-permute-done.19.refs_22_) | copy-start | bytes 1572868
  53.2 3.1 %collective-permute-start.21 = (bf16[4,2,32,1024]{3,2,1,0:T(8,128)(2,1)}, bf16[4,2,32,1024]{3,2,1,0:T(8,128)(2,1)}, u32[]{:S(2)}, u32[]{:S(2)}) collective-permute-start(bf16[4,2,32,1024]{3,2,1,0:T(8,128)(2,1)} %collective-permute-done.9.refs_7_), channel_id=1, source_target_pairs={{0,1},{1,0},{2,3},{3,2},{4,5},{5,4},{6,7},{7,6},{16,17},{17,16},{1... | collective-permute-start | bytes 1572872 | tf_op jit(solution)/shard_map/other_x3/ppermute | solution.py:30
  53.2 3.1 %collective-permute-start.20 = (bf16[4,2,32,1024]{3,2,1,0:T(8,128)(2,1)}, bf16[4,2,32,1024]{3,2,1,0:T(8,128)(2,1)}, u32[]{:S(2)}, u32[]{:S(2)}) collective-permute-start(bf16[4,2,32,1024]{3,2,1,0:T(8,128)(2,1)} %collective-permute-done.7.refs_6_), channel_id=1, source_target_pairs={{0,1},{1,0},{2,3},{3,2},{4,5},{5,4},{6,7},{7,6},{16,17},{17,16},{1... | collective-permute-start | bytes 1572872 | tf_op jit(solution)/shard_map/other_x2/ppermute | solution.py:30

commit v5 on v3

--- a/solution.py
+++ b/solution.py
@@ -54,8 +54,9 @@
 
     def fetch(first_freq, count, slot):
         these = pl.ds(first_freq, count)
-        for step in range(STEPS):
-
+
+        @pl.loop(0, STEPS)
+        def _(step):
             def from_surface(ref):
                 pltpu.make_async_copy(
                     ref.at[these], a_buf.at[step, these], a_sem.at[slot]
@@ -87,7 +88,8 @@
     def _():
         arrive(1, freqs - 1, 1)
 
-    for step in range(STEPS):
+    @pl.loop(0, STEPS)
+    def _(step):
         real = b_buf[step, f, 0]
         imag = b_buf[step, f, 1]
         rhs[0, step, 0] = real
@@ -96,11 +98,14 @@
         rhs[1, step, 1] = real
 
     depth = STEPS * 2 * BLK
-    for first in range(0, lhs.shape[0], ROWS):
-        block = a_buf[:, f, :, :, first : first + ROWS].reshape(depth, ROWS)
-        lhs[first : first + ROWS, :] = block.T
-
-    for part in range(2):
+
+    @pl.loop(0, lhs.shape[0] // ROWS)
+    def _(tile):
+        rows = pl.ds(pl.multiple_of(tile * ROWS, ROWS), ROWS)
+        lhs[rows, :] = a_buf[:, f, :, :, rows].reshape(depth, ROWS).T
+
+    @pl.loop(0, 2)
+    def _(part):
         out[0, part] = jnp.dot(
             lhs[...], rhs[part].reshape(depth, rcvs), preferred_element_type=jnp.float32
         ).astype(out.dtype)
@@ -163,28 +168,28 @@
     def swap(name, value):
         return send(name, value, flip_core=True)
 
-    a_1 = send("a_1", a, dz=1)
+    b_3 = send("b_3", b, dy=-1)
     b_x = send("b_x", b, dx=2)
     a_3 = send("a_3", a, dz=-1)
-    b_3 = send("b_3", b, dy=-1)
     b_1 = send("b_1", b, dy=1)
-    a_x = send("a_x", after(a, a_1), flip_x=True)
-    b_x1 = send("b_x1", b_x, dy=1)
-    other = swap("other", after(a, a_3))
-    a_2 = send("a_2", after(a_1, b_3), dz=1)
-    b_2 = send("b_2", b_1, dy=1)
-    other_3 = swap("other_3", after(a_3, a_x))
-    other_x = swap("other_x", after(a_x, b_x1))
-    a_x1 = send("a_x1", after(a_x, other), dz=1)
-    a_x2 = send("a_x2", a_2, flip_x=True)
-    b_x3 = send("b_x3", after(b_x, b_2), dy=-1)
-    a_x3 = send("a_x3", after(a_x, other_3), dz=-1)
-    b_x2 = send("b_x2", after(b_x1, other_x), dy=1)
+    a_1 = send("a_1", a, dz=1)
+    a_x = send("a_x", after(a, b_3), flip_x=True)
+    other_3 = swap("other_3", after(a_3, b_x))
+    b_x1 = send("b_x1", after(b_x, a_3), dy=1)
+    a_2 = send("a_2", after(a_1, b_1), dz=1)
+    b_x3 = send("b_x3", after(b_x, a_1), dy=-1)
+    a_x3 = send("a_x3", a_x, dz=-1)
+    b_2 = send("b_2", after(b_1, other_3), dy=1)
+    a_x2 = send("a_x2", after(a_2, b_x1), flip_x=True)
+    b_x2 = send("b_x2", after(b_x1, a_2), dy=1)
+    a_x1 = send("a_x1", after(a_x, b_x3), dz=1)
+    other = swap("other", after(a, a_x3))
+    other_2 = swap("other_2", after(a_2, b_2))
+    other_1 = swap("other_1", after(a_1, a_x2))
+    other_x2 = swap("other_x2", after(a_x2, b_x2))
     other_x1 = swap("other_x1", a_x1)
-    other_1 = swap("other_1", after(a_1, a_x2))
-    other_2 = swap("other_2", after(a_2, b_x3))
-    other_x3 = swap("other_x3", a_x3)
-    other_x2 = swap("other_x2", after(a_x2, b_x2))
+    other_x = swap("other_x", after(a_x, other))
+    other_x3 = swap("other_x3", after(a_x3, other_2))
 
     a_parts = [a, a_1, a_2, a_3, a_x, a_x1, a_x2, a_x3]
     a_parts += [other, other_1, other_2, other_3, other_x, other_x1, other_x2, other_x3]

time: 68.5 us -> 69.9 us (1.020)
  waiting for transfers between devices: 25.8 us -> 13.3 us
  starting transfers between devices: 27.9 us -> 38 us
  Pallas kernels: 12 us -> 15.5 us
    ppermute x22, waiting for transfers between devices: 25.8 us -> 13.3 us  [moved(): return lax.ppermute(value, AXES, pairs)]
    ppermute x22, starting transfers between devices: 27.9 us -> 38 us  [moved(): return lax.ppermute(value, AXES, pairs)]
    pallas_call x1, Pallas kernels: 12 us -> 15.5 us  [multiply(): pl.pallas_call(multiply_kernel, out_shape=jax.ShapeDtypeStruct((freqs, 2,...]
  transfers between devices with their start and end apart: 22 -> 22, of which waited for: 8 -> 6; matrix products, arithmetic and copies ran while one was open for 4% -> 4% of each run, Pallas kernels for 0% -> 0%
where the time goes in v5:
time: 69.9 us; the launch traced here: 69.8 us
  starting transfers between devices  38 us (54%)
  Pallas kernels  15.5 us (22%)
  waiting for transfers between devices  13.3 us (19%)
  other arithmetic  2.52 us (4%)
    ppermute x22, starting transfers between devices, moved(): return lax.ppermute(value, AXES, pairs)  38 us
    pallas_call x1, Pallas kernels, multiply(): pl.pallas_call(multiply_kernel, out_shape=jax.ShapeDtypeStruct((freqs, 2,...  15.5 us
    ppermute x22, waiting for transfers between devices, moved(): return lax.ppermute(value, AXES, pairs)  13.3 us
  transfers between devices with their start and end apart: 22, of which 6 were waited for; matrix products, arithmetic and copies ran while one was open for 4% of the time, Pallas kernels for 0%

profile of v5, /device:TPU:1, one launch (start us, length us, event | category | flops | bytes accessed | tf_op | source)
XLA Modules:
  0.0 69.8 jit_solution(8368462788903384404)
XLA Ops:
  0.0 2.1 %collective-permute-start.4 = (bf16[4,2,64,512]{3,2,1,0:T(8,128)(2,1)}, bf16[4,2,64,512]{3,2,1,0:T(8,128)(2,1)S(1)}, u32[]{:S(2)}, u32[]{:S(2)}) collective-permute-start(bf16[4,2,64,512]{3,2,1,0:T(8,128)(2,1)} %refs_16_.1), channel_id=1, source_target_pairs={{0,48},{1,17},{2,50},{3,19},{4,52},{5,21},{6,54},{7,23},{16,0},{17... | collective-permute-start | bytes 1572872 | tf_op jit(solution)/shard_map/b_3/ppermute | solution.py:30
  2.1 2.7 %collective-permute-start.6 = (bf16[4,2,64,512]{3,2,1,0:T(8,128)(2,1)}, bf16[4,2,64,512]{3,2,1,0:T(8,128)(2,1)S(1)}, u32[]{:S(2)}, u32[]{:S(2)}) collective-permute-start(bf16[4,2,64,512]{3,2,1,0:T(8,128)(2,1)} %refs_16_.1), channel_id=1, source_target_pairs={{0,64},{1,65},{2,66},{3,67},{4,68},{5,69},{6,70},{7,71},{16,80},{1... | collective-permute-start | bytes 1572872 | tf_op jit(solution)/shard_map/b_x/ppermute | solution.py:30
  4.9 1.6 %collective-permute-start.3 = (bf16[4,2,32,1024]{3,2,1,0:T(8,128)(2,1)}, bf16[4,2,32,1024]{3,2,1,0:T(8,128)(2,1)S(1)}, u32[]{:S(2)}, u32[]{:S(2)}) collective-permute-start(bf16[4,2,32,1024]{3,2,1,0:T(8,128)(2,1)} %refs_0_.1), channel_id=1, source_target_pairs={{0,6},{1,3},{2,0},{3,5},{4,2},{5,7},{6,4},{7,1},{16,22},{17,19},{1... | collective-permute-start | bytes 1572872 | tf_op jit(solution)/shard_map/a_3/ppermute | solution.py:30
  6.5 1.4 %collective-permute-start.1 = (bf16[4,2,64,512]{3,2,1,0:T(8,128)(2,1)}, bf16[4,2,64,512]{3,2,1,0:T(8,128)(2,1)S(1)}, u32[]{:S(2)}, u32[]{:S(2)}) collective-permute-start(bf16[4,2,64,512]{3,2,1,0:T(8,128)(2,1)} %refs_16_.1), channel_id=1, source_target_pairs={{0,16},{1,49},{2,18},{3,51},{4,20},{5,53},{6,22},{7,55},{16,32},{1... | collective-permute-start | bytes 1572872 | tf_op jit(solution)/shard_map/b_1/ppermute | solution.py:30
  8.0 2.1 %collective-permute-start = (bf16[4,2,32,1024]{3,2,1,0:T(8,128)(2,1)}, bf16[4,2,32,1024]{3,2,1,0:T(8,128)(2,1)S(1)}, u32[]{:S(2)}, u32[]{:S(2)}) collective-permute-start(bf16[4,2,32,1024]{3,2,1,0:T(8,128)(2,1)} %refs_0_.1), channel_id=1, source_target_pairs={{0,2},{1,7},{2,4},{3,1},{4,6},{5,3},{6,0},{7,5},{16,18},{17,23},{1... | collective-permute-start | bytes 1572872 | tf_op jit(solution)/shard_map/a_1/ppermute | solution.py:30
  10.1 0.6 collective-permute-done.4.refs_19_
  10.6 1.1 %collective-permute-start.5 = (bf16[4,2,32,1024]{3,2,1,0:T(8,128)(2,1)}, bf16[4,2,32,1024]{3,2,1,0:T(8,128)(2,1)S(1)}, u32[]{:S(2)}, u32[]{:S(2)}) collective-permute-start(bf16[4,2,32,1024]{3,2,1,0:T(8,128)(2,1)} %refs_0_.1), channel_id=1, source_target_pairs={{0,8},{1,9},{2,10},{3,11},{4,12},{5,13},{6,14},{7,15},{16,24},{17,... | collective-permute-start | bytes 1572872 | tf_op jit(solution)/shard_map/a_x/ppermute | solution.py:30
  11.7 3.2 %collective-permute-done.6.refs_20_ = bf16[4,2,64,512]{3,2,1,0:T(8,128)(2,1)S(1)} collective-permute-done((bf16[4,2,64,512]{3,2,1,0:T(8,128)(2,1)}, bf16[4,2,64,512]{3,2,1,0:T(8,128)(2,1)S(1)}, u32[]{:S(2)}, u32[]{:S(2)}) %collective-permute-start.6) | collective-permute-done | bytes 524320 | tf_op jit(solution)/shard_map/b_x/ppermute | solution.py:30
  14.9 0.8 %collective-permute-done.3.refs_3_ = bf16[4,2,32,1024]{3,2,1,0:T(8,128)(2,1)S(1)} collective-permute-done((bf16[4,2,32,1024]{3,2,1,0:T(8,128)(2,1)}, bf16[4,2,32,1024]{3,2,1,0:T(8,128)(2,1)S(1)}, u32[]{:S(2)}, u32[]{:S(2)}) %collective-permute-start.3) | collective-permute-done | bytes 524320 | tf_op jit(solution)/shard_map/a_3/ppermute | solution.py:30
  15.7 6.8 %collective-permute-start.14 = (bf16[4,2,32,1024]{3,2,1,0:T(8,128)(2,1)S(1)}, bf16[4,2,32,1024]{3,2,1,0:T(8,128)(2,1)S(1)}, u32[]{:S(2)}, u32[]{:S(2)}) collective-permute-start(bf16[4,2,32,1024]{3,2,1,0:T(8,128)(2,1)S(1)} %collective-permute-done.3.refs_3_), channel_id=1, source_target_pairs={{0,1},{1,0},{2,3},{3,2},{4,5},{5,4},{6,7},{7,6},{16,17},{17,16},{1... | collective-permute-start | bytes 1572872 | tf_op jit(solution)/shard_map/other_3/ppermute | solution.py:30
  22.5 1.5 %collective-permute-start.9 = (bf16[4,2,64,512]{3,2,1,0:T(8,128)(2,1)S(1)}, bf16[4,2,64,512]{3,2,1,0:T(8,128)(2,1)S(1)}, u32[]{:S(2)}, u32[]{:S(2)}) collective-permute-start(bf16[4,2,64,512]{3,2,1,0:T(8,128)(2,1)S(1)} %collective-permute-done.6.refs_20_), channel_id=1, source_target_pairs={{0,16},{1,49},{2,18},{3,51},{4,20},{5,53},{6,22},{7,55},{16,32},{1... | collective-permute-start | bytes 1572872 | tf_op jit(solution)/shard_map/b_x1/ppermute | solution.py:30
  24.0 0.0 collective-permute-done.1.refs_17_
  24.0 0.0 collective-permute-done.refs_1_
  24.0 3.4 %collective-permute-start.2 = (bf16[4,2,32,1024]{3,2,1,0:T(8,128)(2,1)S(1)}, bf16[4,2,32,1024]{3,2,1,0:T(8,128)(2,1)S(1)}, u32[]{:S(2)}, u32[]{:S(2)}) collective-permute-start(bf16[4,2,32,1024]{3,2,1,0:T(8,128)(2,1)S(1)} %collective-permute-done.refs_1_), channel_id=1, source_target_pairs={{0,2},{1,7},{2,4},{3,1},{4,6},{5,3},{6,0},{7,5},{16,18},{17,23},{1... | collective-permute-start | bytes 1572872 | tf_op jit(solution)/shard_map/a_2/ppermute | solution.py:30
  27.4 0.0 collective-permute-start.7
  27.4 0.0 collective-permute-done.5.refs_4_
  27.4 0.4 collective-permute-start.11
  27.8 0.0 collective-permute-done.14.refs_11_
  27.8 2.4 %collective-permute-start.15 = (bf16[4,2,64,512]{3,2,1,0:T(8,128)(2,1)S(1)}, bf16[4,2,64,512]{3,2,1,0:T(8,128)(2,1)S(1)}, u32[]{:S(2)}, u32[]{:S(2)}) collective-permute-start(bf16[4,2,64,512]{3,2,1,0:T(8,128)(2,1)S(1)} %collective-permute-done.1.refs_17_), channel_id=1, source_target_pairs={{0,16},{1,49},{2,18},{3,51},{4,20},{5,53},{6,22},{7,55},{16,32},{1... | collective-permute-start | bytes 1572872 | tf_op jit(solution)/shard_map/b_2/ppermute | solution.py:30
  30.3 3.8 %collective-permute-done.9.refs_21_ = bf16[4,2,64,512]{3,2,1,0:T(8,128)(2,1)S(1)} collective-permute-done((bf16[4,2,64,512]{3,2,1,0:T(8,128)(2,1)S(1)}, bf16[4,2,64,512]{3,2,1,0:T(8,128)(2,1)S(1)}, u32[]{:S(2)}, u32[]{:S(2)}) %collective-permute-start.9) | collective-permute-done | bytes 524320 | tf_op jit(solution)/shard_map/b_x1/ppermute | solution.py:30
  34.0 0.0 collective-permute-done.2.refs_2_
  34.0 0.4 collective-permute-start.10
  34.4 1.1 %collective-permute-start.19 = (bf16[4,2,64,512]{3,2,1,0:T(8,128)(2,1)S(1)}, bf16[4,2,64,512]{3,2,1,0:T(8,128)(2,1)S(1)}, u32[]{:S(2)}, u32[]{:S(2)}) collective-permute-start(bf16[4,2,64,512]{3,2,1,0:T(8,128)(2,1)S(1)} %collective-permute-done.9.refs_21_), channel_id=1, source_target_pairs={{0,16},{1,49},{2,18},{3,51},{4,20},{5,53},{6,22},{7,55},{16,32},{1... | collective-permute-start | bytes 1572872 | tf_op jit(solution)/shard_map/b_x2/ppermute | solution.py:30
  35.5 2.8 %collective-permute-done.7.refs_23_ = bf16[4,2,64,512]{3,2,1,0:T(8,128)(2,1)S(1)} collective-permute-done((bf16[4,2,64,512]{3,2,1,0:T(8,128)(2,1)S(1)}, bf16[4,2,64,512]{3,2,1,0:T(8,128)(2,1)S(1)}, u32[]{:S(2)}, u32[]{:S(2)}) %collective-permute-start.7) | collective-permute-done | bytes 524320 | tf_op jit(solution)/shard_map/b_x3/ppermute | solution.py:30
  38.3 4.4 %collective-permute-start.8 = (bf16[4,2,32,1024]{3,2,1,0:T(8,128)(2,1)S(1)}, bf16[4,2,32,1024]{3,2,1,0:T(8,128)(2,1)}, u32[]{:S(2)}, u32[]{:S(2)}) collective-permute-start(bf16[4,2,32,1024]{3,2,1,0:T(8,128)(2,1)S(1)} %collective-permute-done.5.refs_4_), channel_id=1, source_target_pairs={{0,2},{1,7},{2,4},{3,1},{4,6},{5,3},{6,0},{7,5},{16,18},{17,23},{1... | collective-permute-start | bytes 1572872 | tf_op jit(solution)/shard_map/a_x1/ppermute | solution.py:30
  42.8 0.0 collective-permute-done.11.refs_7_
  42.8 0.0 collective-permute-start.12
  42.8 0.0 collective-permute-done.15.refs_18_
  42.8 1.4 %collective-permute-start.16 = (bf16[4,2,32,1024]{3,2,1,0:T(8,128)(2,1)S(1)}, bf16[4,2,32,1024]{3,2,1,0:T(8,128)(2,1)S(1)}, u32[]{:S(2)}, u32[]{:S(2)}) collective-permute-start(bf16[4,2,32,1024]{3,2,1,0:T(8,128)(2,1)S(1)} %collective-permute-done.2.refs_2_), channel_id=1, source_target_pairs={{0,1},{1,0},{2,3},{3,2},{4,5},{5,4},{6,7},{7,6},{16,17},{17,16},{1... | collective-permute-start | bytes 1572872 | tf_op jit(solution)/shard_map/other_2/ppermute | solution.py:30
  44.2 2.1 %collective-permute-done.10.refs_6_ = bf16[4,2,32,1024]{3,2,1,0:T(8,128)(2,1)} collective-permute-done((bf16[4,2,32,1024]{3,2,1,0:T(8,128)(2,1)S(1)}, bf16[4,2,32,1024]{3,2,1,0:T(8,128)(2,1)}, u32[]{:S(2)}, u32[]{:S(2)}) %collective-permute-start.10) | collective-permute-done | bytes 524320 | tf_op jit(solution)/shard_map/a_x2/ppermute | solution.py:30
  46.3 2.3 %collective-permute-start.13 = (bf16[4,2,32,1024]{3,2,1,0:T(8,128)(2,1)S(1)}, bf16[4,2,32,1024]{3,2,1,0:T(8,128)(2,1)}, u32[]{:S(2)}, u32[]{:S(2)}) collective-permute-start(bf16[4,2,32,1024]{3,2,1,0:T(8,128)(2,1)S(1)} %collective-permute-done.refs_1_), channel_id=1, source_target_pairs={{0,1},{1,0},{2,3},{3,2},{4,5},{5,4},{6,7},{7,6},{16,17},{17,16},{1... | collective-permute-start | bytes 1572872 | tf_op jit(solution)/shard_map/other_1/ppermute | solution.py:30
  48.6 0.0 collective-permute-done.19.refs_22_
  48.6 1.2 %collective-permute-start.20 = (bf16[4,2,32,1024]{3,2,1,0:T(8,128)(2,1)}, bf16[4,2,32,1024]{3,2,1,0:T(8,128)(2,1)}, u32[]{:S(2)}, u32[]{:S(2)}) collective-permute-start(bf16[4,2,32,1024]{3,2,1,0:T(8,128)(2,1)} %collective-permute-done.10.refs_6_), channel_id=1, source_target_pairs={{0,1},{1,0},{2,3},{3,2},{4,5},{5,4},{6,7},{7,6},{16,17},{17,16},{1... | collective-permute-start | bytes 1572872 | tf_op jit(solution)/shard_map/other_x2/ppermute | solution.py:30
  49.8 0.0 collective-permute-done.8.refs_5_
  49.8 0.8 %collective-permute-start.18 = (bf16[4,2,32,1024]{3,2,1,0:T(8,128)(2,1)}, bf16[4,2,32,1024]{3,2,1,0:T(8,128)(2,1)}, u32[]{:S(2)}, u32[]{:S(2)}) collective-permute-start(bf16[4,2,32,1024]{3,2,1,0:T(8,128)(2,1)} %collective-permute-done.8.refs_5_), channel_id=1, source_target_pairs={{0,1},{1,0},{2,3},{3,2},{4,5},{5,4},{6,7},{7,6},{16,17},{17,16},{1... | collective-permute-start | bytes 1572872 | tf_op jit(solution)/shard_map/other_x1/ppermute | solution.py:30
  50.6 0.0 collective-permute-done.12.refs_8_
  50.7 0.1 collective-permute-start.17
  50.8 0.0 collective-permute-done.16.refs_10_
  50.8 0.6 collective-permute-start.21
  51.3 0.1 copy-done.12
  51.5 0.2 copy-done.13
  51.6 1.3 %fusion.1 = (s32[12]{0:T(128)}, s32[12]{0:T(128)S(1)}) fusion(pred[]{:T(512)S(6)} %eq.18, s32[]{:T(128)S(6)} %select_n.83, s32[]{:T(128)S(6)} %select_n.80, s32[12]{0:T(128)} %param.5), kind=kLoop, calls=%fused_computation.25 | loop fusion | flops 612 | bytes 153 | tf_op jit(solution)/shard_map/add | solution.py:153
  52.9 1.2 %broadcast_multiply_fusion = (s32[12]{0:T(128)}, s32[12]{0:T(128)}) fusion(s32[12]{0:T(128)} %param.5, s32[12]{0:T(128)S(1)} %get-tuple-element.36, s32[]{:T(128)S(6)} %select_n.75, s32[]{:T(128)S(6)} %select_n.73, s32[]{:T(128)S(6)} %select_n.71), kind=kLoop, calls=%fused_computation.29 | loop fusion | flops 684 | bytes 204 | tf_op jit(solution)/shard_map/mul | solution.py:154
  54.2 0.0 collective-permute-done.13.refs_9_
  54.2 0.0 collective-permute-done.20.refs_14_
  54.2 0.0 collective-permute-done.18.refs_13_
  54.2 0.0 collective-permute-done.17.refs_12_
  54.3 15.5 %shard_map.37 = bf16[4,2,1024,512]{3,2,1,0:T(8,128)(2,1)} custom-call(s32[12]{0:T(128)} %get-tuple-element.38.a_where, s32[12]{0:T(128)} %get-tuple-element.35.b_where, s32[12]{0:T(128)} %get-tuple-element.37.b_row, bf16[4,2,32,1024]{3,2,1,0:T(8,128)(2,1)} %refs_0_.1, bf16[4,2,32,1024]{3,2,1,0:T(8,128)(2,1)} %copy-done.4, ...), custom_call_target="tpu_custom_call" | custom-call | flops 6442450944 | bytes 20971520 | tf_op jit(solution)/shard_map/pallas_call | solution.py:118
  (27 shorter events, 0.1 us)
Async XLA Ops:
  0.0 10.6 %collective-permute-start.4 = (bf16[4,2,64,512]{3,2,1,0:T(8,128)(2,1)}, bf16[4,2,64,512]{3,2,1,0:T(8,128)(2,1)S(1)}, u32[]{:S(2)}, u32[]{:S(2)}) collective-permute-start(bf16[4,2,64,512]{3,2,1,0:T(8,128)(2,1)} %refs_16_.1), channel_id=1, source_target_pairs={{0,48},{1,17},{2,50},{3,19},{4,52},{5,21},{6,54},{7,23},{16,0},{17... | collective-permute-start | bytes 1572872 | tf_op jit(solution)/shard_map/b_3/ppermute | solution.py:30
  2.1 12.7 %collective-permute-start.6 = (bf16[4,2,64,512]{3,2,1,0:T(8,128)(2,1)}, bf16[4,2,64,512]{3,2,1,0:T(8,128)(2,1)S(1)}, u32[]{:S(2)}, u32[]{:S(2)}) collective-permute-start(bf16[4,2,64,512]{3,2,1,0:T(8,128)(2,1)} %refs_16_.1), channel_id=1, source_target_pairs={{0,64},{1,65},{2,66},{3,67},{4,68},{5,69},{6,70},{7,71},{16,80},{1... | collective-permute-start | bytes 1572872 | tf_op jit(solution)/shard_map/b_x/ppermute | solution.py:30
  4.9 10.8 %collective-permute-start.3 = (bf16[4,2,32,1024]{3,2,1,0:T(8,128)(2,1)}, bf16[4,2,32,1024]{3,2,1,0:T(8,128)(2,1)S(1)}, u32[]{:S(2)}, u32[]{:S(2)}) collective-permute-start(bf16[4,2,32,1024]{3,2,1,0:T(8,128)(2,1)} %refs_0_.1), channel_id=1, source_target_pairs={{0,6},{1,3},{2,0},{3,5},{4,2},{5,7},{6,4},{7,1},{16,22},{17,19},{1... | collective-permute-start | bytes 1572872 | tf_op jit(solution)/shard_map/a_3/ppermute | solution.py:30
  6.5 17.5 %collective-permute-start.1 = (bf16[4,2,64,512]{3,2,1,0:T(8,128)(2,1)}, bf16[4,2,64,512]{3,2,1,0:T(8,128)(2,1)S(1)}, u32[]{:S(2)}, u32[]{:S(2)}) collective-permute-start(bf16[4,2,64,512]{3,2,1,0:T(8,128)(2,1)} %refs_16_.1), channel_id=1, source_target_pairs={{0,16},{1,49},{2,18},{3,51},{4,20},{5,53},{6,22},{7,55},{16,32},{1... | collective-permute-start | bytes 1572872 | tf_op jit(solution)/shard_map/b_1/ppermute | solution.py:30
  8.0 16.1 %collective-permute-start = (bf16[4,2,32,1024]{3,2,1,0:T(8,128)(2,1)}, bf16[4,2,32,1024]{3,2,1,0:T(8,128)(2,1)S(1)}, u32[]{:S(2)}, u32[]{:S(2)}) collective-permute-start(bf16[4,2,32,1024]{3,2,1,0:T(8,128)(2,1)} %refs_0_.1), channel_id=1, source_target_pairs={{0,2},{1,7},{2,4},{3,1},{4,6},{5,3},{6,0},{7,5},{16,18},{17,23},{1... | collective-permute-start | bytes 1572872 | tf_op jit(solution)/shard_map/a_1/ppermute | solution.py:30
  10.6 43.6 %copy-start = (bf16[4,2,64,512]{3,2,1,0:T(8,128)(2,1)}, bf16[4,2,64,512]{3,2,1,0:T(8,128)(2,1)S(1)}, u32[]{:S(2)}) copy-start(bf16[4,2,64,512]{3,2,1,0:T(8,128)(2,1)S(1)} %collective-permute-done.4.refs_19_) | copy-start | bytes 1572868
  10.6 16.8 %collective-permute-start.5 = (bf16[4,2,32,1024]{3,2,1,0:T(8,128)(2,1)}, bf16[4,2,32,1024]{3,2,1,0:T(8,128)(2,1)S(1)}, u32[]{:S(2)}, u32[]{:S(2)}) collective-permute-start(bf16[4,2,32,1024]{3,2,1,0:T(8,128)(2,1)} %refs_0_.1), channel_id=1, source_target_pairs={{0,8},{1,9},{2,10},{3,11},{4,12},{5,13},{6,14},{7,15},{16,24},{17,... | collective-permute-start | bytes 1572872 | tf_op jit(solution)/shard_map/a_x/ppermute | solution.py:30
  14.9 39.4 %copy-start.1 = (bf16[4,2,64,512]{3,2,1,0:T(8,128)(2,1)}, bf16[4,2,64,512]{3,2,1,0:T(8,128)(2,1)S(1)}, u32[]{:S(2)}) copy-start(bf16[4,2,64,512]{3,2,1,0:T(8,128)(2,1)S(1)} %collective-permute-done.6.refs_20_) | copy-start | bytes 1572868
  15.7 38.5 %copy-start.2 = (bf16[4,2,32,1024]{3,2,1,0:T(8,128)(2,1)}, bf16[4,2,32,1024]{3,2,1,0:T(8,128)(2,1)S(1)}, u32[]{:S(2)}) copy-start(bf16[4,2,32,1024]{3,2,1,0:T(8,128)(2,1)S(1)} %collective-permute-done.3.refs_3_) | copy-start | bytes 1572868
  15.7 12.1 %collective-permute-start.14 = (bf16[4,2,32,1024]{3,2,1,0:T(8,128)(2,1)S(1)}, bf16[4,2,32,1024]{3,2,1,0:T(8,128)(2,1)S(1)}, u32[]{:S(2)}, u32[]{:S(2)}) collective-permute-start(bf16[4,2,32,1024]{3,2,1,0:T(8,128)(2,1)S(1)} %collective-permute-done.3.refs_3_), channel_id=1, source_target_pairs={{0,1},{1,0},{2,3},{3,2},{4,5},{5,4},{6,7},{7,6},{16,17},{17,16},{1... | collective-permute-start | bytes 1572872 | tf_op jit(solution)/shard_map/other_3/ppermute | solution.py:30
  22.5 11.5 %collective-permute-start.9 = (bf16[4,2,64,512]{3,2,1,0:T(8,128)(2,1)S(1)}, bf16[4,2,64,512]{3,2,1,0:T(8,128)(2,1)S(1)}, u32[]{:S(2)}, u32[]{:S(2)}) collective-permute-start(bf16[4,2,64,512]{3,2,1,0:T(8,128)(2,1)S(1)} %collective-permute-done.6.refs_20_), channel_id=1, source_target_pairs={{0,16},{1,49},{2,18},{3,51},{4,20},{5,53},{6,22},{7,55},{16,32},{1... | collective-permute-start | bytes 1572872 | tf_op jit(solution)/shard_map/b_x1/ppermute | solution.py:30
  24.0 30.2 %copy-start.3 = (bf16[4,2,64,512]{3,2,1,0:T(8,128)(2,1)}, bf16[4,2,64,512]{3,2,1,0:T(8,128)(2,1)S(1)}, u32[]{:S(2)}) copy-start(bf16[4,2,64,512]{3,2,1,0:T(8,128)(2,1)S(1)} %collective-permute-done.1.refs_17_) | copy-start | bytes 1572868
  24.0 30.2 %copy-start.4 = (bf16[4,2,32,1024]{3,2,1,0:T(8,128)(2,1)}, bf16[4,2,32,1024]{3,2,1,0:T(8,128)(2,1)S(1)}, u32[]{:S(2)}) copy-start(bf16[4,2,32,1024]{3,2,1,0:T(8,128)(2,1)S(1)} %collective-permute-done.refs_1_) | copy-start | bytes 1572868
  24.0 10.0 %collective-permute-start.2 = (bf16[4,2,32,1024]{3,2,1,0:T(8,128)(2,1)S(1)}, bf16[4,2,32,1024]{3,2,1,0:T(8,128)(2,1)S(1)}, u32[]{:S(2)}, u32[]{:S(2)}) collective-permute-start(bf16[4,2,32,1024]{3,2,1,0:T(8,128)(2,1)S(1)} %collective-permute-done.refs_1_), channel_id=1, source_target_pairs={{0,2},{1,7},{2,4},{3,1},{4,6},{5,3},{6,0},{7,5},{16,18},{17,23},{1... | collective-permute-start | bytes 1572872 | tf_op jit(solution)/shard_map/a_2/ppermute | solution.py:30
  27.4 10.9 %collective-permute-start.7 = (bf16[4,2,64,512]{3,2,1,0:T(8,128)(2,1)S(1)}, bf16[4,2,64,512]{3,2,1,0:T(8,128)(2,1)S(1)}, u32[]{:S(2)}, u32[]{:S(2)}) collective-permute-start(bf16[4,2,64,512]{3,2,1,0:T(8,128)(2,1)S(1)} %collective-permute-done.6.refs_20_), channel_id=1, source_target_pairs={{0,48},{1,17},{2,50},{3,19},{4,52},{5,21},{6,54},{7,23},{16,0},{17... | collective-permute-start | bytes 1572872 | tf_op jit(solution)/shard_map/b_x3/ppermute | solution.py:30
  27.4 26.9 %copy-start.5 = (bf16[4,2,32,1024]{3,2,1,0:T(8,128)(2,1)}, bf16[4,2,32,1024]{3,2,1,0:T(8,128)(2,1)S(1)}, u32[]{:S(2)}) copy-start(bf16[4,2,32,1024]{3,2,1,0:T(8,128)(2,1)S(1)} %collective-permute-done.5.refs_4_) | copy-start | bytes 1572868
  27.4 15.4 %collective-permute-start.11 = (bf16[4,2,32,1024]{3,2,1,0:T(8,128)(2,1)S(1)}, bf16[4,2,32,1024]{3,2,1,0:T(8,128)(2,1)}, u32[]{:S(2)}, u32[]{:S(2)}) collective-permute-start(bf16[4,2,32,1024]{3,2,1,0:T(8,128)(2,1)S(1)} %collective-permute-done.5.refs_4_), channel_id=1, source_target_pairs={{0,6},{1,3},{2,0},{3,5},{4,2},{5,7},{6,4},{7,1},{16,22},{17,19},{1... | collective-permute-start | bytes 1572872 | tf_op jit(solution)/shard_map/a_x3/ppermute | solution.py:30
  27.8 22.8 %copy-start.6 = (bf16[4,2,32,1024]{3,2,1,0:T(8,128)(2,1)}, bf16[4,2,32,1024]{3,2,1,0:T(8,128)(2,1)S(1)}, u32[]{:S(2)}) copy-start(bf16[4,2,32,1024]{3,2,1,0:T(8,128)(2,1)S(1)} %collective-permute-done.14.refs_11_) | copy-start | bytes 1572868
  27.8 14.9 %collective-permute-start.15 = (bf16[4,2,64,512]{3,2,1,0:T(8,128)(2,1)S(1)}, bf16[4,2,64,512]{3,2,1,0:T(8,128)(2,1)S(1)}, u32[]{:S(2)}, u32[]{:S(2)}) collective-permute-start(bf16[4,2,64,512]{3,2,1,0:T(8,128)(2,1)S(1)} %collective-permute-done.1.refs_17_), channel_id=1, source_target_pairs={{0,16},{1,49},{2,18},{3,51},{4,20},{5,53},{6,22},{7,55},{16,32},{1... | collective-permute-start | bytes 1572872 | tf_op jit(solution)/shard_map/b_2/ppermute | solution.py:30
  34.0 16.6 %copy-start.7 = (bf16[4,2,64,512]{3,2,1,0:T(8,128)(2,1)}, bf16[4,2,64,512]{3,2,1,0:T(8,128)(2,1)S(1)}, u32[]{:S(2)}) copy-start(bf16[4,2,64,512]{3,2,1,0:T(8,128)(2,1)S(1)} %collective-permute-done.9.refs_21_) | copy-start | bytes 1572868
  34.0 16.7 %copy-start.8 = (bf16[4,2,32,1024]{3,2,1,0:T(8,128)(2,1)}, bf16[4,2,32,1024]{3,2,1,0:T(8,128)(2,1)S(1)}, u32[]{:S(2)}) copy-start(bf16[4,2,32,1024]{3,2,1,0:T(8,128)(2,1)S(1)} %collective-permute-done.2.refs_2_) | copy-start | bytes 1572868
  34.0 12.2 %collective-permute-start.10 = (bf16[4,2,32,1024]{3,2,1,0:T(8,128)(2,1)S(1)}, bf16[4,2,32,1024]{3,2,1,0:T(8,128)(2,1)}, u32[]{:S(2)}, u32[]{:S(2)}) collective-permute-start(bf16[4,2,32,1024]{3,2,1,0:T(8,128)(2,1)S(1)} %collective-permute-done.2.refs_2_), channel_id=1, source_target_pairs={{0,8},{1,9},{2,10},{3,11},{4,12},{5,13},{6,14},{7,15},{16,24},{17,... | collective-permute-start | bytes 1572872 | tf_op jit(solution)/shard_map/a_x2/ppermute | solution.py:30
  34.4 14.1 %collective-permute-start.19 = (bf16[4,2,64,512]{3,2,1,0:T(8,128)(2,1)S(1)}, bf16[4,2,64,512]{3,2,1,0:T(8,128)(2,1)S(1)}, u32[]{:S(2)}, u32[]{:S(2)}) collective-permute-start(bf16[4,2,64,512]{3,2,1,0:T(8,128)(2,1)S(1)} %collective-permute-done.9.refs_21_), channel_id=1, source_target_pairs={{0,16},{1,49},{2,18},{3,51},{4,20},{5,53},{6,22},{7,55},{16,32},{1... | collective-permute-start | bytes 1572872 | tf_op jit(solution)/shard_map/b_x2/ppermute | solution.py:30
  38.3 12.5 %copy-start.9 = (bf16[4,2,64,512]{3,2,1,0:T(8,128)(2,1)}, bf16[4,2,64,512]{3,2,1,0:T(8,128)(2,1)S(1)}, u32[]{:S(2)}) copy-start(bf16[4,2,64,512]{3,2,1,0:T(8,128)(2,1)S(1)} %collective-permute-done.7.refs_23_) | copy-start | bytes 1572868
  38.3 11.5 %collective-permute-start.8 = (bf16[4,2,32,1024]{3,2,1,0:T(8,128)(2,1)S(1)}, bf16[4,2,32,1024]{3,2,1,0:T(8,128)(2,1)}, u32[]{:S(2)}, u32[]{:S(2)}) collective-permute-start(bf16[4,2,32,1024]{3,2,1,0:T(8,128)(2,1)S(1)} %collective-permute-done.5.refs_4_), channel_id=1, source_target_pairs={{0,2},{1,7},{2,4},{3,1},{4,6},{5,3},{6,0},{7,5},{16,18},{17,23},{1... | collective-permute-start | bytes 1572872 | tf_op jit(solution)/shard_map/a_x1/ppermute | solution.py:30
  42.8 7.9 %collective-permute-start.12 = (bf16[4,2,32,1024]{3,2,1,0:T(8,128)(2,1)}, bf16[4,2,32,1024]{3,2,1,0:T(8,128)(2,1)S(1)}, u32[]{:S(2)}, u32[]{:S(2)}) collective-permute-start(bf16[4,2,32,1024]{3,2,1,0:T(8,128)(2,1)} %refs_0_.1), channel_id=1, source_target_pairs={{0,1},{1,0},{2,3},{3,2},{4,5},{5,4},{6,7},{7,6},{16,17},{17,16},{1... | collective-permute-start | bytes 1572872 | tf_op jit(solution)/shard_map/other/ppermute | solution.py:30
  42.8 8.6 %copy-start.10 = (bf16[4,2,64,512]{3,2,1,0:T(8,128)(2,1)}, bf16[4,2,64,512]{3,2,1,0:T(8,128)(2,1)S(1)}, u32[]{:S(2)}) copy-start(bf16[4,2,64,512]{3,2,1,0:T(8,128)(2,1)S(1)} %collective-permute-done.15.refs_18_) | copy-start | bytes 1572868
  42.8 8.0 %collective-permute-start.16 = (bf16[4,2,32,1024]{3,2,1,0:T(8,128)(2,1)S(1)}, bf16[4,2,32,1024]{3,2,1,0:T(8,128)(2,1)S(1)}, u32[]{:S(2)}, u32[]{:S(2)}) collective-permute-start(bf16[4,2,32,1024]{3,2,1,0:T(8,128)(2,1)S(1)} %collective-permute-done.2.refs_2_), channel_id=1, source_target_pairs={{0,1},{1,0},{2,3},{3,2},{4,5},{5,4},{6,7},{7,6},{16,17},{17,16},{1... | collective-permute-start | bytes 1572872 | tf_op jit(solution)/shard_map/other_2/ppermute | solution.py:30
  46.3 7.9 %collective-permute-start.13 = (bf16[4,2,32,1024]{3,2,1,0:T(8,128)(2,1)S(1)}, bf16[4,2,32,1024]{3,2,1,0:T(8,128)(2,1)}, u32[]{:S(2)}, u32[]{:S(2)}) collective-permute-start(bf16[4,2,32,1024]{3,2,1,0:T(8,128)(2,1)S(1)} %collective-permute-done.refs_1_), channel_id=1, source_target_pairs={{0,1},{1,0},{2,3},{3,2},{4,5},{5,4},{6,7},{7,6},{16,17},{17,16},{1... | collective-permute-start | bytes 1572872 | tf_op jit(solution)/shard_map/other_1/ppermute | solution.py:30
  48.6 2.8 %copy-start.11 = (bf16[4,2,64,512]{3,2,1,0:T(8,128)(2,1)}, bf16[4,2,64,512]{3,2,1,0:T(8,128)(2,1)S(1)}, u32[]{:S(2)}) copy-start(bf16[4,2,64,512]{3,2,1,0:T(8,128)(2,1)S(1)} %collective-permute-done.19.refs_22_) | copy-start | bytes 1572868
  48.6 5.6 %collective-permute-start.20 = (bf16[4,2,32,1024]{3,2,1,0:T(8,128)(2,1)}, bf16[4,2,32,1024]{3,2,1,0:T(8,128)(2,1)}, u32[]{:S(2)}, u32[]{:S(2)}) collective-permute-start(bf16[4,2,32,1024]{3,2,1,0:T(8,128)(2,1)} %collective-permute-done.10.refs_6_), channel_id=1, source_target_pairs={{0,1},{1,0},{2,3},{3,2},{4,5},{5,4},{6,7},{7,6},{16,17},{17,16},{1... | collective-permute-start | bytes 1572872 | tf_op jit(solution)/shard_map/other_x2/ppermute | solution.py:30
  49.8 4.4 %collective-permute-start.18 = (bf16[4,2,32,1024]{3,2,1,0:T(8,128)(2,1)}, bf16[4,2,32,1024]{3,2,1,0:T(8,128)(2,1)}, u32[]{:S(2)}, u32[]{:S(2)}) collective-permute-start(bf16[4,2,32,1024]{3,2,1,0:T(8,128)(2,1)} %collective-permute-done.8.refs_5_), channel_id=1, source_target_pairs={{0,1},{1,0},{2,3},{3,2},{4,5},{5,4},{6,7},{7,6},{16,17},{17,16},{1... | collective-permute-start | bytes 1572872 | tf_op jit(solution)/shard_map/other_x1/ppermute | solution.py:30
  50.6 0.8 %copy-start.12 = (bf16[4,2,32,1024]{3,2,1,0:T(8,128)(2,1)}, bf16[4,2,32,1024]{3,2,1,0:T(8,128)(2,1)S(1)}, u32[]{:S(2)}) copy-start(bf16[4,2,32,1024]{3,2,1,0:T(8,128)(2,1)S(1)} %collective-permute-done.12.refs_8_) | copy-start | bytes 1572868
  50.7 3.5 %collective-permute-start.17 = (bf16[4,2,32,1024]{3,2,1,0:T(8,128)(2,1)S(1)}, bf16[4,2,32,1024]{3,2,1,0:T(8,128)(2,1)}, u32[]{:S(2)}, u32[]{:S(2)}) collective-permute-start(bf16[4,2,32,1024]{3,2,1,0:T(8,128)(2,1)S(1)} %collective-permute-done.5.refs_4_), channel_id=1, source_target_pairs={{0,1},{1,0},{2,3},{3,2},{4,5},{5,4},{6,7},{7,6},{16,17},{17,16},{1... | collective-permute-start | bytes 1572872 | tf_op jit(solution)/shard_map/other_x/ppermute | solution.py:30
  50.8 0.9 %copy-start.13 = (bf16[4,2,32,1024]{3,2,1,0:T(8,128)(2,1)}, bf16[4,2,32,1024]{3,2,1,0:T(8,128)(2,1)S(1)}, u32[]{:S(2)}) copy-start(bf16[4,2,32,1024]{3,2,1,0:T(8,128)(2,1)S(1)} %collective-permute-done.16.refs_10_) | copy-start | bytes 1572868
  50.8 3.4 %collective-permute-start.21 = (bf16[4,2,32,1024]{3,2,1,0:T(8,128)(2,1)}, bf16[4,2,32,1024]{3,2,1,0:T(8,128)(2,1)}, u32[]{:S(2)}, u32[]{:S(2)}) collective-permute-start(bf16[4,2,32,1024]{3,2,1,0:T(8,128)(2,1)} %collective-permute-done.11.refs_7_), channel_id=1, source_target_pairs={{0,1},{1,0},{2,3},{3,2},{4,5},{5,4},{6,7},{7,6},{16,17},{17,16},{1... | collective-permute-start | bytes 1572872 | tf_op jit(solution)/shard_map/other_x3/ppermute | solution.py:30

commit v6 on v5

--- a/solution.py
+++ b/solution.py
@@ -88,8 +88,7 @@
     def _():
         arrive(1, freqs - 1, 1)
 
-    @pl.loop(0, STEPS)
-    def _(step):
+    for step in range(STEPS):
         real = b_buf[step, f, 0]
         imag = b_buf[step, f, 1]
         rhs[0, step, 0] = real
@@ -98,14 +97,11 @@
         rhs[1, step, 1] = real
 
     depth = STEPS * 2 * BLK
-
-    @pl.loop(0, lhs.shape[0] // ROWS)
-    def _(tile):
-        rows = pl.ds(pl.multiple_of(tile * ROWS, ROWS), ROWS)
-        lhs[rows, :] = a_buf[:, f, :, :, rows].reshape(depth, ROWS).T
-
-    @pl.loop(0, 2)
-    def _(part):
+    for first in range(0, lhs.shape[0], ROWS):
+        block = a_buf[:, f, :, :, first : first + ROWS].reshape(depth, ROWS)
+        lhs[first : first + ROWS, :] = block.T
+
+    for part in range(2):
         out[0, part] = jnp.dot(
             lhs[...], rhs[part].reshape(depth, rcvs), preferred_element_type=jnp.float32
         ).astype(out.dtype)
@@ -160,6 +156,7 @@
 
 def per_device(surface_data, source_traces, block_ids):
     a, b = surface_data, source_traces
+    a_where, b_where, b_row = places(block_ids)
 
     def send(name, value, **way):
         with jax.named_scope(name):
@@ -173,7 +170,7 @@
     a_3 = send("a_3", a, dz=-1)
     b_1 = send("b_1", b, dy=1)
     a_1 = send("a_1", a, dz=1)
-    a_x = send("a_x", after(a, b_3), flip_x=True)
+    a_x = send("a_x", after(a, b_3, a_where, b_where, b_row), flip_x=True)
     other_3 = swap("other_3", after(a_3, b_x))
     b_x1 = send("b_x1", after(b_x, a_3), dy=1)
     a_2 = send("a_2", after(a_1, b_1), dz=1)
@@ -194,7 +191,7 @@
     a_parts = [a, a_1, a_2, a_3, a_x, a_x1, a_x2, a_x3]
     a_parts += [other, other_1, other_2, other_3, other_x, other_x1, other_x2, other_x3]
     b_parts = [b, b_1, b_2, b_3, b_x, b_x1, b_x2, b_x3]
-    return multiply(a_parts, b_parts, *places(block_ids))
+    return multiply(a_parts, b_parts, a_where, b_where, b_row)
 
 
 def solution(mesh):

time: 69.9 us -> 66.6 us (0.953)
  Pallas kernels: 15.5 us -> 11.9 us
    pallas_call x1, Pallas kernels: 15.5 us -> 11.9 us  [multiply(): pl.pallas_call(multiply_kernel, out_shape=jax.ShapeDtypeStruct((freqs, 2,...]
  transfers between devices with their start and end apart: 22 -> 22, of which waited for: 6 -> 8; matrix products, arithmetic and copies ran while one was open for 4% -> 4% of each run, Pallas kernels for 0% -> 0%
where the time goes in v6:
time: 66.6 us; the launch traced here: 66.4 us
  starting transfers between devices  37.4 us (56%)
  waiting for transfers between devices  13.6 us (20%)
  Pallas kernels  11.9 us (18%)
  other arithmetic  2.46 us (4%)
  local copies, waits for them, and re-layouts  0.87 us (1%)
    ppermute x22, starting transfers between devices, moved(): return lax.ppermute(value, AXES, pairs)  37.4 us
    ppermute x22, waiting for transfers between devices, moved(): return lax.ppermute(value, AXES, pairs)  13.6 us
    pallas_call x1, Pallas kernels, multiply(): pl.pallas_call(multiply_kernel, out_shape=jax.ShapeDtypeStruct((freqs, 2,...  11.9 us
  transfers between devices with their start and end apart: 22, of which 8 were waited for; matrix products, arithmetic and copies ran while one was open for 4% of the time, Pallas kernels for 0%

profile of v6, /device:TPU:1, one launch (start us, length us, event | category | flops | bytes accessed | tf_op | source)
XLA Modules:
  0.0 66.4 jit_solution(13804600185296114927)
XLA Ops:
  0.0 2.1 %collective-permute-start.4 = (bf16[4,2,64,512]{3,2,1,0:T(8,128)(2,1)}, bf16[4,2,64,512]{3,2,1,0:T(8,128)(2,1)S(1)}, u32[]{:S(2)}, u32[]{:S(2)}) collective-permute-start(bf16[4,2,64,512]{3,2,1,0:T(8,128)(2,1)} %refs_16_.1), channel_id=1, source_target_pairs={{0,48},{1,17},{2,50},{3,19},{4,52},{5,21},{6,54},{7,23},{16,0},{17... | collective-permute-start | bytes 1572872 | tf_op jit(solution)/shard_map/b_3/ppermute | solution.py:30
  2.1 2.7 %collective-permute-start.6 = (bf16[4,2,64,512]{3,2,1,0:T(8,128)(2,1)}, bf16[4,2,64,512]{3,2,1,0:T(8,128)(2,1)S(1)}, u32[]{:S(2)}, u32[]{:S(2)}) collective-permute-start(bf16[4,2,64,512]{3,2,1,0:T(8,128)(2,1)} %refs_16_.1), channel_id=1, source_target_pairs={{0,64},{1,65},{2,66},{3,67},{4,68},{5,69},{6,70},{7,71},{16,80},{1... | collective-permute-start | bytes 1572872 | tf_op jit(solution)/shard_map/b_x/ppermute | solution.py:30
  4.9 1.6 %collective-permute-start.3 = (bf16[4,2,32,1024]{3,2,1,0:T(8,128)(2,1)}, bf16[4,2,32,1024]{3,2,1,0:T(8,128)(2,1)S(1)}, u32[]{:S(2)}, u32[]{:S(2)}) collective-permute-start(bf16[4,2,32,1024]{3,2,1,0:T(8,128)(2,1)} %refs_0_.1), channel_id=1, source_target_pairs={{0,6},{1,3},{2,0},{3,5},{4,2},{5,7},{6,4},{7,1},{16,22},{17,19},{1... | collective-permute-start | bytes 1572872 | tf_op jit(solution)/shard_map/a_3/ppermute | solution.py:30
  6.5 1.4 %collective-permute-start.1 = (bf16[4,2,64,512]{3,2,1,0:T(8,128)(2,1)}, bf16[4,2,64,512]{3,2,1,0:T(8,128)(2,1)S(1)}, u32[]{:S(2)}, u32[]{:S(2)}) collective-permute-start(bf16[4,2,64,512]{3,2,1,0:T(8,128)(2,1)} %refs_16_.1), channel_id=1, source_target_pairs={{0,16},{1,49},{2,18},{3,51},{4,20},{5,53},{6,22},{7,55},{16,32},{1... | collective-permute-start | bytes 1572872 | tf_op jit(solution)/shard_map/b_1/ppermute | solution.py:30
  8.0 2.1 %collective-permute-start = (bf16[4,2,32,1024]{3,2,1,0:T(8,128)(2,1)}, bf16[4,2,32,1024]{3,2,1,0:T(8,128)(2,1)S(1)}, u32[]{:S(2)}, u32[]{:S(2)}) collective-permute-start(bf16[4,2,32,1024]{3,2,1,0:T(8,128)(2,1)} %refs_0_.1), channel_id=1, source_target_pairs={{0,2},{1,7},{2,4},{3,1},{4,6},{5,3},{6,0},{7,5},{16,18},{17,23},{1... | collective-permute-start | bytes 1572872 | tf_op jit(solution)/shard_map/a_1/ppermute | solution.py:30
  10.1 1.2 %fusion.1 = (s32[12]{0:T(128)}, s32[12]{0:T(128)S(1)}) fusion(pred[]{:T(512)S(6)} %eq.18, s32[]{:T(128)S(6)} %select_n.83, s32[]{:T(128)S(6)} %select_n.80, s32[12]{0:T(128)} %param.5), kind=kLoop, calls=%fused_computation.25 | loop fusion | flops 612 | bytes 153 | tf_op jit(solution)/shard_map/add | solution.py:149
  11.3 1.2 %broadcast_multiply_fusion = (s32[12]{0:T(128)}, s32[12]{0:T(128)}) fusion(s32[12]{0:T(128)} %param.5, s32[12]{0:T(128)S(1)} %get-tuple-element.36, s32[]{:T(128)S(6)} %select_n.75, s32[]{:T(128)S(6)} %select_n.73, s32[]{:T(128)S(6)} %select_n.71), kind=kLoop, calls=%fused_computation.29 | loop fusion | flops 684 | bytes 204 | tf_op jit(solution)/shard_map/mul | solution.py:150
  12.5 0.0 collective-permute-done.4.refs_19_
  12.5 0.3 collective-permute-start.5
  12.9 2.0 %collective-permute-done.6.refs_20_ = bf16[4,2,64,512]{3,2,1,0:T(8,128)(2,1)S(1)} collective-permute-done((bf16[4,2,64,512]{3,2,1,0:T(8,128)(2,1)}, bf16[4,2,64,512]{3,2,1,0:T(8,128)(2,1)S(1)}, u32[]{:S(2)}, u32[]{:S(2)}) %collective-permute-start.6) | collective-permute-done | bytes 524320 | tf_op jit(solution)/shard_map/b_x/ppermute | solution.py:30
  14.9 0.8 %collective-permute-done.3.refs_3_ = bf16[4,2,32,1024]{3,2,1,0:T(8,128)(2,1)S(1)} collective-permute-done((bf16[4,2,32,1024]{3,2,1,0:T(8,128)(2,1)}, bf16[4,2,32,1024]{3,2,1,0:T(8,128)(2,1)S(1)}, u32[]{:S(2)}, u32[]{:S(2)}) %collective-permute-start.3) | collective-permute-done | bytes 524320 | tf_op jit(solution)/shard_map/a_3/ppermute | solution.py:30
  15.7 6.8 %collective-permute-start.14 = (bf16[4,2,32,1024]{3,2,1,0:T(8,128)(2,1)S(1)}, bf16[4,2,32,1024]{3,2,1,0:T(8,128)(2,1)S(1)}, u32[]{:S(2)}, u32[]{:S(2)}) collective-permute-start(bf16[4,2,32,1024]{3,2,1,0:T(8,128)(2,1)S(1)} %collective-permute-done.3.refs_3_), channel_id=1, source_target_pairs={{0,1},{1,0},{2,3},{3,2},{4,5},{5,4},{6,7},{7,6},{16,17},{17,16},{1... | collective-permute-start | bytes 1572872 | tf_op jit(solution)/shard_map/other_3/ppermute | solution.py:30
  22.5 1.5 %collective-permute-start.9 = (bf16[4,2,64,512]{3,2,1,0:T(8,128)(2,1)S(1)}, bf16[4,2,64,512]{3,2,1,0:T(8,128)(2,1)S(1)}, u32[]{:S(2)}, u32[]{:S(2)}) collective-permute-start(bf16[4,2,64,512]{3,2,1,0:T(8,128)(2,1)S(1)} %collective-permute-done.6.refs_20_), channel_id=1, source_target_pairs={{0,16},{1,49},{2,18},{3,51},{4,20},{5,53},{6,22},{7,55},{16,32},{1... | collective-permute-start | bytes 1572872 | tf_op jit(solution)/shard_map/b_x1/ppermute | solution.py:30
  24.0 0.0 collective-permute-done.1.refs_17_
  24.0 0.0 collective-permute-done.refs_1_
  24.0 3.4 %collective-permute-start.2 = (bf16[4,2,32,1024]{3,2,1,0:T(8,128)(2,1)S(1)}, bf16[4,2,32,1024]{3,2,1,0:T(8,128)(2,1)S(1)}, u32[]{:S(2)}, u32[]{:S(2)}) collective-permute-start(bf16[4,2,32,1024]{3,2,1,0:T(8,128)(2,1)S(1)} %collective-permute-done.refs_1_), channel_id=1, source_target_pairs={{0,2},{1,7},{2,4},{3,1},{4,6},{5,3},{6,0},{7,5},{16,18},{17,23},{1... | collective-permute-start | bytes 1572872 | tf_op jit(solution)/shard_map/a_2/ppermute | solution.py:30
  27.4 0.0 collective-permute-start.7
  27.4 0.0 collective-permute-done.5.refs_4_
  27.4 0.4 collective-permute-start.11
  27.8 0.0 collective-permute-done.14.refs_11_
  27.8 2.4 %collective-permute-start.15 = (bf16[4,2,64,512]{3,2,1,0:T(8,128)(2,1)S(1)}, bf16[4,2,64,512]{3,2,1,0:T(8,128)(2,1)S(1)}, u32[]{:S(2)}, u32[]{:S(2)}) collective-permute-start(bf16[4,2,64,512]{3,2,1,0:T(8,128)(2,1)S(1)} %collective-permute-done.1.refs_17_), channel_id=1, source_target_pairs={{0,16},{1,49},{2,18},{3,51},{4,20},{5,53},{6,22},{7,55},{16,32},{1... | collective-permute-start | bytes 1572872 | tf_op jit(solution)/shard_map/b_2/ppermute | solution.py:30
  30.3 3.7 %collective-permute-done.9.refs_21_ = bf16[4,2,64,512]{3,2,1,0:T(8,128)(2,1)S(1)} collective-permute-done((bf16[4,2,64,512]{3,2,1,0:T(8,128)(2,1)S(1)}, bf16[4,2,64,512]{3,2,1,0:T(8,128)(2,1)S(1)}, u32[]{:S(2)}, u32[]{:S(2)}) %collective-permute-start.9) | collective-permute-done | bytes 524320 | tf_op jit(solution)/shard_map/b_x1/ppermute | solution.py:30
  33.9 0.0 collective-permute-done.2.refs_2_
  33.9 0.4 collective-permute-start.10
  34.3 1.2 %collective-permute-start.19 = (bf16[4,2,64,512]{3,2,1,0:T(8,128)(2,1)S(1)}, bf16[4,2,64,512]{3,2,1,0:T(8,128)(2,1)S(1)}, u32[]{:S(2)}, u32[]{:S(2)}) collective-permute-start(bf16[4,2,64,512]{3,2,1,0:T(8,128)(2,1)S(1)} %collective-permute-done.9.refs_21_), channel_id=1, source_target_pairs={{0,16},{1,49},{2,18},{3,51},{4,20},{5,53},{6,22},{7,55},{16,32},{1... | collective-permute-start | bytes 1572872 | tf_op jit(solution)/shard_map/b_x2/ppermute | solution.py:30
  35.5 2.8 %collective-permute-done.7.refs_23_ = bf16[4,2,64,512]{3,2,1,0:T(8,128)(2,1)S(1)} collective-permute-done((bf16[4,2,64,512]{3,2,1,0:T(8,128)(2,1)S(1)}, bf16[4,2,64,512]{3,2,1,0:T(8,128)(2,1)S(1)}, u32[]{:S(2)}, u32[]{:S(2)}) %collective-permute-start.7) | collective-permute-done | bytes 524320 | tf_op jit(solution)/shard_map/b_x3/ppermute | solution.py:30
  38.3 4.3 %collective-permute-start.8 = (bf16[4,2,32,1024]{3,2,1,0:T(8,128)(2,1)S(1)}, bf16[4,2,32,1024]{3,2,1,0:T(8,128)(2,1)S(1)}, u32[]{:S(2)}, u32[]{:S(2)}) collective-permute-start(bf16[4,2,32,1024]{3,2,1,0:T(8,128)(2,1)S(1)} %collective-permute-done.5.refs_4_), channel_id=1, source_target_pairs={{0,2},{1,7},{2,4},{3,1},{4,6},{5,3},{6,0},{7,5},{16,18},{17,23},{1... | collective-permute-start | bytes 1572872 | tf_op jit(solution)/shard_map/a_x1/ppermute | solution.py:30
  42.6 0.0 collective-permute-done.11.refs_7_
  42.7 0.0 collective-permute-start.12
  42.7 0.0 collective-permute-done.15.refs_18_
  42.7 1.5 %collective-permute-start.16 = (bf16[4,2,32,1024]{3,2,1,0:T(8,128)(2,1)S(1)}, bf16[4,2,32,1024]{3,2,1,0:T(8,128)(2,1)S(1)}, u32[]{:S(2)}, u32[]{:S(2)}) collective-permute-start(bf16[4,2,32,1024]{3,2,1,0:T(8,128)(2,1)S(1)} %collective-permute-done.2.refs_2_), channel_id=1, source_target_pairs={{0,1},{1,0},{2,3},{3,2},{4,5},{5,4},{6,7},{7,6},{16,17},{17,16},{1... | collective-permute-start | bytes 1572872 | tf_op jit(solution)/shard_map/other_2/ppermute | solution.py:30
  44.2 1.8 %collective-permute-done.10.refs_6_ = bf16[4,2,32,1024]{3,2,1,0:T(8,128)(2,1)S(1)} collective-permute-done((bf16[4,2,32,1024]{3,2,1,0:T(8,128)(2,1)S(1)}, bf16[4,2,32,1024]{3,2,1,0:T(8,128)(2,1)S(1)}, u32[]{:S(2)}, u32[]{:S(2)}) %collective-permute-start.10) | collective-permute-done | bytes 524320 | tf_op jit(solution)/shard_map/a_x2/ppermute | solution.py:30
  45.9 2.4 %collective-permute-start.13 = (bf16[4,2,32,1024]{3,2,1,0:T(8,128)(2,1)S(1)}, bf16[4,2,32,1024]{3,2,1,0:T(8,128)(2,1)S(1)}, u32[]{:S(2)}, u32[]{:S(2)}) collective-permute-start(bf16[4,2,32,1024]{3,2,1,0:T(8,128)(2,1)S(1)} %collective-permute-done.refs_1_), channel_id=1, source_target_pairs={{0,1},{1,0},{2,3},{3,2},{4,5},{5,4},{6,7},{7,6},{16,17},{17,16},{1... | collective-permute-start | bytes 1572872 | tf_op jit(solution)/shard_map/other_1/ppermute | solution.py:30
  48.4 0.0 collective-permute-done.19.refs_22_
  48.4 1.4 %collective-permute-start.20 = (bf16[4,2,32,1024]{3,2,1,0:T(8,128)(2,1)S(1)}, bf16[4,2,32,1024]{3,2,1,0:T(8,128)(2,1)S(1)}, u32[]{:S(2)}, u32[]{:S(2)}) collective-permute-start(bf16[4,2,32,1024]{3,2,1,0:T(8,128)(2,1)S(1)} %collective-permute-done.10.refs_6_), channel_id=1, source_target_pairs={{0,1},{1,0},{2,3},{3,2},{4,5},{5,4},{6,7},{7,6},{16,17},{17,16},{1... | collective-permute-start | bytes 1572872 | tf_op jit(solution)/shard_map/other_x2/ppermute | solution.py:30
  49.8 0.0 collective-permute-done.8.refs_5_
  49.8 0.7 %collective-permute-start.18 = (bf16[4,2,32,1024]{3,2,1,0:T(8,128)(2,1)S(1)}, bf16[4,2,32,1024]{3,2,1,0:T(8,128)(2,1)S(1)}, u32[]{:S(2)}, u32[]{:S(2)}) collective-permute-start(bf16[4,2,32,1024]{3,2,1,0:T(8,128)(2,1)S(1)} %collective-permute-done.8.refs_5_), channel_id=1, source_target_pairs={{0,1},{1,0},{2,3},{3,2},{4,5},{5,4},{6,7},{7,6},{16,17},{17,16},{1... | collective-permute-start | bytes 1572872 | tf_op jit(solution)/shard_map/other_x1/ppermute | solution.py:30
  50.5 0.0 collective-permute-done.12.refs_8_
  50.5 0.1 collective-permute-start.17
  50.6 0.0 collective-permute-done.16.refs_10_
  50.6 0.4 collective-permute-start.21
  51.0 0.0 collective-permute-done.13.refs_9_
  51.1 0.3 collective-permute-done.20.refs_14_
  51.3 0.7 %collective-permute-done.18.refs_13_ = bf16[4,2,32,1024]{3,2,1,0:T(8,128)(2,1)S(1)} collective-permute-done((bf16[4,2,32,1024]{3,2,1,0:T(8,128)(2,1)S(1)}, bf16[4,2,32,1024]{3,2,1,0:T(8,128)(2,1)S(1)}, u32[]{:S(2)}, u32[]{:S(2)}) %collective-permute-start.18) | collective-permute-done | bytes 524320 | tf_op jit(solution)/shard_map/other_x1/ppermute | solution.py:30
  52.1 1.5 %collective-permute-done.17.refs_12_ = bf16[4,2,32,1024]{3,2,1,0:T(8,128)(2,1)S(1)} collective-permute-done((bf16[4,2,32,1024]{3,2,1,0:T(8,128)(2,1)S(1)}, bf16[4,2,32,1024]{3,2,1,0:T(8,128)(2,1)S(1)}, u32[]{:S(2)}, u32[]{:S(2)}) %collective-permute-start.17) | collective-permute-done | bytes 524320 | tf_op jit(solution)/shard_map/other_x/ppermute | solution.py:30
  53.6 0.8 %copy-done.20 = bf16[4,2,32,1024]{3,2,1,0:T(8,128)(2,1)} copy-done((bf16[4,2,32,1024]{3,2,1,0:T(8,128)(2,1)}, bf16[4,2,32,1024]{3,2,1,0:T(8,128)(2,1)S(1)}, u32[]{:S(2)}) %copy-start.20) | copy-done | bytes 524312
  54.4 0.0 collective-permute-done.21.refs_15_
  54.5 11.9 %shard_map.37 = bf16[4,2,1024,512]{3,2,1,0:T(8,128)(2,1)} custom-call(s32[12]{0:T(128)} %get-tuple-element.38.a_where, s32[12]{0:T(128)} %get-tuple-element.35.b_where, s32[12]{0:T(128)} %get-tuple-element.37.b_row, bf16[4,2,32,1024]{3,2,1,0:T(8,128)(2,1)} %refs_0_.1, bf16[4,2,32,1024]{3,2,1,0:T(8,128)(2,1)} %copy-done.4, ...), custom_call_target="tpu_custom_call" | custom-call | flops 6442450944 | bytes 20971520 | tf_op jit(solution)/shard_map/pallas_call | solution.py:114
  (41 shorter events, 0.1 us)
Async XLA Ops:
  0.0 12.5 %collective-permute-start.4 = (bf16[4,2,64,512]{3,2,1,0:T(8,128)(2,1)}, bf16[4,2,64,512]{3,2,1,0:T(8,128)(2,1)S(1)}, u32[]{:S(2)}, u32[]{:S(2)}) collective-permute-start(bf16[4,2,64,512]{3,2,1,0:T(8,128)(2,1)} %refs_16_.1), channel_id=1, source_target_pairs={{0,48},{1,17},{2,50},{3,19},{4,52},{5,21},{6,54},{7,23},{16,0},{17... | collective-permute-start | bytes 1572872 | tf_op jit(solution)/shard_map/b_3/ppermute | solution.py:30
  2.1 12.7 %collective-permute-start.6 = (bf16[4,2,64,512]{3,2,1,0:T(8,128)(2,1)}, bf16[4,2,64,512]{3,2,1,0:T(8,128)(2,1)S(1)}, u32[]{:S(2)}, u32[]{:S(2)}) collective-permute-start(bf16[4,2,64,512]{3,2,1,0:T(8,128)(2,1)} %refs_16_.1), channel_id=1, source_target_pairs={{0,64},{1,65},{2,66},{3,67},{4,68},{5,69},{6,70},{7,71},{16,80},{1... | collective-permute-start | bytes 1572872 | tf_op jit(solution)/shard_map/b_x/ppermute | solution.py:30
  4.9 10.8 %collective-permute-start.3 = (bf16[4,2,32,1024]{3,2,1,0:T(8,128)(2,1)}, bf16[4,2,32,1024]{3,2,1,0:T(8,128)(2,1)S(1)}, u32[]{:S(2)}, u32[]{:S(2)}) collective-permute-start(bf16[4,2,32,1024]{3,2,1,0:T(8,128)(2,1)} %refs_0_.1), channel_id=1, source_target_pairs={{0,6},{1,3},{2,0},{3,5},{4,2},{5,7},{6,4},{7,1},{16,22},{17,19},{1... | collective-permute-start | bytes 1572872 | tf_op jit(solution)/shard_map/a_3/ppermute | solution.py:30
  6.5 17.5 %collective-permute-start.1 = (bf16[4,2,64,512]{3,2,1,0:T(8,128)(2,1)}, bf16[4,2,64,512]{3,2,1,0:T(8,128)(2,1)S(1)}, u32[]{:S(2)}, u32[]{:S(2)}) collective-permute-start(bf16[4,2,64,512]{3,2,1,0:T(8,128)(2,1)} %refs_16_.1), channel_id=1, source_target_pairs={{0,16},{1,49},{2,18},{3,51},{4,20},{5,53},{6,22},{7,55},{16,32},{1... | collective-permute-start | bytes 1572872 | tf_op jit(solution)/shard_map/b_1/ppermute | solution.py:30
  8.0 16.1 %collective-permute-start = (bf16[4,2,32,1024]{3,2,1,0:T(8,128)(2,1)}, bf16[4,2,32,1024]{3,2,1,0:T(8,128)(2,1)S(1)}, u32[]{:S(2)}, u32[]{:S(2)}) collective-permute-start(bf16[4,2,32,1024]{3,2,1,0:T(8,128)(2,1)} %refs_0_.1), channel_id=1, source_target_pairs={{0,2},{1,7},{2,4},{3,1},{4,6},{5,3},{6,0},{7,5},{16,18},{17,23},{1... | collective-permute-start | bytes 1572872 | tf_op jit(solution)/shard_map/a_1/ppermute | solution.py:30
  12.5 41.9 %copy-start = (bf16[4,2,64,512]{3,2,1,0:T(8,128)(2,1)}, bf16[4,2,64,512]{3,2,1,0:T(8,128)(2,1)S(1)}, u32[]{:S(2)}) copy-start(bf16[4,2,64,512]{3,2,1,0:T(8,128)(2,1)S(1)} %collective-permute-done.4.refs_19_) | copy-start | bytes 1572868
  12.5 14.9 %collective-permute-start.5 = (bf16[4,2,32,1024]{3,2,1,0:T(8,128)(2,1)}, bf16[4,2,32,1024]{3,2,1,0:T(8,128)(2,1)S(1)}, u32[]{:S(2)}, u32[]{:S(2)}) collective-permute-start(bf16[4,2,32,1024]{3,2,1,0:T(8,128)(2,1)} %refs_0_.1), channel_id=1, source_target_pairs={{0,8},{1,9},{2,10},{3,11},{4,12},{5,13},{6,14},{7,15},{16,24},{17,... | collective-permute-start | bytes 1572872 | tf_op jit(solution)/shard_map/a_x/ppermute | solution.py:30
  14.9 39.5 %copy-start.1 = (bf16[4,2,64,512]{3,2,1,0:T(8,128)(2,1)}, bf16[4,2,64,512]{3,2,1,0:T(8,128)(2,1)S(1)}, u32[]{:S(2)}) copy-start(bf16[4,2,64,512]{3,2,1,0:T(8,128)(2,1)S(1)} %collective-permute-done.6.refs_20_) | copy-start | bytes 1572868
  15.7 38.7 %copy-start.2 = (bf16[4,2,32,1024]{3,2,1,0:T(8,128)(2,1)}, bf16[4,2,32,1024]{3,2,1,0:T(8,128)(2,1)S(1)}, u32[]{:S(2)}) copy-start(bf16[4,2,32,1024]{3,2,1,0:T(8,128)(2,1)S(1)} %collective-permute-done.3.refs_3_) | copy-start | bytes 1572868
  15.7 12.1 %collective-permute-start.14 = (bf16[4,2,32,1024]{3,2,1,0:T(8,128)(2,1)S(1)}, bf16[4,2,32,1024]{3,2,1,0:T(8,128)(2,1)S(1)}, u32[]{:S(2)}, u32[]{:S(2)}) collective-permute-start(bf16[4,2,32,1024]{3,2,1,0:T(8,128)(2,1)S(1)} %collective-permute-done.3.refs_3_), channel_id=1, source_target_pairs={{0,1},{1,0},{2,3},{3,2},{4,5},{5,4},{6,7},{7,6},{16,17},{17,16},{1... | collective-permute-start | bytes 1572872 | tf_op jit(solution)/shard_map/other_3/ppermute | solution.py:30
  22.5 11.4 %collective-permute-start.9 = (bf16[4,2,64,512]{3,2,1,0:T(8,128)(2,1)S(1)}, bf16[4,2,64,512]{3,2,1,0:T(8,128)(2,1)S(1)}, u32[]{:S(2)}, u32[]{:S(2)}) collective-permute-start(bf16[4,2,64,512]{3,2,1,0:T(8,128)(2,1)S(1)} %collective-permute-done.6.refs_20_), channel_id=1, source_target_pairs={{0,16},{1,49},{2,18},{3,51},{4,20},{5,53},{6,22},{7,55},{16,32},{1... | collective-permute-start | bytes 1572872 | tf_op jit(solution)/shard_map/b_x1/ppermute | solution.py:30
  24.0 30.4 %copy-start.3 = (bf16[4,2,64,512]{3,2,1,0:T(8,128)(2,1)}, bf16[4,2,64,512]{3,2,1,0:T(8,128)(2,1)S(1)}, u32[]{:S(2)}) copy-start(bf16[4,2,64,512]{3,2,1,0:T(8,128)(2,1)S(1)} %collective-permute-done.1.refs_17_) | copy-start | bytes 1572868
  24.0 30.4 %copy-start.4 = (bf16[4,2,32,1024]{3,2,1,0:T(8,128)(2,1)}, bf16[4,2,32,1024]{3,2,1,0:T(8,128)(2,1)S(1)}, u32[]{:S(2)}) copy-start(bf16[4,2,32,1024]{3,2,1,0:T(8,128)(2,1)S(1)} %collective-permute-done.refs_1_) | copy-start | bytes 1572868
  24.0 9.9 %collective-permute-start.2 = (bf16[4,2,32,1024]{3,2,1,0:T(8,128)(2,1)S(1)}, bf16[4,2,32,1024]{3,2,1,0:T(8,128)(2,1)S(1)}, u32[]{:S(2)}, u32[]{:S(2)}) collective-permute-start(bf16[4,2,32,1024]{3,2,1,0:T(8,128)(2,1)S(1)} %collective-permute-done.refs_1_), channel_id=1, source_target_pairs={{0,2},{1,7},{2,4},{3,1},{4,6},{5,3},{6,0},{7,5},{16,18},{17,23},{1... | collective-permute-start | bytes 1572872 | tf_op jit(solution)/shard_map/a_2/ppermute | solution.py:30
  27.4 10.9 %collective-permute-start.7 = (bf16[4,2,64,512]{3,2,1,0:T(8,128)(2,1)S(1)}, bf16[4,2,64,512]{3,2,1,0:T(8,128)(2,1)S(1)}, u32[]{:S(2)}, u32[]{:S(2)}) collective-permute-start(bf16[4,2,64,512]{3,2,1,0:T(8,128)(2,1)S(1)} %collective-permute-done.6.refs_20_), channel_id=1, source_target_pairs={{0,48},{1,17},{2,50},{3,19},{4,52},{5,21},{6,54},{7,23},{16,0},{17... | collective-permute-start | bytes 1572872 | tf_op jit(solution)/shard_map/b_x3/ppermute | solution.py:30
  27.4 27.0 %copy-start.5 = (bf16[4,2,32,1024]{3,2,1,0:T(8,128)(2,1)}, bf16[4,2,32,1024]{3,2,1,0:T(8,128)(2,1)S(1)}, u32[]{:S(2)}) copy-start(bf16[4,2,32,1024]{3,2,1,0:T(8,128)(2,1)S(1)} %collective-permute-done.5.refs_4_) | copy-start | bytes 1572868
  27.4 15.2 %collective-permute-start.11 = (bf16[4,2,32,1024]{3,2,1,0:T(8,128)(2,1)S(1)}, bf16[4,2,32,1024]{3,2,1,0:T(8,128)(2,1)S(1)}, u32[]{:S(2)}, u32[]{:S(2)}) collective-permute-start(bf16[4,2,32,1024]{3,2,1,0:T(8,128)(2,1)S(1)} %collective-permute-done.5.refs_4_), channel_id=1, source_target_pairs={{0,6},{1,3},{2,0},{3,5},{4,2},{5,7},{6,4},{7,1},{16,22},{17,19},{1... | collective-permute-start | bytes 1572872 | tf_op jit(solution)/shard_map/a_x3/ppermute | solution.py:30
  27.8 26.6 %copy-start.6 = (bf16[4,2,32,1024]{3,2,1,0:T(8,128)(2,1)}, bf16[4,2,32,1024]{3,2,1,0:T(8,128)(2,1)S(1)}, u32[]{:S(2)}) copy-start(bf16[4,2,32,1024]{3,2,1,0:T(8,128)(2,1)S(1)} %collective-permute-done.14.refs_11_) | copy-start | bytes 1572868
  27.8 14.8 %collective-permute-start.15 = (bf16[4,2,64,512]{3,2,1,0:T(8,128)(2,1)S(1)}, bf16[4,2,64,512]{3,2,1,0:T(8,128)(2,1)S(1)}, u32[]{:S(2)}, u32[]{:S(2)}) collective-permute-start(bf16[4,2,64,512]{3,2,1,0:T(8,128)(2,1)S(1)} %collective-permute-done.1.refs_17_), channel_id=1, source_target_pairs={{0,16},{1,49},{2,18},{3,51},{4,20},{5,53},{6,22},{7,55},{16,32},{1... | collective-permute-start | bytes 1572872 | tf_op jit(solution)/shard_map/b_2/ppermute | solution.py:30
  33.9 20.5 %copy-start.7 = (bf16[4,2,64,512]{3,2,1,0:T(8,128)(2,1)}, bf16[4,2,64,512]{3,2,1,0:T(8,128)(2,1)S(1)}, u32[]{:S(2)}) copy-start(bf16[4,2,64,512]{3,2,1,0:T(8,128)(2,1)S(1)} %collective-permute-done.9.refs_21_) | copy-start | bytes 1572868
  33.9 20.5 %copy-start.8 = (bf16[4,2,32,1024]{3,2,1,0:T(8,128)(2,1)}, bf16[4,2,32,1024]{3,2,1,0:T(8,128)(2,1)S(1)}, u32[]{:S(2)}) copy-start(bf16[4,2,32,1024]{3,2,1,0:T(8,128)(2,1)S(1)} %collective-permute-done.2.refs_2_) | copy-start | bytes 1572868
  33.9 12.0 %collective-permute-start.10 = (bf16[4,2,32,1024]{3,2,1,0:T(8,128)(2,1)S(1)}, bf16[4,2,32,1024]{3,2,1,0:T(8,128)(2,1)S(1)}, u32[]{:S(2)}, u32[]{:S(2)}) collective-permute-start(bf16[4,2,32,1024]{3,2,1,0:T(8,128)(2,1)S(1)} %collective-permute-done.2.refs_2_), channel_id=1, source_target_pairs={{0,8},{1,9},{2,10},{3,11},{4,12},{5,13},{6,14},{7,15},{16,24},{17,... | collective-permute-start | bytes 1572872 | tf_op jit(solution)/shard_map/a_x2/ppermute | solution.py:30
  34.3 14.0 %collective-permute-start.19 = (bf16[4,2,64,512]{3,2,1,0:T(8,128)(2,1)S(1)}, bf16[4,2,64,512]{3,2,1,0:T(8,128)(2,1)S(1)}, u32[]{:S(2)}, u32[]{:S(2)}) collective-permute-start(bf16[4,2,64,512]{3,2,1,0:T(8,128)(2,1)S(1)} %collective-permute-done.9.refs_21_), channel_id=1, source_target_pairs={{0,16},{1,49},{2,18},{3,51},{4,20},{5,53},{6,22},{7,55},{16,32},{1... | collective-permute-start | bytes 1572872 | tf_op jit(solution)/shard_map/b_x2/ppermute | solution.py:30
  38.3 16.2 %copy-start.9 = (bf16[4,2,64,512]{3,2,1,0:T(8,128)(2,1)}, bf16[4,2,64,512]{3,2,1,0:T(8,128)(2,1)S(1)}, u32[]{:S(2)}) copy-start(bf16[4,2,64,512]{3,2,1,0:T(8,128)(2,1)S(1)} %collective-permute-done.7.refs_23_) | copy-start | bytes 1572868
  38.3 11.5 %collective-permute-start.8 = (bf16[4,2,32,1024]{3,2,1,0:T(8,128)(2,1)S(1)}, bf16[4,2,32,1024]{3,2,1,0:T(8,128)(2,1)S(1)}, u32[]{:S(2)}, u32[]{:S(2)}) collective-permute-start(bf16[4,2,32,1024]{3,2,1,0:T(8,128)(2,1)S(1)} %collective-permute-done.5.refs_4_), channel_id=1, source_target_pairs={{0,2},{1,7},{2,4},{3,1},{4,6},{5,3},{6,0},{7,5},{16,18},{17,23},{1... | collective-permute-start | bytes 1572872 | tf_op jit(solution)/shard_map/a_x1/ppermute | solution.py:30
  42.7 11.8 %copy-start.10 = (bf16[4,2,32,1024]{3,2,1,0:T(8,128)(2,1)}, bf16[4,2,32,1024]{3,2,1,0:T(8,128)(2,1)S(1)}, u32[]{:S(2)}) copy-start(bf16[4,2,32,1024]{3,2,1,0:T(8,128)(2,1)S(1)} %collective-permute-done.11.refs_7_) | copy-start | bytes 1572868
  42.7 7.9 %collective-permute-start.12 = (bf16[4,2,32,1024]{3,2,1,0:T(8,128)(2,1)}, bf16[4,2,32,1024]{3,2,1,0:T(8,128)(2,1)S(1)}, u32[]{:S(2)}, u32[]{:S(2)}) collective-permute-start(bf16[4,2,32,1024]{3,2,1,0:T(8,128)(2,1)} %refs_0_.1), channel_id=1, source_target_pairs={{0,1},{1,0},{2,3},{3,2},{4,5},{5,4},{6,7},{7,6},{16,17},{17,16},{1... | collective-permute-start | bytes 1572872 | tf_op jit(solution)/shard_map/other/ppermute | solution.py:30
  42.7 11.8 %copy-start.11 = (bf16[4,2,64,512]{3,2,1,0:T(8,128)(2,1)}, bf16[4,2,64,512]{3,2,1,0:T(8,128)(2,1)S(1)}, u32[]{:S(2)}) copy-start(bf16[4,2,64,512]{3,2,1,0:T(8,128)(2,1)S(1)} %collective-permute-done.15.refs_18_) | copy-start | bytes 1572868
  42.7 7.9 %collective-permute-start.16 = (bf16[4,2,32,1024]{3,2,1,0:T(8,128)(2,1)S(1)}, bf16[4,2,32,1024]{3,2,1,0:T(8,128)(2,1)S(1)}, u32[]{:S(2)}, u32[]{:S(2)}) collective-permute-start(bf16[4,2,32,1024]{3,2,1,0:T(8,128)(2,1)S(1)} %collective-permute-done.2.refs_2_), channel_id=1, source_target_pairs={{0,1},{1,0},{2,3},{3,2},{4,5},{5,4},{6,7},{7,6},{16,17},{17,16},{1... | collective-permute-start | bytes 1572872 | tf_op jit(solution)/shard_map/other_2/ppermute | solution.py:30
  45.9 8.6 %copy-start.12 = (bf16[4,2,32,1024]{3,2,1,0:T(8,128)(2,1)}, bf16[4,2,32,1024]{3,2,1,0:T(8,128)(2,1)S(1)}, u32[]{:S(2)}) copy-start(bf16[4,2,32,1024]{3,2,1,0:T(8,128)(2,1)S(1)} %collective-permute-done.10.refs_6_) | copy-start | bytes 1572868
  45.9 5.1 %collective-permute-start.13 = (bf16[4,2,32,1024]{3,2,1,0:T(8,128)(2,1)S(1)}, bf16[4,2,32,1024]{3,2,1,0:T(8,128)(2,1)S(1)}, u32[]{:S(2)}, u32[]{:S(2)}) collective-permute-start(bf16[4,2,32,1024]{3,2,1,0:T(8,128)(2,1)S(1)} %collective-permute-done.refs_1_), channel_id=1, source_target_pairs={{0,1},{1,0},{2,3},{3,2},{4,5},{5,4},{6,7},{7,6},{16,17},{17,16},{1... | collective-permute-start | bytes 1572872 | tf_op jit(solution)/shard_map/other_1/ppermute | solution.py:30
  48.4 6.2 %copy-start.13 = (bf16[4,2,64,512]{3,2,1,0:T(8,128)(2,1)}, bf16[4,2,64,512]{3,2,1,0:T(8,128)(2,1)S(1)}, u32[]{:S(2)}) copy-start(bf16[4,2,64,512]{3,2,1,0:T(8,128)(2,1)S(1)} %collective-permute-done.19.refs_22_) | copy-start | bytes 1572868
  48.4 3.0 %collective-permute-start.20 = (bf16[4,2,32,1024]{3,2,1,0:T(8,128)(2,1)S(1)}, bf16[4,2,32,1024]{3,2,1,0:T(8,128)(2,1)S(1)}, u32[]{:S(2)}, u32[]{:S(2)}) collective-permute-start(bf16[4,2,32,1024]{3,2,1,0:T(8,128)(2,1)S(1)} %collective-permute-done.10.refs_6_), channel_id=1, source_target_pairs={{0,1},{1,0},{2,3},{3,2},{4,5},{5,4},{6,7},{7,6},{16,17},{17,16},{1... | collective-permute-start | bytes 1572872 | tf_op jit(solution)/shard_map/other_x2/ppermute | solution.py:30
  49.8 4.7 %copy-start.14 = (bf16[4,2,32,1024]{3,2,1,0:T(8,128)(2,1)}, bf16[4,2,32,1024]{3,2,1,0:T(8,128)(2,1)S(1)}, u32[]{:S(2)}) copy-start(bf16[4,2,32,1024]{3,2,1,0:T(8,128)(2,1)S(1)} %collective-permute-done.8.refs_5_) | copy-start | bytes 1572868
  49.8 2.3 %collective-permute-start.18 = (bf16[4,2,32,1024]{3,2,1,0:T(8,128)(2,1)S(1)}, bf16[4,2,32,1024]{3,2,1,0:T(8,128)(2,1)S(1)}, u32[]{:S(2)}, u32[]{:S(2)}) collective-permute-start(bf16[4,2,32,1024]{3,2,1,0:T(8,128)(2,1)S(1)} %collective-permute-done.8.refs_5_), channel_id=1, source_target_pairs={{0,1},{1,0},{2,3},{3,2},{4,5},{5,4},{6,7},{7,6},{16,17},{17,16},{1... | collective-permute-start | bytes 1572872 | tf_op jit(solution)/shard_map/other_x1/ppermute | solution.py:30
  50.5 3.0 %copy-start.15 = (bf16[4,2,32,1024]{3,2,1,0:T(8,128)(2,1)}, bf16[4,2,32,1024]{3,2,1,0:T(8,128)(2,1)S(1)}, u32[]{:S(2)}) copy-start(bf16[4,2,32,1024]{3,2,1,0:T(8,128)(2,1)S(1)} %collective-permute-done.12.refs_8_) | copy-start | bytes 1572868
  50.5 3.0 %collective-permute-start.17 = (bf16[4,2,32,1024]{3,2,1,0:T(8,128)(2,1)S(1)}, bf16[4,2,32,1024]{3,2,1,0:T(8,128)(2,1)S(1)}, u32[]{:S(2)}, u32[]{:S(2)}) collective-permute-start(bf16[4,2,32,1024]{3,2,1,0:T(8,128)(2,1)S(1)} %collective-permute-done.5.refs_4_), channel_id=1, source_target_pairs={{0,1},{1,0},{2,3},{3,2},{4,5},{5,4},{6,7},{7,6},{16,17},{17,16},{1... | collective-permute-start | bytes 1572872 | tf_op jit(solution)/shard_map/other_x/ppermute | solution.py:30
  50.6 2.9 %copy-start.16 = (bf16[4,2,32,1024]{3,2,1,0:T(8,128)(2,1)}, bf16[4,2,32,1024]{3,2,1,0:T(8,128)(2,1)S(1)}, u32[]{:S(2)}) copy-start(bf16[4,2,32,1024]{3,2,1,0:T(8,128)(2,1)S(1)} %collective-permute-done.16.refs_10_) | copy-start | bytes 1572868
  50.6 3.8 %collective-permute-start.21 = (bf16[4,2,32,1024]{3,2,1,0:T(8,128)(2,1)S(1)}, bf16[4,2,32,1024]{3,2,1,0:T(8,128)(2,1)}, u32[]{:S(2)}, u32[]{:S(2)}) collective-permute-start(bf16[4,2,32,1024]{3,2,1,0:T(8,128)(2,1)S(1)} %collective-permute-done.11.refs_7_), channel_id=1, source_target_pairs={{0,1},{1,0},{2,3},{3,2},{4,5},{5,4},{6,7},{7,6},{16,17},{17,16},{1... | collective-permute-start | bytes 1572872 | tf_op jit(solution)/shard_map/other_x3/ppermute | solution.py:30
  51.1 2.5 %copy-start.17 = (bf16[4,2,32,1024]{3,2,1,0:T(8,128)(2,1)}, bf16[4,2,32,1024]{3,2,1,0:T(8,128)(2,1)S(1)}, u32[]{:S(2)}) copy-start(bf16[4,2,32,1024]{3,2,1,0:T(8,128)(2,1)S(1)} %collective-permute-done.13.refs_9_) | copy-start | bytes 1572868
  51.3 2.3 %copy-start.18 = (bf16[4,2,32,1024]{3,2,1,0:T(8,128)(2,1)}, bf16[4,2,32,1024]{3,2,1,0:T(8,128)(2,1)S(1)}, u32[]{:S(2)}) copy-start(bf16[4,2,32,1024]{3,2,1,0:T(8,128)(2,1)S(1)} %collective-permute-done.20.refs_14_) | copy-start | bytes 1572868
  52.1 1.5 %copy-start.19 = (bf16[4,2,32,1024]{3,2,1,0:T(8,128)(2,1)}, bf16[4,2,32,1024]{3,2,1,0:T(8,128)(2,1)S(1)}, u32[]{:S(2)}) copy-start(bf16[4,2,32,1024]{3,2,1,0:T(8,128)(2,1)S(1)} %collective-permute-done.18.refs_13_) | copy-start | bytes 1572868
  53.6 0.8 %copy-start.20 = (bf16[4,2,32,1024]{3,2,1,0:T(8,128)(2,1)}, bf16[4,2,32,1024]{3,2,1,0:T(8,128)(2,1)S(1)}, u32[]{:S(2)}) copy-start(bf16[4,2,32,1024]{3,2,1,0:T(8,128)(2,1)S(1)} %collective-permute-done.17.refs_12_) | copy-start | bytes 1572868

commit v7 on v6

--- a/solution.py
+++ b/solution.py
@@ -45,21 +45,39 @@
         choose(refs[half:], which - half, act)
 
 
+def transpose_kernel(block, out):
+    for pair in range(out.shape[0]):
+        rows = block[2 * pair : 2 * pair + 2].reshape(4 * BLK, block.shape[3])
+        out[pair] = rows.T
+
+
+def transposed(block):
+    freqs, _, _, shots = block.shape
+    return pl.pallas_call(
+        transpose_kernel,
+        out_shape=jax.ShapeDtypeStruct((freqs // 2, shots, 4 * BLK), block.dtype),
+        in_specs=[pl.BlockSpec(memory_space=pltpu.VMEM)],
+        out_specs=pl.BlockSpec(memory_space=pltpu.VMEM),
+        cost_estimate=pl.CostEstimate(
+            flops=0, bytes_accessed=2 * block.size * 2, transcendentals=0
+        ),
+    )(block)
+
+
 def multiply_kernel(a_where, b_where, b_row, *refs):
     a_refs, b_refs = refs[:16], refs[16:24]
     out, a_buf, b_buf, lhs, rhs, a_sem, b_sem = refs[24:]
-    freqs = a_buf.shape[1]
     f = pl.program_id(0)
+    pair, second = f // 2, f % 2
     rcvs = b_buf.shape[4]
 
-    def fetch(first_freq, count, slot):
-        these = pl.ds(first_freq, count)
-
-        @pl.loop(0, STEPS)
-        def _(step):
+    def fetch(slot):
+        these = pl.ds(2 * slot, 2)
+        for step in range(STEPS):
+
             def from_surface(ref):
                 pltpu.make_async_copy(
-                    ref.at[these], a_buf.at[step, these], a_sem.at[slot]
+                    ref.at[slot], a_buf.at[slot, step], a_sem.at[slot]
                 ).start()
 
             choose(a_refs, a_where[step], from_surface)
@@ -72,21 +90,19 @@
 
             choose(b_refs, b_where[step], from_traces)
 
-    def arrive(first_freq, count, slot):
-        these = pl.ds(first_freq, count)
-        for buf, sem in ((a_buf, a_sem), (b_buf, b_sem)):
-            part = buf.at[:, these]
+    def arrive(slot):
+        for part, sem in ((a_buf.at[slot], a_sem), (b_buf.at[:, pl.ds(2 * slot, 2)], b_sem)):
             pltpu.make_async_copy(part, part, sem.at[slot]).wait()
 
     @pl.when(f == 0)
     def _():
-        fetch(0, 1, 0)
-        fetch(1, freqs - 1, 1)
-        arrive(0, 1, 0)
-
-    @pl.when(f == 1)
-    def _():
-        arrive(1, freqs - 1, 1)
+        fetch(0)
+        fetch(1)
+        arrive(0)
+
+    @pl.when(f == 2)
+    def _():
+        arrive(1)
 
     for step in range(STEPS):
         real = b_buf[step, f, 0]
@@ -97,9 +113,13 @@
         rhs[1, step, 1] = real
 
     depth = STEPS * 2 * BLK
-    for first in range(0, lhs.shape[0], ROWS):
-        block = a_buf[:, f, :, :, first : first + ROWS].reshape(depth, ROWS)
-        lhs[first : first + ROWS, :] = block.T
+    columns = 4 * BLK
+    lane = lax.broadcasted_iota(jnp.int32, (lhs.shape[0], columns), 1)
+    for chunk in range(STEPS // 2):
+        left = pltpu.roll(a_buf[pair, 2 * chunk], second * (columns // 2), 1)
+        right = pltpu.roll(a_buf[pair, 2 * chunk + 1], (1 - second) * (columns // 2), 1)
+        joined = jnp.where(lane < columns // 2, left, right)
+        lhs[:, chunk * columns : (chunk + 1) * columns] = joined
 
     for part in range(2):
         out[0, part] = jnp.dot(
@@ -108,8 +128,8 @@
 
 
 def multiply(a_parts, b_parts, a_where, b_where, b_row):
-    freqs, _, _, shots = a_parts[0].shape
-    rcvs = b_parts[0].shape[3]
+    pairs, shots, columns = a_parts[0].shape
+    freqs, _, _, rcvs = b_parts[0].shape
     depth = STEPS * 2 * BLK
     return pl.pallas_call(
         multiply_kernel,
@@ -120,7 +140,7 @@
             in_specs=[pl.BlockSpec(memory_space=pl.ANY)] * (len(a_parts) + len(b_parts)),
             out_specs=pl.BlockSpec((1, 2, shots, rcvs), lambda f, *_: (f, 0, 0, 0)),
             scratch_shapes=[
-                pltpu.VMEM((STEPS, freqs, 2, BLK, shots), jnp.bfloat16),
+                pltpu.VMEM((pairs, STEPS, shots, columns), jnp.bfloat16),
                 pltpu.VMEM((STEPS, freqs, 2, BLK, rcvs), jnp.bfloat16),
                 pltpu.VMEM((shots, depth), jnp.bfloat16),
                 pltpu.VMEM((2, STEPS, 2, BLK, rcvs), jnp.bfloat16),
@@ -155,7 +175,7 @@
 
 
 def per_device(surface_data, source_traces, block_ids):
-    a, b = surface_data, source_traces
+    a, b = transposed(surface_data), source_traces
     a_where, b_where, b_row = places(block_ids)
 
     def send(name, value, **way):
@@ -175,18 +195,18 @@
     b_x1 = send("b_x1", after(b_x, a_3), dy=1)
     a_2 = send("a_2", after(a_1, b_1), dz=1)
     b_x3 = send("b_x3", after(b_x, a_1), dy=-1)
-    a_x3 = send("a_x3", a_x, dz=-1)
-    b_2 = send("b_2", after(b_1, other_3), dy=1)
+    b_2 = send("b_2", after(b_1, a_x), dy=1)
+    a_x3 = send("a_x3", after(a_x, other_3, b_x1), dz=-1)
     a_x2 = send("a_x2", after(a_2, b_x1), flip_x=True)
     b_x2 = send("b_x2", after(b_x1, a_2), dy=1)
     a_x1 = send("a_x1", after(a_x, b_x3), dz=1)
-    other = swap("other", after(a, a_x3))
     other_2 = swap("other_2", after(a_2, b_2))
-    other_1 = swap("other_1", after(a_1, a_x2))
-    other_x2 = swap("other_x2", after(a_x2, b_x2))
+    other_1 = swap("other_1", after(a_1, a_x3))
+    other_x2 = swap("other_x2", a_x2)
+    other = swap("other", after(a, b_x2))
     other_x1 = swap("other_x1", a_x1)
-    other_x = swap("other_x", after(a_x, other))
     other_x3 = swap("other_x3", after(a_x3, other_2))
+    other_x = swap("other_x", after(a_x, other_1))
 
     a_parts = [a, a_1, a_2, a_3, a_x, a_x1, a_x2, a_x3]
     a_parts += [other, other_1, other_2, other_3, other_x, other_x1, other_x2, other_x3]

time: 66.6 us -> 76.5 us (1.15)
  starting transfers between devices: 37.4 us -> 46.3 us
  Pallas kernels: 11.9 us -> 15.7 us
  waiting for transfers between devices: 13.6 us -> 10.8 us
    ppermute x22, starting transfers between devices: 37.4 us -> 46.3 us  [moved(): return lax.ppermute(value, AXES, pairs)]
    ppermute x22, waiting for transfers between devices: 13.6 us -> 10.8 us  [moved(): return lax.ppermute(value, AXES, pairs)]
    pallas_call x0 -> x1, Pallas kernels: none -> 2.03 us  [transposed(): pl.pallas_call(transpose_kernel, out_shape=jax.ShapeDtypeStruct((freqs //...]
    pallas_call x1, Pallas kernels: 11.9 us -> 13.7 us  [multiply(): pl.pallas_call(multiply_kernel, out_shape=jax.ShapeDtypeStruct((freqs, 2,...]
  transfers between devices with their start and end apart: 22 -> 22, of which waited for: 8 -> 6; matrix products, arithmetic and copies ran while one was open for 4% -> 3% of each run, Pallas kernels for 0% -> 3%
where the time goes in v7:
time: 76.5 us; the launch traced here: 76.3 us
  starting transfers between devices  46.3 us (61%)
  Pallas kernels  15.7 us (21%)
  waiting for transfers between devices  10.8 us (14%)
  other arithmetic  2.43 us (3%)
  local copies, waits for them, and re-layouts  0.85 us (1%)
    ppermute x22, starting transfers between devices, moved(): return lax.ppermute(value, AXES, pairs)  46.3 us
    pallas_call x1, Pallas kernels, multiply(): pl.pallas_call(multiply_kernel, out_shape=jax.ShapeDtypeStruct((freqs, 2,...  13.7 us
    ppermute x22, waiting for transfers between devices, moved(): return lax.ppermute(value, AXES, pairs)  10.8 us
    pallas_call x1, Pallas kernels, transposed(): pl.pallas_call(transpose_kernel, out_shape=jax.ShapeDtypeStruct((freqs //...  2.03 us
  transfers between devices with their start and end apart: 22, of which 6 were waited for; matrix products, arithmetic and copies ran while one was open for 3% of the time, Pallas kernels for 3%

profile of v7, /device:TPU:1, one launch (start us, length us, event | category | flops | bytes accessed | tf_op | source)
XLA Modules:
  0.0 76.3 jit_solution(6413798801193023992)
XLA Ops:
  0.0 2.1 %collective-permute-start.4 = (bf16[4,2,64,512]{3,2,1,0:T(8,128)(2,1)}, bf16[4,2,64,512]{3,2,1,0:T(8,128)(2,1)S(1)}, u32[]{:S(2)}, u32[]{:S(2)}) collective-permute-start(bf16[4,2,64,512]{3,2,1,0:T(8,128)(2,1)} %refs_16_.1), channel_id=1, source_target_pairs={{0,48},{1,17},{2,50},{3,19},{4,52},{5,21},{6,54},{7,23},{16,0},{17... | collective-permute-start | bytes 1572872 | tf_op jit(solution)/shard_map/b_3/ppermute | solution.py:30
  2.1 2.0 %shard_map.37.refs_0_ = bf16[2,1024,128]{2,1,0:T(8,128)(2,1)} custom-call(bf16[4,2,32,1024]{3,2,1,0:T(8,128)(2,1)} %block.1), custom_call_target="tpu_custom_call" | custom-call | bytes 1048576 | tf_op jit(solution)/shard_map/pallas_call | solution.py:56
  4.2 1.6 %collective-permute-start.3 = (bf16[2,1024,128]{2,1,0:T(8,128)(2,1)}, bf16[2,1024,128]{2,1,0:T(8,128)(2,1)S(1)}, u32[]{:S(2)}, u32[]{:S(2)}) collective-permute-start(bf16[2,1024,128]{2,1,0:T(8,128)(2,1)} %shard_map.37.refs_0_), channel_id=1, source_target_pairs={{0,6},{1,3},{2,0},{3,5},{4,2},{5,7},{6,4},{7,1},{16,22},{17,19},{1... | collective-permute-start | bytes 1572872 | tf_op jit(solution)/shard_map/a_3/ppermute | solution.py:30
  5.8 2.7 %collective-permute-start.6 = (bf16[4,2,64,512]{3,2,1,0:T(8,128)(2,1)}, bf16[4,2,64,512]{3,2,1,0:T(8,128)(2,1)S(1)}, u32[]{:S(2)}, u32[]{:S(2)}) collective-permute-start(bf16[4,2,64,512]{3,2,1,0:T(8,128)(2,1)} %refs_16_.1), channel_id=1, source_target_pairs={{0,64},{1,65},{2,66},{3,67},{4,68},{5,69},{6,70},{7,71},{16,80},{1... | collective-permute-start | bytes 1572872 | tf_op jit(solution)/shard_map/b_x/ppermute | solution.py:30
  8.5 2.1 %collective-permute-start = (bf16[2,1024,128]{2,1,0:T(8,128)(2,1)}, bf16[2,1024,128]{2,1,0:T(8,128)(2,1)S(1)}, u32[]{:S(2)}, u32[]{:S(2)}) collective-permute-start(bf16[2,1024,128]{2,1,0:T(8,128)(2,1)} %shard_map.37.refs_0_), channel_id=1, source_target_pairs={{0,2},{1,7},{2,4},{3,1},{4,6},{5,3},{6,0},{7,5},{16,18},{17,23},{1... | collective-permute-start | bytes 1572872 | tf_op jit(solution)/shard_map/a_1/ppermute | solution.py:30
  10.7 1.4 %collective-permute-start.1 = (bf16[4,2,64,512]{3,2,1,0:T(8,128)(2,1)}, bf16[4,2,64,512]{3,2,1,0:T(8,128)(2,1)S(1)}, u32[]{:S(2)}, u32[]{:S(2)}) collective-permute-start(bf16[4,2,64,512]{3,2,1,0:T(8,128)(2,1)} %refs_16_.1), channel_id=1, source_target_pairs={{0,16},{1,49},{2,18},{3,51},{4,20},{5,53},{6,22},{7,55},{16,32},{1... | collective-permute-start | bytes 1572872 | tf_op jit(solution)/shard_map/b_1/ppermute | solution.py:30
  12.1 1.2 %fusion.1 = (s32[12]{0:T(128)}, s32[12]{0:T(128)S(1)}) fusion(pred[]{:T(512)S(6)} %eq.18, s32[]{:T(128)S(6)} %select_n.83, s32[]{:T(128)S(6)} %select_n.80, s32[12]{0:T(128)} %param.5), kind=kLoop, calls=%fused_computation.25 | loop fusion | flops 612 | bytes 153 | tf_op jit(solution)/shard_map/add | solution.py:169
  13.3 1.2 %broadcast_multiply_fusion = (s32[12]{0:T(128)}, s32[12]{0:T(128)}) fusion(s32[12]{0:T(128)} %param.5, s32[12]{0:T(128)S(1)} %get-tuple-element.36, s32[]{:T(128)S(6)} %select_n.75, s32[]{:T(128)S(6)} %select_n.73, s32[]{:T(128)S(6)} %select_n.71), kind=kLoop, calls=%fused_computation.29 | loop fusion | flops 684 | bytes 204 | tf_op jit(solution)/shard_map/mul | solution.py:170
  14.5 0.0 collective-permute-done.4.refs_19_
  14.5 0.3 collective-permute-start.5
  14.9 0.0 collective-permute-done.3.refs_3_
  14.9 1.3 %collective-permute-done.6.refs_20_ = bf16[4,2,64,512]{3,2,1,0:T(8,128)(2,1)S(1)} collective-permute-done((bf16[4,2,64,512]{3,2,1,0:T(8,128)(2,1)}, bf16[4,2,64,512]{3,2,1,0:T(8,128)(2,1)S(1)}, u32[]{:S(2)}, u32[]{:S(2)}) %collective-permute-start.6) | collective-permute-done | bytes 524320 | tf_op jit(solution)/shard_map/b_x/ppermute | solution.py:30
  16.1 2.4 %collective-permute-start.9 = (bf16[4,2,64,512]{3,2,1,0:T(8,128)(2,1)S(1)}, bf16[4,2,64,512]{3,2,1,0:T(8,128)(2,1)S(1)}, u32[]{:S(2)}, u32[]{:S(2)}) collective-permute-start(bf16[4,2,64,512]{3,2,1,0:T(8,128)(2,1)S(1)} %collective-permute-done.6.refs_20_), channel_id=1, source_target_pairs={{0,16},{1,49},{2,18},{3,51},{4,20},{5,53},{6,22},{7,55},{16,32},{1... | collective-permute-start | bytes 1572872 | tf_op jit(solution)/shard_map/b_x1/ppermute | solution.py:30
  18.6 7.6 %collective-permute-start.11 = (bf16[2,1024,128]{2,1,0:T(8,128)(2,1)S(1)}, bf16[2,1024,128]{2,1,0:T(8,128)(2,1)S(1)}, u32[]{:S(2)}, u32[]{:S(2)}) collective-permute-start(bf16[2,1024,128]{2,1,0:T(8,128)(2,1)S(1)} %collective-permute-done.3.refs_3_), channel_id=1, source_target_pairs={{0,1},{1,0},{2,3},{3,2},{4,5},{5,4},{6,7},{7,6},{16,17},{17,16},{1... | collective-permute-start | bytes 1572872 | tf_op jit(solution)/shard_map/other_3/ppermute | solution.py:30
  26.2 0.0 collective-permute-done.refs_1_
  26.2 1.3 %collective-permute-start.7 = (bf16[4,2,64,512]{3,2,1,0:T(8,128)(2,1)S(1)}, bf16[4,2,64,512]{3,2,1,0:T(8,128)(2,1)S(1)}, u32[]{:S(2)}, u32[]{:S(2)}) collective-permute-start(bf16[4,2,64,512]{3,2,1,0:T(8,128)(2,1)S(1)} %collective-permute-done.6.refs_20_), channel_id=1, source_target_pairs={{0,48},{1,17},{2,50},{3,19},{4,52},{5,21},{6,54},{7,23},{16,0},{17... | collective-permute-start | bytes 1572872 | tf_op jit(solution)/shard_map/b_x3/ppermute | solution.py:30
  27.5 0.0 collective-permute-done.1.refs_17_
  27.5 0.0 collective-permute-start.2
  27.5 1.2 %collective-permute-done.5.refs_4_ = bf16[2,1024,128]{2,1,0:T(8,128)(2,1)S(1)} collective-permute-done((bf16[2,1024,128]{2,1,0:T(8,128)(2,1)}, bf16[2,1024,128]{2,1,0:T(8,128)(2,1)S(1)}, u32[]{:S(2)}, u32[]{:S(2)}) %collective-permute-start.5) | collective-permute-done | bytes 524320 | tf_op jit(solution)/shard_map/a_x/ppermute | solution.py:30
  28.8 1.6 %collective-permute-start.16 = (bf16[4,2,64,512]{3,2,1,0:T(8,128)(2,1)S(1)}, bf16[4,2,64,512]{3,2,1,0:T(8,128)(2,1)S(1)}, u32[]{:S(2)}, u32[]{:S(2)}) collective-permute-start(bf16[4,2,64,512]{3,2,1,0:T(8,128)(2,1)S(1)} %collective-permute-done.1.refs_17_), channel_id=1, source_target_pairs={{0,16},{1,49},{2,18},{3,51},{4,20},{5,53},{6,22},{7,55},{16,32},{1... | collective-permute-start | bytes 1572872 | tf_op jit(solution)/shard_map/b_2/ppermute | solution.py:30
  30.4 0.0 collective-permute-done.9.refs_21_
  30.4 0.0 collective-permute-done.11.refs_11_
  30.4 5.3 %collective-permute-start.12 = (bf16[2,1024,128]{2,1,0:T(8,128)(2,1)S(1)}, bf16[2,1024,128]{2,1,0:T(8,128)(2,1)S(1)}, u32[]{:S(2)}, u32[]{:S(2)}) collective-permute-start(bf16[2,1024,128]{2,1,0:T(8,128)(2,1)S(1)} %collective-permute-done.5.refs_4_), channel_id=1, source_target_pairs={{0,6},{1,3},{2,0},{3,5},{4,2},{5,7},{6,4},{7,1},{16,22},{17,19},{1... | collective-permute-start | bytes 1572872 | tf_op jit(solution)/shard_map/a_x3/ppermute | solution.py:30
  35.7 5.5 %collective-permute-done.7.refs_23_ = bf16[4,2,64,512]{3,2,1,0:T(8,128)(2,1)S(1)} collective-permute-done((bf16[4,2,64,512]{3,2,1,0:T(8,128)(2,1)S(1)}, bf16[4,2,64,512]{3,2,1,0:T(8,128)(2,1)S(1)}, u32[]{:S(2)}, u32[]{:S(2)}) %collective-permute-start.7) | collective-permute-done | bytes 524320 | tf_op jit(solution)/shard_map/b_x3/ppermute | solution.py:30
  41.2 1.4 %collective-permute-start.8 = (bf16[2,1024,128]{2,1,0:T(8,128)(2,1)S(1)}, bf16[2,1024,128]{2,1,0:T(8,128)(2,1)S(1)}, u32[]{:S(2)}, u32[]{:S(2)}) collective-permute-start(bf16[2,1024,128]{2,1,0:T(8,128)(2,1)S(1)} %collective-permute-done.5.refs_4_), channel_id=1, source_target_pairs={{0,2},{1,7},{2,4},{3,1},{4,6},{5,3},{6,0},{7,5},{16,18},{17,23},{1... | collective-permute-start | bytes 1572872 | tf_op jit(solution)/shard_map/a_x1/ppermute | solution.py:30
  42.6 0.0 collective-permute-done.2.refs_2_
  42.6 1.7 %collective-permute-start.13 = (bf16[4,2,64,512]{3,2,1,0:T(8,128)(2,1)S(1)}, bf16[4,2,64,512]{3,2,1,0:T(8,128)(2,1)S(1)}, u32[]{:S(2)}, u32[]{:S(2)}) collective-permute-start(bf16[4,2,64,512]{3,2,1,0:T(8,128)(2,1)S(1)} %collective-permute-done.9.refs_21_), channel_id=1, source_target_pairs={{0,16},{1,49},{2,18},{3,51},{4,20},{5,53},{6,22},{7,55},{16,32},{1... | collective-permute-start | bytes 1572872 | tf_op jit(solution)/shard_map/b_x2/ppermute | solution.py:30
  44.3 1.2 %collective-permute-start.10 = (bf16[2,1024,128]{2,1,0:T(8,128)(2,1)S(1)}, bf16[2,1024,128]{2,1,0:T(8,128)(2,1)S(1)}, u32[]{:S(2)}, u32[]{:S(2)}) collective-permute-start(bf16[2,1024,128]{2,1,0:T(8,128)(2,1)S(1)} %collective-permute-done.2.refs_2_), channel_id=1, source_target_pairs={{0,8},{1,9},{2,10},{3,11},{4,12},{5,13},{6,14},{7,15},{16,24},{17,... | collective-permute-start | bytes 1572872 | tf_op jit(solution)/shard_map/a_x2/ppermute | solution.py:30
  45.5 0.0 collective-permute-done.16.refs_18_
  45.5 2.1 %collective-permute-start.17 = (bf16[2,1024,128]{2,1,0:T(8,128)(2,1)S(1)}, bf16[2,1024,128]{2,1,0:T(8,128)(2,1)S(1)}, u32[]{:S(2)}, u32[]{:S(2)}) collective-permute-start(bf16[2,1024,128]{2,1,0:T(8,128)(2,1)S(1)} %collective-permute-done.2.refs_2_), channel_id=1, source_target_pairs={{0,1},{1,0},{2,3},{3,2},{4,5},{5,4},{6,7},{7,6},{16,17},{17,16},{1... | collective-permute-start | bytes 1572872 | tf_op jit(solution)/shard_map/other_2/ppermute | solution.py:30
  47.6 0.0 collective-permute-done.12.refs_7_
  47.6 8.0 %collective-permute-start.15 = (bf16[2,1024,128]{2,1,0:T(8,128)(2,1)S(1)}, bf16[2,1024,128]{2,1,0:T(8,128)(2,1)S(1)}, u32[]{:S(2)}, u32[]{:S(2)}) collective-permute-start(bf16[2,1024,128]{2,1,0:T(8,128)(2,1)S(1)} %collective-permute-done.refs_1_), channel_id=1, source_target_pairs={{0,1},{1,0},{2,3},{3,2},{4,5},{5,4},{6,7},{7,6},{16,17},{17,16},{1... | collective-permute-start | bytes 1572872 | tf_op jit(solution)/shard_map/other_1/ppermute | solution.py:30
  55.5 0.0 collective-permute-done.13.refs_22_
  55.5 0.1 collective-permute-start.14
  55.6 0.0 collective-permute-done.8.refs_5_
  55.6 0.4 collective-permute-start.19
  56.1 0.4 collective-permute-done.10.refs_6_
  56.4 2.2 %collective-permute-start.20 = (bf16[2,1024,128]{2,1,0:T(8,128)(2,1)S(1)}, bf16[2,1024,128]{2,1,0:T(8,128)(2,1)S(1)}, u32[]{:S(2)}, u32[]{:S(2)}) collective-permute-start(bf16[2,1024,128]{2,1,0:T(8,128)(2,1)S(1)} %collective-permute-done.10.refs_6_), channel_id=1, source_target_pairs={{0,1},{1,0},{2,3},{3,2},{4,5},{5,4},{6,7},{7,6},{16,17},{17,16},{1... | collective-permute-start | bytes 1572872 | tf_op jit(solution)/shard_map/other_x2/ppermute | solution.py:30
  58.6 0.0 collective-permute-done.17.refs_10_
  58.6 0.0 collective-permute-done.15.refs_9_
  58.6 0.1 collective-permute-start.18
  58.7 0.5 collective-permute-start.21
  59.2 0.0 collective-permute-done.19.refs_13_
  59.2 0.9 %collective-permute-done.20.refs_14_ = bf16[2,1024,128]{2,1,0:T(8,128)(2,1)S(1)} collective-permute-done((bf16[2,1024,128]{2,1,0:T(8,128)(2,1)S(1)}, bf16[2,1024,128]{2,1,0:T(8,128)(2,1)S(1)}, u32[]{:S(2)}, u32[]{:S(2)}) %collective-permute-start.20) | collective-permute-done | bytes 524320 | tf_op jit(solution)/shard_map/other_x2/ppermute | solution.py:30
  60.1 0.0 collective-permute-done.14.refs_8_
  60.2 1.5 %collective-permute-done.18.refs_12_ = bf16[2,1024,128]{2,1,0:T(8,128)(2,1)S(1)} collective-permute-done((bf16[2,1024,128]{2,1,0:T(8,128)(2,1)S(1)}, bf16[2,1024,128]{2,1,0:T(8,128)(2,1)S(1)}, u32[]{:S(2)}, u32[]{:S(2)}) %collective-permute-start.18) | collective-permute-done | bytes 524320 | tf_op jit(solution)/shard_map/other_x/ppermute | solution.py:30
  61.7 0.8 %copy-done.20 = bf16[2,1024,128]{2,1,0:T(8,128)(2,1)} copy-done((bf16[2,1024,128]{2,1,0:T(8,128)(2,1)}, bf16[2,1024,128]{2,1,0:T(8,128)(2,1)S(1)}, u32[]{:S(2)}) %copy-start.20) | copy-done | bytes 524312
  62.6 13.7 %shard_map.38 = bf16[4,2,1024,512]{3,2,1,0:T(8,128)(2,1)} custom-call(s32[12]{0:T(128)} %get-tuple-element.38.a_where, s32[12]{0:T(128)} %get-tuple-element.35.b_where, s32[12]{0:T(128)} %get-tuple-element.37.b_row, bf16[2,1024,128]{2,1,0:T(8,128)(2,1)} %shard_map.37.refs_0_, bf16[2,1024,128]{2,1,0:T(8,128)(2,1)} %copy-done.3, ...), custom_call_target="tpu_custom_call" | custom-call | flops 6442450944 | bytes 20971520 | tf_op jit(solution)/shard_map/pallas_call | solution.py:134
  (42 shorter events, 0.1 us)
Async XLA Ops:
  0.0 14.5 %collective-permute-start.4 = (bf16[4,2,64,512]{3,2,1,0:T(8,128)(2,1)}, bf16[4,2,64,512]{3,2,1,0:T(8,128)(2,1)S(1)}, u32[]{:S(2)}, u32[]{:S(2)}) collective-permute-start(bf16[4,2,64,512]{3,2,1,0:T(8,128)(2,1)} %refs_16_.1), channel_id=1, source_target_pairs={{0,48},{1,17},{2,50},{3,19},{4,52},{5,21},{6,54},{7,23},{16,0},{17... | collective-permute-start | bytes 1572872 | tf_op jit(solution)/shard_map/b_3/ppermute | solution.py:30
  4.2 10.7 %collective-permute-start.3 = (bf16[2,1024,128]{2,1,0:T(8,128)(2,1)}, bf16[2,1024,128]{2,1,0:T(8,128)(2,1)S(1)}, u32[]{:S(2)}, u32[]{:S(2)}) collective-permute-start(bf16[2,1024,128]{2,1,0:T(8,128)(2,1)} %shard_map.37.refs_0_), channel_id=1, source_target_pairs={{0,6},{1,3},{2,0},{3,5},{4,2},{5,7},{6,4},{7,1},{16,22},{17,19},{1... | collective-permute-start | bytes 1572872 | tf_op jit(solution)/shard_map/a_3/ppermute | solution.py:30
  5.8 10.3 %collective-permute-start.6 = (bf16[4,2,64,512]{3,2,1,0:T(8,128)(2,1)}, bf16[4,2,64,512]{3,2,1,0:T(8,128)(2,1)S(1)}, u32[]{:S(2)}, u32[]{:S(2)}) collective-permute-start(bf16[4,2,64,512]{3,2,1,0:T(8,128)(2,1)} %refs_16_.1), channel_id=1, source_target_pairs={{0,64},{1,65},{2,66},{3,67},{4,68},{5,69},{6,70},{7,71},{16,80},{1... | collective-permute-start | bytes 1572872 | tf_op jit(solution)/shard_map/b_x/ppermute | solution.py:30
  8.5 17.6 %collective-permute-start = (bf16[2,1024,128]{2,1,0:T(8,128)(2,1)}, bf16[2,1024,128]{2,1,0:T(8,128)(2,1)S(1)}, u32[]{:S(2)}, u32[]{:S(2)}) collective-permute-start(bf16[2,1024,128]{2,1,0:T(8,128)(2,1)} %shard_map.37.refs_0_), channel_id=1, source_target_pairs={{0,2},{1,7},{2,4},{3,1},{4,6},{5,3},{6,0},{7,5},{16,18},{17,23},{1... | collective-permute-start | bytes 1572872 | tf_op jit(solution)/shard_map/a_1/ppermute | solution.py:30
  10.7 16.8 %collective-permute-start.1 = (bf16[4,2,64,512]{3,2,1,0:T(8,128)(2,1)}, bf16[4,2,64,512]{3,2,1,0:T(8,128)(2,1)S(1)}, u32[]{:S(2)}, u32[]{:S(2)}) collective-permute-start(bf16[4,2,64,512]{3,2,1,0:T(8,128)(2,1)} %refs_16_.1), channel_id=1, source_target_pairs={{0,16},{1,49},{2,18},{3,51},{4,20},{5,53},{6,22},{7,55},{16,32},{1... | collective-permute-start | bytes 1572872 | tf_op jit(solution)/shard_map/b_1/ppermute | solution.py:30
  14.5 47.9 %copy-start = (bf16[4,2,64,512]{3,2,1,0:T(8,128)(2,1)}, bf16[4,2,64,512]{3,2,1,0:T(8,128)(2,1)S(1)}, u32[]{:S(2)}) copy-start(bf16[4,2,64,512]{3,2,1,0:T(8,128)(2,1)S(1)} %collective-permute-done.4.refs_19_) | copy-start | bytes 1572868
  14.5 14.2 %collective-permute-start.5 = (bf16[2,1024,128]{2,1,0:T(8,128)(2,1)}, bf16[2,1024,128]{2,1,0:T(8,128)(2,1)S(1)}, u32[]{:S(2)}, u32[]{:S(2)}) collective-permute-start(bf16[2,1024,128]{2,1,0:T(8,128)(2,1)} %shard_map.37.refs_0_), channel_id=1, source_target_pairs={{0,8},{1,9},{2,10},{3,11},{4,12},{5,13},{6,14},{7,15},{16,24},{17,... | collective-permute-start | bytes 1572872 | tf_op jit(solution)/shard_map/a_x/ppermute | solution.py:30
  14.9 47.6 %copy-start.1 = (bf16[2,1024,128]{2,1,0:T(8,128)(2,1)}, bf16[2,1024,128]{2,1,0:T(8,128)(2,1)S(1)}, u32[]{:S(2)}) copy-start(bf16[2,1024,128]{2,1,0:T(8,128)(2,1)S(1)} %collective-permute-done.3.refs_3_) | copy-start | bytes 1572868
  16.1 46.3 %copy-start.2 = (bf16[4,2,64,512]{3,2,1,0:T(8,128)(2,1)}, bf16[4,2,64,512]{3,2,1,0:T(8,128)(2,1)S(1)}, u32[]{:S(2)}) copy-start(bf16[4,2,64,512]{3,2,1,0:T(8,128)(2,1)S(1)} %collective-permute-done.6.refs_20_) | copy-start | bytes 1572868
  16.1 14.2 %collective-permute-start.9 = (bf16[4,2,64,512]{3,2,1,0:T(8,128)(2,1)S(1)}, bf16[4,2,64,512]{3,2,1,0:T(8,128)(2,1)S(1)}, u32[]{:S(2)}, u32[]{:S(2)}) collective-permute-start(bf16[4,2,64,512]{3,2,1,0:T(8,128)(2,1)S(1)} %collective-permute-done.6.refs_20_), channel_id=1, source_target_pairs={{0,16},{1,49},{2,18},{3,51},{4,20},{5,53},{6,22},{7,55},{16,32},{1... | collective-permute-start | bytes 1572872 | tf_op jit(solution)/shard_map/b_x1/ppermute | solution.py:30
  18.6 11.8 %collective-permute-start.11 = (bf16[2,1024,128]{2,1,0:T(8,128)(2,1)S(1)}, bf16[2,1024,128]{2,1,0:T(8,128)(2,1)S(1)}, u32[]{:S(2)}, u32[]{:S(2)}) collective-permute-start(bf16[2,1024,128]{2,1,0:T(8,128)(2,1)S(1)} %collective-permute-done.3.refs_3_), channel_id=1, source_target_pairs={{0,1},{1,0},{2,3},{3,2},{4,5},{5,4},{6,7},{7,6},{16,17},{17,16},{1... | collective-permute-start | bytes 1572872 | tf_op jit(solution)/shard_map/other_3/ppermute | solution.py:30
  26.2 36.3 %copy-start.3 = (bf16[2,1024,128]{2,1,0:T(8,128)(2,1)}, bf16[2,1024,128]{2,1,0:T(8,128)(2,1)S(1)}, u32[]{:S(2)}) copy-start(bf16[2,1024,128]{2,1,0:T(8,128)(2,1)S(1)} %collective-permute-done.refs_1_) | copy-start | bytes 1572868
  26.2 15.0 %collective-permute-start.7 = (bf16[4,2,64,512]{3,2,1,0:T(8,128)(2,1)S(1)}, bf16[4,2,64,512]{3,2,1,0:T(8,128)(2,1)S(1)}, u32[]{:S(2)}, u32[]{:S(2)}) collective-permute-start(bf16[4,2,64,512]{3,2,1,0:T(8,128)(2,1)S(1)} %collective-permute-done.6.refs_20_), channel_id=1, source_target_pairs={{0,48},{1,17},{2,50},{3,19},{4,52},{5,21},{6,54},{7,23},{16,0},{17... | collective-permute-start | bytes 1572872 | tf_op jit(solution)/shard_map/b_x3/ppermute | solution.py:30
  27.5 35.0 %copy-start.4 = (bf16[4,2,64,512]{3,2,1,0:T(8,128)(2,1)}, bf16[4,2,64,512]{3,2,1,0:T(8,128)(2,1)S(1)}, u32[]{:S(2)}) copy-start(bf16[4,2,64,512]{3,2,1,0:T(8,128)(2,1)S(1)} %collective-permute-done.1.refs_17_) | copy-start | bytes 1572868
  27.5 15.1 %collective-permute-start.2 = (bf16[2,1024,128]{2,1,0:T(8,128)(2,1)S(1)}, bf16[2,1024,128]{2,1,0:T(8,128)(2,1)S(1)}, u32[]{:S(2)}, u32[]{:S(2)}) collective-permute-start(bf16[2,1024,128]{2,1,0:T(8,128)(2,1)S(1)} %collective-permute-done.refs_1_), channel_id=1, source_target_pairs={{0,2},{1,7},{2,4},{3,1},{4,6},{5,3},{6,0},{7,5},{16,18},{17,23},{1... | collective-permute-start | bytes 1572872 | tf_op jit(solution)/shard_map/a_2/ppermute | solution.py:30
  28.8 33.7 %copy-start.5 = (bf16[2,1024,128]{2,1,0:T(8,128)(2,1)}, bf16[2,1024,128]{2,1,0:T(8,128)(2,1)S(1)}, u32[]{:S(2)}) copy-start(bf16[2,1024,128]{2,1,0:T(8,128)(2,1)S(1)} %collective-permute-done.5.refs_4_) | copy-start | bytes 1572868
  28.8 16.7 %collective-permute-start.16 = (bf16[4,2,64,512]{3,2,1,0:T(8,128)(2,1)S(1)}, bf16[4,2,64,512]{3,2,1,0:T(8,128)(2,1)S(1)}, u32[]{:S(2)}, u32[]{:S(2)}) collective-permute-start(bf16[4,2,64,512]{3,2,1,0:T(8,128)(2,1)S(1)} %collective-permute-done.1.refs_17_), channel_id=1, source_target_pairs={{0,16},{1,49},{2,18},{3,51},{4,20},{5,53},{6,22},{7,55},{16,32},{1... | collective-permute-start | bytes 1572872 | tf_op jit(solution)/shard_map/b_2/ppermute | solution.py:30
  30.4 32.2 %copy-start.6 = (bf16[4,2,64,512]{3,2,1,0:T(8,128)(2,1)}, bf16[4,2,64,512]{3,2,1,0:T(8,128)(2,1)S(1)}, u32[]{:S(2)}) copy-start(bf16[4,2,64,512]{3,2,1,0:T(8,128)(2,1)S(1)} %collective-permute-done.9.refs_21_) | copy-start | bytes 1572868
  30.4 32.2 %copy-start.7 = (bf16[2,1024,128]{2,1,0:T(8,128)(2,1)}, bf16[2,1024,128]{2,1,0:T(8,128)(2,1)S(1)}, u32[]{:S(2)}) copy-start(bf16[2,1024,128]{2,1,0:T(8,128)(2,1)S(1)} %collective-permute-done.11.refs_11_) | copy-start | bytes 1572868
  30.4 17.2 %collective-permute-start.12 = (bf16[2,1024,128]{2,1,0:T(8,128)(2,1)S(1)}, bf16[2,1024,128]{2,1,0:T(8,128)(2,1)S(1)}, u32[]{:S(2)}, u32[]{:S(2)}) collective-permute-start(bf16[2,1024,128]{2,1,0:T(8,128)(2,1)S(1)} %collective-permute-done.5.refs_4_), channel_id=1, source_target_pairs={{0,6},{1,3},{2,0},{3,5},{4,2},{5,7},{6,4},{7,1},{16,22},{17,19},{1... | collective-permute-start | bytes 1572872 | tf_op jit(solution)/shard_map/a_x3/ppermute | solution.py:30
  41.2 21.3 %copy-start.8 = (bf16[4,2,64,512]{3,2,1,0:T(8,128)(2,1)}, bf16[4,2,64,512]{3,2,1,0:T(8,128)(2,1)S(1)}, u32[]{:S(2)}) copy-start(bf16[4,2,64,512]{3,2,1,0:T(8,128)(2,1)S(1)} %collective-permute-done.7.refs_23_) | copy-start | bytes 1572868
  41.2 14.4 %collective-permute-start.8 = (bf16[2,1024,128]{2,1,0:T(8,128)(2,1)S(1)}, bf16[2,1024,128]{2,1,0:T(8,128)(2,1)S(1)}, u32[]{:S(2)}, u32[]{:S(2)}) collective-permute-start(bf16[2,1024,128]{2,1,0:T(8,128)(2,1)S(1)} %collective-permute-done.5.refs_4_), channel_id=1, source_target_pairs={{0,2},{1,7},{2,4},{3,1},{4,6},{5,3},{6,0},{7,5},{16,18},{17,23},{1... | collective-permute-start | bytes 1572872 | tf_op jit(solution)/shard_map/a_x1/ppermute | solution.py:30
  42.6 20.0 %copy-start.9 = (bf16[2,1024,128]{2,1,0:T(8,128)(2,1)}, bf16[2,1024,128]{2,1,0:T(8,128)(2,1)S(1)}, u32[]{:S(2)}) copy-start(bf16[2,1024,128]{2,1,0:T(8,128)(2,1)S(1)} %collective-permute-done.2.refs_2_) | copy-start | bytes 1572868
  42.6 13.0 %collective-permute-start.13 = (bf16[4,2,64,512]{3,2,1,0:T(8,128)(2,1)S(1)}, bf16[4,2,64,512]{3,2,1,0:T(8,128)(2,1)S(1)}, u32[]{:S(2)}, u32[]{:S(2)}) collective-permute-start(bf16[4,2,64,512]{3,2,1,0:T(8,128)(2,1)S(1)} %collective-permute-done.9.refs_21_), channel_id=1, source_target_pairs={{0,16},{1,49},{2,18},{3,51},{4,20},{5,53},{6,22},{7,55},{16,32},{1... | collective-permute-start | bytes 1572872 | tf_op jit(solution)/shard_map/b_x2/ppermute | solution.py:30
  44.3 12.1 %collective-permute-start.10 = (bf16[2,1024,128]{2,1,0:T(8,128)(2,1)S(1)}, bf16[2,1024,128]{2,1,0:T(8,128)(2,1)S(1)}, u32[]{:S(2)}, u32[]{:S(2)}) collective-permute-start(bf16[2,1024,128]{2,1,0:T(8,128)(2,1)S(1)} %collective-permute-done.2.refs_2_), channel_id=1, source_target_pairs={{0,8},{1,9},{2,10},{3,11},{4,12},{5,13},{6,14},{7,15},{16,24},{17,... | collective-permute-start | bytes 1572872 | tf_op jit(solution)/shard_map/a_x2/ppermute | solution.py:30
  45.5 17.1 %copy-start.10 = (bf16[4,2,64,512]{3,2,1,0:T(8,128)(2,1)}, bf16[4,2,64,512]{3,2,1,0:T(8,128)(2,1)S(1)}, u32[]{:S(2)}) copy-start(bf16[4,2,64,512]{3,2,1,0:T(8,128)(2,1)S(1)} %collective-permute-done.16.refs_18_) | copy-start | bytes 1572868
  45.5 13.1 %collective-permute-start.17 = (bf16[2,1024,128]{2,1,0:T(8,128)(2,1)S(1)}, bf16[2,1024,128]{2,1,0:T(8,128)(2,1)S(1)}, u32[]{:S(2)}, u32[]{:S(2)}) collective-permute-start(bf16[2,1024,128]{2,1,0:T(8,128)(2,1)S(1)} %collective-permute-done.2.refs_2_), channel_id=1, source_target_pairs={{0,1},{1,0},{2,3},{3,2},{4,5},{5,4},{6,7},{7,6},{16,17},{17,16},{1... | collective-permute-start | bytes 1572872 | tf_op jit(solution)/shard_map/other_2/ppermute | solution.py:30
  47.6 15.0 %copy-start.11 = (bf16[2,1024,128]{2,1,0:T(8,128)(2,1)}, bf16[2,1024,128]{2,1,0:T(8,128)(2,1)S(1)}, u32[]{:S(2)}) copy-start(bf16[2,1024,128]{2,1,0:T(8,128)(2,1)S(1)} %collective-permute-done.12.refs_7_) | copy-start | bytes 1572868
  47.6 11.0 %collective-permute-start.15 = (bf16[2,1024,128]{2,1,0:T(8,128)(2,1)S(1)}, bf16[2,1024,128]{2,1,0:T(8,128)(2,1)S(1)}, u32[]{:S(2)}, u32[]{:S(2)}) collective-permute-start(bf16[2,1024,128]{2,1,0:T(8,128)(2,1)S(1)} %collective-permute-done.refs_1_), channel_id=1, source_target_pairs={{0,1},{1,0},{2,3},{3,2},{4,5},{5,4},{6,7},{7,6},{16,17},{17,16},{1... | collective-permute-start | bytes 1572872 | tf_op jit(solution)/shard_map/other_1/ppermute | solution.py:30
  55.5 7.0 %copy-start.13 = (bf16[4,2,64,512]{3,2,1,0:T(8,128)(2,1)}, bf16[4,2,64,512]{3,2,1,0:T(8,128)(2,1)S(1)}, u32[]{:S(2)}) copy-start(bf16[4,2,64,512]{3,2,1,0:T(8,128)(2,1)S(1)} %collective-permute-done.13.refs_22_) | copy-start | bytes 1572868
  55.5 4.6 %collective-permute-start.14 = (bf16[2,1024,128]{2,1,0:T(8,128)(2,1)}, bf16[2,1024,128]{2,1,0:T(8,128)(2,1)S(1)}, u32[]{:S(2)}, u32[]{:S(2)}) collective-permute-start(bf16[2,1024,128]{2,1,0:T(8,128)(2,1)} %shard_map.37.refs_0_), channel_id=1, source_target_pairs={{0,1},{1,0},{2,3},{3,2},{4,5},{5,4},{6,7},{7,6},{16,17},{17,16},{1... | collective-permute-start | bytes 1572872 | tf_op jit(solution)/shard_map/other/ppermute | solution.py:30
  55.6 6.9 %copy-start.12 = (bf16[2,1024,128]{2,1,0:T(8,128)(2,1)}, bf16[2,1024,128]{2,1,0:T(8,128)(2,1)S(1)}, u32[]{:S(2)}) copy-start(bf16[2,1024,128]{2,1,0:T(8,128)(2,1)S(1)} %collective-permute-done.8.refs_5_) | copy-start | bytes 1572868
  55.6 3.6 %collective-permute-start.19 = (bf16[2,1024,128]{2,1,0:T(8,128)(2,1)S(1)}, bf16[2,1024,128]{2,1,0:T(8,128)(2,1)S(1)}, u32[]{:S(2)}, u32[]{:S(2)}) collective-permute-start(bf16[2,1024,128]{2,1,0:T(8,128)(2,1)S(1)} %collective-permute-done.8.refs_5_), channel_id=1, source_target_pairs={{0,1},{1,0},{2,3},{3,2},{4,5},{5,4},{6,7},{7,6},{16,17},{17,16},{1... | collective-permute-start | bytes 1572872 | tf_op jit(solution)/shard_map/other_x1/ppermute | solution.py:30
  56.4 6.2 %copy-start.14 = (bf16[2,1024,128]{2,1,0:T(8,128)(2,1)}, bf16[2,1024,128]{2,1,0:T(8,128)(2,1)S(1)}, u32[]{:S(2)}) copy-start(bf16[2,1024,128]{2,1,0:T(8,128)(2,1)S(1)} %collective-permute-done.10.refs_6_) | copy-start | bytes 1572868
  56.4 3.7 %collective-permute-start.20 = (bf16[2,1024,128]{2,1,0:T(8,128)(2,1)S(1)}, bf16[2,1024,128]{2,1,0:T(8,128)(2,1)S(1)}, u32[]{:S(2)}, u32[]{:S(2)}) collective-permute-start(bf16[2,1024,128]{2,1,0:T(8,128)(2,1)S(1)} %collective-permute-done.10.refs_6_), channel_id=1, source_target_pairs={{0,1},{1,0},{2,3},{3,2},{4,5},{5,4},{6,7},{7,6},{16,17},{17,16},{1... | collective-permute-start | bytes 1572872 | tf_op jit(solution)/shard_map/other_x2/ppermute | solution.py:30
  58.6 3.0 %copy-start.15 = (bf16[2,1024,128]{2,1,0:T(8,128)(2,1)}, bf16[2,1024,128]{2,1,0:T(8,128)(2,1)S(1)}, u32[]{:S(2)}) copy-start(bf16[2,1024,128]{2,1,0:T(8,128)(2,1)S(1)} %collective-permute-done.17.refs_10_) | copy-start | bytes 1572868
  58.6 3.0 %copy-start.16 = (bf16[2,1024,128]{2,1,0:T(8,128)(2,1)}, bf16[2,1024,128]{2,1,0:T(8,128)(2,1)S(1)}, u32[]{:S(2)}) copy-start(bf16[2,1024,128]{2,1,0:T(8,128)(2,1)S(1)} %collective-permute-done.15.refs_9_) | copy-start | bytes 1572868
  58.6 3.0 %collective-permute-start.18 = (bf16[2,1024,128]{2,1,0:T(8,128)(2,1)S(1)}, bf16[2,1024,128]{2,1,0:T(8,128)(2,1)S(1)}, u32[]{:S(2)}, u32[]{:S(2)}) collective-permute-start(bf16[2,1024,128]{2,1,0:T(8,128)(2,1)S(1)} %collective-permute-done.5.refs_4_), channel_id=1, source_target_pairs={{0,1},{1,0},{2,3},{3,2},{4,5},{5,4},{6,7},{7,6},{16,17},{17,16},{1... | collective-permute-start | bytes 1572872 | tf_op jit(solution)/shard_map/other_x/ppermute | solution.py:30
  58.7 3.7 %collective-permute-start.21 = (bf16[2,1024,128]{2,1,0:T(8,128)(2,1)S(1)}, bf16[2,1024,128]{2,1,0:T(8,128)(2,1)}, u32[]{:S(2)}, u32[]{:S(2)}) collective-permute-start(bf16[2,1024,128]{2,1,0:T(8,128)(2,1)S(1)} %collective-permute-done.12.refs_7_), channel_id=1, source_target_pairs={{0,1},{1,0},{2,3},{3,2},{4,5},{5,4},{6,7},{7,6},{16,17},{17,16},{1... | collective-permute-start | bytes 1572872 | tf_op jit(solution)/shard_map/other_x3/ppermute | solution.py:30
  59.2 2.4 %copy-start.18 = (bf16[2,1024,128]{2,1,0:T(8,128)(2,1)}, bf16[2,1024,128]{2,1,0:T(8,128)(2,1)S(1)}, u32[]{:S(2)}) copy-start(bf16[2,1024,128]{2,1,0:T(8,128)(2,1)S(1)} %collective-permute-done.19.refs_13_) | copy-start | bytes 1572868
  60.1 1.5 %copy-start.19 = (bf16[2,1024,128]{2,1,0:T(8,128)(2,1)}, bf16[2,1024,128]{2,1,0:T(8,128)(2,1)S(1)}, u32[]{:S(2)}) copy-start(bf16[2,1024,128]{2,1,0:T(8,128)(2,1)S(1)} %collective-permute-done.20.refs_14_) | copy-start | bytes 1572868
  60.2 1.5 %copy-start.17 = (bf16[2,1024,128]{2,1,0:T(8,128)(2,1)}, bf16[2,1024,128]{2,1,0:T(8,128)(2,1)S(1)}, u32[]{:S(2)}) copy-start(bf16[2,1024,128]{2,1,0:T(8,128)(2,1)S(1)} %collective-permute-done.14.refs_8_) | copy-start | bytes 1572868
  61.7 0.8 %copy-start.20 = (bf16[2,1024,128]{2,1,0:T(8,128)(2,1)}, bf16[2,1024,128]{2,1,0:T(8,128)(2,1)S(1)}, u32[]{:S(2)}) copy-start(bf16[2,1024,128]{2,1,0:T(8,128)(2,1)S(1)} %collective-permute-done.18.refs_12_) | copy-start | bytes 1572868

commit v8 on v6

--- a/solution.py
+++ b/solution.py
@@ -54,9 +54,8 @@
 
     def fetch(first_freq, count, slot):
         these = pl.ds(first_freq, count)
-
-        @pl.loop(0, STEPS)
-        def _(step):
+        for step in range(STEPS):
+
             def from_surface(ref):
                 pltpu.make_async_copy(
                     ref.at[these], a_buf.at[step, these], a_sem.at[slot]
@@ -91,20 +90,21 @@
     for step in range(STEPS):
         real = b_buf[step, f, 0]
         imag = b_buf[step, f, 1]
-        rhs[0, step, 0] = real
-        rhs[0, step, 1] = -imag
-        rhs[1, step, 0] = imag
-        rhs[1, step, 1] = real
+        rhs[step, 0, :, :rcvs] = real
+        rhs[step, 0, :, rcvs:] = imag
+        rhs[step, 1, :, :rcvs] = -imag
+        rhs[step, 1, :, rcvs:] = real
 
     depth = STEPS * 2 * BLK
     for first in range(0, lhs.shape[0], ROWS):
         block = a_buf[:, f, :, :, first : first + ROWS].reshape(depth, ROWS)
         lhs[first : first + ROWS, :] = block.T
 
-    for part in range(2):
-        out[0, part] = jnp.dot(
-            lhs[...], rhs[part].reshape(depth, rcvs), preferred_element_type=jnp.float32
-        ).astype(out.dtype)
+    product = jnp.dot(
+        lhs[...], rhs[...].reshape(depth, 2 * rcvs), preferred_element_type=jnp.float32
+    ).astype(out.dtype)
+    out[0, 0] = product[:, :rcvs]
+    out[0, 1] = product[:, rcvs:]
 
 
 def multiply(a_parts, b_parts, a_where, b_where, b_row):
@@ -123,7 +123,7 @@
                 pltpu.VMEM((STEPS, freqs, 2, BLK, shots), jnp.bfloat16),
                 pltpu.VMEM((STEPS, freqs, 2, BLK, rcvs), jnp.bfloat16),
                 pltpu.VMEM((shots, depth), jnp.bfloat16),
-                pltpu.VMEM((2, STEPS, 2, BLK, rcvs), jnp.bfloat16),
+                pltpu.VMEM((STEPS, 2, BLK, 2 * rcvs), jnp.bfloat16),
                 pltpu.SemaphoreType.DMA((2,)),
                 pltpu.SemaphoreType.DMA((2,)),
             ],
@@ -175,18 +175,18 @@
     b_x1 = send("b_x1", after(b_x, a_3), dy=1)
     a_2 = send("a_2", after(a_1, b_1), dz=1)
     b_x3 = send("b_x3", after(b_x, a_1), dy=-1)
-    a_x3 = send("a_x3", a_x, dz=-1)
-    b_2 = send("b_2", after(b_1, other_3), dy=1)
+    b_2 = send("b_2", after(b_1, a_x), dy=1)
+    a_x3 = send("a_x3", after(a_x, other_3, b_x1), dz=-1)
     a_x2 = send("a_x2", after(a_2, b_x1), flip_x=True)
     b_x2 = send("b_x2", after(b_x1, a_2), dy=1)
     a_x1 = send("a_x1", after(a_x, b_x3), dz=1)
-    other = swap("other", after(a, a_x3))
     other_2 = swap("other_2", after(a_2, b_2))
-    other_1 = swap("other_1", after(a_1, a_x2))
-    other_x2 = swap("other_x2", after(a_x2, b_x2))
+    other_1 = swap("other_1", after(a_1, a_x3))
+    other_x2 = swap("other_x2", a_x2)
+    other = swap("other", after(a, b_x2))
     other_x1 = swap("other_x1", a_x1)
-    other_x = swap("other_x", after(a_x, other))
     other_x3 = swap("other_x3", after(a_x3, other_2))
+    other_x = swap("other_x", after(a_x, other_1))
 
     a_parts = [a, a_1, a_2, a_3, a_x, a_x1, a_x2, a_x3]
     a_parts += [other, other_1, other_2, other_3, other_x, other_x1, other_x2, other_x3]

time: 66.6 us -> 72.1 us (1.083)
  starting transfers between devices: 37.4 us -> 41.6 us
  waiting for transfers between devices: 13.6 us -> 14.9 us
    ppermute x22, starting transfers between devices: 37.4 us -> 41.6 us  [moved(): return lax.ppermute(value, AXES, pairs)]
    ppermute x22, waiting for transfers between devices: 13.6 us -> 14.9 us  [moved(): return lax.ppermute(value, AXES, pairs)]
  transfers between devices with their start and end apart: 22 -> 22, of which waited for: 8 -> 9; matrix products, arithmetic and copies ran while one was open for 4% -> 3% of each run, Pallas kernels for 0% -> 0%
where the time goes in v8:
time: 72.1 us; the launch traced here: 71.9 us
  starting transfers between devices  41.6 us (58%)
  waiting for transfers between devices  14.9 us (21%)
  Pallas kernels  11.8 us (16%)
  other arithmetic  2.46 us (3%)
  local copies, waits for them, and re-layouts  0.94 us (1%)
    ppermute x22, starting transfers between devices, moved(): return lax.ppermute(value, AXES, pairs)  41.6 us
    ppermute x22, waiting for transfers between devices, moved(): return lax.ppermute(value, AXES, pairs)  14.9 us
    pallas_call x1, Pallas kernels, multiply(): pl.pallas_call(multiply_kernel, out_shape=jax.ShapeDtypeStruct((freqs, 2,...  11.8 us
  transfers between devices with their start and end apart: 22, of which 9 were waited for; matrix products, arithmetic and copies ran while one was open for 3% of the time, Pallas kernels for 0%

profile of v8, /device:TPU:1, one launch (start us, length us, event | category | flops | bytes accessed | tf_op | source)
XLA Modules:
  0.0 71.9 jit_solution(8950232120807222249)
XLA Ops:
  0.0 2.1 %collective-permute-start.4 = (bf16[4,2,64,512]{3,2,1,0:T(8,128)(2,1)}, bf16[4,2,64,512]{3,2,1,0:T(8,128)(2,1)S(1)}, u32[]{:S(2)}, u32[]{:S(2)}) collective-permute-start(bf16[4,2,64,512]{3,2,1,0:T(8,128)(2,1)} %refs_16_.1), channel_id=1, source_target_pairs={{0,48},{1,17},{2,50},{3,19},{4,52},{5,21},{6,54},{7,23},{16,0},{17... | collective-permute-start | bytes 1572872 | tf_op jit(solution)/shard_map/b_3/ppermute | solution.py:30
  2.1 2.7 %collective-permute-start.6 = (bf16[4,2,64,512]{3,2,1,0:T(8,128)(2,1)}, bf16[4,2,64,512]{3,2,1,0:T(8,128)(2,1)S(1)}, u32[]{:S(2)}, u32[]{:S(2)}) collective-permute-start(bf16[4,2,64,512]{3,2,1,0:T(8,128)(2,1)} %refs_16_.1), channel_id=1, source_target_pairs={{0,64},{1,65},{2,66},{3,67},{4,68},{5,69},{6,70},{7,71},{16,80},{1... | collective-permute-start | bytes 1572872 | tf_op jit(solution)/shard_map/b_x/ppermute | solution.py:30
  4.9 1.6 %collective-permute-start.3 = (bf16[4,2,32,1024]{3,2,1,0:T(8,128)(2,1)}, bf16[4,2,32,1024]{3,2,1,0:T(8,128)(2,1)S(1)}, u32[]{:S(2)}, u32[]{:S(2)}) collective-permute-start(bf16[4,2,32,1024]{3,2,1,0:T(8,128)(2,1)} %refs_0_.1), channel_id=1, source_target_pairs={{0,6},{1,3},{2,0},{3,5},{4,2},{5,7},{6,4},{7,1},{16,22},{17,19},{1... | collective-permute-start | bytes 1572872 | tf_op jit(solution)/shard_map/a_3/ppermute | solution.py:30
  6.5 1.4 %collective-permute-start.1 = (bf16[4,2,64,512]{3,2,1,0:T(8,128)(2,1)}, bf16[4,2,64,512]{3,2,1,0:T(8,128)(2,1)S(1)}, u32[]{:S(2)}, u32[]{:S(2)}) collective-permute-start(bf16[4,2,64,512]{3,2,1,0:T(8,128)(2,1)} %refs_16_.1), channel_id=1, source_target_pairs={{0,16},{1,49},{2,18},{3,51},{4,20},{5,53},{6,22},{7,55},{16,32},{1... | collective-permute-start | bytes 1572872 | tf_op jit(solution)/shard_map/b_1/ppermute | solution.py:30
  8.0 2.1 %collective-permute-start = (bf16[4,2,32,1024]{3,2,1,0:T(8,128)(2,1)}, bf16[4,2,32,1024]{3,2,1,0:T(8,128)(2,1)S(1)}, u32[]{:S(2)}, u32[]{:S(2)}) collective-permute-start(bf16[4,2,32,1024]{3,2,1,0:T(8,128)(2,1)} %refs_0_.1), channel_id=1, source_target_pairs={{0,2},{1,7},{2,4},{3,1},{4,6},{5,3},{6,0},{7,5},{16,18},{17,23},{1... | collective-permute-start | bytes 1572872 | tf_op jit(solution)/shard_map/a_1/ppermute | solution.py:30
  10.1 1.2 %fusion.1 = (s32[12]{0:T(128)}, s32[12]{0:T(128)S(1)}) fusion(pred[]{:T(512)S(6)} %eq.18, s32[]{:T(128)S(6)} %select_n.83, s32[]{:T(128)S(6)} %select_n.80, s32[12]{0:T(128)} %param.5), kind=kLoop, calls=%fused_computation.25 | loop fusion | flops 612 | bytes 153 | tf_op jit(solution)/shard_map/add | solution.py:149
  11.3 1.2 %broadcast_multiply_fusion = (s32[12]{0:T(128)}, s32[12]{0:T(128)}) fusion(s32[12]{0:T(128)} %param.5, s32[12]{0:T(128)S(1)} %get-tuple-element.36, s32[]{:T(128)S(6)} %select_n.75, s32[]{:T(128)S(6)} %select_n.73, s32[]{:T(128)S(6)} %select_n.71), kind=kLoop, calls=%fused_computation.29 | loop fusion | flops 684 | bytes 204 | tf_op jit(solution)/shard_map/mul | solution.py:150
  12.5 0.0 collective-permute-done.4.refs_19_
  12.5 0.3 collective-permute-start.5
  12.9 2.0 %collective-permute-done.6.refs_20_ = bf16[4,2,64,512]{3,2,1,0:T(8,128)(2,1)S(1)} collective-permute-done((bf16[4,2,64,512]{3,2,1,0:T(8,128)(2,1)}, bf16[4,2,64,512]{3,2,1,0:T(8,128)(2,1)S(1)}, u32[]{:S(2)}, u32[]{:S(2)}) %collective-permute-start.6) | collective-permute-done | bytes 524320 | tf_op jit(solution)/shard_map/b_x/ppermute | solution.py:30
  14.9 0.8 %collective-permute-done.3.refs_3_ = bf16[4,2,32,1024]{3,2,1,0:T(8,128)(2,1)S(1)} collective-permute-done((bf16[4,2,32,1024]{3,2,1,0:T(8,128)(2,1)}, bf16[4,2,32,1024]{3,2,1,0:T(8,128)(2,1)S(1)}, u32[]{:S(2)}, u32[]{:S(2)}) %collective-permute-start.3) | collective-permute-done | bytes 524320 | tf_op jit(solution)/shard_map/a_3/ppermute | solution.py:30
  15.7 1.7 %collective-permute-start.9 = (bf16[4,2,64,512]{3,2,1,0:T(8,128)(2,1)S(1)}, bf16[4,2,64,512]{3,2,1,0:T(8,128)(2,1)S(1)}, u32[]{:S(2)}, u32[]{:S(2)}) collective-permute-start(bf16[4,2,64,512]{3,2,1,0:T(8,128)(2,1)S(1)} %collective-permute-done.6.refs_20_), channel_id=1, source_target_pairs={{0,16},{1,49},{2,18},{3,51},{4,20},{5,53},{6,22},{7,55},{16,32},{1... | collective-permute-start | bytes 1572872 | tf_op jit(solution)/shard_map/b_x1/ppermute | solution.py:30
  17.4 5.5 %collective-permute-start.11 = (bf16[4,2,32,1024]{3,2,1,0:T(8,128)(2,1)S(1)}, bf16[4,2,32,1024]{3,2,1,0:T(8,128)(2,1)S(1)}, u32[]{:S(2)}, u32[]{:S(2)}) collective-permute-start(bf16[4,2,32,1024]{3,2,1,0:T(8,128)(2,1)S(1)} %collective-permute-done.3.refs_3_), channel_id=1, source_target_pairs={{0,1},{1,0},{2,3},{3,2},{4,5},{5,4},{6,7},{7,6},{16,17},{17,16},{1... | collective-permute-start | bytes 1572872 | tf_op jit(solution)/shard_map/other_3/ppermute | solution.py:30
  22.8 0.0 collective-permute-done.1.refs_17_
  22.8 0.0 collective-permute-done.refs_1_
  22.9 3.4 %collective-permute-start.2 = (bf16[4,2,32,1024]{3,2,1,0:T(8,128)(2,1)S(1)}, bf16[4,2,32,1024]{3,2,1,0:T(8,128)(2,1)S(1)}, u32[]{:S(2)}, u32[]{:S(2)}) collective-permute-start(bf16[4,2,32,1024]{3,2,1,0:T(8,128)(2,1)S(1)} %collective-permute-done.refs_1_), channel_id=1, source_target_pairs={{0,2},{1,7},{2,4},{3,1},{4,6},{5,3},{6,0},{7,5},{16,18},{17,23},{1... | collective-permute-start | bytes 1572872 | tf_op jit(solution)/shard_map/a_2/ppermute | solution.py:30
  26.2 1.3 %collective-permute-start.7 = (bf16[4,2,64,512]{3,2,1,0:T(8,128)(2,1)S(1)}, bf16[4,2,64,512]{3,2,1,0:T(8,128)(2,1)S(1)}, u32[]{:S(2)}, u32[]{:S(2)}) collective-permute-start(bf16[4,2,64,512]{3,2,1,0:T(8,128)(2,1)S(1)} %collective-permute-done.6.refs_20_), channel_id=1, source_target_pairs={{0,48},{1,17},{2,50},{3,19},{4,52},{5,21},{6,54},{7,23},{16,0},{17... | collective-permute-start | bytes 1572872 | tf_op jit(solution)/shard_map/b_x3/ppermute | solution.py:30
  27.5 0.0 collective-permute-done.5.refs_4_
  27.5 1.4 %collective-permute-start.16 = (bf16[4,2,64,512]{3,2,1,0:T(8,128)(2,1)S(1)}, bf16[4,2,64,512]{3,2,1,0:T(8,128)(2,1)S(1)}, u32[]{:S(2)}, u32[]{:S(2)}) collective-permute-start(bf16[4,2,64,512]{3,2,1,0:T(8,128)(2,1)S(1)} %collective-permute-done.1.refs_17_), channel_id=1, source_target_pairs={{0,16},{1,49},{2,18},{3,51},{4,20},{5,53},{6,22},{7,55},{16,32},{1... | collective-permute-start | bytes 1572872 | tf_op jit(solution)/shard_map/b_2/ppermute | solution.py:30
  29.0 0.0 collective-permute-done.9.refs_21_
  29.0 0.0 collective-permute-done.11.refs_11_
  29.0 1.4 %collective-permute-start.12 = (bf16[4,2,32,1024]{3,2,1,0:T(8,128)(2,1)S(1)}, bf16[4,2,32,1024]{3,2,1,0:T(8,128)(2,1)S(1)}, u32[]{:S(2)}, u32[]{:S(2)}) collective-permute-start(bf16[4,2,32,1024]{3,2,1,0:T(8,128)(2,1)S(1)} %collective-permute-done.5.refs_4_), channel_id=1, source_target_pairs={{0,6},{1,3},{2,0},{3,5},{4,2},{5,7},{6,4},{7,1},{16,22},{17,19},{1... | collective-permute-start | bytes 1572872 | tf_op jit(solution)/shard_map/a_x3/ppermute | solution.py:30
  30.3 2.0 %collective-permute-done.2.refs_2_ = bf16[4,2,32,1024]{3,2,1,0:T(8,128)(2,1)S(1)} collective-permute-done((bf16[4,2,32,1024]{3,2,1,0:T(8,128)(2,1)S(1)}, bf16[4,2,32,1024]{3,2,1,0:T(8,128)(2,1)S(1)}, u32[]{:S(2)}, u32[]{:S(2)}) %collective-permute-start.2) | collective-permute-done | bytes 524320 | tf_op jit(solution)/shard_map/a_2/ppermute | solution.py:30
  32.4 0.3 collective-permute-start.10
  32.7 2.7 %collective-permute-start.13 = (bf16[4,2,64,512]{3,2,1,0:T(8,128)(2,1)S(1)}, bf16[4,2,64,512]{3,2,1,0:T(8,128)(2,1)S(1)}, u32[]{:S(2)}, u32[]{:S(2)}) collective-permute-start(bf16[4,2,64,512]{3,2,1,0:T(8,128)(2,1)S(1)} %collective-permute-done.9.refs_21_), channel_id=1, source_target_pairs={{0,16},{1,49},{2,18},{3,51},{4,20},{5,53},{6,22},{7,55},{16,32},{1... | collective-permute-start | bytes 1572872 | tf_op jit(solution)/shard_map/b_x2/ppermute | solution.py:30
  35.3 6.1 %collective-permute-done.7.refs_23_ = bf16[4,2,64,512]{3,2,1,0:T(8,128)(2,1)S(1)} collective-permute-done((bf16[4,2,64,512]{3,2,1,0:T(8,128)(2,1)S(1)}, bf16[4,2,64,512]{3,2,1,0:T(8,128)(2,1)S(1)}, u32[]{:S(2)}, u32[]{:S(2)}) %collective-permute-start.7) | collective-permute-done | bytes 524320 | tf_op jit(solution)/shard_map/b_x3/ppermute | solution.py:30
  41.5 0.2 collective-permute-start.8
  41.6 0.0 collective-permute-done.16.refs_18_
  41.6 2.5 %collective-permute-start.17 = (bf16[4,2,32,1024]{3,2,1,0:T(8,128)(2,1)S(1)}, bf16[4,2,32,1024]{3,2,1,0:T(8,128)(2,1)S(1)}, u32[]{:S(2)}, u32[]{:S(2)}) collective-permute-start(bf16[4,2,32,1024]{3,2,1,0:T(8,128)(2,1)S(1)} %collective-permute-done.2.refs_2_), channel_id=1, source_target_pairs={{0,1},{1,0},{2,3},{3,2},{4,5},{5,4},{6,7},{7,6},{16,17},{17,16},{1... | collective-permute-start | bytes 1572872 | tf_op jit(solution)/shard_map/other_2/ppermute | solution.py:30
  44.2 0.0 collective-permute-done.12.refs_7_
  44.2 9.6 %collective-permute-start.15 = (bf16[4,2,32,1024]{3,2,1,0:T(8,128)(2,1)S(1)}, bf16[4,2,32,1024]{3,2,1,0:T(8,128)(2,1)S(1)}, u32[]{:S(2)}, u32[]{:S(2)}) collective-permute-start(bf16[4,2,32,1024]{3,2,1,0:T(8,128)(2,1)S(1)} %collective-permute-done.refs_1_), channel_id=1, source_target_pairs={{0,1},{1,0},{2,3},{3,2},{4,5},{5,4},{6,7},{7,6},{16,17},{17,16},{1... | collective-permute-start | bytes 1572872 | tf_op jit(solution)/shard_map/other_1/ppermute | solution.py:30
  53.8 0.1 collective-permute-start.14
  53.8 0.0 collective-permute-done.10.refs_6_
  53.9 0.4 collective-permute-start.20
  54.3 0.0 collective-permute-done.8.refs_5_
  54.3 0.1 collective-permute-start.19
  54.4 0.0 collective-permute-done.17.refs_10_
  54.4 0.4 collective-permute-start.21
  54.8 0.5 collective-permute-done.15.refs_9_
  55.3 0.4 collective-permute-start.18
  55.7 1.1 %collective-permute-done.20.refs_14_ = bf16[4,2,32,1024]{3,2,1,0:T(8,128)(2,1)S(1)} collective-permute-done((bf16[4,2,32,1024]{3,2,1,0:T(8,128)(2,1)S(1)}, bf16[4,2,32,1024]{3,2,1,0:T(8,128)(2,1)S(1)}, u32[]{:S(2)}, u32[]{:S(2)}) %collective-permute-start.20) | collective-permute-done | bytes 524320 | tf_op jit(solution)/shard_map/other_x2/ppermute | solution.py:30
  56.8 0.2 collective-permute-done.14.refs_8_
  57.0 1.3 %collective-permute-done.19.refs_13_ = bf16[4,2,32,1024]{3,2,1,0:T(8,128)(2,1)S(1)} collective-permute-done((bf16[4,2,32,1024]{3,2,1,0:T(8,128)(2,1)S(1)}, bf16[4,2,32,1024]{3,2,1,0:T(8,128)(2,1)S(1)}, u32[]{:S(2)}, u32[]{:S(2)}) %collective-permute-start.19) | collective-permute-done | bytes 524320 | tf_op jit(solution)/shard_map/other_x1/ppermute | solution.py:30
  58.3 0.7 %collective-permute-done.21.refs_15_ = bf16[4,2,32,1024]{3,2,1,0:T(8,128)(2,1)S(1)} collective-permute-done((bf16[4,2,32,1024]{3,2,1,0:T(8,128)(2,1)S(1)}, bf16[4,2,32,1024]{3,2,1,0:T(8,128)(2,1)S(1)}, u32[]{:S(2)}, u32[]{:S(2)}) %collective-permute-start.21) | collective-permute-done | bytes 524320 | tf_op jit(solution)/shard_map/other_x3/ppermute | solution.py:30
  59.1 0.0 copy-done.19
  59.1 0.8 %copy-done.20 = bf16[4,2,32,1024]{3,2,1,0:T(8,128)(2,1)} copy-done((bf16[4,2,32,1024]{3,2,1,0:T(8,128)(2,1)}, bf16[4,2,32,1024]{3,2,1,0:T(8,128)(2,1)S(1)}, u32[]{:S(2)}) %copy-start.20) | copy-done | bytes 524312
  59.9 0.0 collective-permute-done.18.refs_12_
  60.1 11.8 %shard_map.37 = bf16[4,2,1024,512]{3,2,1,0:T(8,128)(2,1)} custom-call(s32[12]{0:T(128)} %get-tuple-element.38.a_where, s32[12]{0:T(128)} %get-tuple-element.35.b_where, s32[12]{0:T(128)} %get-tuple-element.37.b_row, bf16[4,2,32,1024]{3,2,1,0:T(8,128)(2,1)} %refs_0_.1, bf16[4,2,32,1024]{3,2,1,0:T(8,128)(2,1)} %copy-done.4, ...), custom_call_target="tpu_custom_call" | custom-call | flops 6442450944 | bytes 20971520 | tf_op jit(solution)/shard_map/pallas_call | solution.py:114
  (41 shorter events, 0.1 us)
Async XLA Ops:
  0.0 12.5 %collective-permute-start.4 = (bf16[4,2,64,512]{3,2,1,0:T(8,128)(2,1)}, bf16[4,2,64,512]{3,2,1,0:T(8,128)(2,1)S(1)}, u32[]{:S(2)}, u32[]{:S(2)}) collective-permute-start(bf16[4,2,64,512]{3,2,1,0:T(8,128)(2,1)} %refs_16_.1), channel_id=1, source_target_pairs={{0,48},{1,17},{2,50},{3,19},{4,52},{5,21},{6,54},{7,23},{16,0},{17... | collective-permute-start | bytes 1572872 | tf_op jit(solution)/shard_map/b_3/ppermute | solution.py:30
  2.1 12.7 %collective-permute-start.6 = (bf16[4,2,64,512]{3,2,1,0:T(8,128)(2,1)}, bf16[4,2,64,512]{3,2,1,0:T(8,128)(2,1)S(1)}, u32[]{:S(2)}, u32[]{:S(2)}) collective-permute-start(bf16[4,2,64,512]{3,2,1,0:T(8,128)(2,1)} %refs_16_.1), channel_id=1, source_target_pairs={{0,64},{1,65},{2,66},{3,67},{4,68},{5,69},{6,70},{7,71},{16,80},{1... | collective-permute-start | bytes 1572872 | tf_op jit(solution)/shard_map/b_x/ppermute | solution.py:30
  4.9 10.8 %collective-permute-start.3 = (bf16[4,2,32,1024]{3,2,1,0:T(8,128)(2,1)}, bf16[4,2,32,1024]{3,2,1,0:T(8,128)(2,1)S(1)}, u32[]{:S(2)}, u32[]{:S(2)}) collective-permute-start(bf16[4,2,32,1024]{3,2,1,0:T(8,128)(2,1)} %refs_0_.1), channel_id=1, source_target_pairs={{0,6},{1,3},{2,0},{3,5},{4,2},{5,7},{6,4},{7,1},{16,22},{17,19},{1... | collective-permute-start | bytes 1572872 | tf_op jit(solution)/shard_map/a_3/ppermute | solution.py:30
  6.5 16.3 %collective-permute-start.1 = (bf16[4,2,64,512]{3,2,1,0:T(8,128)(2,1)}, bf16[4,2,64,512]{3,2,1,0:T(8,128)(2,1)S(1)}, u32[]{:S(2)}, u32[]{:S(2)}) collective-permute-start(bf16[4,2,64,512]{3,2,1,0:T(8,128)(2,1)} %refs_16_.1), channel_id=1, source_target_pairs={{0,16},{1,49},{2,18},{3,51},{4,20},{5,53},{6,22},{7,55},{16,32},{1... | collective-permute-start | bytes 1572872 | tf_op jit(solution)/shard_map/b_1/ppermute | solution.py:30
  8.0 14.9 %collective-permute-start = (bf16[4,2,32,1024]{3,2,1,0:T(8,128)(2,1)}, bf16[4,2,32,1024]{3,2,1,0:T(8,128)(2,1)S(1)}, u32[]{:S(2)}, u32[]{:S(2)}) collective-permute-start(bf16[4,2,32,1024]{3,2,1,0:T(8,128)(2,1)} %refs_0_.1), channel_id=1, source_target_pairs={{0,2},{1,7},{2,4},{3,1},{4,6},{5,3},{6,0},{7,5},{16,18},{17,23},{1... | collective-permute-start | bytes 1572872 | tf_op jit(solution)/shard_map/a_1/ppermute | solution.py:30
  12.5 47.4 %copy-start = (bf16[4,2,64,512]{3,2,1,0:T(8,128)(2,1)}, bf16[4,2,64,512]{3,2,1,0:T(8,128)(2,1)S(1)}, u32[]{:S(2)}) copy-start(bf16[4,2,64,512]{3,2,1,0:T(8,128)(2,1)S(1)} %collective-permute-done.4.refs_19_) | copy-start | bytes 1572868
  12.5 15.0 %collective-permute-start.5 = (bf16[4,2,32,1024]{3,2,1,0:T(8,128)(2,1)}, bf16[4,2,32,1024]{3,2,1,0:T(8,128)(2,1)S(1)}, u32[]{:S(2)}, u32[]{:S(2)}) collective-permute-start(bf16[4,2,32,1024]{3,2,1,0:T(8,128)(2,1)} %refs_0_.1), channel_id=1, source_target_pairs={{0,8},{1,9},{2,10},{3,11},{4,12},{5,13},{6,14},{7,15},{16,24},{17,... | collective-permute-start | bytes 1572872 | tf_op jit(solution)/shard_map/a_x/ppermute | solution.py:30
  14.9 45.1 %copy-start.1 = (bf16[4,2,64,512]{3,2,1,0:T(8,128)(2,1)}, bf16[4,2,64,512]{3,2,1,0:T(8,128)(2,1)S(1)}, u32[]{:S(2)}) copy-start(bf16[4,2,64,512]{3,2,1,0:T(8,128)(2,1)S(1)} %collective-permute-done.6.refs_20_) | copy-start | bytes 1572868
  15.7 44.2 %copy-start.2 = (bf16[4,2,32,1024]{3,2,1,0:T(8,128)(2,1)}, bf16[4,2,32,1024]{3,2,1,0:T(8,128)(2,1)S(1)}, u32[]{:S(2)}) copy-start(bf16[4,2,32,1024]{3,2,1,0:T(8,128)(2,1)S(1)} %collective-permute-done.3.refs_3_) | copy-start | bytes 1572868
  15.7 13.3 %collective-permute-start.9 = (bf16[4,2,64,512]{3,2,1,0:T(8,128)(2,1)S(1)}, bf16[4,2,64,512]{3,2,1,0:T(8,128)(2,1)S(1)}, u32[]{:S(2)}, u32[]{:S(2)}) collective-permute-start(bf16[4,2,64,512]{3,2,1,0:T(8,128)(2,1)S(1)} %collective-permute-done.6.refs_20_), channel_id=1, source_target_pairs={{0,16},{1,49},{2,18},{3,51},{4,20},{5,53},{6,22},{7,55},{16,32},{1... | collective-permute-start | bytes 1572872 | tf_op jit(solution)/shard_map/b_x1/ppermute | solution.py:30
  17.4 11.6 %collective-permute-start.11 = (bf16[4,2,32,1024]{3,2,1,0:T(8,128)(2,1)S(1)}, bf16[4,2,32,1024]{3,2,1,0:T(8,128)(2,1)S(1)}, u32[]{:S(2)}, u32[]{:S(2)}) collective-permute-start(bf16[4,2,32,1024]{3,2,1,0:T(8,128)(2,1)S(1)} %collective-permute-done.3.refs_3_), channel_id=1, source_target_pairs={{0,1},{1,0},{2,3},{3,2},{4,5},{5,4},{6,7},{7,6},{16,17},{17,16},{1... | collective-permute-start | bytes 1572872 | tf_op jit(solution)/shard_map/other_3/ppermute | solution.py:30
  22.8 37.1 %copy-start.3 = (bf16[4,2,64,512]{3,2,1,0:T(8,128)(2,1)}, bf16[4,2,64,512]{3,2,1,0:T(8,128)(2,1)S(1)}, u32[]{:S(2)}) copy-start(bf16[4,2,64,512]{3,2,1,0:T(8,128)(2,1)S(1)} %collective-permute-done.1.refs_17_) | copy-start | bytes 1572868
  22.8 37.1 %copy-start.4 = (bf16[4,2,32,1024]{3,2,1,0:T(8,128)(2,1)}, bf16[4,2,32,1024]{3,2,1,0:T(8,128)(2,1)S(1)}, u32[]{:S(2)}) copy-start(bf16[4,2,32,1024]{3,2,1,0:T(8,128)(2,1)S(1)} %collective-permute-done.refs_1_) | copy-start | bytes 1572868
  22.9 9.5 %collective-permute-start.2 = (bf16[4,2,32,1024]{3,2,1,0:T(8,128)(2,1)S(1)}, bf16[4,2,32,1024]{3,2,1,0:T(8,128)(2,1)S(1)}, u32[]{:S(2)}, u32[]{:S(2)}) collective-permute-start(bf16[4,2,32,1024]{3,2,1,0:T(8,128)(2,1)S(1)} %collective-permute-done.refs_1_), channel_id=1, source_target_pairs={{0,2},{1,7},{2,4},{3,1},{4,6},{5,3},{6,0},{7,5},{16,18},{17,23},{1... | collective-permute-start | bytes 1572872 | tf_op jit(solution)/shard_map/a_2/ppermute | solution.py:30
  26.2 15.2 %collective-permute-start.7 = (bf16[4,2,64,512]{3,2,1,0:T(8,128)(2,1)S(1)}, bf16[4,2,64,512]{3,2,1,0:T(8,128)(2,1)S(1)}, u32[]{:S(2)}, u32[]{:S(2)}) collective-permute-start(bf16[4,2,64,512]{3,2,1,0:T(8,128)(2,1)S(1)} %collective-permute-done.6.refs_20_), channel_id=1, source_target_pairs={{0,48},{1,17},{2,50},{3,19},{4,52},{5,21},{6,54},{7,23},{16,0},{17... | collective-permute-start | bytes 1572872 | tf_op jit(solution)/shard_map/b_x3/ppermute | solution.py:30
  27.5 32.4 %copy-start.5 = (bf16[4,2,32,1024]{3,2,1,0:T(8,128)(2,1)}, bf16[4,2,32,1024]{3,2,1,0:T(8,128)(2,1)S(1)}, u32[]{:S(2)}) copy-start(bf16[4,2,32,1024]{3,2,1,0:T(8,128)(2,1)S(1)} %collective-permute-done.5.refs_4_) | copy-start | bytes 1572868
  27.5 14.1 %collective-permute-start.16 = (bf16[4,2,64,512]{3,2,1,0:T(8,128)(2,1)S(1)}, bf16[4,2,64,512]{3,2,1,0:T(8,128)(2,1)S(1)}, u32[]{:S(2)}, u32[]{:S(2)}) collective-permute-start(bf16[4,2,64,512]{3,2,1,0:T(8,128)(2,1)S(1)} %collective-permute-done.1.refs_17_), channel_id=1, source_target_pairs={{0,16},{1,49},{2,18},{3,51},{4,20},{5,53},{6,22},{7,55},{16,32},{1... | collective-permute-start | bytes 1572872 | tf_op jit(solution)/shard_map/b_2/ppermute | solution.py:30
  29.0 31.0 %copy-start.6 = (bf16[4,2,64,512]{3,2,1,0:T(8,128)(2,1)}, bf16[4,2,64,512]{3,2,1,0:T(8,128)(2,1)S(1)}, u32[]{:S(2)}) copy-start(bf16[4,2,64,512]{3,2,1,0:T(8,128)(2,1)S(1)} %collective-permute-done.9.refs_21_) | copy-start | bytes 1572868
  29.0 31.0 %copy-start.7 = (bf16[4,2,32,1024]{3,2,1,0:T(8,128)(2,1)}, bf16[4,2,32,1024]{3,2,1,0:T(8,128)(2,1)S(1)}, u32[]{:S(2)}) copy-start(bf16[4,2,32,1024]{3,2,1,0:T(8,128)(2,1)S(1)} %collective-permute-done.11.refs_11_) | copy-start | bytes 1572868
  29.0 15.2 %collective-permute-start.12 = (bf16[4,2,32,1024]{3,2,1,0:T(8,128)(2,1)S(1)}, bf16[4,2,32,1024]{3,2,1,0:T(8,128)(2,1)S(1)}, u32[]{:S(2)}, u32[]{:S(2)}) collective-permute-start(bf16[4,2,32,1024]{3,2,1,0:T(8,128)(2,1)S(1)} %collective-permute-done.5.refs_4_), channel_id=1, source_target_pairs={{0,6},{1,3},{2,0},{3,5},{4,2},{5,7},{6,4},{7,1},{16,22},{17,19},{1... | collective-permute-start | bytes 1572872 | tf_op jit(solution)/shard_map/a_x3/ppermute | solution.py:30
  32.4 27.6 %copy-start.8 = (bf16[4,2,32,1024]{3,2,1,0:T(8,128)(2,1)}, bf16[4,2,32,1024]{3,2,1,0:T(8,128)(2,1)S(1)}, u32[]{:S(2)}) copy-start(bf16[4,2,32,1024]{3,2,1,0:T(8,128)(2,1)S(1)} %collective-permute-done.2.refs_2_) | copy-start | bytes 1572868
  32.4 21.5 %collective-permute-start.10 = (bf16[4,2,32,1024]{3,2,1,0:T(8,128)(2,1)S(1)}, bf16[4,2,32,1024]{3,2,1,0:T(8,128)(2,1)S(1)}, u32[]{:S(2)}, u32[]{:S(2)}) collective-permute-start(bf16[4,2,32,1024]{3,2,1,0:T(8,128)(2,1)S(1)} %collective-permute-done.2.refs_2_), channel_id=1, source_target_pairs={{0,8},{1,9},{2,10},{3,11},{4,12},{5,13},{6,14},{7,15},{16,24},{17,... | collective-permute-start | bytes 1572872 | tf_op jit(solution)/shard_map/a_x2/ppermute | solution.py:30
  32.7 21.1 %collective-permute-start.13 = (bf16[4,2,64,512]{3,2,1,0:T(8,128)(2,1)S(1)}, bf16[4,2,64,512]{3,2,1,0:T(8,128)(2,1)S(1)}, u32[]{:S(2)}, u32[]{:S(2)}) collective-permute-start(bf16[4,2,64,512]{3,2,1,0:T(8,128)(2,1)S(1)} %collective-permute-done.9.refs_21_), channel_id=1, source_target_pairs={{0,16},{1,49},{2,18},{3,51},{4,20},{5,53},{6,22},{7,55},{16,32},{1... | collective-permute-start | bytes 1572872 | tf_op jit(solution)/shard_map/b_x2/ppermute | solution.py:30
  41.5 18.6 %copy-start.9 = (bf16[4,2,64,512]{3,2,1,0:T(8,128)(2,1)}, bf16[4,2,64,512]{3,2,1,0:T(8,128)(2,1)S(1)}, u32[]{:S(2)}) copy-start(bf16[4,2,64,512]{3,2,1,0:T(8,128)(2,1)S(1)} %collective-permute-done.7.refs_23_) | copy-start | bytes 1572868
  41.5 12.8 %collective-permute-start.8 = (bf16[4,2,32,1024]{3,2,1,0:T(8,128)(2,1)S(1)}, bf16[4,2,32,1024]{3,2,1,0:T(8,128)(2,1)S(1)}, u32[]{:S(2)}, u32[]{:S(2)}) collective-permute-start(bf16[4,2,32,1024]{3,2,1,0:T(8,128)(2,1)S(1)} %collective-permute-done.5.refs_4_), channel_id=1, source_target_pairs={{0,2},{1,7},{2,4},{3,1},{4,6},{5,3},{6,0},{7,5},{16,18},{17,23},{1... | collective-permute-start | bytes 1572872 | tf_op jit(solution)/shard_map/a_x1/ppermute | solution.py:30
  41.6 18.4 %copy-start.10 = (bf16[4,2,64,512]{3,2,1,0:T(8,128)(2,1)}, bf16[4,2,64,512]{3,2,1,0:T(8,128)(2,1)S(1)}, u32[]{:S(2)}) copy-start(bf16[4,2,64,512]{3,2,1,0:T(8,128)(2,1)S(1)} %collective-permute-done.16.refs_18_) | copy-start | bytes 1572868
  41.6 12.8 %collective-permute-start.17 = (bf16[4,2,32,1024]{3,2,1,0:T(8,128)(2,1)S(1)}, bf16[4,2,32,1024]{3,2,1,0:T(8,128)(2,1)S(1)}, u32[]{:S(2)}, u32[]{:S(2)}) collective-permute-start(bf16[4,2,32,1024]{3,2,1,0:T(8,128)(2,1)S(1)} %collective-permute-done.2.refs_2_), channel_id=1, source_target_pairs={{0,1},{1,0},{2,3},{3,2},{4,5},{5,4},{6,7},{7,6},{16,17},{17,16},{1... | collective-permute-start | bytes 1572872 | tf_op jit(solution)/shard_map/other_2/ppermute | solution.py:30
  44.2 15.9 %copy-start.11 = (bf16[4,2,32,1024]{3,2,1,0:T(8,128)(2,1)}, bf16[4,2,32,1024]{3,2,1,0:T(8,128)(2,1)S(1)}, u32[]{:S(2)}) copy-start(bf16[4,2,32,1024]{3,2,1,0:T(8,128)(2,1)S(1)} %collective-permute-done.12.refs_7_) | copy-start | bytes 1572868
  44.2 11.1 %collective-permute-start.15 = (bf16[4,2,32,1024]{3,2,1,0:T(8,128)(2,1)S(1)}, bf16[4,2,32,1024]{3,2,1,0:T(8,128)(2,1)S(1)}, u32[]{:S(2)}, u32[]{:S(2)}) collective-permute-start(bf16[4,2,32,1024]{3,2,1,0:T(8,128)(2,1)S(1)} %collective-permute-done.refs_1_), channel_id=1, source_target_pairs={{0,1},{1,0},{2,3},{3,2},{4,5},{5,4},{6,7},{7,6},{16,17},{17,16},{1... | collective-permute-start | bytes 1572872 | tf_op jit(solution)/shard_map/other_1/ppermute | solution.py:30
  53.8 6.3 %copy-start.13 = (bf16[4,2,64,512]{3,2,1,0:T(8,128)(2,1)}, bf16[4,2,64,512]{3,2,1,0:T(8,128)(2,1)S(1)}, u32[]{:S(2)}) copy-start(bf16[4,2,64,512]{3,2,1,0:T(8,128)(2,1)S(1)} %collective-permute-done.13.refs_22_) | copy-start | bytes 1572868
  53.8 3.2 %collective-permute-start.14 = (bf16[4,2,32,1024]{3,2,1,0:T(8,128)(2,1)}, bf16[4,2,32,1024]{3,2,1,0:T(8,128)(2,1)S(1)}, u32[]{:S(2)}, u32[]{:S(2)}) collective-permute-start(bf16[4,2,32,1024]{3,2,1,0:T(8,128)(2,1)} %refs_0_.1), channel_id=1, source_target_pairs={{0,1},{1,0},{2,3},{3,2},{4,5},{5,4},{6,7},{7,6},{16,17},{17,16},{1... | collective-permute-start | bytes 1572872 | tf_op jit(solution)/shard_map/other/ppermute | solution.py:30
  53.9 6.2 %copy-start.12 = (bf16[4,2,32,1024]{3,2,1,0:T(8,128)(2,1)}, bf16[4,2,32,1024]{3,2,1,0:T(8,128)(2,1)S(1)}, u32[]{:S(2)}) copy-start(bf16[4,2,32,1024]{3,2,1,0:T(8,128)(2,1)S(1)} %collective-permute-done.10.refs_6_) | copy-start | bytes 1572868
  53.9 2.9 %collective-permute-start.20 = (bf16[4,2,32,1024]{3,2,1,0:T(8,128)(2,1)S(1)}, bf16[4,2,32,1024]{3,2,1,0:T(8,128)(2,1)S(1)}, u32[]{:S(2)}, u32[]{:S(2)}) collective-permute-start(bf16[4,2,32,1024]{3,2,1,0:T(8,128)(2,1)S(1)} %collective-permute-done.10.refs_6_), channel_id=1, source_target_pairs={{0,1},{1,0},{2,3},{3,2},{4,5},{5,4},{6,7},{7,6},{16,17},{17,16},{1... | collective-permute-start | bytes 1572872 | tf_op jit(solution)/shard_map/other_x2/ppermute | solution.py:30
  54.3 5.8 %copy-start.14 = (bf16[4,2,32,1024]{3,2,1,0:T(8,128)(2,1)}, bf16[4,2,32,1024]{3,2,1,0:T(8,128)(2,1)S(1)}, u32[]{:S(2)}) copy-start(bf16[4,2,32,1024]{3,2,1,0:T(8,128)(2,1)S(1)} %collective-permute-done.8.refs_5_) | copy-start | bytes 1572868
  54.3 4.0 %collective-permute-start.19 = (bf16[4,2,32,1024]{3,2,1,0:T(8,128)(2,1)S(1)}, bf16[4,2,32,1024]{3,2,1,0:T(8,128)(2,1)S(1)}, u32[]{:S(2)}, u32[]{:S(2)}) collective-permute-start(bf16[4,2,32,1024]{3,2,1,0:T(8,128)(2,1)S(1)} %collective-permute-done.8.refs_5_), channel_id=1, source_target_pairs={{0,1},{1,0},{2,3},{3,2},{4,5},{5,4},{6,7},{7,6},{16,17},{17,16},{1... | collective-permute-start | bytes 1572872 | tf_op jit(solution)/shard_map/other_x1/ppermute | solution.py:30
  54.4 4.7 %copy-start.15 = (bf16[4,2,32,1024]{3,2,1,0:T(8,128)(2,1)}, bf16[4,2,32,1024]{3,2,1,0:T(8,128)(2,1)S(1)}, u32[]{:S(2)}) copy-start(bf16[4,2,32,1024]{3,2,1,0:T(8,128)(2,1)S(1)} %collective-permute-done.17.refs_10_) | copy-start | bytes 1572868
  54.4 4.7 %collective-permute-start.21 = (bf16[4,2,32,1024]{3,2,1,0:T(8,128)(2,1)S(1)}, bf16[4,2,32,1024]{3,2,1,0:T(8,128)(2,1)S(1)}, u32[]{:S(2)}, u32[]{:S(2)}) collective-permute-start(bf16[4,2,32,1024]{3,2,1,0:T(8,128)(2,1)S(1)} %collective-permute-done.12.refs_7_), channel_id=1, source_target_pairs={{0,1},{1,0},{2,3},{3,2},{4,5},{5,4},{6,7},{7,6},{16,17},{17,16},{1... | collective-permute-start | bytes 1572872 | tf_op jit(solution)/shard_map/other_x3/ppermute | solution.py:30
  55.3 3.8 %copy-start.16 = (bf16[4,2,32,1024]{3,2,1,0:T(8,128)(2,1)}, bf16[4,2,32,1024]{3,2,1,0:T(8,128)(2,1)S(1)}, u32[]{:S(2)}) copy-start(bf16[4,2,32,1024]{3,2,1,0:T(8,128)(2,1)S(1)} %collective-permute-done.15.refs_9_) | copy-start | bytes 1572868
  55.3 4.6 %collective-permute-start.18 = (bf16[4,2,32,1024]{3,2,1,0:T(8,128)(2,1)S(1)}, bf16[4,2,32,1024]{3,2,1,0:T(8,128)(2,1)}, u32[]{:S(2)}, u32[]{:S(2)}) collective-permute-start(bf16[4,2,32,1024]{3,2,1,0:T(8,128)(2,1)S(1)} %collective-permute-done.5.refs_4_), channel_id=1, source_target_pairs={{0,1},{1,0},{2,3},{3,2},{4,5},{5,4},{6,7},{7,6},{16,17},{17,16},{1... | collective-permute-start | bytes 1572872 | tf_op jit(solution)/shard_map/other_x/ppermute | solution.py:30
  56.8 2.3 %copy-start.18 = (bf16[4,2,32,1024]{3,2,1,0:T(8,128)(2,1)}, bf16[4,2,32,1024]{3,2,1,0:T(8,128)(2,1)S(1)}, u32[]{:S(2)}) copy-start(bf16[4,2,32,1024]{3,2,1,0:T(8,128)(2,1)S(1)} %collective-permute-done.20.refs_14_) | copy-start | bytes 1572868
  57.0 2.0 %copy-start.17 = (bf16[4,2,32,1024]{3,2,1,0:T(8,128)(2,1)}, bf16[4,2,32,1024]{3,2,1,0:T(8,128)(2,1)S(1)}, u32[]{:S(2)}) copy-start(bf16[4,2,32,1024]{3,2,1,0:T(8,128)(2,1)S(1)} %collective-permute-done.14.refs_8_) | copy-start | bytes 1572868
  58.3 0.8 %copy-start.19 = (bf16[4,2,32,1024]{3,2,1,0:T(8,128)(2,1)}, bf16[4,2,32,1024]{3,2,1,0:T(8,128)(2,1)S(1)}, u32[]{:S(2)}) copy-start(bf16[4,2,32,1024]{3,2,1,0:T(8,128)(2,1)S(1)} %collective-permute-done.19.refs_13_) | copy-start | bytes 1572868
  59.1 0.8 %copy-start.20 = (bf16[4,2,32,1024]{3,2,1,0:T(8,128)(2,1)}, bf16[4,2,32,1024]{3,2,1,0:T(8,128)(2,1)S(1)}, u32[]{:S(2)}) copy-start(bf16[4,2,32,1024]{3,2,1,0:T(8,128)(2,1)S(1)} %collective-permute-done.21.refs_15_) | copy-start | bytes 1572868

commit v9 on v8

--- a/solution.py
+++ b/solution.py
@@ -175,18 +175,18 @@
     b_x1 = send("b_x1", after(b_x, a_3), dy=1)
     a_2 = send("a_2", after(a_1, b_1), dz=1)
     b_x3 = send("b_x3", after(b_x, a_1), dy=-1)
-    b_2 = send("b_2", after(b_1, a_x), dy=1)
-    a_x3 = send("a_x3", after(a_x, other_3, b_x1), dz=-1)
+    a_x3 = send("a_x3", a_x, dz=-1)
+    b_2 = send("b_2", after(b_1, other_3), dy=1)
     a_x2 = send("a_x2", after(a_2, b_x1), flip_x=True)
     b_x2 = send("b_x2", after(b_x1, a_2), dy=1)
     a_x1 = send("a_x1", after(a_x, b_x3), dz=1)
+    other = swap("other", after(a, a_x3))
     other_2 = swap("other_2", after(a_2, b_2))
-    other_1 = swap("other_1", after(a_1, a_x3))
-    other_x2 = swap("other_x2", a_x2)
-    other = swap("other", after(a, b_x2))
+    other_1 = swap("other_1", after(a_1, a_x2))
+    other_x2 = swap("other_x2", after(a_x2, b_x2))
     other_x1 = swap("other_x1", a_x1)
+    other_x = swap("other_x", after(a_x, other))
     other_x3 = swap("other_x3", after(a_x3, other_2))
-    other_x = swap("other_x", after(a_x, other_1))
 
     a_parts = [a, a_1, a_2, a_3, a_x, a_x1, a_x2, a_x3]
     a_parts += [other, other_1, other_2, other_3, other_x, other_x1, other_x2, other_x3]

time: 72.1 us -> 66.6 us (0.924)
  starting transfers between devices: 41.6 us -> 37.4 us
  waiting for transfers between devices: 14.9 us -> 13.6 us
    ppermute x22, starting transfers between devices: 41.6 us -> 37.4 us  [moved(): return lax.ppermute(value, AXES, pairs)]
    ppermute x22, waiting for transfers between devices: 14.9 us -> 13.6 us  [moved(): return lax.ppermute(value, AXES, pairs)]
  transfers between devices with their start and end apart: 22 -> 22, of which waited for: 9 -> 8; matrix products, arithmetic and copies ran while one was open for 3% -> 4% of each run, Pallas kernels for 0% -> 0%
where the time goes in v9:
time: 66.6 us; the launch traced here: 66.5 us
  starting transfers between devices  37.4 us (56%)
  waiting for transfers between devices  13.6 us (20%)
  Pallas kernels  12 us (18%)
  other arithmetic  2.46 us (4%)
  local copies, waits for them, and re-layouts  0.87 us (1%)
    ppermute x22, starting transfers between devices, moved(): return lax.ppermute(value, AXES, pairs)  37.4 us
    ppermute x22, waiting for transfers between devices, moved(): return lax.ppermute(value, AXES, pairs)  13.6 us
    pallas_call x1, Pallas kernels, multiply(): pl.pallas_call(multiply_kernel, out_shape=jax.ShapeDtypeStruct((freqs, 2,...  12 us
  transfers between devices with their start and end apart: 22, of which 8 were waited for; matrix products, arithmetic and copies ran while one was open for 4% of the time, Pallas kernels for 0%

profile of v9, /device:TPU:1, one launch (start us, length us, event | category | flops | bytes accessed | tf_op | source)
XLA Modules:
  0.0 66.5 jit_solution(13308622303485500267)
XLA Ops:
  0.0 2.1 %collective-permute-start.4 = (bf16[4,2,64,512]{3,2,1,0:T(8,128)(2,1)}, bf16[4,2,64,512]{3,2,1,0:T(8,128)(2,1)S(1)}, u32[]{:S(2)}, u32[]{:S(2)}) collective-permute-start(bf16[4,2,64,512]{3,2,1,0:T(8,128)(2,1)} %refs_16_.1), channel_id=1, source_target_pairs={{0,48},{1,17},{2,50},{3,19},{4,52},{5,21},{6,54},{7,23},{16,0},{17... | collective-permute-start | bytes 1572872 | tf_op jit(solution)/shard_map/b_3/ppermute | solution.py:30
  2.1 2.7 %collective-permute-start.6 = (bf16[4,2,64,512]{3,2,1,0:T(8,128)(2,1)}, bf16[4,2,64,512]{3,2,1,0:T(8,128)(2,1)S(1)}, u32[]{:S(2)}, u32[]{:S(2)}) collective-permute-start(bf16[4,2,64,512]{3,2,1,0:T(8,128)(2,1)} %refs_16_.1), channel_id=1, source_target_pairs={{0,64},{1,65},{2,66},{3,67},{4,68},{5,69},{6,70},{7,71},{16,80},{1... | collective-permute-start | bytes 1572872 | tf_op jit(solution)/shard_map/b_x/ppermute | solution.py:30
  4.9 1.6 %collective-permute-start.3 = (bf16[4,2,32,1024]{3,2,1,0:T(8,128)(2,1)}, bf16[4,2,32,1024]{3,2,1,0:T(8,128)(2,1)S(1)}, u32[]{:S(2)}, u32[]{:S(2)}) collective-permute-start(bf16[4,2,32,1024]{3,2,1,0:T(8,128)(2,1)} %refs_0_.1), channel_id=1, source_target_pairs={{0,6},{1,3},{2,0},{3,5},{4,2},{5,7},{6,4},{7,1},{16,22},{17,19},{1... | collective-permute-start | bytes 1572872 | tf_op jit(solution)/shard_map/a_3/ppermute | solution.py:30
  6.5 1.4 %collective-permute-start.1 = (bf16[4,2,64,512]{3,2,1,0:T(8,128)(2,1)}, bf16[4,2,64,512]{3,2,1,0:T(8,128)(2,1)S(1)}, u32[]{:S(2)}, u32[]{:S(2)}) collective-permute-start(bf16[4,2,64,512]{3,2,1,0:T(8,128)(2,1)} %refs_16_.1), channel_id=1, source_target_pairs={{0,16},{1,49},{2,18},{3,51},{4,20},{5,53},{6,22},{7,55},{16,32},{1... | collective-permute-start | bytes 1572872 | tf_op jit(solution)/shard_map/b_1/ppermute | solution.py:30
  8.0 2.1 %collective-permute-start = (bf16[4,2,32,1024]{3,2,1,0:T(8,128)(2,1)}, bf16[4,2,32,1024]{3,2,1,0:T(8,128)(2,1)S(1)}, u32[]{:S(2)}, u32[]{:S(2)}) collective-permute-start(bf16[4,2,32,1024]{3,2,1,0:T(8,128)(2,1)} %refs_0_.1), channel_id=1, source_target_pairs={{0,2},{1,7},{2,4},{3,1},{4,6},{5,3},{6,0},{7,5},{16,18},{17,23},{1... | collective-permute-start | bytes 1572872 | tf_op jit(solution)/shard_map/a_1/ppermute | solution.py:30
  10.1 1.2 %fusion.1 = (s32[12]{0:T(128)}, s32[12]{0:T(128)S(1)}) fusion(pred[]{:T(512)S(6)} %eq.18, s32[]{:T(128)S(6)} %select_n.83, s32[]{:T(128)S(6)} %select_n.80, s32[12]{0:T(128)} %param.5), kind=kLoop, calls=%fused_computation.25 | loop fusion | flops 612 | bytes 153 | tf_op jit(solution)/shard_map/add | solution.py:149
  11.3 1.2 %broadcast_multiply_fusion = (s32[12]{0:T(128)}, s32[12]{0:T(128)}) fusion(s32[12]{0:T(128)} %param.5, s32[12]{0:T(128)S(1)} %get-tuple-element.36, s32[]{:T(128)S(6)} %select_n.75, s32[]{:T(128)S(6)} %select_n.73, s32[]{:T(128)S(6)} %select_n.71), kind=kLoop, calls=%fused_computation.29 | loop fusion | flops 684 | bytes 204 | tf_op jit(solution)/shard_map/mul | solution.py:150
  12.5 0.0 collective-permute-done.4.refs_19_
  12.5 0.3 collective-permute-start.5
  12.9 2.0 %collective-permute-done.6.refs_20_ = bf16[4,2,64,512]{3,2,1,0:T(8,128)(2,1)S(1)} collective-permute-done((bf16[4,2,64,512]{3,2,1,0:T(8,128)(2,1)}, bf16[4,2,64,512]{3,2,1,0:T(8,128)(2,1)S(1)}, u32[]{:S(2)}, u32[]{:S(2)}) %collective-permute-start.6) | collective-permute-done | bytes 524320 | tf_op jit(solution)/shard_map/b_x/ppermute | solution.py:30
  14.9 0.8 %collective-permute-done.3.refs_3_ = bf16[4,2,32,1024]{3,2,1,0:T(8,128)(2,1)S(1)} collective-permute-done((bf16[4,2,32,1024]{3,2,1,0:T(8,128)(2,1)}, bf16[4,2,32,1024]{3,2,1,0:T(8,128)(2,1)S(1)}, u32[]{:S(2)}, u32[]{:S(2)}) %collective-permute-start.3) | collective-permute-done | bytes 524320 | tf_op jit(solution)/shard_map/a_3/ppermute | solution.py:30
  15.7 6.8 %collective-permute-start.14 = (bf16[4,2,32,1024]{3,2,1,0:T(8,128)(2,1)S(1)}, bf16[4,2,32,1024]{3,2,1,0:T(8,128)(2,1)S(1)}, u32[]{:S(2)}, u32[]{:S(2)}) collective-permute-start(bf16[4,2,32,1024]{3,2,1,0:T(8,128)(2,1)S(1)} %collective-permute-done.3.refs_3_), channel_id=1, source_target_pairs={{0,1},{1,0},{2,3},{3,2},{4,5},{5,4},{6,7},{7,6},{16,17},{17,16},{1... | collective-permute-start | bytes 1572872 | tf_op jit(solution)/shard_map/other_3/ppermute | solution.py:30
  22.5 1.5 %collective-permute-start.9 = (bf16[4,2,64,512]{3,2,1,0:T(8,128)(2,1)S(1)}, bf16[4,2,64,512]{3,2,1,0:T(8,128)(2,1)S(1)}, u32[]{:S(2)}, u32[]{:S(2)}) collective-permute-start(bf16[4,2,64,512]{3,2,1,0:T(8,128)(2,1)S(1)} %collective-permute-done.6.refs_20_), channel_id=1, source_target_pairs={{0,16},{1,49},{2,18},{3,51},{4,20},{5,53},{6,22},{7,55},{16,32},{1... | collective-permute-start | bytes 1572872 | tf_op jit(solution)/shard_map/b_x1/ppermute | solution.py:30
  24.0 0.0 collective-permute-done.1.refs_17_
  24.0 0.0 collective-permute-done.refs_1_
  24.0 3.4 %collective-permute-start.2 = (bf16[4,2,32,1024]{3,2,1,0:T(8,128)(2,1)S(1)}, bf16[4,2,32,1024]{3,2,1,0:T(8,128)(2,1)S(1)}, u32[]{:S(2)}, u32[]{:S(2)}) collective-permute-start(bf16[4,2,32,1024]{3,2,1,0:T(8,128)(2,1)S(1)} %collective-permute-done.refs_1_), channel_id=1, source_target_pairs={{0,2},{1,7},{2,4},{3,1},{4,6},{5,3},{6,0},{7,5},{16,18},{17,23},{1... | collective-permute-start | bytes 1572872 | tf_op jit(solution)/shard_map/a_2/ppermute | solution.py:30
  27.4 0.0 collective-permute-start.7
  27.4 0.0 collective-permute-done.5.refs_4_
  27.4 0.4 collective-permute-start.11
  27.8 0.0 collective-permute-done.14.refs_11_
  27.8 2.4 %collective-permute-start.15 = (bf16[4,2,64,512]{3,2,1,0:T(8,128)(2,1)S(1)}, bf16[4,2,64,512]{3,2,1,0:T(8,128)(2,1)S(1)}, u32[]{:S(2)}, u32[]{:S(2)}) collective-permute-start(bf16[4,2,64,512]{3,2,1,0:T(8,128)(2,1)S(1)} %collective-permute-done.1.refs_17_), channel_id=1, source_target_pairs={{0,16},{1,49},{2,18},{3,51},{4,20},{5,53},{6,22},{7,55},{16,32},{1... | collective-permute-start | bytes 1572872 | tf_op jit(solution)/shard_map/b_2/ppermute | solution.py:30
  30.3 3.7 %collective-permute-done.9.refs_21_ = bf16[4,2,64,512]{3,2,1,0:T(8,128)(2,1)S(1)} collective-permute-done((bf16[4,2,64,512]{3,2,1,0:T(8,128)(2,1)S(1)}, bf16[4,2,64,512]{3,2,1,0:T(8,128)(2,1)S(1)}, u32[]{:S(2)}, u32[]{:S(2)}) %collective-permute-start.9) | collective-permute-done | bytes 524320 | tf_op jit(solution)/shard_map/b_x1/ppermute | solution.py:30
  33.9 0.0 collective-permute-done.2.refs_2_
  33.9 0.4 collective-permute-start.10
  34.3 1.2 %collective-permute-start.19 = (bf16[4,2,64,512]{3,2,1,0:T(8,128)(2,1)S(1)}, bf16[4,2,64,512]{3,2,1,0:T(8,128)(2,1)S(1)}, u32[]{:S(2)}, u32[]{:S(2)}) collective-permute-start(bf16[4,2,64,512]{3,2,1,0:T(8,128)(2,1)S(1)} %collective-permute-done.9.refs_21_), channel_id=1, source_target_pairs={{0,16},{1,49},{2,18},{3,51},{4,20},{5,53},{6,22},{7,55},{16,32},{1... | collective-permute-start | bytes 1572872 | tf_op jit(solution)/shard_map/b_x2/ppermute | solution.py:30
  35.5 2.8 %collective-permute-done.7.refs_23_ = bf16[4,2,64,512]{3,2,1,0:T(8,128)(2,1)S(1)} collective-permute-done((bf16[4,2,64,512]{3,2,1,0:T(8,128)(2,1)S(1)}, bf16[4,2,64,512]{3,2,1,0:T(8,128)(2,1)S(1)}, u32[]{:S(2)}, u32[]{:S(2)}) %collective-permute-start.7) | collective-permute-done | bytes 524320 | tf_op jit(solution)/shard_map/b_x3/ppermute | solution.py:30
  38.3 4.3 %collective-permute-start.8 = (bf16[4,2,32,1024]{3,2,1,0:T(8,128)(2,1)S(1)}, bf16[4,2,32,1024]{3,2,1,0:T(8,128)(2,1)S(1)}, u32[]{:S(2)}, u32[]{:S(2)}) collective-permute-start(bf16[4,2,32,1024]{3,2,1,0:T(8,128)(2,1)S(1)} %collective-permute-done.5.refs_4_), channel_id=1, source_target_pairs={{0,2},{1,7},{2,4},{3,1},{4,6},{5,3},{6,0},{7,5},{16,18},{17,23},{1... | collective-permute-start | bytes 1572872 | tf_op jit(solution)/shard_map/a_x1/ppermute | solution.py:30
  42.6 0.0 collective-permute-done.11.refs_7_
  42.7 0.0 collective-permute-start.12
  42.7 0.0 collective-permute-done.15.refs_18_
  42.7 1.5 %collective-permute-start.16 = (bf16[4,2,32,1024]{3,2,1,0:T(8,128)(2,1)S(1)}, bf16[4,2,32,1024]{3,2,1,0:T(8,128)(2,1)S(1)}, u32[]{:S(2)}, u32[]{:S(2)}) collective-permute-start(bf16[4,2,32,1024]{3,2,1,0:T(8,128)(2,1)S(1)} %collective-permute-done.2.refs_2_), channel_id=1, source_target_pairs={{0,1},{1,0},{2,3},{3,2},{4,5},{5,4},{6,7},{7,6},{16,17},{17,16},{1... | collective-permute-start | bytes 1572872 | tf_op jit(solution)/shard_map/other_2/ppermute | solution.py:30
  44.2 1.8 %collective-permute-done.10.refs_6_ = bf16[4,2,32,1024]{3,2,1,0:T(8,128)(2,1)S(1)} collective-permute-done((bf16[4,2,32,1024]{3,2,1,0:T(8,128)(2,1)S(1)}, bf16[4,2,32,1024]{3,2,1,0:T(8,128)(2,1)S(1)}, u32[]{:S(2)}, u32[]{:S(2)}) %collective-permute-start.10) | collective-permute-done | bytes 524320 | tf_op jit(solution)/shard_map/a_x2/ppermute | solution.py:30
  45.9 2.4 %collective-permute-start.13 = (bf16[4,2,32,1024]{3,2,1,0:T(8,128)(2,1)S(1)}, bf16[4,2,32,1024]{3,2,1,0:T(8,128)(2,1)S(1)}, u32[]{:S(2)}, u32[]{:S(2)}) collective-permute-start(bf16[4,2,32,1024]{3,2,1,0:T(8,128)(2,1)S(1)} %collective-permute-done.refs_1_), channel_id=1, source_target_pairs={{0,1},{1,0},{2,3},{3,2},{4,5},{5,4},{6,7},{7,6},{16,17},{17,16},{1... | collective-permute-start | bytes 1572872 | tf_op jit(solution)/shard_map/other_1/ppermute | solution.py:30
  48.4 0.0 collective-permute-done.19.refs_22_
  48.4 1.4 %collective-permute-start.20 = (bf16[4,2,32,1024]{3,2,1,0:T(8,128)(2,1)S(1)}, bf16[4,2,32,1024]{3,2,1,0:T(8,128)(2,1)S(1)}, u32[]{:S(2)}, u32[]{:S(2)}) collective-permute-start(bf16[4,2,32,1024]{3,2,1,0:T(8,128)(2,1)S(1)} %collective-permute-done.10.refs_6_), channel_id=1, source_target_pairs={{0,1},{1,0},{2,3},{3,2},{4,5},{5,4},{6,7},{7,6},{16,17},{17,16},{1... | collective-permute-start | bytes 1572872 | tf_op jit(solution)/shard_map/other_x2/ppermute | solution.py:30
  49.8 0.0 collective-permute-done.8.refs_5_
  49.8 0.7 %collective-permute-start.18 = (bf16[4,2,32,1024]{3,2,1,0:T(8,128)(2,1)S(1)}, bf16[4,2,32,1024]{3,2,1,0:T(8,128)(2,1)S(1)}, u32[]{:S(2)}, u32[]{:S(2)}) collective-permute-start(bf16[4,2,32,1024]{3,2,1,0:T(8,128)(2,1)S(1)} %collective-permute-done.8.refs_5_), channel_id=1, source_target_pairs={{0,1},{1,0},{2,3},{3,2},{4,5},{5,4},{6,7},{7,6},{16,17},{17,16},{1... | collective-permute-start | bytes 1572872 | tf_op jit(solution)/shard_map/other_x1/ppermute | solution.py:30
  50.5 0.0 collective-permute-done.12.refs_8_
  50.5 0.1 collective-permute-start.17
  50.6 0.0 collective-permute-done.16.refs_10_
  50.6 0.4 collective-permute-start.21
  51.0 0.0 collective-permute-done.13.refs_9_
  51.1 0.3 collective-permute-done.20.refs_14_
  51.3 0.7 %collective-permute-done.18.refs_13_ = bf16[4,2,32,1024]{3,2,1,0:T(8,128)(2,1)S(1)} collective-permute-done((bf16[4,2,32,1024]{3,2,1,0:T(8,128)(2,1)S(1)}, bf16[4,2,32,1024]{3,2,1,0:T(8,128)(2,1)S(1)}, u32[]{:S(2)}, u32[]{:S(2)}) %collective-permute-start.18) | collective-permute-done | bytes 524320 | tf_op jit(solution)/shard_map/other_x1/ppermute | solution.py:30
  52.1 1.5 %collective-permute-done.17.refs_12_ = bf16[4,2,32,1024]{3,2,1,0:T(8,128)(2,1)S(1)} collective-permute-done((bf16[4,2,32,1024]{3,2,1,0:T(8,128)(2,1)S(1)}, bf16[4,2,32,1024]{3,2,1,0:T(8,128)(2,1)S(1)}, u32[]{:S(2)}, u32[]{:S(2)}) %collective-permute-start.17) | collective-permute-done | bytes 524320 | tf_op jit(solution)/shard_map/other_x/ppermute | solution.py:30
  53.6 0.8 %copy-done.20 = bf16[4,2,32,1024]{3,2,1,0:T(8,128)(2,1)} copy-done((bf16[4,2,32,1024]{3,2,1,0:T(8,128)(2,1)}, bf16[4,2,32,1024]{3,2,1,0:T(8,128)(2,1)S(1)}, u32[]{:S(2)}) %copy-start.20) | copy-done | bytes 524312
  54.4 0.0 collective-permute-done.21.refs_15_
  54.5 12.0 %shard_map.37 = bf16[4,2,1024,512]{3,2,1,0:T(8,128)(2,1)} custom-call(s32[12]{0:T(128)} %get-tuple-element.38.a_where, s32[12]{0:T(128)} %get-tuple-element.35.b_where, s32[12]{0:T(128)} %get-tuple-element.37.b_row, bf16[4,2,32,1024]{3,2,1,0:T(8,128)(2,1)} %refs_0_.1, bf16[4,2,32,1024]{3,2,1,0:T(8,128)(2,1)} %copy-done.4, ...), custom_call_target="tpu_custom_call" | custom-call | flops 6442450944 | bytes 20971520 | tf_op jit(solution)/shard_map/pallas_call | solution.py:114
  (41 shorter events, 0.1 us)
Async XLA Ops:
  0.0 12.5 %collective-permute-start.4 = (bf16[4,2,64,512]{3,2,1,0:T(8,128)(2,1)}, bf16[4,2,64,512]{3,2,1,0:T(8,128)(2,1)S(1)}, u32[]{:S(2)}, u32[]{:S(2)}) collective-permute-start(bf16[4,2,64,512]{3,2,1,0:T(8,128)(2,1)} %refs_16_.1), channel_id=1, source_target_pairs={{0,48},{1,17},{2,50},{3,19},{4,52},{5,21},{6,54},{7,23},{16,0},{17... | collective-permute-start | bytes 1572872 | tf_op jit(solution)/shard_map/b_3/ppermute | solution.py:30
  2.1 12.7 %collective-permute-start.6 = (bf16[4,2,64,512]{3,2,1,0:T(8,128)(2,1)}, bf16[4,2,64,512]{3,2,1,0:T(8,128)(2,1)S(1)}, u32[]{:S(2)}, u32[]{:S(2)}) collective-permute-start(bf16[4,2,64,512]{3,2,1,0:T(8,128)(2,1)} %refs_16_.1), channel_id=1, source_target_pairs={{0,64},{1,65},{2,66},{3,67},{4,68},{5,69},{6,70},{7,71},{16,80},{1... | collective-permute-start | bytes 1572872 | tf_op jit(solution)/shard_map/b_x/ppermute | solution.py:30
  4.9 10.8 %collective-permute-start.3 = (bf16[4,2,32,1024]{3,2,1,0:T(8,128)(2,1)}, bf16[4,2,32,1024]{3,2,1,0:T(8,128)(2,1)S(1)}, u32[]{:S(2)}, u32[]{:S(2)}) collective-permute-start(bf16[4,2,32,1024]{3,2,1,0:T(8,128)(2,1)} %refs_0_.1), channel_id=1, source_target_pairs={{0,6},{1,3},{2,0},{3,5},{4,2},{5,7},{6,4},{7,1},{16,22},{17,19},{1... | collective-permute-start | bytes 1572872 | tf_op jit(solution)/shard_map/a_3/ppermute | solution.py:30
  6.5 17.5 %collective-permute-start.1 = (bf16[4,2,64,512]{3,2,1,0:T(8,128)(2,1)}, bf16[4,2,64,512]{3,2,1,0:T(8,128)(2,1)S(1)}, u32[]{:S(2)}, u32[]{:S(2)}) collective-permute-start(bf16[4,2,64,512]{3,2,1,0:T(8,128)(2,1)} %refs_16_.1), channel_id=1, source_target_pairs={{0,16},{1,49},{2,18},{3,51},{4,20},{5,53},{6,22},{7,55},{16,32},{1... | collective-permute-start | bytes 1572872 | tf_op jit(solution)/shard_map/b_1/ppermute | solution.py:30
  8.0 16.1 %collective-permute-start = (bf16[4,2,32,1024]{3,2,1,0:T(8,128)(2,1)}, bf16[4,2,32,1024]{3,2,1,0:T(8,128)(2,1)S(1)}, u32[]{:S(2)}, u32[]{:S(2)}) collective-permute-start(bf16[4,2,32,1024]{3,2,1,0:T(8,128)(2,1)} %refs_0_.1), channel_id=1, source_target_pairs={{0,2},{1,7},{2,4},{3,1},{4,6},{5,3},{6,0},{7,5},{16,18},{17,23},{1... | collective-permute-start | bytes 1572872 | tf_op jit(solution)/shard_map/a_1/ppermute | solution.py:30
  12.5 41.9 %copy-start = (bf16[4,2,64,512]{3,2,1,0:T(8,128)(2,1)}, bf16[4,2,64,512]{3,2,1,0:T(8,128)(2,1)S(1)}, u32[]{:S(2)}) copy-start(bf16[4,2,64,512]{3,2,1,0:T(8,128)(2,1)S(1)} %collective-permute-done.4.refs_19_) | copy-start | bytes 1572868
  12.5 14.9 %collective-permute-start.5 = (bf16[4,2,32,1024]{3,2,1,0:T(8,128)(2,1)}, bf16[4,2,32,1024]{3,2,1,0:T(8,128)(2,1)S(1)}, u32[]{:S(2)}, u32[]{:S(2)}) collective-permute-start(bf16[4,2,32,1024]{3,2,1,0:T(8,128)(2,1)} %refs_0_.1), channel_id=1, source_target_pairs={{0,8},{1,9},{2,10},{3,11},{4,12},{5,13},{6,14},{7,15},{16,24},{17,... | collective-permute-start | bytes 1572872 | tf_op jit(solution)/shard_map/a_x/ppermute | solution.py:30
  14.9 39.5 %copy-start.1 = (bf16[4,2,64,512]{3,2,1,0:T(8,128)(2,1)}, bf16[4,2,64,512]{3,2,1,0:T(8,128)(2,1)S(1)}, u32[]{:S(2)}) copy-start(bf16[4,2,64,512]{3,2,1,0:T(8,128)(2,1)S(1)} %collective-permute-done.6.refs_20_) | copy-start | bytes 1572868
  15.7 38.7 %copy-start.2 = (bf16[4,2,32,1024]{3,2,1,0:T(8,128)(2,1)}, bf16[4,2,32,1024]{3,2,1,0:T(8,128)(2,1)S(1)}, u32[]{:S(2)}) copy-start(bf16[4,2,32,1024]{3,2,1,0:T(8,128)(2,1)S(1)} %collective-permute-done.3.refs_3_) | copy-start | bytes 1572868
  15.7 12.1 %collective-permute-start.14 = (bf16[4,2,32,1024]{3,2,1,0:T(8,128)(2,1)S(1)}, bf16[4,2,32,1024]{3,2,1,0:T(8,128)(2,1)S(1)}, u32[]{:S(2)}, u32[]{:S(2)}) collective-permute-start(bf16[4,2,32,1024]{3,2,1,0:T(8,128)(2,1)S(1)} %collective-permute-done.3.refs_3_), channel_id=1, source_target_pairs={{0,1},{1,0},{2,3},{3,2},{4,5},{5,4},{6,7},{7,6},{16,17},{17,16},{1... | collective-permute-start | bytes 1572872 | tf_op jit(solution)/shard_map/other_3/ppermute | solution.py:30
  22.5 11.4 %collective-permute-start.9 = (bf16[4,2,64,512]{3,2,1,0:T(8,128)(2,1)S(1)}, bf16[4,2,64,512]{3,2,1,0:T(8,128)(2,1)S(1)}, u32[]{:S(2)}, u32[]{:S(2)}) collective-permute-start(bf16[4,2,64,512]{3,2,1,0:T(8,128)(2,1)S(1)} %collective-permute-done.6.refs_20_), channel_id=1, source_target_pairs={{0,16},{1,49},{2,18},{3,51},{4,20},{5,53},{6,22},{7,55},{16,32},{1... | collective-permute-start | bytes 1572872 | tf_op jit(solution)/shard_map/b_x1/ppermute | solution.py:30
  24.0 30.4 %copy-start.3 = (bf16[4,2,64,512]{3,2,1,0:T(8,128)(2,1)}, bf16[4,2,64,512]{3,2,1,0:T(8,128)(2,1)S(1)}, u32[]{:S(2)}) copy-start(bf16[4,2,64,512]{3,2,1,0:T(8,128)(2,1)S(1)} %collective-permute-done.1.refs_17_) | copy-start | bytes 1572868
  24.0 30.4 %copy-start.4 = (bf16[4,2,32,1024]{3,2,1,0:T(8,128)(2,1)}, bf16[4,2,32,1024]{3,2,1,0:T(8,128)(2,1)S(1)}, u32[]{:S(2)}) copy-start(bf16[4,2,32,1024]{3,2,1,0:T(8,128)(2,1)S(1)} %collective-permute-done.refs_1_) | copy-start | bytes 1572868
  24.0 9.9 %collective-permute-start.2 = (bf16[4,2,32,1024]{3,2,1,0:T(8,128)(2,1)S(1)}, bf16[4,2,32,1024]{3,2,1,0:T(8,128)(2,1)S(1)}, u32[]{:S(2)}, u32[]{:S(2)}) collective-permute-start(bf16[4,2,32,1024]{3,2,1,0:T(8,128)(2,1)S(1)} %collective-permute-done.refs_1_), channel_id=1, source_target_pairs={{0,2},{1,7},{2,4},{3,1},{4,6},{5,3},{6,0},{7,5},{16,18},{17,23},{1... | collective-permute-start | bytes 1572872 | tf_op jit(solution)/shard_map/a_2/ppermute | solution.py:30
  27.4 10.9 %collective-permute-start.7 = (bf16[4,2,64,512]{3,2,1,0:T(8,128)(2,1)S(1)}, bf16[4,2,64,512]{3,2,1,0:T(8,128)(2,1)S(1)}, u32[]{:S(2)}, u32[]{:S(2)}) collective-permute-start(bf16[4,2,64,512]{3,2,1,0:T(8,128)(2,1)S(1)} %collective-permute-done.6.refs_20_), channel_id=1, source_target_pairs={{0,48},{1,17},{2,50},{3,19},{4,52},{5,21},{6,54},{7,23},{16,0},{17... | collective-permute-start | bytes 1572872 | tf_op jit(solution)/shard_map/b_x3/ppermute | solution.py:30
  27.4 27.0 %copy-start.5 = (bf16[4,2,32,1024]{3,2,1,0:T(8,128)(2,1)}, bf16[4,2,32,1024]{3,2,1,0:T(8,128)(2,1)S(1)}, u32[]{:S(2)}) copy-start(bf16[4,2,32,1024]{3,2,1,0:T(8,128)(2,1)S(1)} %collective-permute-done.5.refs_4_) | copy-start | bytes 1572868
  27.4 15.2 %collective-permute-start.11 = (bf16[4,2,32,1024]{3,2,1,0:T(8,128)(2,1)S(1)}, bf16[4,2,32,1024]{3,2,1,0:T(8,128)(2,1)S(1)}, u32[]{:S(2)}, u32[]{:S(2)}) collective-permute-start(bf16[4,2,32,1024]{3,2,1,0:T(8,128)(2,1)S(1)} %collective-permute-done.5.refs_4_), channel_id=1, source_target_pairs={{0,6},{1,3},{2,0},{3,5},{4,2},{5,7},{6,4},{7,1},{16,22},{17,19},{1... | collective-permute-start | bytes 1572872 | tf_op jit(solution)/shard_map/a_x3/ppermute | solution.py:30
  27.8 26.6 %copy-start.6 = (bf16[4,2,32,1024]{3,2,1,0:T(8,128)(2,1)}, bf16[4,2,32,1024]{3,2,1,0:T(8,128)(2,1)S(1)}, u32[]{:S(2)}) copy-start(bf16[4,2,32,1024]{3,2,1,0:T(8,128)(2,1)S(1)} %collective-permute-done.14.refs_11_) | copy-start | bytes 1572868
  27.8 14.8 %collective-permute-start.15 = (bf16[4,2,64,512]{3,2,1,0:T(8,128)(2,1)S(1)}, bf16[4,2,64,512]{3,2,1,0:T(8,128)(2,1)S(1)}, u32[]{:S(2)}, u32[]{:S(2)}) collective-permute-start(bf16[4,2,64,512]{3,2,1,0:T(8,128)(2,1)S(1)} %collective-permute-done.1.refs_17_), channel_id=1, source_target_pairs={{0,16},{1,49},{2,18},{3,51},{4,20},{5,53},{6,22},{7,55},{16,32},{1... | collective-permute-start | bytes 1572872 | tf_op jit(solution)/shard_map/b_2/ppermute | solution.py:30
  33.9 20.5 %copy-start.7 = (bf16[4,2,64,512]{3,2,1,0:T(8,128)(2,1)}, bf16[4,2,64,512]{3,2,1,0:T(8,128)(2,1)S(1)}, u32[]{:S(2)}) copy-start(bf16[4,2,64,512]{3,2,1,0:T(8,128)(2,1)S(1)} %collective-permute-done.9.refs_21_) | copy-start | bytes 1572868
  33.9 20.5 %copy-start.8 = (bf16[4,2,32,1024]{3,2,1,0:T(8,128)(2,1)}, bf16[4,2,32,1024]{3,2,1,0:T(8,128)(2,1)S(1)}, u32[]{:S(2)}) copy-start(bf16[4,2,32,1024]{3,2,1,0:T(8,128)(2,1)S(1)} %collective-permute-done.2.refs_2_) | copy-start | bytes 1572868
  33.9 12.0 %collective-permute-start.10 = (bf16[4,2,32,1024]{3,2,1,0:T(8,128)(2,1)S(1)}, bf16[4,2,32,1024]{3,2,1,0:T(8,128)(2,1)S(1)}, u32[]{:S(2)}, u32[]{:S(2)}) collective-permute-start(bf16[4,2,32,1024]{3,2,1,0:T(8,128)(2,1)S(1)} %collective-permute-done.2.refs_2_), channel_id=1, source_target_pairs={{0,8},{1,9},{2,10},{3,11},{4,12},{5,13},{6,14},{7,15},{16,24},{17,... | collective-permute-start | bytes 1572872 | tf_op jit(solution)/shard_map/a_x2/ppermute | solution.py:30
  34.3 14.0 %collective-permute-start.19 = (bf16[4,2,64,512]{3,2,1,0:T(8,128)(2,1)S(1)}, bf16[4,2,64,512]{3,2,1,0:T(8,128)(2,1)S(1)}, u32[]{:S(2)}, u32[]{:S(2)}) collective-permute-start(bf16[4,2,64,512]{3,2,1,0:T(8,128)(2,1)S(1)} %collective-permute-done.9.refs_21_), channel_id=1, source_target_pairs={{0,16},{1,49},{2,18},{3,51},{4,20},{5,53},{6,22},{7,55},{16,32},{1... | collective-permute-start | bytes 1572872 | tf_op jit(solution)/shard_map/b_x2/ppermute | solution.py:30
  38.3 16.2 %copy-start.9 = (bf16[4,2,64,512]{3,2,1,0:T(8,128)(2,1)}, bf16[4,2,64,512]{3,2,1,0:T(8,128)(2,1)S(1)}, u32[]{:S(2)}) copy-start(bf16[4,2,64,512]{3,2,1,0:T(8,128)(2,1)S(1)} %collective-permute-done.7.refs_23_) | copy-start | bytes 1572868
  38.3 11.5 %collective-permute-start.8 = (bf16[4,2,32,1024]{3,2,1,0:T(8,128)(2,1)S(1)}, bf16[4,2,32,1024]{3,2,1,0:T(8,128)(2,1)S(1)}, u32[]{:S(2)}, u32[]{:S(2)}) collective-permute-start(bf16[4,2,32,1024]{3,2,1,0:T(8,128)(2,1)S(1)} %collective-permute-done.5.refs_4_), channel_id=1, source_target_pairs={{0,2},{1,7},{2,4},{3,1},{4,6},{5,3},{6,0},{7,5},{16,18},{17,23},{1... | collective-permute-start | bytes 1572872 | tf_op jit(solution)/shard_map/a_x1/ppermute | solution.py:30
  42.7 11.8 %copy-start.10 = (bf16[4,2,32,1024]{3,2,1,0:T(8,128)(2,1)}, bf16[4,2,32,1024]{3,2,1,0:T(8,128)(2,1)S(1)}, u32[]{:S(2)}) copy-start(bf16[4,2,32,1024]{3,2,1,0:T(8,128)(2,1)S(1)} %collective-permute-done.11.refs_7_) | copy-start | bytes 1572868
  42.7 7.9 %collective-permute-start.12 = (bf16[4,2,32,1024]{3,2,1,0:T(8,128)(2,1)}, bf16[4,2,32,1024]{3,2,1,0:T(8,128)(2,1)S(1)}, u32[]{:S(2)}, u32[]{:S(2)}) collective-permute-start(bf16[4,2,32,1024]{3,2,1,0:T(8,128)(2,1)} %refs_0_.1), channel_id=1, source_target_pairs={{0,1},{1,0},{2,3},{3,2},{4,5},{5,4},{6,7},{7,6},{16,17},{17,16},{1... | collective-permute-start | bytes 1572872 | tf_op jit(solution)/shard_map/other/ppermute | solution.py:30
  42.7 11.8 %copy-start.11 = (bf16[4,2,64,512]{3,2,1,0:T(8,128)(2,1)}, bf16[4,2,64,512]{3,2,1,0:T(8,128)(2,1)S(1)}, u32[]{:S(2)}) copy-start(bf16[4,2,64,512]{3,2,1,0:T(8,128)(2,1)S(1)} %collective-permute-done.15.refs_18_) | copy-start | bytes 1572868
  42.7 7.9 %collective-permute-start.16 = (bf16[4,2,32,1024]{3,2,1,0:T(8,128)(2,1)S(1)}, bf16[4,2,32,1024]{3,2,1,0:T(8,128)(2,1)S(1)}, u32[]{:S(2)}, u32[]{:S(2)}) collective-permute-start(bf16[4,2,32,1024]{3,2,1,0:T(8,128)(2,1)S(1)} %collective-permute-done.2.refs_2_), channel_id=1, source_target_pairs={{0,1},{1,0},{2,3},{3,2},{4,5},{5,4},{6,7},{7,6},{16,17},{17,16},{1... | collective-permute-start | bytes 1572872 | tf_op jit(solution)/shard_map/other_2/ppermute | solution.py:30
  45.9 8.6 %copy-start.12 = (bf16[4,2,32,1024]{3,2,1,0:T(8,128)(2,1)}, bf16[4,2,32,1024]{3,2,1,0:T(8,128)(2,1)S(1)}, u32[]{:S(2)}) copy-start(bf16[4,2,32,1024]{3,2,1,0:T(8,128)(2,1)S(1)} %collective-permute-done.10.refs_6_) | copy-start | bytes 1572868
  45.9 5.1 %collective-permute-start.13 = (bf16[4,2,32,1024]{3,2,1,0:T(8,128)(2,1)S(1)}, bf16[4,2,32,1024]{3,2,1,0:T(8,128)(2,1)S(1)}, u32[]{:S(2)}, u32[]{:S(2)}) collective-permute-start(bf16[4,2,32,1024]{3,2,1,0:T(8,128)(2,1)S(1)} %collective-permute-done.refs_1_), channel_id=1, source_target_pairs={{0,1},{1,0},{2,3},{3,2},{4,5},{5,4},{6,7},{7,6},{16,17},{17,16},{1... | collective-permute-start | bytes 1572872 | tf_op jit(solution)/shard_map/other_1/ppermute | solution.py:30
  48.4 6.2 %copy-start.13 = (bf16[4,2,64,512]{3,2,1,0:T(8,128)(2,1)}, bf16[4,2,64,512]{3,2,1,0:T(8,128)(2,1)S(1)}, u32[]{:S(2)}) copy-start(bf16[4,2,64,512]{3,2,1,0:T(8,128)(2,1)S(1)} %collective-permute-done.19.refs_22_) | copy-start | bytes 1572868
  48.4 3.0 %collective-permute-start.20 = (bf16[4,2,32,1024]{3,2,1,0:T(8,128)(2,1)S(1)}, bf16[4,2,32,1024]{3,2,1,0:T(8,128)(2,1)S(1)}, u32[]{:S(2)}, u32[]{:S(2)}) collective-permute-start(bf16[4,2,32,1024]{3,2,1,0:T(8,128)(2,1)S(1)} %collective-permute-done.10.refs_6_), channel_id=1, source_target_pairs={{0,1},{1,0},{2,3},{3,2},{4,5},{5,4},{6,7},{7,6},{16,17},{17,16},{1... | collective-permute-start | bytes 1572872 | tf_op jit(solution)/shard_map/other_x2/ppermute | solution.py:30
  49.8 4.7 %copy-start.14 = (bf16[4,2,32,1024]{3,2,1,0:T(8,128)(2,1)}, bf16[4,2,32,1024]{3,2,1,0:T(8,128)(2,1)S(1)}, u32[]{:S(2)}) copy-start(bf16[4,2,32,1024]{3,2,1,0:T(8,128)(2,1)S(1)} %collective-permute-done.8.refs_5_) | copy-start | bytes 1572868
  49.8 2.3 %collective-permute-start.18 = (bf16[4,2,32,1024]{3,2,1,0:T(8,128)(2,1)S(1)}, bf16[4,2,32,1024]{3,2,1,0:T(8,128)(2,1)S(1)}, u32[]{:S(2)}, u32[]{:S(2)}) collective-permute-start(bf16[4,2,32,1024]{3,2,1,0:T(8,128)(2,1)S(1)} %collective-permute-done.8.refs_5_), channel_id=1, source_target_pairs={{0,1},{1,0},{2,3},{3,2},{4,5},{5,4},{6,7},{7,6},{16,17},{17,16},{1... | collective-permute-start | bytes 1572872 | tf_op jit(solution)/shard_map/other_x1/ppermute | solution.py:30
  50.5 3.0 %copy-start.15 = (bf16[4,2,32,1024]{3,2,1,0:T(8,128)(2,1)}, bf16[4,2,32,1024]{3,2,1,0:T(8,128)(2,1)S(1)}, u32[]{:S(2)}) copy-start(bf16[4,2,32,1024]{3,2,1,0:T(8,128)(2,1)S(1)} %collective-permute-done.12.refs_8_) | copy-start | bytes 1572868
  50.5 3.0 %collective-permute-start.17 = (bf16[4,2,32,1024]{3,2,1,0:T(8,128)(2,1)S(1)}, bf16[4,2,32,1024]{3,2,1,0:T(8,128)(2,1)S(1)}, u32[]{:S(2)}, u32[]{:S(2)}) collective-permute-start(bf16[4,2,32,1024]{3,2,1,0:T(8,128)(2,1)S(1)} %collective-permute-done.5.refs_4_), channel_id=1, source_target_pairs={{0,1},{1,0},{2,3},{3,2},{4,5},{5,4},{6,7},{7,6},{16,17},{17,16},{1... | collective-permute-start | bytes 1572872 | tf_op jit(solution)/shard_map/other_x/ppermute | solution.py:30
  50.6 2.9 %copy-start.16 = (bf16[4,2,32,1024]{3,2,1,0:T(8,128)(2,1)}, bf16[4,2,32,1024]{3,2,1,0:T(8,128)(2,1)S(1)}, u32[]{:S(2)}) copy-start(bf16[4,2,32,1024]{3,2,1,0:T(8,128)(2,1)S(1)} %collective-permute-done.16.refs_10_) | copy-start | bytes 1572868
  50.6 3.8 %collective-permute-start.21 = (bf16[4,2,32,1024]{3,2,1,0:T(8,128)(2,1)S(1)}, bf16[4,2,32,1024]{3,2,1,0:T(8,128)(2,1)}, u32[]{:S(2)}, u32[]{:S(2)}) collective-permute-start(bf16[4,2,32,1024]{3,2,1,0:T(8,128)(2,1)S(1)} %collective-permute-done.11.refs_7_), channel_id=1, source_target_pairs={{0,1},{1,0},{2,3},{3,2},{4,5},{5,4},{6,7},{7,6},{16,17},{17,16},{1... | collective-permute-start | bytes 1572872 | tf_op jit(solution)/shard_map/other_x3/ppermute | solution.py:30
  51.1 2.5 %copy-start.17 = (bf16[4,2,32,1024]{3,2,1,0:T(8,128)(2,1)}, bf16[4,2,32,1024]{3,2,1,0:T(8,128)(2,1)S(1)}, u32[]{:S(2)}) copy-start(bf16[4,2,32,1024]{3,2,1,0:T(8,128)(2,1)S(1)} %collective-permute-done.13.refs_9_) | copy-start | bytes 1572868
  51.3 2.3 %copy-start.18 = (bf16[4,2,32,1024]{3,2,1,0:T(8,128)(2,1)}, bf16[4,2,32,1024]{3,2,1,0:T(8,128)(2,1)S(1)}, u32[]{:S(2)}) copy-start(bf16[4,2,32,1024]{3,2,1,0:T(8,128)(2,1)S(1)} %collective-permute-done.20.refs_14_) | copy-start | bytes 1572868
  52.1 1.5 %copy-start.19 = (bf16[4,2,32,1024]{3,2,1,0:T(8,128)(2,1)}, bf16[4,2,32,1024]{3,2,1,0:T(8,128)(2,1)S(1)}, u32[]{:S(2)}) copy-start(bf16[4,2,32,1024]{3,2,1,0:T(8,128)(2,1)S(1)} %collective-permute-done.18.refs_13_) | copy-start | bytes 1572868
  53.6 0.8 %copy-start.20 = (bf16[4,2,32,1024]{3,2,1,0:T(8,128)(2,1)}, bf16[4,2,32,1024]{3,2,1,0:T(8,128)(2,1)S(1)}, u32[]{:S(2)}) copy-start(bf16[4,2,32,1024]{3,2,1,0:T(8,128)(2,1)S(1)} %collective-permute-done.17.refs_12_) | copy-start | bytes 1572868

commit v10 on v2

v10 whole, which is shorter than its diff:
```python
import functools

import jax
import jax.numpy as jnp
from jax import lax
from jax.experimental import pallas as pl
from jax.experimental.pallas import tpu as pltpu
from jax.sharding import PartitionSpec as P

BLK = 32
STEPS = 12
ROWS = 256
AXES = ("shot", "rcv")
X, Y, Z, CORES = 4, 4, 4, 2


def moved(value, dx=0, dy=0, dz=0, flip_x=False, flip_core=False):
    def index(x, y, z, core):
        x_hi, x_lo = divmod(x, 2)
        return (((x_hi * Y + y) * 2 + x_lo) * Z + z) * CORES + core

    pairs = []
    for x in range(X):
        for y in range(Y):
            for z in range(Z):
                for core in range(CORES):
                    way = 1 - 2 * core
                    to_x = x ^ 1 if flip_x else (x + way * dx) % X
                    to_core = core ^ 1 if flip_core else core
                    target = index(to_x, (y + way * dy) % Y, (z + way * dz) % Z, to_core)
                    pairs.append((index(x, y, z, core), target))
    return lax.ppermute(value, AXES, pairs)


def choose(refs, which, act):
    if len(refs) == 1:
        act(refs[0])
        return
    half = len(refs) // 2

    @pl.when(which < half)
    def _():
        choose(refs[:half], which, act)

    @pl.when(which >= half)
    def _():
        choose(refs[half:], which - half, act)


def multiply_kernel(carried_by_other, ids, place, *refs):
    a_refs, b_refs = refs[:8], refs[8:16]
    out, a_buf, b_buf, lhs, rhs, a_sem, b_sem = refs[-7:]
    f = pl.program_id(0)
    rcvs = b_buf.shape[4]
    shot, rcv = place[0], place[1]
    core, z, x_lo = rcv % CORES, rcv // CORES % Z, rcv // (CORES * Z)
    y, x_hi = shot % Y, shot // Y
    carrier = core ^ carried_by_other

    def fetch(freq):
        for step in range(STEPS):
            block = ids[step]
            of_core, of_z, of_x = block % CORES, block // CORES % Z, block // (CORES * Z)
            distance = jnp.where(carrier == 0, z - of_z, of_z - z) & (Z - 1)
            slot = of_core ^ carrier

            def from_surface(ref):
                pltpu.make_async_copy(
                    ref.at[slot, freq], a_buf.at[freq, step], a_sem.at[freq]
                ).start()

            choose(a_refs, (of_x ^ x_lo) * Z + distance, from_surface)

            owner = block // 2
            distance = jnp.where(core == 0, y - owner % Y, owner % Y - y) & (Y - 1)
            rows = pl.ds(pl.multiple_of(block % 2 * BLK, BLK), BLK)

            def from_traces(ref):
                pltpu.make_async_copy(
                    ref.at[2 * carrier + freq, :, rows], b_buf.at[freq, step], b_sem.at[freq]
                ).start()

            choose(b_refs, (owner // Y ^ x_hi) * Y + distance, from_traces)

    @pl.when(f == 0)
    def _():
        for freq in range(a_buf.shape[0]):
            fetch(freq)

    for buf, sem in ((a_buf, a_sem), (b_buf, b_sem)):
        pltpu.make_async_copy(buf.at[f], buf.at[f], sem.at[f]).wait()

    for step in range(STEPS):
        real = b_buf[f, step, 0]
        imag = b_buf[f, step, 1]
        rhs[0, step, 0] = real
        rhs[0, step, 1] = -imag
        rhs[1, step, 0] = imag
        rhs[1, step, 1] = real

    depth = STEPS * 2 * BLK
    for first in range(0, lhs.shape[0], ROWS):
        block = a_buf[f, :, :, :, first : first + ROWS].reshape(depth, ROWS)
        lhs[first : first + ROWS, :] = block.T

    for part in range(2):
        out[0, part] = jnp.dot(
            lhs[...], rhs[part].reshape(depth, rcvs), preferred_element_type=jnp.float32
        ).astype(out.dtype)


def multiply(a_parts, b_parts, block_ids, place, done=None):
    _, count, _, _, shots = a_parts[0].shape
    freqs, _, _, rcvs = b_parts[0].shape
    depth = STEPS * 2 * BLK
    by_other = int(done is not None)
    operands = [block_ids, place, *a_parts, *b_parts] + ([done] if by_other else [])
    return pl.pallas_call(
        functools.partial(multiply_kernel, by_other),
        out_shape=jax.ShapeDtypeStruct((freqs, 2, shots, rcvs), jnp.bfloat16),
        grid_spec=pltpu.PrefetchScalarGridSpec(
            num_scalar_prefetch=2,
            grid=(count,),
            in_specs=[pl.BlockSpec(memory_space=pl.ANY)] * (len(operands) - 2),
            out_specs=pl.BlockSpec(
                (1, 2, shots, rcvs),
                lambda f, ids, place: (2 * (place[1] % CORES ^ by_other) + f, 0, 0, 0),
            ),
            scratch_shapes=[
                pltpu.VMEM((count, STEPS, 2, BLK, shots), jnp.bfloat16),
                pltpu.VMEM((count, STEPS, 2, BLK, rcvs), jnp.bfloat16),
                pltpu.VMEM((shots, depth), jnp.bfloat16),
                pltpu.VMEM((2, STEPS, 2, BLK, rcvs), jnp.bfloat16),
                pltpu.SemaphoreType.DMA((count,)),
                pltpu.SemaphoreType.DMA((count,)),
            ],
        ),
        input_output_aliases={len(operands) - 1: 0} if by_other else {},
        compiler_params=pltpu.CompilerParams(vmem_limit_bytes=56 * 1024 * 1024),
        cost_estimate=pl.CostEstimate(
            flops=2 * count * shots * 2 * rcvs * depth,
            bytes_accessed=10 * 1024 * 1024,
            transcendentals=0,
        ),
    )(*operands)


def after(value, *earlier):
    return lax.optimization_barrier((value, *earlier))[0]


def per_device(surface_data, source_traces, block_ids):
    a, b = surface_data, source_traces
    core = lax.axis_index("rcv") % CORES
    place = jnp.stack([lax.axis_index("shot"), lax.axis_index("rcv")]).astype(jnp.int32)

    def send(name, value, **way):
        with jax.named_scope(name):
            return moved(value, **way)

    def swap(name, value):
        return send(name, value, flip_core=True)

    other = swap("other", a)
    own = jnp.where(core == 0, jnp.stack([a[:2], other[:2]]), jnp.stack([a[2:], other[2:]]))
    b_1 = send("b_1", b, dy=1)
    b_x = send("b_x", b, dx=2)
    a_1 = send("a_1", own, dz=1)
    b_3 = send("b_3", after(b, other), dy=-1)
    a_3 = send("a_3", after(own, other, place), dz=-1)
    b_2 = send("b_2", b_1, dy=1)
    a_x = send("a_x", after(own, b_x), flip_x=True)
    a_2 = send("a_2", a_1, dz=1)
    b_x1 = send("b_x1", after(b_x, b_3), dy=1)
    b_x3 = send("b_x3", after(b_x, a_3), dy=-1)
    their = swap("their", after(own, b_2))
    a_x1 = send("a_x1", after(a_x, a_2), dz=1)
    a_x2 = send("a_x2", a_2, flip_x=True)
    a_x3 = send("a_x3", after(a_x, b_x1), dz=-1)
    b_x2 = send("b_x2", after(b_x1, b_x3), dy=1)
    their_x = swap("their_x", after(a_x, their))
    their_3 = swap("their_3", after(a_3, a_x1))
    their_2 = swap("their_2", after(a_2, a_x2))
    their_1 = swap("their_1", after(a_1, a_x3))
    their_x3 = swap("their_x3", after(a_x3, b_x2))
    their_x1 = swap("their_x1", after(a_x1, their_x))
    their_x2 = swap("their_x2", after(a_x2, their_3))

    b_parts = [b, b_1, b_2, b_3, b_x, b_x1, b_x2, b_x3]
    a_parts = [own, a_1, a_2, a_3, a_x, a_x1, a_x2, a_x3]
    result = multiply(a_parts, b_parts, block_ids, place)
    a_parts = [their, their_1, their_2, their_3, their_x, their_x1, their_x2, their_x3]
    return multiply(a_parts, b_parts, block_ids, place, result)


def solution(mesh):
    in_specs = (P(None, None, "rcv", "shot"), P(None, None, "shot", "rcv"), P())
    out_specs = P(None, None, "shot", "rcv")
    return jax.shard_map(
        per_device, mesh=mesh, in_specs=in_specs, out_specs=out_specs, check_vma=False
    )
```

time: 67.8 us -> 71.6 us (1.056)
  Pallas kernels: 12 us -> 15.2 us
  local copies, waits for them, and re-layouts: 0.05 us -> 2.67 us
  other arithmetic: 2.52 us -> 0.7 us
  waiting for transfers between devices: 15.2 us -> 13.5 us
  starting transfers between devices: 37.8 us -> 39 us
    pallas_call x1 -> x2, Pallas kernels: 12 us -> 15.2 us  [multiply(): pl.pallas_call(functools.partial(multiply_kernel, by_other), out_shape=ja...]
    ppermute x23, waiting for transfers between devices: 15.2 us -> 13.5 us  [moved(): return lax.ppermute(value, AXES, pairs)]
    unnamed x26 -> x34, local copies, waits for them, and re-layouts: 0.05 us -> 1.56 us
    add x1 -> x0, other arithmetic: 1.28 us -> none  [places(): b_where = (shot // Y != owner // Y) * Y + distance]
    mul x1 -> x0, other arithmetic: 1.24 us -> none  [places(): block_ids % 2 * BLK]
    ppermute x23, starting transfers between devices: 37.8 us -> 39 us  [moved(): return lax.ppermute(value, AXES, pairs)]
    another operation x0 -> x2, local copies, waits for them, and re-layouts: none -> 1.11 us  [per_device(): jnp.stack([a[2:], other[2:]])]
  transfers between devices with their start and end apart: 23 -> 23, of which waited for: 5 -> 6; matrix products, arithmetic and copies ran while one was open for 4% -> 3% of each run, Pallas kernels for 0% -> 11%
where the time goes in v10:
time: 71.6 us; the launch traced here: 71.5 us
  starting transfers between devices  39 us (54%)
  Pallas kernels  15.2 us (21%)
  waiting for transfers between devices  13.5 us (19%)
  local copies, waits for them, and re-layouts  2.67 us (4%)
    ppermute x23, starting transfers between devices, moved(): return lax.ppermute(value, AXES, pairs)  39 us
    pallas_call x2, Pallas kernels, multiply(): pl.pallas_call(functools.partial(multiply_kernel, by_other), out_shape=ja...  15.2 us
    ppermute x23, waiting for transfers between devices, moved(): return lax.ppermute(value, AXES, pairs)  13.5 us
    unnamed x34, local copies, waits for them, and re-layouts  1.56 us
  transfers between devices with their start and end apart: 23, of which 6 were waited for; matrix products, arithmetic and copies ran while one was open for 3% of the time, Pallas kernels for 11%

profile of v10, /device:TPU:1, one launch (start us, length us, event | category | flops | bytes accessed | tf_op | source)
XLA Modules:
  0.0 71.5 jit_solution(13856812654449475096)
XLA Ops:
  0.0 1.4 %collective-permute-start = (bf16[4,2,32,1024]{3,2,1,0:T(8,128)(2,1)}, bf16[4,2,32,1024]{3,2,1,0:T(8,128)(2,1)S(1)}, u32[]{:S(2)}, u32[]{:S(2)}) collective-permute-start(bf16[4,2,32,1024]{3,2,1,0:T(8,128)(2,1)} %param.3), channel_id=1, source_target_pairs={{0,1},{1,0},{2,3},{3,2},{4,5},{5,4},{6,7},{7,6},{16,17},{17,16},{1... | collective-permute-start | bytes 1572872 | tf_op jit(solution)/shard_map/other/ppermute | solution.py:32
  1.4 2.8 %collective-permute-start.5 = (bf16[4,2,64,512]{3,2,1,0:T(8,128)(2,1)}, bf16[4,2,64,512]{3,2,1,0:T(8,128)(2,1)S(1)}, u32[]{:S(2)}, u32[]{:S(2)}) collective-permute-start(bf16[4,2,64,512]{3,2,1,0:T(8,128)(2,1)} %refs_8_.3), channel_id=1, source_target_pairs={{0,64},{1,65},{2,66},{3,67},{4,68},{5,69},{6,70},{7,71},{16,80},{1... | collective-permute-start | bytes 1572872 | tf_op jit(solution)/shard_map/b_x/ppermute | solution.py:32
  4.2 2.7 %collective-permute-start.1 = (bf16[4,2,64,512]{3,2,1,0:T(8,128)(2,1)}, bf16[4,2,64,512]{3,2,1,0:T(8,128)(2,1)S(1)}, u32[]{:S(2)}, u32[]{:S(2)}) collective-permute-start(bf16[4,2,64,512]{3,2,1,0:T(8,128)(2,1)} %refs_8_.3), channel_id=1, source_target_pairs={{0,16},{1,49},{2,18},{3,51},{4,20},{5,53},{6,22},{7,55},{16,32},{1... | collective-permute-start | bytes 1572872 | tf_op jit(solution)/shard_map/b_1/ppermute | solution.py:32
  7.0 1.1 %slice_bitcast_fusion.2 = (bf16[1,2,2,32,1024]{4,3,2,1,0:T(8,128)(2,1)S(1)}, bf16[1,2,2,32,1024]{4,3,2,1,0:T(8,128)(2,1)S(1)}) fusion(bf16[4,2,32,1024]{3,2,1,0:T(8,128)(2,1)} %param.3), kind=kLoop, calls=%fused_computation.3 | loop fusion | bytes 1048576 | tf_op jit(solution)/shard_map/stack | solution.py:165
  8.1 0.0 collective-permute-done
  8.1 0.1 maximum_select_fusion.refs_0_
  8.2 3.8 %collective-permute-start.4 = (bf16[2,2,2,32,1024]{4,3,2,1,0:T(8,128)(2,1)S(1)}, bf16[2,2,2,32,1024]{4,3,2,1,0:T(8,128)(2,1)S(1)}, u32[]{:S(2)}, u32[]{:S(2)}) collective-permute-start(bf16[2,2,2,32,1024]{4,3,2,1,0:T(8,128)(2,1)S(1)} %maximum_select_fusion.refs_0_), channel_id=1, source_target_pairs={{0,2},{1,7},{2,4},{3,1},{4,6},{5,3},{6,0},{7,5},{16,18},{17,23},{1... | collective-permute-start | bytes 1572872 | tf_op jit(solution)/shard_map/a_1/ppermute | solution.py:32
  12.1 0.0 collective-permute-start.7
  12.1 0.6 pad_add_fusion.place
  12.7 0.0 collective-permute-start.14
  12.7 2.1 %collective-permute-done.1.refs_9_ = bf16[4,2,64,512]{3,2,1,0:T(8,128)(2,1)S(1)} collective-permute-done((bf16[4,2,64,512]{3,2,1,0:T(8,128)(2,1)}, bf16[4,2,64,512]{3,2,1,0:T(8,128)(2,1)S(1)}, u32[]{:S(2)}, u32[]{:S(2)}) %collective-permute-start.1) | collective-permute-done | bytes 524320 | tf_op jit(solution)/shard_map/b_1/ppermute | solution.py:32
  14.8 3.3 %collective-permute-start.2 = (bf16[4,2,64,512]{3,2,1,0:T(8,128)(2,1)S(1)}, bf16[4,2,64,512]{3,2,1,0:T(8,128)(2,1)S(1)}, u32[]{:S(2)}, u32[]{:S(2)}) collective-permute-start(bf16[4,2,64,512]{3,2,1,0:T(8,128)(2,1)S(1)} %collective-permute-done.1.refs_9_), channel_id=1, source_target_pairs={{0,16},{1,49},{2,18},{3,51},{4,20},{5,53},{6,22},{7,55},{16,32},{1... | collective-permute-start | bytes 1572872 | tf_op jit(solution)/shard_map/b_2/ppermute | solution.py:32
  18.1 0.0 collective-permute-done.5.refs_12_
  18.1 0.3 collective-permute-start.6
  18.4 3.4 %collective-permute-done.4.refs_1_ = bf16[2,2,2,32,1024]{4,3,2,1,0:T(8,128)(2,1)S(1)} collective-permute-done((bf16[2,2,2,32,1024]{4,3,2,1,0:T(8,128)(2,1)S(1)}, bf16[2,2,2,32,1024]{4,3,2,1,0:T(8,128)(2,1)S(1)}, u32[]{:S(2)}, u32[]{:S(2)}) %collective-permute-start.4) | collective-permute-done | bytes 524320 | tf_op jit(solution)/shard_map/a_1/ppermute | solution.py:32
  21.8 3.4 %collective-permute-start.11 = (bf16[2,2,2,32,1024]{4,3,2,1,0:T(8,128)(2,1)S(1)}, bf16[2,2,2,32,1024]{4,3,2,1,0:T(8,128)(2,1)S(1)}, u32[]{:S(2)}, u32[]{:S(2)}) collective-permute-start(bf16[2,2,2,32,1024]{4,3,2,1,0:T(8,128)(2,1)S(1)} %collective-permute-done.4.refs_1_), channel_id=1, source_target_pairs={{0,2},{1,7},{2,4},{3,1},{4,6},{5,3},{6,0},{7,5},{16,18},{17,23},{1... | collective-permute-start | bytes 1572872 | tf_op jit(solution)/shard_map/a_2/ppermute | solution.py:32
  25.2 0.0 collective-permute-done.7.refs_11_
  25.2 0.0 collective-permute-start.8
  25.2 0.0 collective-permute-done.14.refs_3_
  25.2 1.4 %collective-permute-start.20 = (bf16[4,2,64,512]{3,2,1,0:T(8,128)(2,1)S(1)}, bf16[4,2,64,512]{3,2,1,0:T(8,128)(2,1)S(1)}, u32[]{:S(2)}, u32[]{:S(2)}) collective-permute-start(bf16[4,2,64,512]{3,2,1,0:T(8,128)(2,1)S(1)} %collective-permute-done.5.refs_12_), channel_id=1, source_target_pairs={{0,48},{1,17},{2,50},{3,19},{4,52},{5,21},{6,54},{7,23},{16,0},{17... | collective-permute-start | bytes 1572872 | tf_op jit(solution)/shard_map/b_x3/ppermute | solution.py:32
  26.7 0.0 collective-permute-done.2.refs_10_
  26.7 1.1 %collective-permute-start.3 = (bf16[2,2,2,32,1024]{4,3,2,1,0:T(8,128)(2,1)S(1)}, bf16[2,2,2,32,1024]{4,3,2,1,0:T(8,128)(2,1)S(1)}, u32[]{:S(2)}, u32[]{:S(2)}) collective-permute-start(bf16[2,2,2,32,1024]{4,3,2,1,0:T(8,128)(2,1)S(1)} %maximum_select_fusion.refs_0_), channel_id=1, source_target_pairs={{0,1},{1,0},{2,3},{3,2},{4,5},{5,4},{6,7},{7,6},{16,17},{17,16},{1... | collective-permute-start | bytes 1572872 | tf_op jit(solution)/shard_map/their/ppermute | solution.py:32
  27.8 4.1 %collective-permute-done.6.refs_4_ = bf16[2,2,2,32,1024]{4,3,2,1,0:T(8,128)(2,1)S(1)} collective-permute-done((bf16[2,2,2,32,1024]{4,3,2,1,0:T(8,128)(2,1)S(1)}, bf16[2,2,2,32,1024]{4,3,2,1,0:T(8,128)(2,1)S(1)}, u32[]{:S(2)}, u32[]{:S(2)}) %collective-permute-start.6) | collective-permute-done | bytes 524320 | tf_op jit(solution)/shard_map/a_x/ppermute | solution.py:32
  31.9 0.0 collective-permute-done.11.refs_2_
  31.9 5.8 %collective-permute-start.15 = (bf16[2,2,2,32,1024]{4,3,2,1,0:T(8,128)(2,1)S(1)}, bf16[2,2,2,32,1024]{4,3,2,1,0:T(8,128)(2,1)S(1)}, u32[]{:S(2)}, u32[]{:S(2)}) collective-permute-start(bf16[2,2,2,32,1024]{4,3,2,1,0:T(8,128)(2,1)S(1)} %collective-permute-done.6.refs_4_), channel_id=1, source_target_pairs={{0,2},{1,7},{2,4},{3,1},{4,6},{5,3},{6,0},{7,5},{16,18},{17,23},{1... | collective-permute-start | bytes 1572872 | tf_op jit(solution)/shard_map/a_x1/ppermute | solution.py:32
  37.7 0.3 collective-permute-start.12
  38.0 0.9 %collective-permute-done.8.refs_13_ = bf16[4,2,64,512]{3,2,1,0:T(8,128)(2,1)S(1)} collective-permute-done((bf16[4,2,64,512]{3,2,1,0:T(8,128)(2,1)S(1)}, bf16[4,2,64,512]{3,2,1,0:T(8,128)(2,1)S(1)}, u32[]{:S(2)}, u32[]{:S(2)}) %collective-permute-start.8) | collective-permute-done | bytes 524320 | tf_op jit(solution)/shard_map/b_x1/ppermute | solution.py:32
  38.9 0.0 collective-permute-start.9
  38.9 0.0 collective-permute-done.20.refs_15_
  38.9 0.9 %collective-permute-start.21 = (bf16[4,2,64,512]{3,2,1,0:T(8,128)(2,1)S(1)}, bf16[4,2,64,512]{3,2,1,0:T(8,128)(2,1)S(1)}, u32[]{:S(2)}, u32[]{:S(2)}) collective-permute-start(bf16[4,2,64,512]{3,2,1,0:T(8,128)(2,1)S(1)} %collective-permute-done.8.refs_13_), channel_id=1, source_target_pairs={{0,16},{1,49},{2,18},{3,51},{4,20},{5,53},{6,22},{7,55},{16,32},{1... | collective-permute-start | bytes 1572872 | tf_op jit(solution)/shard_map/b_x2/ppermute | solution.py:32
  39.9 4.1 %collective-permute-start.17 = (bf16[2,2,2,32,1024]{4,3,2,1,0:T(8,128)(2,1)S(1)}, bf16[2,2,2,32,1024]{4,3,2,1,0:T(8,128)(2,1)S(1)}, u32[]{:S(2)}, u32[]{:S(2)}) collective-permute-start(bf16[2,2,2,32,1024]{4,3,2,1,0:T(8,128)(2,1)S(1)} %collective-permute-done.6.refs_4_), channel_id=1, source_target_pairs={{0,1},{1,0},{2,3},{3,2},{4,5},{5,4},{6,7},{7,6},{16,17},{17,16},{1... | collective-permute-start | bytes 1572872 | tf_op jit(solution)/shard_map/their_x/ppermute | solution.py:32
  44.0 3.8 %collective-permute-start.16 = (bf16[2,2,2,32,1024]{4,3,2,1,0:T(8,128)(2,1)S(1)}, bf16[2,2,2,32,1024]{4,3,2,1,0:T(8,128)(2,1)S(1)}, u32[]{:S(2)}, u32[]{:S(2)}) collective-permute-start(bf16[2,2,2,32,1024]{4,3,2,1,0:T(8,128)(2,1)S(1)} %collective-permute-done.14.refs_3_), channel_id=1, source_target_pairs={{0,1},{1,0},{2,3},{3,2},{4,5},{5,4},{6,7},{7,6},{16,17},{17,16},{1... | collective-permute-start | bytes 1572872 | tf_op jit(solution)/shard_map/their_3/ppermute | solution.py:32
  47.8 1.0 %collective-permute-done.12.refs_6_ = bf16[2,2,2,32,1024]{4,3,2,1,0:T(8,128)(2,1)S(1)} collective-permute-done((bf16[2,2,2,32,1024]{4,3,2,1,0:T(8,128)(2,1)S(1)}, bf16[2,2,2,32,1024]{4,3,2,1,0:T(8,128)(2,1)S(1)}, u32[]{:S(2)}, u32[]{:S(2)}) %collective-permute-start.12) | collective-permute-done | bytes 524320 | tf_op jit(solution)/shard_map/a_x2/ppermute | solution.py:32
  48.8 0.0 collective-permute-start.13
  48.8 1.9 %collective-permute-done.9.refs_7_ = bf16[2,2,2,32,1024]{4,3,2,1,0:T(8,128)(2,1)} collective-permute-done((bf16[2,2,2,32,1024]{4,3,2,1,0:T(8,128)(2,1)S(1)}, bf16[2,2,2,32,1024]{4,3,2,1,0:T(8,128)(2,1)}, u32[]{:S(2)}, u32[]{:S(2)}) %collective-permute-start.9) | collective-permute-done | bytes 524320 | tf_op jit(solution)/shard_map/a_x3/ppermute | solution.py:32
  50.8 0.0 collective-permute-start.10
  50.8 0.0 collective-permute-done.21.refs_14_
  50.8 3.4 %collective-permute-start.22 = (bf16[2,2,2,32,1024]{4,3,2,1,0:T(8,128)(2,1)}, bf16[2,2,2,32,1024]{4,3,2,1,0:T(8,128)(2,1)}, u32[]{:S(2)}, u32[]{:S(2)}) collective-permute-start(bf16[2,2,2,32,1024]{4,3,2,1,0:T(8,128)(2,1)} %collective-permute-done.9.refs_7_), channel_id=1, source_target_pairs={{0,1},{1,0},{2,3},{3,2},{4,5},{5,4},{6,7},{7,6},{16,17},{17,16},{1... | collective-permute-start | bytes 1572872 | tf_op jit(solution)/shard_map/their_x3/ppermute | solution.py:32
  54.2 0.0 collective-permute-done.17.refs_4_
  54.2 0.1 collective-permute-start.18
  54.3 0.7 %copy-done.15 = bf16[2,2,2,32,1024]{4,3,2,1,0:T(8,128)(2,1)} copy-done((bf16[2,2,2,32,1024]{4,3,2,1,0:T(8,128)(2,1)}, bf16[2,2,2,32,1024]{4,3,2,1,0:T(8,128)(2,1)S(1)}, u32[]{:S(2)}) %copy-start.15) | copy-done | bytes 524312
  55.0 0.8 %copy-done.16 = bf16[2,2,2,32,1024]{4,3,2,1,0:T(8,128)(2,1)} copy-done((bf16[2,2,2,32,1024]{4,3,2,1,0:T(8,128)(2,1)}, bf16[2,2,2,32,1024]{4,3,2,1,0:T(8,128)(2,1)S(1)}, u32[]{:S(2)}) %copy-start.16) | copy-done | bytes 524312
  55.8 0.0 collective-permute-start.19
  56.0 7.6 %shard_map.37.refs_16_ = bf16[4,2,1024,512]{3,2,1,0:T(8,128)(2,1)} custom-call(s32[12]{0:T(128)} %ids.3, s32[2]{0:T(128)} %pad_add_fusion.place, bf16[2,2,2,32,1024]{4,3,2,1,0:T(8,128)(2,1)} %copy-done.7, bf16[2,2,2,32,1024]{4,3,2,1,0:T(8,128)(2,1)} %copy-done.8, bf16[2,2,2,32,1024]{4,3,2,1,0:T(8,128)(2,1)} %copy-done.12, ...), custom_call_target="tpu_custom_call" | custom-call | flops 3221225472 | bytes 10485760 | tf_op jit(solution)/shard_map/pallas_call | solution.py:118
  63.6 0.0 collective-permute-done.13.refs_2_
  63.6 0.0 collective-permute-done.22.refs_7_
  63.6 0.0 collective-permute-done.18.refs_5_
  63.7 7.6 %shard_map.38 = bf16[4,2,1024,512]{3,2,1,0:T(8,128)(2,1)} custom-call(s32[12]{0:T(128)} %ids.3, s32[2]{0:T(128)} %pad_add_fusion.place, bf16[2,2,2,32,1024]{4,3,2,1,0:T(8,128)(2,1)} %copy-done.10, bf16[2,2,2,32,1024]{4,3,2,1,0:T(8,128)(2,1)} %collective-permute-done.10.refs_1_, ...), custom_call_target="tpu_custom_call", output_to_operand_aliasing={{}: (18, {})} | custom-call | flops 3221225472 | bytes 10485760 | tf_op jit(solution)/shard_map/pallas_call | solution.py:118
  (38 shorter events, 0.1 us)
Async XLA Ops:
  0.0 8.1 %collective-permute-start = (bf16[4,2,32,1024]{3,2,1,0:T(8,128)(2,1)}, bf16[4,2,32,1024]{3,2,1,0:T(8,128)(2,1)S(1)}, u32[]{:S(2)}, u32[]{:S(2)}) collective-permute-start(bf16[4,2,32,1024]{3,2,1,0:T(8,128)(2,1)} %param.3), channel_id=1, source_target_pairs={{0,1},{1,0},{2,3},{3,2},{4,5},{5,4},{6,7},{7,6},{16,17},{17,16},{1... | collective-permute-start | bytes 1572872 | tf_op jit(solution)/shard_map/other/ppermute | solution.py:32
  1.4 16.7 %collective-permute-start.5 = (bf16[4,2,64,512]{3,2,1,0:T(8,128)(2,1)}, bf16[4,2,64,512]{3,2,1,0:T(8,128)(2,1)S(1)}, u32[]{:S(2)}, u32[]{:S(2)}) collective-permute-start(bf16[4,2,64,512]{3,2,1,0:T(8,128)(2,1)} %refs_8_.3), channel_id=1, source_target_pairs={{0,64},{1,65},{2,66},{3,67},{4,68},{5,69},{6,70},{7,71},{16,80},{1... | collective-permute-start | bytes 1572872 | tf_op jit(solution)/shard_map/b_x/ppermute | solution.py:32
  4.2 10.5 %collective-permute-start.1 = (bf16[4,2,64,512]{3,2,1,0:T(8,128)(2,1)}, bf16[4,2,64,512]{3,2,1,0:T(8,128)(2,1)S(1)}, u32[]{:S(2)}, u32[]{:S(2)}) collective-permute-start(bf16[4,2,64,512]{3,2,1,0:T(8,128)(2,1)} %refs_8_.3), channel_id=1, source_target_pairs={{0,16},{1,49},{2,18},{3,51},{4,20},{5,53},{6,22},{7,55},{16,32},{1... | collective-permute-start | bytes 1572872 | tf_op jit(solution)/shard_map/b_1/ppermute | solution.py:32
  8.2 47.6 %copy-start.7 = (bf16[2,2,2,32,1024]{4,3,2,1,0:T(8,128)(2,1)}, bf16[2,2,2,32,1024]{4,3,2,1,0:T(8,128)(2,1)S(1)}, u32[]{:S(2)}) copy-start(bf16[2,2,2,32,1024]{4,3,2,1,0:T(8,128)(2,1)S(1)} %maximum_select_fusion.refs_0_) | copy-start | bytes 1572868
  8.2 13.6 %collective-permute-start.4 = (bf16[2,2,2,32,1024]{4,3,2,1,0:T(8,128)(2,1)S(1)}, bf16[2,2,2,32,1024]{4,3,2,1,0:T(8,128)(2,1)S(1)}, u32[]{:S(2)}, u32[]{:S(2)}) collective-permute-start(bf16[2,2,2,32,1024]{4,3,2,1,0:T(8,128)(2,1)S(1)} %maximum_select_fusion.refs_0_), channel_id=1, source_target_pairs={{0,2},{1,7},{2,4},{3,1},{4,6},{5,3},{6,0},{7,5},{16,18},{17,23},{1... | collective-permute-start | bytes 1572872 | tf_op jit(solution)/shard_map/a_1/ppermute | solution.py:32
  12.1 13.2 %collective-permute-start.7 = (bf16[4,2,64,512]{3,2,1,0:T(8,128)(2,1)}, bf16[4,2,64,512]{3,2,1,0:T(8,128)(2,1)S(1)}, u32[]{:S(2)}, u32[]{:S(2)}) collective-permute-start(bf16[4,2,64,512]{3,2,1,0:T(8,128)(2,1)} %refs_8_.3), channel_id=1, source_target_pairs={{0,48},{1,17},{2,50},{3,19},{4,52},{5,21},{6,54},{7,23},{16,0},{17... | collective-permute-start | bytes 1572872 | tf_op jit(solution)/shard_map/b_3/ppermute | solution.py:32
  12.7 12.6 %collective-permute-start.14 = (bf16[2,2,2,32,1024]{4,3,2,1,0:T(8,128)(2,1)S(1)}, bf16[2,2,2,32,1024]{4,3,2,1,0:T(8,128)(2,1)S(1)}, u32[]{:S(2)}, u32[]{:S(2)}) collective-permute-start(bf16[2,2,2,32,1024]{4,3,2,1,0:T(8,128)(2,1)S(1)} %maximum_select_fusion.refs_0_), channel_id=1, source_target_pairs={{0,6},{1,3},{2,0},{3,5},{4,2},{5,7},{6,4},{7,1},{16,22},{17,19},{1... | collective-permute-start | bytes 1572872 | tf_op jit(solution)/shard_map/a_3/ppermute | solution.py:32
  14.8 41.1 %copy-start.1 = (bf16[4,2,64,512]{3,2,1,0:T(8,128)(2,1)}, bf16[4,2,64,512]{3,2,1,0:T(8,128)(2,1)S(1)}, u32[]{:S(2)}) copy-start(bf16[4,2,64,512]{3,2,1,0:T(8,128)(2,1)S(1)} %collective-permute-done.1.refs_9_) | copy-start | bytes 1572868
  14.8 11.9 %collective-permute-start.2 = (bf16[4,2,64,512]{3,2,1,0:T(8,128)(2,1)S(1)}, bf16[4,2,64,512]{3,2,1,0:T(8,128)(2,1)S(1)}, u32[]{:S(2)}, u32[]{:S(2)}) collective-permute-start(bf16[4,2,64,512]{3,2,1,0:T(8,128)(2,1)S(1)} %collective-permute-done.1.refs_9_), channel_id=1, source_target_pairs={{0,16},{1,49},{2,18},{3,51},{4,20},{5,53},{6,22},{7,55},{16,32},{1... | collective-permute-start | bytes 1572872 | tf_op jit(solution)/shard_map/b_2/ppermute | solution.py:32
  18.1 37.8 %copy-start = (bf16[4,2,64,512]{3,2,1,0:T(8,128)(2,1)}, bf16[4,2,64,512]{3,2,1,0:T(8,128)(2,1)S(1)}, u32[]{:S(2)}) copy-start(bf16[4,2,64,512]{3,2,1,0:T(8,128)(2,1)S(1)} %collective-permute-done.5.refs_12_) | copy-start | bytes 1572868
  18.1 13.8 %collective-permute-start.6 = (bf16[2,2,2,32,1024]{4,3,2,1,0:T(8,128)(2,1)S(1)}, bf16[2,2,2,32,1024]{4,3,2,1,0:T(8,128)(2,1)S(1)}, u32[]{:S(2)}, u32[]{:S(2)}) collective-permute-start(bf16[2,2,2,32,1024]{4,3,2,1,0:T(8,128)(2,1)S(1)} %maximum_select_fusion.refs_0_), channel_id=1, source_target_pairs={{0,8},{1,9},{2,10},{3,11},{4,12},{5,13},{6,14},{7,15},{16,24},{17,... | collective-permute-start | bytes 1572872 | tf_op jit(solution)/shard_map/a_x/ppermute | solution.py:32
  21.8 34.1 %copy-start.8 = (bf16[2,2,2,32,1024]{4,3,2,1,0:T(8,128)(2,1)}, bf16[2,2,2,32,1024]{4,3,2,1,0:T(8,128)(2,1)S(1)}, u32[]{:S(2)}) copy-start(bf16[2,2,2,32,1024]{4,3,2,1,0:T(8,128)(2,1)S(1)} %collective-permute-done.4.refs_1_) | copy-start | bytes 1572868
  21.8 10.1 %collective-permute-start.11 = (bf16[2,2,2,32,1024]{4,3,2,1,0:T(8,128)(2,1)S(1)}, bf16[2,2,2,32,1024]{4,3,2,1,0:T(8,128)(2,1)S(1)}, u32[]{:S(2)}, u32[]{:S(2)}) collective-permute-start(bf16[2,2,2,32,1024]{4,3,2,1,0:T(8,128)(2,1)S(1)} %collective-permute-done.4.refs_1_), channel_id=1, source_target_pairs={{0,2},{1,7},{2,4},{3,1},{4,6},{5,3},{6,0},{7,5},{16,18},{17,23},{1... | collective-permute-start | bytes 1572872 | tf_op jit(solution)/shard_map/a_2/ppermute | solution.py:32
  25.2 30.7 %copy-start.2 = (bf16[4,2,64,512]{3,2,1,0:T(8,128)(2,1)}, bf16[4,2,64,512]{3,2,1,0:T(8,128)(2,1)S(1)}, u32[]{:S(2)}) copy-start(bf16[4,2,64,512]{3,2,1,0:T(8,128)(2,1)S(1)} %collective-permute-done.7.refs_11_) | copy-start | bytes 1572868
  25.2 13.7 %collective-permute-start.8 = (bf16[4,2,64,512]{3,2,1,0:T(8,128)(2,1)S(1)}, bf16[4,2,64,512]{3,2,1,0:T(8,128)(2,1)S(1)}, u32[]{:S(2)}, u32[]{:S(2)}) collective-permute-start(bf16[4,2,64,512]{3,2,1,0:T(8,128)(2,1)S(1)} %collective-permute-done.5.refs_12_), channel_id=1, source_target_pairs={{0,16},{1,49},{2,18},{3,51},{4,20},{5,53},{6,22},{7,55},{16,32},{1... | collective-permute-start | bytes 1572872 | tf_op jit(solution)/shard_map/b_x1/ppermute | solution.py:32
  25.2 30.7 %copy-start.9 = (bf16[2,2,2,32,1024]{4,3,2,1,0:T(8,128)(2,1)}, bf16[2,2,2,32,1024]{4,3,2,1,0:T(8,128)(2,1)S(1)}, u32[]{:S(2)}) copy-start(bf16[2,2,2,32,1024]{4,3,2,1,0:T(8,128)(2,1)S(1)} %collective-permute-done.14.refs_3_) | copy-start | bytes 1572868
  25.2 13.7 %collective-permute-start.20 = (bf16[4,2,64,512]{3,2,1,0:T(8,128)(2,1)S(1)}, bf16[4,2,64,512]{3,2,1,0:T(8,128)(2,1)S(1)}, u32[]{:S(2)}, u32[]{:S(2)}) collective-permute-start(bf16[4,2,64,512]{3,2,1,0:T(8,128)(2,1)S(1)} %collective-permute-done.5.refs_12_), channel_id=1, source_target_pairs={{0,48},{1,17},{2,50},{3,19},{4,52},{5,21},{6,54},{7,23},{16,0},{17... | collective-permute-start | bytes 1572872 | tf_op jit(solution)/shard_map/b_x3/ppermute | solution.py:32
  26.7 29.2 %copy-start.3 = (bf16[4,2,64,512]{3,2,1,0:T(8,128)(2,1)}, bf16[4,2,64,512]{3,2,1,0:T(8,128)(2,1)S(1)}, u32[]{:S(2)}) copy-start(bf16[4,2,64,512]{3,2,1,0:T(8,128)(2,1)S(1)} %collective-permute-done.2.refs_10_) | copy-start | bytes 1572868
  26.7 13.2 %collective-permute-start.3 = (bf16[2,2,2,32,1024]{4,3,2,1,0:T(8,128)(2,1)S(1)}, bf16[2,2,2,32,1024]{4,3,2,1,0:T(8,128)(2,1)S(1)}, u32[]{:S(2)}, u32[]{:S(2)}) collective-permute-start(bf16[2,2,2,32,1024]{4,3,2,1,0:T(8,128)(2,1)S(1)} %maximum_select_fusion.refs_0_), channel_id=1, source_target_pairs={{0,1},{1,0},{2,3},{3,2},{4,5},{5,4},{6,7},{7,6},{16,17},{17,16},{1... | collective-permute-start | bytes 1572872 | tf_op jit(solution)/shard_map/their/ppermute | solution.py:32
  31.9 24.0 %copy-start.11 = (bf16[2,2,2,32,1024]{4,3,2,1,0:T(8,128)(2,1)}, bf16[2,2,2,32,1024]{4,3,2,1,0:T(8,128)(2,1)S(1)}, u32[]{:S(2)}) copy-start(bf16[2,2,2,32,1024]{4,3,2,1,0:T(8,128)(2,1)S(1)} %collective-permute-done.6.refs_4_) | copy-start | bytes 1572868
  31.9 24.0 %copy-start.12 = (bf16[2,2,2,32,1024]{4,3,2,1,0:T(8,128)(2,1)}, bf16[2,2,2,32,1024]{4,3,2,1,0:T(8,128)(2,1)S(1)}, u32[]{:S(2)}) copy-start(bf16[2,2,2,32,1024]{4,3,2,1,0:T(8,128)(2,1)S(1)} %collective-permute-done.11.refs_2_) | copy-start | bytes 1572868
  31.9 12.1 %collective-permute-start.15 = (bf16[2,2,2,32,1024]{4,3,2,1,0:T(8,128)(2,1)S(1)}, bf16[2,2,2,32,1024]{4,3,2,1,0:T(8,128)(2,1)S(1)}, u32[]{:S(2)}, u32[]{:S(2)}) collective-permute-start(bf16[2,2,2,32,1024]{4,3,2,1,0:T(8,128)(2,1)S(1)} %collective-permute-done.6.refs_4_), channel_id=1, source_target_pairs={{0,2},{1,7},{2,4},{3,1},{4,6},{5,3},{6,0},{7,5},{16,18},{17,23},{1... | collective-permute-start | bytes 1572872 | tf_op jit(solution)/shard_map/a_x1/ppermute | solution.py:32
  37.7 11.1 %collective-permute-start.12 = (bf16[2,2,2,32,1024]{4,3,2,1,0:T(8,128)(2,1)S(1)}, bf16[2,2,2,32,1024]{4,3,2,1,0:T(8,128)(2,1)S(1)}, u32[]{:S(2)}, u32[]{:S(2)}) collective-permute-start(bf16[2,2,2,32,1024]{4,3,2,1,0:T(8,128)(2,1)S(1)} %collective-permute-done.11.refs_2_), channel_id=1, source_target_pairs={{0,8},{1,9},{2,10},{3,11},{4,12},{5,13},{6,14},{7,15},{16,24},{17,... | collective-permute-start | bytes 1572872 | tf_op jit(solution)/shard_map/a_x2/ppermute | solution.py:32
  38.9 17.0 %copy-start.4 = (bf16[4,2,64,512]{3,2,1,0:T(8,128)(2,1)}, bf16[4,2,64,512]{3,2,1,0:T(8,128)(2,1)S(1)}, u32[]{:S(2)}) copy-start(bf16[4,2,64,512]{3,2,1,0:T(8,128)(2,1)S(1)} %collective-permute-done.8.refs_13_) | copy-start | bytes 1572868
  38.9 11.9 %collective-permute-start.9 = (bf16[2,2,2,32,1024]{4,3,2,1,0:T(8,128)(2,1)S(1)}, bf16[2,2,2,32,1024]{4,3,2,1,0:T(8,128)(2,1)}, u32[]{:S(2)}, u32[]{:S(2)}) collective-permute-start(bf16[2,2,2,32,1024]{4,3,2,1,0:T(8,128)(2,1)S(1)} %collective-permute-done.6.refs_4_), channel_id=1, source_target_pairs={{0,6},{1,3},{2,0},{3,5},{4,2},{5,7},{6,4},{7,1},{16,22},{17,19},{1... | collective-permute-start | bytes 1572872 | tf_op jit(solution)/shard_map/a_x3/ppermute | solution.py:32
  38.9 17.0 %copy-start.5 = (bf16[4,2,64,512]{3,2,1,0:T(8,128)(2,1)}, bf16[4,2,64,512]{3,2,1,0:T(8,128)(2,1)S(1)}, u32[]{:S(2)}) copy-start(bf16[4,2,64,512]{3,2,1,0:T(8,128)(2,1)S(1)} %collective-permute-done.20.refs_15_) | copy-start | bytes 1572868
  38.9 11.9 %collective-permute-start.21 = (bf16[4,2,64,512]{3,2,1,0:T(8,128)(2,1)S(1)}, bf16[4,2,64,512]{3,2,1,0:T(8,128)(2,1)S(1)}, u32[]{:S(2)}, u32[]{:S(2)}) collective-permute-start(bf16[4,2,64,512]{3,2,1,0:T(8,128)(2,1)S(1)} %collective-permute-done.8.refs_13_), channel_id=1, source_target_pairs={{0,16},{1,49},{2,18},{3,51},{4,20},{5,53},{6,22},{7,55},{16,32},{1... | collective-permute-start | bytes 1572872 | tf_op jit(solution)/shard_map/b_x2/ppermute | solution.py:32
  39.9 23.8 %copy-start.10 = (bf16[2,2,2,32,1024]{4,3,2,1,0:T(8,128)(2,1)}, bf16[2,2,2,32,1024]{4,3,2,1,0:T(8,128)(2,1)S(1)}, u32[]{:S(2)}) copy-start(bf16[2,2,2,32,1024]{4,3,2,1,0:T(8,128)(2,1)S(1)} %collective-permute-done.3.refs_0_) | copy-start | bytes 1572868
  39.9 14.4 %collective-permute-start.17 = (bf16[2,2,2,32,1024]{4,3,2,1,0:T(8,128)(2,1)S(1)}, bf16[2,2,2,32,1024]{4,3,2,1,0:T(8,128)(2,1)S(1)}, u32[]{:S(2)}, u32[]{:S(2)}) collective-permute-start(bf16[2,2,2,32,1024]{4,3,2,1,0:T(8,128)(2,1)S(1)} %collective-permute-done.6.refs_4_), channel_id=1, source_target_pairs={{0,1},{1,0},{2,3},{3,2},{4,5},{5,4},{6,7},{7,6},{16,17},{17,16},{1... | collective-permute-start | bytes 1572872 | tf_op jit(solution)/shard_map/their_x/ppermute | solution.py:32
  44.0 12.0 %copy-start.13 = (bf16[2,2,2,32,1024]{4,3,2,1,0:T(8,128)(2,1)}, bf16[2,2,2,32,1024]{4,3,2,1,0:T(8,128)(2,1)S(1)}, u32[]{:S(2)}) copy-start(bf16[2,2,2,32,1024]{4,3,2,1,0:T(8,128)(2,1)S(1)} %collective-permute-done.15.refs_5_) | copy-start | bytes 1572868
  44.0 10.4 %collective-permute-start.16 = (bf16[2,2,2,32,1024]{4,3,2,1,0:T(8,128)(2,1)S(1)}, bf16[2,2,2,32,1024]{4,3,2,1,0:T(8,128)(2,1)S(1)}, u32[]{:S(2)}, u32[]{:S(2)}) collective-permute-start(bf16[2,2,2,32,1024]{4,3,2,1,0:T(8,128)(2,1)S(1)} %collective-permute-done.14.refs_3_), channel_id=1, source_target_pairs={{0,1},{1,0},{2,3},{3,2},{4,5},{5,4},{6,7},{7,6},{16,17},{17,16},{1... | collective-permute-start | bytes 1572872 | tf_op jit(solution)/shard_map/their_3/ppermute | solution.py:32
  48.8 7.1 %copy-start.14 = (bf16[2,2,2,32,1024]{4,3,2,1,0:T(8,128)(2,1)}, bf16[2,2,2,32,1024]{4,3,2,1,0:T(8,128)(2,1)S(1)}, u32[]{:S(2)}) copy-start(bf16[2,2,2,32,1024]{4,3,2,1,0:T(8,128)(2,1)S(1)} %collective-permute-done.12.refs_6_) | copy-start | bytes 1572868
  48.8 14.8 %collective-permute-start.13 = (bf16[2,2,2,32,1024]{4,3,2,1,0:T(8,128)(2,1)S(1)}, bf16[2,2,2,32,1024]{4,3,2,1,0:T(8,128)(2,1)}, u32[]{:S(2)}, u32[]{:S(2)}) collective-permute-start(bf16[2,2,2,32,1024]{4,3,2,1,0:T(8,128)(2,1)S(1)} %collective-permute-done.11.refs_2_), channel_id=1, source_target_pairs={{0,1},{1,0},{2,3},{3,2},{4,5},{5,4},{6,7},{7,6},{16,17},{17,16},{1... | collective-permute-start | bytes 1572872 | tf_op jit(solution)/shard_map/their_2/ppermute | solution.py:32
  50.8 12.9 %collective-permute-start.10 = (bf16[2,2,2,32,1024]{4,3,2,1,0:T(8,128)(2,1)S(1)}, bf16[2,2,2,32,1024]{4,3,2,1,0:T(8,128)(2,1)}, u32[]{:S(2)}, u32[]{:S(2)}) collective-permute-start(bf16[2,2,2,32,1024]{4,3,2,1,0:T(8,128)(2,1)S(1)} %collective-permute-done.4.refs_1_), channel_id=1, source_target_pairs={{0,1},{1,0},{2,3},{3,2},{4,5},{5,4},{6,7},{7,6},{16,17},{17,16},{1... | collective-permute-start | bytes 1572872 | tf_op jit(solution)/shard_map/their_1/ppermute | solution.py:32
  50.8 5.2 %copy-start.6 = (bf16[4,2,64,512]{3,2,1,0:T(8,128)(2,1)}, bf16[4,2,64,512]{3,2,1,0:T(8,128)(2,1)S(1)}, u32[]{:S(2)}) copy-start(bf16[4,2,64,512]{3,2,1,0:T(8,128)(2,1)S(1)} %collective-permute-done.21.refs_14_) | copy-start | bytes 1572868
  50.8 12.9 %collective-permute-start.22 = (bf16[2,2,2,32,1024]{4,3,2,1,0:T(8,128)(2,1)}, bf16[2,2,2,32,1024]{4,3,2,1,0:T(8,128)(2,1)}, u32[]{:S(2)}, u32[]{:S(2)}) collective-permute-start(bf16[2,2,2,32,1024]{4,3,2,1,0:T(8,128)(2,1)} %collective-permute-done.9.refs_7_), channel_id=1, source_target_pairs={{0,1},{1,0},{2,3},{3,2},{4,5},{5,4},{6,7},{7,6},{16,17},{17,16},{1... | collective-permute-start | bytes 1572872 | tf_op jit(solution)/shard_map/their_x3/ppermute | solution.py:32
  54.2 0.8 %copy-start.15 = (bf16[2,2,2,32,1024]{4,3,2,1,0:T(8,128)(2,1)}, bf16[2,2,2,32,1024]{4,3,2,1,0:T(8,128)(2,1)S(1)}, u32[]{:S(2)}) copy-start(bf16[2,2,2,32,1024]{4,3,2,1,0:T(8,128)(2,1)S(1)} %collective-permute-done.17.refs_4_) | copy-start | bytes 1572868
  54.2 9.4 %collective-permute-start.18 = (bf16[2,2,2,32,1024]{4,3,2,1,0:T(8,128)(2,1)S(1)}, bf16[2,2,2,32,1024]{4,3,2,1,0:T(8,128)(2,1)}, u32[]{:S(2)}, u32[]{:S(2)}) collective-permute-start(bf16[2,2,2,32,1024]{4,3,2,1,0:T(8,128)(2,1)S(1)} %collective-permute-done.15.refs_5_), channel_id=1, source_target_pairs={{0,1},{1,0},{2,3},{3,2},{4,5},{5,4},{6,7},{7,6},{16,17},{17,16},{1... | collective-permute-start | bytes 1572872 | tf_op jit(solution)/shard_map/their_x1/ppermute | solution.py:32
  55.0 0.8 %copy-start.16 = (bf16[2,2,2,32,1024]{4,3,2,1,0:T(8,128)(2,1)}, bf16[2,2,2,32,1024]{4,3,2,1,0:T(8,128)(2,1)S(1)}, u32[]{:S(2)}) copy-start(bf16[2,2,2,32,1024]{4,3,2,1,0:T(8,128)(2,1)S(1)} %collective-permute-done.16.refs_3_) | copy-start | bytes 1572868
  55.8 7.8 %collective-permute-start.19 = (bf16[2,2,2,32,1024]{4,3,2,1,0:T(8,128)(2,1)S(1)}, bf16[2,2,2,32,1024]{4,3,2,1,0:T(8,128)(2,1)}, u32[]{:S(2)}, u32[]{:S(2)}) collective-permute-start(bf16[2,2,2,32,1024]{4,3,2,1,0:T(8,128)(2,1)S(1)} %collective-permute-done.12.refs_6_), channel_id=1, source_target_pairs={{0,1},{1,0},{2,3},{3,2},{4,5},{5,4},{6,7},{7,6},{16,17},{17,16},{1... | collective-permute-start | bytes 1572872 | tf_op jit(solution)/shard_map/their_x2/ppermute | solution.py:32

commit v11 on v9

--- a/solution.py
+++ b/solution.py
@@ -8,6 +8,7 @@
 BLK = 32
 STEPS = 12
 ROWS = 256
+SURFACE_ORDER = (3, 4, 5, 6, 7, 8, 9, 10, 11, 12, 13, 14, 1, 2, 15, 0)
 AXES = ("shot", "rcv")
 X, Y, Z, CORES = 4, 4, 4, 2
 
@@ -46,7 +47,7 @@
 
 
 def multiply_kernel(a_where, b_where, b_row, *refs):
-    a_refs, b_refs = refs[:16], refs[16:24]
+    a_refs, b_refs = [refs[i] for i in SURFACE_ORDER], refs[16:24]
     out, a_buf, b_buf, lhs, rhs, a_sem, b_sem = refs[24:]
     freqs = a_buf.shape[1]
     f = pl.program_id(0)
@@ -128,7 +129,7 @@
                 pltpu.SemaphoreType.DMA((2,)),
             ],
         ),
-        compiler_params=pltpu.CompilerParams(vmem_limit_bytes=56 * 1024 * 1024),
+        compiler_params=pltpu.CompilerParams(vmem_limit_bytes=52 * 1024 * 1024),
         cost_estimate=pl.CostEstimate(
             flops=2 * freqs * shots * 2 * rcvs * depth,
             bytes_accessed=20 * 1024 * 1024,
@@ -188,8 +189,8 @@
     other_x = swap("other_x", after(a_x, other))
     other_x3 = swap("other_x3", after(a_x3, other_2))
 
-    a_parts = [a, a_1, a_2, a_3, a_x, a_x1, a_x2, a_x3]
-    a_parts += [other, other_1, other_2, other_3, other_x, other_x1, other_x2, other_x3]
+    a_parts = [other_x3, other_x, other_x1, a, a_1, a_2, a_3, a_x]
+    a_parts += [a_x1, a_x2, a_x3, other, other_1, other_2, other_3, other_x2]
     b_parts = [b, b_1, b_2, b_3, b_x, b_x1, b_x2, b_x3]
     return multiply(a_parts, b_parts, a_where, b_where, b_row)
 

time: 66.6 us -> 66 us (level)
  other arithmetic: 2.46 us -> 1.36 us
  waiting for transfers between devices: 13.6 us -> 14.6 us
  local copies, waits for them, and re-layouts: 0.87 us -> 0.07 us
    ppermute x22, waiting for transfers between devices: 13.6 us -> 14.6 us  [moved(): return lax.ppermute(value, AXES, pairs)]
    unnamed x42 -> x38, local copies, waits for them, and re-layouts: 0.87 us -> 0.07 us
  transfers between devices with their start and end apart: 22 -> 22, of which waited for: 8 -> 9; matrix products, arithmetic and copies ran while one was open for 4% -> 2% of each run, Pallas kernels for 0% -> 0%
where the time goes in v11:
time: 66 us; the launch traced here: 65.6 us
  starting transfers between devices  37.5 us (57%)
  waiting for transfers between devices  14.6 us (22%)
  Pallas kernels  11.9 us (18%)
  other arithmetic  1.36 us (2%)
    ppermute x22, starting transfers between devices, moved(): return lax.ppermute(value, AXES, pairs)  37.5 us
    ppermute x22, waiting for transfers between devices, moved(): return lax.ppermute(value, AXES, pairs)  14.6 us
    pallas_call x1, Pallas kernels, multiply(): pl.pallas_call(multiply_kernel, out_shape=jax.ShapeDtypeStruct((freqs, 2,...  11.9 us
  transfers between devices with their start and end apart: 22, of which 9 were waited for; matrix products, arithmetic and copies ran while one was open for 2% of the time, Pallas kernels for 0%

profile of v11, /device:TPU:1, one launch (start us, length us, event | category | flops | bytes accessed | tf_op | source)
XLA Modules:
  0.0 65.6 jit_solution(5982787386324307486)
XLA Ops:
  0.0 2.1 %collective-permute-start = (bf16[4,2,64,512]{3,2,1,0:T(8,128)(2,1)}, bf16[4,2,64,512]{3,2,1,0:T(8,128)(2,1)S(1)}, u32[]{:S(2)}, u32[]{:S(2)}) collective-permute-start(bf16[4,2,64,512]{3,2,1,0:T(8,128)(2,1)} %refs_16_.1), channel_id=1, source_target_pairs={{0,48},{1,17},{2,50},{3,19},{4,52},{5,21},{6,54},{7,23},{16,0},{17... | collective-permute-start | bytes 1572872 | tf_op jit(solution)/shard_map/b_3/ppermute | solution.py:31
  2.1 2.7 %collective-permute-start.7 = (bf16[4,2,64,512]{3,2,1,0:T(8,128)(2,1)}, bf16[4,2,64,512]{3,2,1,0:T(8,128)(2,1)S(1)}, u32[]{:S(2)}, u32[]{:S(2)}) collective-permute-start(bf16[4,2,64,512]{3,2,1,0:T(8,128)(2,1)} %refs_16_.1), channel_id=1, source_target_pairs={{0,64},{1,65},{2,66},{3,67},{4,68},{5,69},{6,70},{7,71},{16,80},{1... | collective-permute-start | bytes 1572872 | tf_op jit(solution)/shard_map/b_x/ppermute | solution.py:31
  4.9 1.6 %collective-permute-start.6 = (bf16[4,2,32,1024]{3,2,1,0:T(8,128)(2,1)}, bf16[4,2,32,1024]{3,2,1,0:T(8,128)(2,1)S(1)}, u32[]{:S(2)}, u32[]{:S(2)}) collective-permute-start(bf16[4,2,32,1024]{3,2,1,0:T(8,128)(2,1)} %refs_3_.1), channel_id=1, source_target_pairs={{0,6},{1,3},{2,0},{3,5},{4,2},{5,7},{6,4},{7,1},{16,22},{17,19},{1... | collective-permute-start | bytes 1572872 | tf_op jit(solution)/shard_map/a_3/ppermute | solution.py:31
  6.5 1.4 %collective-permute-start.4 = (bf16[4,2,64,512]{3,2,1,0:T(8,128)(2,1)}, bf16[4,2,64,512]{3,2,1,0:T(8,128)(2,1)S(1)}, u32[]{:S(2)}, u32[]{:S(2)}) collective-permute-start(bf16[4,2,64,512]{3,2,1,0:T(8,128)(2,1)} %refs_16_.1), channel_id=1, source_target_pairs={{0,16},{1,49},{2,18},{3,51},{4,20},{5,53},{6,22},{7,55},{16,32},{1... | collective-permute-start | bytes 1572872 | tf_op jit(solution)/shard_map/b_1/ppermute | solution.py:31
  8.0 2.1 %collective-permute-start.3 = (bf16[4,2,32,1024]{3,2,1,0:T(8,128)(2,1)}, bf16[4,2,32,1024]{3,2,1,0:T(8,128)(2,1)S(1)}, u32[]{:S(2)}, u32[]{:S(2)}) collective-permute-start(bf16[4,2,32,1024]{3,2,1,0:T(8,128)(2,1)} %refs_3_.1), channel_id=1, source_target_pairs={{0,2},{1,7},{2,4},{3,1},{4,6},{5,3},{6,0},{7,5},{16,18},{17,23},{1... | collective-permute-start | bytes 1572872 | tf_op jit(solution)/shard_map/a_1/ppermute | solution.py:31
  10.1 0.7 %fusion.1 = (s32[12]{0:T(128)S(1)}, s32[12]{0:T(128)S(1)}) fusion(pred[]{:T(512)S(6)} %eq.18, s32[]{:T(128)S(6)} %select_n.83, s32[]{:T(128)S(6)} %select_n.80, s32[12]{0:T(128)} %param.5), kind=kLoop, calls=%fused_computation.25 | loop fusion | flops 612 | bytes 153 | tf_op jit(solution)/shard_map/add | solution.py:150
  10.8 0.7 %broadcast_multiply_fusion = (s32[12]{0:T(128)S(1)}, s32[12]{0:T(128)S(1)}) fusion(s32[12]{0:T(128)} %param.5, s32[12]{0:T(128)S(1)} %get-tuple-element.36, s32[]{:T(128)S(6)} %select_n.75, s32[]{:T(128)S(6)} %select_n.73, s32[]{:T(128)S(6)} %select_n.71), kind=kLoop, calls=%fused_computation.29 | loop fusion | flops 684 | bytes 204 | tf_op jit(solution)/shard_map/mul | solution.py:151
  11.4 0.0 collective-permute-done.refs_19_
  11.5 0.4 collective-permute-start.1
  11.8 3.0 %collective-permute-done.7.refs_20_ = bf16[4,2,64,512]{3,2,1,0:T(8,128)(2,1)S(1)} collective-permute-done((bf16[4,2,64,512]{3,2,1,0:T(8,128)(2,1)}, bf16[4,2,64,512]{3,2,1,0:T(8,128)(2,1)S(1)}, u32[]{:S(2)}, u32[]{:S(2)}) %collective-permute-start.7) | collective-permute-done | bytes 524320 | tf_op jit(solution)/shard_map/b_x/ppermute | solution.py:31
  14.9 0.8 %collective-permute-done.6.refs_6_ = bf16[4,2,32,1024]{3,2,1,0:T(8,128)(2,1)S(1)} collective-permute-done((bf16[4,2,32,1024]{3,2,1,0:T(8,128)(2,1)}, bf16[4,2,32,1024]{3,2,1,0:T(8,128)(2,1)S(1)}, u32[]{:S(2)}, u32[]{:S(2)}) %collective-permute-start.6) | collective-permute-done | bytes 524320 | tf_op jit(solution)/shard_map/a_3/ppermute | solution.py:31
  15.7 6.8 %collective-permute-start.8 = (bf16[4,2,32,1024]{3,2,1,0:T(8,128)(2,1)S(1)}, bf16[4,2,32,1024]{3,2,1,0:T(8,128)(2,1)S(1)}, u32[]{:S(2)}, u32[]{:S(2)}) collective-permute-start(bf16[4,2,32,1024]{3,2,1,0:T(8,128)(2,1)S(1)} %collective-permute-done.6.refs_6_), channel_id=1, source_target_pairs={{0,1},{1,0},{2,3},{3,2},{4,5},{5,4},{6,7},{7,6},{16,17},{17,16},{1... | collective-permute-start | bytes 1572872 | tf_op jit(solution)/shard_map/other_3/ppermute | solution.py:31
  22.5 1.5 %collective-permute-start.17 = (bf16[4,2,64,512]{3,2,1,0:T(8,128)(2,1)S(1)}, bf16[4,2,64,512]{3,2,1,0:T(8,128)(2,1)S(1)}, u32[]{:S(2)}, u32[]{:S(2)}) collective-permute-start(bf16[4,2,64,512]{3,2,1,0:T(8,128)(2,1)S(1)} %collective-permute-done.7.refs_20_), channel_id=1, source_target_pairs={{0,16},{1,49},{2,18},{3,51},{4,20},{5,53},{6,22},{7,55},{16,32},{1... | collective-permute-start | bytes 1572872 | tf_op jit(solution)/shard_map/b_x1/ppermute | solution.py:31
  24.0 0.0 collective-permute-done.4.refs_17_
  24.0 0.0 collective-permute-done.3.refs_4_
  24.0 3.4 %collective-permute-start.5 = (bf16[4,2,32,1024]{3,2,1,0:T(8,128)(2,1)S(1)}, bf16[4,2,32,1024]{3,2,1,0:T(8,128)(2,1)S(1)}, u32[]{:S(2)}, u32[]{:S(2)}) collective-permute-start(bf16[4,2,32,1024]{3,2,1,0:T(8,128)(2,1)S(1)} %collective-permute-done.3.refs_4_), channel_id=1, source_target_pairs={{0,2},{1,7},{2,4},{3,1},{4,6},{5,3},{6,0},{7,5},{16,18},{17,23},{1... | collective-permute-start | bytes 1572872 | tf_op jit(solution)/shard_map/a_2/ppermute | solution.py:31
  27.4 0.0 collective-permute-start.14
  27.4 0.0 collective-permute-done.1.refs_7_
  27.4 0.4 collective-permute-start.2
  27.8 0.0 collective-permute-done.8.refs_14_
  27.8 2.4 %collective-permute-start.9 = (bf16[4,2,64,512]{3,2,1,0:T(8,128)(2,1)S(1)}, bf16[4,2,64,512]{3,2,1,0:T(8,128)(2,1)S(1)}, u32[]{:S(2)}, u32[]{:S(2)}) collective-permute-start(bf16[4,2,64,512]{3,2,1,0:T(8,128)(2,1)S(1)} %collective-permute-done.4.refs_17_), channel_id=1, source_target_pairs={{0,16},{1,49},{2,18},{3,51},{4,20},{5,53},{6,22},{7,55},{16,32},{1... | collective-permute-start | bytes 1572872 | tf_op jit(solution)/shard_map/b_2/ppermute | solution.py:31
  30.3 3.7 %collective-permute-done.17.refs_21_ = bf16[4,2,64,512]{3,2,1,0:T(8,128)(2,1)S(1)} collective-permute-done((bf16[4,2,64,512]{3,2,1,0:T(8,128)(2,1)S(1)}, bf16[4,2,64,512]{3,2,1,0:T(8,128)(2,1)S(1)}, u32[]{:S(2)}, u32[]{:S(2)}) %collective-permute-start.17) | collective-permute-done | bytes 524320 | tf_op jit(solution)/shard_map/b_x1/ppermute | solution.py:31
  33.9 0.0 collective-permute-done.5.refs_5_
  33.9 0.4 collective-permute-start.18
  34.3 1.2 %collective-permute-start.20 = (bf16[4,2,64,512]{3,2,1,0:T(8,128)(2,1)S(1)}, bf16[4,2,64,512]{3,2,1,0:T(8,128)(2,1)S(1)}, u32[]{:S(2)}, u32[]{:S(2)}) collective-permute-start(bf16[4,2,64,512]{3,2,1,0:T(8,128)(2,1)S(1)} %collective-permute-done.17.refs_21_), channel_id=1, source_target_pairs={{0,16},{1,49},{2,18},{3,51},{4,20},{5,53},{6,22},{7,55},{16,32},{1... | collective-permute-start | bytes 1572872 | tf_op jit(solution)/shard_map/b_x2/ppermute | solution.py:31
  35.5 2.8 %collective-permute-done.14.refs_23_ = bf16[4,2,64,512]{3,2,1,0:T(8,128)(2,1)S(1)} collective-permute-done((bf16[4,2,64,512]{3,2,1,0:T(8,128)(2,1)S(1)}, bf16[4,2,64,512]{3,2,1,0:T(8,128)(2,1)S(1)}, u32[]{:S(2)}, u32[]{:S(2)}) %collective-permute-start.14) | collective-permute-done | bytes 524320 | tf_op jit(solution)/shard_map/b_x3/ppermute | solution.py:31
  38.3 4.3 %collective-permute-start.15 = (bf16[4,2,32,1024]{3,2,1,0:T(8,128)(2,1)S(1)}, bf16[4,2,32,1024]{3,2,1,0:T(8,128)(2,1)S(1)}, u32[]{:S(2)}, u32[]{:S(2)}) collective-permute-start(bf16[4,2,32,1024]{3,2,1,0:T(8,128)(2,1)S(1)} %collective-permute-done.1.refs_7_), channel_id=1, source_target_pairs={{0,2},{1,7},{2,4},{3,1},{4,6},{5,3},{6,0},{7,5},{16,18},{17,23},{1... | collective-permute-start | bytes 1572872 | tf_op jit(solution)/shard_map/a_x1/ppermute | solution.py:31
  42.6 0.0 collective-permute-done.2.refs_10_
  42.7 0.0 collective-permute-start.12
  42.7 0.0 collective-permute-done.9.refs_18_
  42.7 1.5 %collective-permute-start.10 = (bf16[4,2,32,1024]{3,2,1,0:T(8,128)(2,1)S(1)}, bf16[4,2,32,1024]{3,2,1,0:T(8,128)(2,1)S(1)}, u32[]{:S(2)}, u32[]{:S(2)}) collective-permute-start(bf16[4,2,32,1024]{3,2,1,0:T(8,128)(2,1)S(1)} %collective-permute-done.5.refs_5_), channel_id=1, source_target_pairs={{0,1},{1,0},{2,3},{3,2},{4,5},{5,4},{6,7},{7,6},{16,17},{17,16},{1... | collective-permute-start | bytes 1572872 | tf_op jit(solution)/shard_map/other_2/ppermute | solution.py:31
  44.2 1.8 %collective-permute-done.18.refs_9_ = bf16[4,2,32,1024]{3,2,1,0:T(8,128)(2,1)S(1)} collective-permute-done((bf16[4,2,32,1024]{3,2,1,0:T(8,128)(2,1)S(1)}, bf16[4,2,32,1024]{3,2,1,0:T(8,128)(2,1)S(1)}, u32[]{:S(2)}, u32[]{:S(2)}) %collective-permute-start.18) | collective-permute-done | bytes 524320 | tf_op jit(solution)/shard_map/a_x2/ppermute | solution.py:31
  45.9 2.4 %collective-permute-start.19 = (bf16[4,2,32,1024]{3,2,1,0:T(8,128)(2,1)S(1)}, bf16[4,2,32,1024]{3,2,1,0:T(8,128)(2,1)S(1)}, u32[]{:S(2)}, u32[]{:S(2)}) collective-permute-start(bf16[4,2,32,1024]{3,2,1,0:T(8,128)(2,1)S(1)} %collective-permute-done.3.refs_4_), channel_id=1, source_target_pairs={{0,1},{1,0},{2,3},{3,2},{4,5},{5,4},{6,7},{7,6},{16,17},{17,16},{1... | collective-permute-start | bytes 1572872 | tf_op jit(solution)/shard_map/other_1/ppermute | solution.py:31
  48.4 0.0 collective-permute-done.20.refs_22_
  48.4 1.4 %collective-permute-start.21 = (bf16[4,2,32,1024]{3,2,1,0:T(8,128)(2,1)S(1)}, bf16[4,2,32,1024]{3,2,1,0:T(8,128)(2,1)S(1)}, u32[]{:S(2)}, u32[]{:S(2)}) collective-permute-start(bf16[4,2,32,1024]{3,2,1,0:T(8,128)(2,1)S(1)} %collective-permute-done.18.refs_9_), channel_id=1, source_target_pairs={{0,1},{1,0},{2,3},{3,2},{4,5},{5,4},{6,7},{7,6},{16,17},{17,16},{1... | collective-permute-start | bytes 1572872 | tf_op jit(solution)/shard_map/other_x2/ppermute | solution.py:31
  49.8 0.0 collective-permute-done.15.refs_8_
  49.8 0.7 %collective-permute-start.16 = (bf16[4,2,32,1024]{3,2,1,0:T(8,128)(2,1)S(1)}, bf16[4,2,32,1024]{3,2,1,0:T(8,128)(2,1)S(1)}, u32[]{:S(2)}, u32[]{:S(2)}) collective-permute-start(bf16[4,2,32,1024]{3,2,1,0:T(8,128)(2,1)S(1)} %collective-permute-done.15.refs_8_), channel_id=1, source_target_pairs={{0,1},{1,0},{2,3},{3,2},{4,5},{5,4},{6,7},{7,6},{16,17},{17,16},{1... | collective-permute-start | bytes 1572872 | tf_op jit(solution)/shard_map/other_x1/ppermute | solution.py:31
  50.5 0.0 collective-permute-done.12.refs_11_
  50.5 0.1 collective-permute-start.13
  50.6 0.0 collective-permute-done.10.refs_13_
  50.6 0.4 collective-permute-start.11
  51.0 0.0 collective-permute-done.19.refs_12_
  51.1 0.3 collective-permute-done.21.refs_15_
  51.3 0.7 %collective-permute-done.16.refs_2_ = bf16[4,2,32,1024]{3,2,1,0:T(8,128)(2,1)S(1)} collective-permute-done((bf16[4,2,32,1024]{3,2,1,0:T(8,128)(2,1)S(1)}, bf16[4,2,32,1024]{3,2,1,0:T(8,128)(2,1)S(1)}, u32[]{:S(2)}, u32[]{:S(2)}) %collective-permute-start.16) | collective-permute-done | bytes 524320 | tf_op jit(solution)/shard_map/other_x1/ppermute | solution.py:31
  52.1 0.7 %collective-permute-done.13.refs_1_ = bf16[4,2,32,1024]{3,2,1,0:T(8,128)(2,1)S(1)} collective-permute-done((bf16[4,2,32,1024]{3,2,1,0:T(8,128)(2,1)S(1)}, bf16[4,2,32,1024]{3,2,1,0:T(8,128)(2,1)S(1)}, u32[]{:S(2)}, u32[]{:S(2)}) %collective-permute-start.13) | collective-permute-done | bytes 524320 | tf_op jit(solution)/shard_map/other_x/ppermute | solution.py:31
  52.8 0.7 %collective-permute-done.11.refs_0_ = bf16[4,2,32,1024]{3,2,1,0:T(8,128)(2,1)S(1)} collective-permute-done((bf16[4,2,32,1024]{3,2,1,0:T(8,128)(2,1)S(1)}, bf16[4,2,32,1024]{3,2,1,0:T(8,128)(2,1)S(1)}, u32[]{:S(2)}, u32[]{:S(2)}) %collective-permute-start.11) | collective-permute-done | bytes 524320 | tf_op jit(solution)/shard_map/other_x3/ppermute | solution.py:31
  53.6 0.0 copy-done.1
  53.7 11.9 %shard_map.37 = bf16[4,2,1024,512]{3,2,1,0:T(8,128)(2,1)} custom-call(s32[12]{0:T(128)S(1)} %get-tuple-element.38.a_where, s32[12]{0:T(128)S(1)} %get-tuple-element.35.b_where, s32[12]{0:T(128)S(1)} %get-tuple-element.37.b_row, bf16[4,2,32,1024]{3,2,1,0:T(8,128)(2,1)S(1)} %collective-permute-done.11.refs_0_, ...), custom_call_target="tpu_custom_call" | custom-call | flops 6442450944 | bytes 20971520 | tf_op jit(solution)/shard_map/pallas_call | solution.py:115
  (37 shorter events, 0.1 us)
Async XLA Ops:
  0.0 11.4 %collective-permute-start = (bf16[4,2,64,512]{3,2,1,0:T(8,128)(2,1)}, bf16[4,2,64,512]{3,2,1,0:T(8,128)(2,1)S(1)}, u32[]{:S(2)}, u32[]{:S(2)}) collective-permute-start(bf16[4,2,64,512]{3,2,1,0:T(8,128)(2,1)} %refs_16_.1), channel_id=1, source_target_pairs={{0,48},{1,17},{2,50},{3,19},{4,52},{5,21},{6,54},{7,23},{16,0},{17... | collective-permute-start | bytes 1572872 | tf_op jit(solution)/shard_map/b_3/ppermute | solution.py:31
  2.1 12.7 %collective-permute-start.7 = (bf16[4,2,64,512]{3,2,1,0:T(8,128)(2,1)}, bf16[4,2,64,512]{3,2,1,0:T(8,128)(2,1)S(1)}, u32[]{:S(2)}, u32[]{:S(2)}) collective-permute-start(bf16[4,2,64,512]{3,2,1,0:T(8,128)(2,1)} %refs_16_.1), channel_id=1, source_target_pairs={{0,64},{1,65},{2,66},{3,67},{4,68},{5,69},{6,70},{7,71},{16,80},{1... | collective-permute-start | bytes 1572872 | tf_op jit(solution)/shard_map/b_x/ppermute | solution.py:31
  4.9 10.8 %collective-permute-start.6 = (bf16[4,2,32,1024]{3,2,1,0:T(8,128)(2,1)}, bf16[4,2,32,1024]{3,2,1,0:T(8,128)(2,1)S(1)}, u32[]{:S(2)}, u32[]{:S(2)}) collective-permute-start(bf16[4,2,32,1024]{3,2,1,0:T(8,128)(2,1)} %refs_3_.1), channel_id=1, source_target_pairs={{0,6},{1,3},{2,0},{3,5},{4,2},{5,7},{6,4},{7,1},{16,22},{17,19},{1... | collective-permute-start | bytes 1572872 | tf_op jit(solution)/shard_map/a_3/ppermute | solution.py:31
  6.5 17.5 %collective-permute-start.4 = (bf16[4,2,64,512]{3,2,1,0:T(8,128)(2,1)}, bf16[4,2,64,512]{3,2,1,0:T(8,128)(2,1)S(1)}, u32[]{:S(2)}, u32[]{:S(2)}) collective-permute-start(bf16[4,2,64,512]{3,2,1,0:T(8,128)(2,1)} %refs_16_.1), channel_id=1, source_target_pairs={{0,16},{1,49},{2,18},{3,51},{4,20},{5,53},{6,22},{7,55},{16,32},{1... | collective-permute-start | bytes 1572872 | tf_op jit(solution)/shard_map/b_1/ppermute | solution.py:31
  8.0 16.1 %collective-permute-start.3 = (bf16[4,2,32,1024]{3,2,1,0:T(8,128)(2,1)}, bf16[4,2,32,1024]{3,2,1,0:T(8,128)(2,1)S(1)}, u32[]{:S(2)}, u32[]{:S(2)}) collective-permute-start(bf16[4,2,32,1024]{3,2,1,0:T(8,128)(2,1)} %refs_3_.1), channel_id=1, source_target_pairs={{0,2},{1,7},{2,4},{3,1},{4,6},{5,3},{6,0},{7,5},{16,18},{17,23},{1... | collective-permute-start | bytes 1572872 | tf_op jit(solution)/shard_map/a_1/ppermute | solution.py:31
  11.4 42.1 %copy-start = (bf16[4,2,64,512]{3,2,1,0:T(8,128)(2,1)}, bf16[4,2,64,512]{3,2,1,0:T(8,128)(2,1)S(1)}, u32[]{:S(2)}) copy-start(bf16[4,2,64,512]{3,2,1,0:T(8,128)(2,1)S(1)} %collective-permute-done.refs_19_) | copy-start | bytes 1572868
  11.5 15.9 %collective-permute-start.1 = (bf16[4,2,32,1024]{3,2,1,0:T(8,128)(2,1)}, bf16[4,2,32,1024]{3,2,1,0:T(8,128)(2,1)S(1)}, u32[]{:S(2)}, u32[]{:S(2)}) collective-permute-start(bf16[4,2,32,1024]{3,2,1,0:T(8,128)(2,1)} %refs_3_.1), channel_id=1, source_target_pairs={{0,8},{1,9},{2,10},{3,11},{4,12},{5,13},{6,14},{7,15},{16,24},{17,... | collective-permute-start | bytes 1572872 | tf_op jit(solution)/shard_map/a_x/ppermute | solution.py:31
  14.9 38.7 %copy-start.1 = (bf16[4,2,64,512]{3,2,1,0:T(8,128)(2,1)}, bf16[4,2,64,512]{3,2,1,0:T(8,128)(2,1)S(1)}, u32[]{:S(2)}) copy-start(bf16[4,2,64,512]{3,2,1,0:T(8,128)(2,1)S(1)} %collective-permute-done.7.refs_20_) | copy-start | bytes 1572868
  15.7 37.9 %copy-start.2 = (bf16[4,2,32,1024]{3,2,1,0:T(8,128)(2,1)}, bf16[4,2,32,1024]{3,2,1,0:T(8,128)(2,1)S(1)}, u32[]{:S(2)}) copy-start(bf16[4,2,32,1024]{3,2,1,0:T(8,128)(2,1)S(1)} %collective-permute-done.6.refs_6_) | copy-start | bytes 1572868
  15.7 12.1 %collective-permute-start.8 = (bf16[4,2,32,1024]{3,2,1,0:T(8,128)(2,1)S(1)}, bf16[4,2,32,1024]{3,2,1,0:T(8,128)(2,1)S(1)}, u32[]{:S(2)}, u32[]{:S(2)}) collective-permute-start(bf16[4,2,32,1024]{3,2,1,0:T(8,128)(2,1)S(1)} %collective-permute-done.6.refs_6_), channel_id=1, source_target_pairs={{0,1},{1,0},{2,3},{3,2},{4,5},{5,4},{6,7},{7,6},{16,17},{17,16},{1... | collective-permute-start | bytes 1572872 | tf_op jit(solution)/shard_map/other_3/ppermute | solution.py:31
  22.5 11.4 %collective-permute-start.17 = (bf16[4,2,64,512]{3,2,1,0:T(8,128)(2,1)S(1)}, bf16[4,2,64,512]{3,2,1,0:T(8,128)(2,1)S(1)}, u32[]{:S(2)}, u32[]{:S(2)}) collective-permute-start(bf16[4,2,64,512]{3,2,1,0:T(8,128)(2,1)S(1)} %collective-permute-done.7.refs_20_), channel_id=1, source_target_pairs={{0,16},{1,49},{2,18},{3,51},{4,20},{5,53},{6,22},{7,55},{16,32},{1... | collective-permute-start | bytes 1572872 | tf_op jit(solution)/shard_map/b_x1/ppermute | solution.py:31
  24.0 29.6 %copy-start.3 = (bf16[4,2,64,512]{3,2,1,0:T(8,128)(2,1)}, bf16[4,2,64,512]{3,2,1,0:T(8,128)(2,1)S(1)}, u32[]{:S(2)}) copy-start(bf16[4,2,64,512]{3,2,1,0:T(8,128)(2,1)S(1)} %collective-permute-done.4.refs_17_) | copy-start | bytes 1572868
  24.0 29.6 %copy-start.4 = (bf16[4,2,32,1024]{3,2,1,0:T(8,128)(2,1)}, bf16[4,2,32,1024]{3,2,1,0:T(8,128)(2,1)S(1)}, u32[]{:S(2)}) copy-start(bf16[4,2,32,1024]{3,2,1,0:T(8,128)(2,1)S(1)} %collective-permute-done.3.refs_4_) | copy-start | bytes 1572868
  24.0 9.9 %collective-permute-start.5 = (bf16[4,2,32,1024]{3,2,1,0:T(8,128)(2,1)S(1)}, bf16[4,2,32,1024]{3,2,1,0:T(8,128)(2,1)S(1)}, u32[]{:S(2)}, u32[]{:S(2)}) collective-permute-start(bf16[4,2,32,1024]{3,2,1,0:T(8,128)(2,1)S(1)} %collective-permute-done.3.refs_4_), channel_id=1, source_target_pairs={{0,2},{1,7},{2,4},{3,1},{4,6},{5,3},{6,0},{7,5},{16,18},{17,23},{1... | collective-permute-start | bytes 1572872 | tf_op jit(solution)/shard_map/a_2/ppermute | solution.py:31
  27.4 10.9 %collective-permute-start.14 = (bf16[4,2,64,512]{3,2,1,0:T(8,128)(2,1)S(1)}, bf16[4,2,64,512]{3,2,1,0:T(8,128)(2,1)S(1)}, u32[]{:S(2)}, u32[]{:S(2)}) collective-permute-start(bf16[4,2,64,512]{3,2,1,0:T(8,128)(2,1)S(1)} %collective-permute-done.7.refs_20_), channel_id=1, source_target_pairs={{0,48},{1,17},{2,50},{3,19},{4,52},{5,21},{6,54},{7,23},{16,0},{17... | collective-permute-start | bytes 1572872 | tf_op jit(solution)/shard_map/b_x3/ppermute | solution.py:31
  27.4 26.2 %copy-start.5 = (bf16[4,2,32,1024]{3,2,1,0:T(8,128)(2,1)}, bf16[4,2,32,1024]{3,2,1,0:T(8,128)(2,1)S(1)}, u32[]{:S(2)}) copy-start(bf16[4,2,32,1024]{3,2,1,0:T(8,128)(2,1)S(1)} %collective-permute-done.1.refs_7_) | copy-start | bytes 1572868
  27.4 15.2 %collective-permute-start.2 = (bf16[4,2,32,1024]{3,2,1,0:T(8,128)(2,1)S(1)}, bf16[4,2,32,1024]{3,2,1,0:T(8,128)(2,1)S(1)}, u32[]{:S(2)}, u32[]{:S(2)}) collective-permute-start(bf16[4,2,32,1024]{3,2,1,0:T(8,128)(2,1)S(1)} %collective-permute-done.1.refs_7_), channel_id=1, source_target_pairs={{0,6},{1,3},{2,0},{3,5},{4,2},{5,7},{6,4},{7,1},{16,22},{17,19},{1... | collective-permute-start | bytes 1572872 | tf_op jit(solution)/shard_map/a_x3/ppermute | solution.py:31
  27.8 25.8 %copy-start.6 = (bf16[4,2,32,1024]{3,2,1,0:T(8,128)(2,1)}, bf16[4,2,32,1024]{3,2,1,0:T(8,128)(2,1)S(1)}, u32[]{:S(2)}) copy-start(bf16[4,2,32,1024]{3,2,1,0:T(8,128)(2,1)S(1)} %collective-permute-done.8.refs_14_) | copy-start | bytes 1572868
  27.8 14.8 %collective-permute-start.9 = (bf16[4,2,64,512]{3,2,1,0:T(8,128)(2,1)S(1)}, bf16[4,2,64,512]{3,2,1,0:T(8,128)(2,1)S(1)}, u32[]{:S(2)}, u32[]{:S(2)}) collective-permute-start(bf16[4,2,64,512]{3,2,1,0:T(8,128)(2,1)S(1)} %collective-permute-done.4.refs_17_), channel_id=1, source_target_pairs={{0,16},{1,49},{2,18},{3,51},{4,20},{5,53},{6,22},{7,55},{16,32},{1... | collective-permute-start | bytes 1572872 | tf_op jit(solution)/shard_map/b_2/ppermute | solution.py:31
  33.9 19.7 %copy-start.7 = (bf16[4,2,64,512]{3,2,1,0:T(8,128)(2,1)}, bf16[4,2,64,512]{3,2,1,0:T(8,128)(2,1)S(1)}, u32[]{:S(2)}) copy-start(bf16[4,2,64,512]{3,2,1,0:T(8,128)(2,1)S(1)} %collective-permute-done.17.refs_21_) | copy-start | bytes 1572868
  33.9 19.7 %copy-start.8 = (bf16[4,2,32,1024]{3,2,1,0:T(8,128)(2,1)}, bf16[4,2,32,1024]{3,2,1,0:T(8,128)(2,1)S(1)}, u32[]{:S(2)}) copy-start(bf16[4,2,32,1024]{3,2,1,0:T(8,128)(2,1)S(1)} %collective-permute-done.5.refs_5_) | copy-start | bytes 1572868
  33.9 12.0 %collective-permute-start.18 = (bf16[4,2,32,1024]{3,2,1,0:T(8,128)(2,1)S(1)}, bf16[4,2,32,1024]{3,2,1,0:T(8,128)(2,1)S(1)}, u32[]{:S(2)}, u32[]{:S(2)}) collective-permute-start(bf16[4,2,32,1024]{3,2,1,0:T(8,128)(2,1)S(1)} %collective-permute-done.5.refs_5_), channel_id=1, source_target_pairs={{0,8},{1,9},{2,10},{3,11},{4,12},{5,13},{6,14},{7,15},{16,24},{17,... | collective-permute-start | bytes 1572872 | tf_op jit(solution)/shard_map/a_x2/ppermute | solution.py:31
  34.3 14.0 %collective-permute-start.20 = (bf16[4,2,64,512]{3,2,1,0:T(8,128)(2,1)S(1)}, bf16[4,2,64,512]{3,2,1,0:T(8,128)(2,1)S(1)}, u32[]{:S(2)}, u32[]{:S(2)}) collective-permute-start(bf16[4,2,64,512]{3,2,1,0:T(8,128)(2,1)S(1)} %collective-permute-done.17.refs_21_), channel_id=1, source_target_pairs={{0,16},{1,49},{2,18},{3,51},{4,20},{5,53},{6,22},{7,55},{16,32},{1... | collective-permute-start | bytes 1572872 | tf_op jit(solution)/shard_map/b_x2/ppermute | solution.py:31
  38.3 15.3 %copy-start.9 = (bf16[4,2,64,512]{3,2,1,0:T(8,128)(2,1)}, bf16[4,2,64,512]{3,2,1,0:T(8,128)(2,1)S(1)}, u32[]{:S(2)}) copy-start(bf16[4,2,64,512]{3,2,1,0:T(8,128)(2,1)S(1)} %collective-permute-done.14.refs_23_) | copy-start | bytes 1572868
  38.3 11.5 %collective-permute-start.15 = (bf16[4,2,32,1024]{3,2,1,0:T(8,128)(2,1)S(1)}, bf16[4,2,32,1024]{3,2,1,0:T(8,128)(2,1)S(1)}, u32[]{:S(2)}, u32[]{:S(2)}) collective-permute-start(bf16[4,2,32,1024]{3,2,1,0:T(8,128)(2,1)S(1)} %collective-permute-done.1.refs_7_), channel_id=1, source_target_pairs={{0,2},{1,7},{2,4},{3,1},{4,6},{5,3},{6,0},{7,5},{16,18},{17,23},{1... | collective-permute-start | bytes 1572872 | tf_op jit(solution)/shard_map/a_x1/ppermute | solution.py:31
  42.7 11.0 %copy-start.10 = (bf16[4,2,32,1024]{3,2,1,0:T(8,128)(2,1)}, bf16[4,2,32,1024]{3,2,1,0:T(8,128)(2,1)S(1)}, u32[]{:S(2)}) copy-start(bf16[4,2,32,1024]{3,2,1,0:T(8,128)(2,1)S(1)} %collective-permute-done.2.refs_10_) | copy-start | bytes 1572868
  42.7 7.9 %collective-permute-start.12 = (bf16[4,2,32,1024]{3,2,1,0:T(8,128)(2,1)}, bf16[4,2,32,1024]{3,2,1,0:T(8,128)(2,1)S(1)}, u32[]{:S(2)}, u32[]{:S(2)}) collective-permute-start(bf16[4,2,32,1024]{3,2,1,0:T(8,128)(2,1)} %refs_3_.1), channel_id=1, source_target_pairs={{0,1},{1,0},{2,3},{3,2},{4,5},{5,4},{6,7},{7,6},{16,17},{17,16},{1... | collective-permute-start | bytes 1572872 | tf_op jit(solution)/shard_map/other/ppermute | solution.py:31
  42.7 11.0 %copy-start.11 = (bf16[4,2,64,512]{3,2,1,0:T(8,128)(2,1)}, bf16[4,2,64,512]{3,2,1,0:T(8,128)(2,1)S(1)}, u32[]{:S(2)}) copy-start(bf16[4,2,64,512]{3,2,1,0:T(8,128)(2,1)S(1)} %collective-permute-done.9.refs_18_) | copy-start | bytes 1572868
  42.7 7.9 %collective-permute-start.10 = (bf16[4,2,32,1024]{3,2,1,0:T(8,128)(2,1)S(1)}, bf16[4,2,32,1024]{3,2,1,0:T(8,128)(2,1)S(1)}, u32[]{:S(2)}, u32[]{:S(2)}) collective-permute-start(bf16[4,2,32,1024]{3,2,1,0:T(8,128)(2,1)S(1)} %collective-permute-done.5.refs_5_), channel_id=1, source_target_pairs={{0,1},{1,0},{2,3},{3,2},{4,5},{5,4},{6,7},{7,6},{16,17},{17,16},{1... | collective-permute-start | bytes 1572872 | tf_op jit(solution)/shard_map/other_2/ppermute | solution.py:31
  45.9 7.7 %copy-start.12 = (bf16[4,2,32,1024]{3,2,1,0:T(8,128)(2,1)}, bf16[4,2,32,1024]{3,2,1,0:T(8,128)(2,1)S(1)}, u32[]{:S(2)}) copy-start(bf16[4,2,32,1024]{3,2,1,0:T(8,128)(2,1)S(1)} %collective-permute-done.18.refs_9_) | copy-start | bytes 1572868
  45.9 5.1 %collective-permute-start.19 = (bf16[4,2,32,1024]{3,2,1,0:T(8,128)(2,1)S(1)}, bf16[4,2,32,1024]{3,2,1,0:T(8,128)(2,1)S(1)}, u32[]{:S(2)}, u32[]{:S(2)}) collective-permute-start(bf16[4,2,32,1024]{3,2,1,0:T(8,128)(2,1)S(1)} %collective-permute-done.3.refs_4_), channel_id=1, source_target_pairs={{0,1},{1,0},{2,3},{3,2},{4,5},{5,4},{6,7},{7,6},{16,17},{17,16},{1... | collective-permute-start | bytes 1572872 | tf_op jit(solution)/shard_map/other_1/ppermute | solution.py:31
  48.4 5.3 %copy-start.13 = (bf16[4,2,64,512]{3,2,1,0:T(8,128)(2,1)}, bf16[4,2,64,512]{3,2,1,0:T(8,128)(2,1)S(1)}, u32[]{:S(2)}) copy-start(bf16[4,2,64,512]{3,2,1,0:T(8,128)(2,1)S(1)} %collective-permute-done.20.refs_22_) | copy-start | bytes 1572868
  48.4 3.0 %collective-permute-start.21 = (bf16[4,2,32,1024]{3,2,1,0:T(8,128)(2,1)S(1)}, bf16[4,2,32,1024]{3,2,1,0:T(8,128)(2,1)S(1)}, u32[]{:S(2)}, u32[]{:S(2)}) collective-permute-start(bf16[4,2,32,1024]{3,2,1,0:T(8,128)(2,1)S(1)} %collective-permute-done.18.refs_9_), channel_id=1, source_target_pairs={{0,1},{1,0},{2,3},{3,2},{4,5},{5,4},{6,7},{7,6},{16,17},{17,16},{1... | collective-permute-start | bytes 1572872 | tf_op jit(solution)/shard_map/other_x2/ppermute | solution.py:31
  49.8 3.9 %copy-start.14 = (bf16[4,2,32,1024]{3,2,1,0:T(8,128)(2,1)}, bf16[4,2,32,1024]{3,2,1,0:T(8,128)(2,1)S(1)}, u32[]{:S(2)}) copy-start(bf16[4,2,32,1024]{3,2,1,0:T(8,128)(2,1)S(1)} %collective-permute-done.15.refs_8_) | copy-start | bytes 1572868
  49.8 2.3 %collective-permute-start.16 = (bf16[4,2,32,1024]{3,2,1,0:T(8,128)(2,1)S(1)}, bf16[4,2,32,1024]{3,2,1,0:T(8,128)(2,1)S(1)}, u32[]{:S(2)}, u32[]{:S(2)}) collective-permute-start(bf16[4,2,32,1024]{3,2,1,0:T(8,128)(2,1)S(1)} %collective-permute-done.15.refs_8_), channel_id=1, source_target_pairs={{0,1},{1,0},{2,3},{3,2},{4,5},{5,4},{6,7},{7,6},{16,17},{17,16},{1... | collective-permute-start | bytes 1572872 | tf_op jit(solution)/shard_map/other_x1/ppermute | solution.py:31
  50.5 3.2 %copy-start.15 = (bf16[4,2,32,1024]{3,2,1,0:T(8,128)(2,1)}, bf16[4,2,32,1024]{3,2,1,0:T(8,128)(2,1)S(1)}, u32[]{:S(2)}) copy-start(bf16[4,2,32,1024]{3,2,1,0:T(8,128)(2,1)S(1)} %collective-permute-done.12.refs_11_) | copy-start | bytes 1572868
  50.5 2.3 %collective-permute-start.13 = (bf16[4,2,32,1024]{3,2,1,0:T(8,128)(2,1)S(1)}, bf16[4,2,32,1024]{3,2,1,0:T(8,128)(2,1)S(1)}, u32[]{:S(2)}, u32[]{:S(2)}) collective-permute-start(bf16[4,2,32,1024]{3,2,1,0:T(8,128)(2,1)S(1)} %collective-permute-done.1.refs_7_), channel_id=1, source_target_pairs={{0,1},{1,0},{2,3},{3,2},{4,5},{5,4},{6,7},{7,6},{16,17},{17,16},{1... | collective-permute-start | bytes 1572872 | tf_op jit(solution)/shard_map/other_x/ppermute | solution.py:31
  50.6 3.1 %copy-start.16 = (bf16[4,2,32,1024]{3,2,1,0:T(8,128)(2,1)}, bf16[4,2,32,1024]{3,2,1,0:T(8,128)(2,1)S(1)}, u32[]{:S(2)}) copy-start(bf16[4,2,32,1024]{3,2,1,0:T(8,128)(2,1)S(1)} %collective-permute-done.10.refs_13_) | copy-start | bytes 1572868
  50.6 2.9 %collective-permute-start.11 = (bf16[4,2,32,1024]{3,2,1,0:T(8,128)(2,1)S(1)}, bf16[4,2,32,1024]{3,2,1,0:T(8,128)(2,1)S(1)}, u32[]{:S(2)}, u32[]{:S(2)}) collective-permute-start(bf16[4,2,32,1024]{3,2,1,0:T(8,128)(2,1)S(1)} %collective-permute-done.2.refs_10_), channel_id=1, source_target_pairs={{0,1},{1,0},{2,3},{3,2},{4,5},{5,4},{6,7},{7,6},{16,17},{17,16},{1... | collective-permute-start | bytes 1572872 | tf_op jit(solution)/shard_map/other_x3/ppermute | solution.py:31
  51.1 2.7 %copy-start.17 = (bf16[4,2,32,1024]{3,2,1,0:T(8,128)(2,1)}, bf16[4,2,32,1024]{3,2,1,0:T(8,128)(2,1)S(1)}, u32[]{:S(2)}) copy-start(bf16[4,2,32,1024]{3,2,1,0:T(8,128)(2,1)S(1)} %collective-permute-done.19.refs_12_) | copy-start | bytes 1572868
  51.3 2.4 %copy-start.18 = (bf16[4,2,32,1024]{3,2,1,0:T(8,128)(2,1)}, bf16[4,2,32,1024]{3,2,1,0:T(8,128)(2,1)S(1)}, u32[]{:S(2)}) copy-start(bf16[4,2,32,1024]{3,2,1,0:T(8,128)(2,1)S(1)} %collective-permute-done.21.refs_15_) | copy-start | bytes 1572868

commit v12 on v8

--- a/solution.py
+++ b/solution.py
@@ -176,7 +176,7 @@
     a_2 = send("a_2", after(a_1, b_1), dz=1)
     b_x3 = send("b_x3", after(b_x, a_1), dy=-1)
     b_2 = send("b_2", after(b_1, a_x), dy=1)
-    a_x3 = send("a_x3", after(a_x, other_3, b_x1), dz=-1)
+    a_x3 = send("a_x3", after(a_x, other_3), dz=-1)
     a_x2 = send("a_x2", after(a_2, b_x1), flip_x=True)
     b_x2 = send("b_x2", after(b_x1, a_2), dy=1)
     a_x1 = send("a_x1", after(a_x, b_x3), dz=1)

time: 72.1 us -> 67.5 us (0.936)
  starting transfers between devices: 41.6 us -> 31.2 us
  waiting for transfers between devices: 14.9 us -> 20.6 us
    ppermute x22, starting transfers between devices: 41.6 us -> 31.2 us  [moved(): return lax.ppermute(value, AXES, pairs)]
    ppermute x22, waiting for transfers between devices: 14.9 us -> 20.6 us  [moved(): return lax.ppermute(value, AXES, pairs)]
  transfers between devices with their start and end apart: 22 -> 22, of which waited for: 9 -> 9; matrix products, arithmetic and copies ran while one was open for 3% -> 4% of each run, Pallas kernels for 0% -> 0%
where the time goes in v12:
time: 67.5 us; the launch traced here: 67.3 us
  starting transfers between devices  31.2 us (46%)
  waiting for transfers between devices  20.6 us (31%)
  Pallas kernels  12 us (18%)
  other arithmetic  2.46 us (4%)
  local copies, waits for them, and re-layouts  0.94 us (1%)
    ppermute x22, starting transfers between devices, moved(): return lax.ppermute(value, AXES, pairs)  31.2 us
    ppermute x22, waiting for transfers between devices, moved(): return lax.ppermute(value, AXES, pairs)  20.6 us
    pallas_call x1, Pallas kernels, multiply(): pl.pallas_call(multiply_kernel, out_shape=jax.ShapeDtypeStruct((freqs, 2,...  12 us
  transfers between devices with their start and end apart: 22, of which 9 were waited for; matrix products, arithmetic and copies ran while one was open for 4% of the time, Pallas kernels for 0%

profile of v12, /device:TPU:1, one launch (start us, length us, event | category | flops | bytes accessed | tf_op | source)
XLA Modules:
  0.0 67.3 jit_solution(13497761282722482770)
XLA Ops:
  0.0 2.1 %collective-permute-start.4 = (bf16[4,2,64,512]{3,2,1,0:T(8,128)(2,1)}, bf16[4,2,64,512]{3,2,1,0:T(8,128)(2,1)S(1)}, u32[]{:S(2)}, u32[]{:S(2)}) collective-permute-start(bf16[4,2,64,512]{3,2,1,0:T(8,128)(2,1)} %refs_16_.1), channel_id=1, source_target_pairs={{0,48},{1,17},{2,50},{3,19},{4,52},{5,21},{6,54},{7,23},{16,0},{17... | collective-permute-start | bytes 1572872 | tf_op jit(solution)/shard_map/b_3/ppermute | solution.py:30
  2.1 2.7 %collective-permute-start.6 = (bf16[4,2,64,512]{3,2,1,0:T(8,128)(2,1)}, bf16[4,2,64,512]{3,2,1,0:T(8,128)(2,1)S(1)}, u32[]{:S(2)}, u32[]{:S(2)}) collective-permute-start(bf16[4,2,64,512]{3,2,1,0:T(8,128)(2,1)} %refs_16_.1), channel_id=1, source_target_pairs={{0,64},{1,65},{2,66},{3,67},{4,68},{5,69},{6,70},{7,71},{16,80},{1... | collective-permute-start | bytes 1572872 | tf_op jit(solution)/shard_map/b_x/ppermute | solution.py:30
  4.9 1.6 %collective-permute-start.3 = (bf16[4,2,32,1024]{3,2,1,0:T(8,128)(2,1)}, bf16[4,2,32,1024]{3,2,1,0:T(8,128)(2,1)S(1)}, u32[]{:S(2)}, u32[]{:S(2)}) collective-permute-start(bf16[4,2,32,1024]{3,2,1,0:T(8,128)(2,1)} %refs_0_.1), channel_id=1, source_target_pairs={{0,6},{1,3},{2,0},{3,5},{4,2},{5,7},{6,4},{7,1},{16,22},{17,19},{1... | collective-permute-start | bytes 1572872 | tf_op jit(solution)/shard_map/a_3/ppermute | solution.py:30
  6.5 1.4 %collective-permute-start.1 = (bf16[4,2,64,512]{3,2,1,0:T(8,128)(2,1)}, bf16[4,2,64,512]{3,2,1,0:T(8,128)(2,1)S(1)}, u32[]{:S(2)}, u32[]{:S(2)}) collective-permute-start(bf16[4,2,64,512]{3,2,1,0:T(8,128)(2,1)} %refs_16_.1), channel_id=1, source_target_pairs={{0,16},{1,49},{2,18},{3,51},{4,20},{5,53},{6,22},{7,55},{16,32},{1... | collective-permute-start | bytes 1572872 | tf_op jit(solution)/shard_map/b_1/ppermute | solution.py:30
  8.0 2.1 %collective-permute-start = (bf16[4,2,32,1024]{3,2,1,0:T(8,128)(2,1)}, bf16[4,2,32,1024]{3,2,1,0:T(8,128)(2,1)S(1)}, u32[]{:S(2)}, u32[]{:S(2)}) collective-permute-start(bf16[4,2,32,1024]{3,2,1,0:T(8,128)(2,1)} %refs_0_.1), channel_id=1, source_target_pairs={{0,2},{1,7},{2,4},{3,1},{4,6},{5,3},{6,0},{7,5},{16,18},{17,23},{1... | collective-permute-start | bytes 1572872 | tf_op jit(solution)/shard_map/a_1/ppermute | solution.py:30
  10.1 1.2 %fusion.1 = (s32[12]{0:T(128)}, s32[12]{0:T(128)S(1)}) fusion(pred[]{:T(512)S(6)} %eq.18, s32[]{:T(128)S(6)} %select_n.83, s32[]{:T(128)S(6)} %select_n.80, s32[12]{0:T(128)} %param.5), kind=kLoop, calls=%fused_computation.25 | loop fusion | flops 612 | bytes 153 | tf_op jit(solution)/shard_map/add | solution.py:149
  11.3 1.2 %broadcast_multiply_fusion = (s32[12]{0:T(128)}, s32[12]{0:T(128)}) fusion(s32[12]{0:T(128)} %param.5, s32[12]{0:T(128)S(1)} %get-tuple-element.36, s32[]{:T(128)S(6)} %select_n.75, s32[]{:T(128)S(6)} %select_n.73, s32[]{:T(128)S(6)} %select_n.71), kind=kLoop, calls=%fused_computation.29 | loop fusion | flops 684 | bytes 204 | tf_op jit(solution)/shard_map/mul | solution.py:150
  12.5 0.0 collective-permute-done.4.refs_19_
  12.5 0.3 collective-permute-start.5
  12.9 2.0 %collective-permute-done.6.refs_20_ = bf16[4,2,64,512]{3,2,1,0:T(8,128)(2,1)S(1)} collective-permute-done((bf16[4,2,64,512]{3,2,1,0:T(8,128)(2,1)}, bf16[4,2,64,512]{3,2,1,0:T(8,128)(2,1)S(1)}, u32[]{:S(2)}, u32[]{:S(2)}) %collective-permute-start.6) | collective-permute-done | bytes 524320 | tf_op jit(solution)/shard_map/b_x/ppermute | solution.py:30
  14.9 0.8 %collective-permute-done.3.refs_3_ = bf16[4,2,32,1024]{3,2,1,0:T(8,128)(2,1)S(1)} collective-permute-done((bf16[4,2,32,1024]{3,2,1,0:T(8,128)(2,1)}, bf16[4,2,32,1024]{3,2,1,0:T(8,128)(2,1)S(1)}, u32[]{:S(2)}, u32[]{:S(2)}) %collective-permute-start.3) | collective-permute-done | bytes 524320 | tf_op jit(solution)/shard_map/a_3/ppermute | solution.py:30
  15.7 6.8 %collective-permute-start.11 = (bf16[4,2,32,1024]{3,2,1,0:T(8,128)(2,1)S(1)}, bf16[4,2,32,1024]{3,2,1,0:T(8,128)(2,1)S(1)}, u32[]{:S(2)}, u32[]{:S(2)}) collective-permute-start(bf16[4,2,32,1024]{3,2,1,0:T(8,128)(2,1)S(1)} %collective-permute-done.3.refs_3_), channel_id=1, source_target_pairs={{0,1},{1,0},{2,3},{3,2},{4,5},{5,4},{6,7},{7,6},{16,17},{17,16},{1... | collective-permute-start | bytes 1572872 | tf_op jit(solution)/shard_map/other_3/ppermute | solution.py:30
  22.5 1.5 %collective-permute-start.9 = (bf16[4,2,64,512]{3,2,1,0:T(8,128)(2,1)S(1)}, bf16[4,2,64,512]{3,2,1,0:T(8,128)(2,1)S(1)}, u32[]{:S(2)}, u32[]{:S(2)}) collective-permute-start(bf16[4,2,64,512]{3,2,1,0:T(8,128)(2,1)S(1)} %collective-permute-done.6.refs_20_), channel_id=1, source_target_pairs={{0,16},{1,49},{2,18},{3,51},{4,20},{5,53},{6,22},{7,55},{16,32},{1... | collective-permute-start | bytes 1572872 | tf_op jit(solution)/shard_map/b_x1/ppermute | solution.py:30
  24.0 0.0 collective-permute-done.1.refs_17_
  24.0 0.0 collective-permute-done.refs_1_
  24.0 3.4 %collective-permute-start.2 = (bf16[4,2,32,1024]{3,2,1,0:T(8,128)(2,1)S(1)}, bf16[4,2,32,1024]{3,2,1,0:T(8,128)(2,1)S(1)}, u32[]{:S(2)}, u32[]{:S(2)}) collective-permute-start(bf16[4,2,32,1024]{3,2,1,0:T(8,128)(2,1)S(1)} %collective-permute-done.refs_1_), channel_id=1, source_target_pairs={{0,2},{1,7},{2,4},{3,1},{4,6},{5,3},{6,0},{7,5},{16,18},{17,23},{1... | collective-permute-start | bytes 1572872 | tf_op jit(solution)/shard_map/a_2/ppermute | solution.py:30
  27.4 0.0 collective-permute-start.7
  27.4 0.0 collective-permute-done.5.refs_4_
  27.4 2.7 %collective-permute-start.16 = (bf16[4,2,64,512]{3,2,1,0:T(8,128)(2,1)S(1)}, bf16[4,2,64,512]{3,2,1,0:T(8,128)(2,1)S(1)}, u32[]{:S(2)}, u32[]{:S(2)}) collective-permute-start(bf16[4,2,64,512]{3,2,1,0:T(8,128)(2,1)S(1)} %collective-permute-done.1.refs_17_), channel_id=1, source_target_pairs={{0,16},{1,49},{2,18},{3,51},{4,20},{5,53},{6,22},{7,55},{16,32},{1... | collective-permute-start | bytes 1572872 | tf_op jit(solution)/shard_map/b_2/ppermute | solution.py:30
  30.1 0.0 collective-permute-done.11.refs_11_
  30.1 0.2 collective-permute-start.12
  30.3 3.7 %collective-permute-done.9.refs_21_ = bf16[4,2,64,512]{3,2,1,0:T(8,128)(2,1)S(1)} collective-permute-done((bf16[4,2,64,512]{3,2,1,0:T(8,128)(2,1)S(1)}, bf16[4,2,64,512]{3,2,1,0:T(8,128)(2,1)S(1)}, u32[]{:S(2)}, u32[]{:S(2)}) %collective-permute-start.9) | collective-permute-done | bytes 524320 | tf_op jit(solution)/shard_map/b_x1/ppermute | solution.py:30
  33.9 0.0 collective-permute-done.2.refs_2_
  33.9 0.4 collective-permute-start.10
  34.3 1.2 %collective-permute-start.13 = (bf16[4,2,64,512]{3,2,1,0:T(8,128)(2,1)S(1)}, bf16[4,2,64,512]{3,2,1,0:T(8,128)(2,1)S(1)}, u32[]{:S(2)}, u32[]{:S(2)}) collective-permute-start(bf16[4,2,64,512]{3,2,1,0:T(8,128)(2,1)S(1)} %collective-permute-done.9.refs_21_), channel_id=1, source_target_pairs={{0,16},{1,49},{2,18},{3,51},{4,20},{5,53},{6,22},{7,55},{16,32},{1... | collective-permute-start | bytes 1572872 | tf_op jit(solution)/shard_map/b_x2/ppermute | solution.py:30
  35.5 6.8 %collective-permute-done.7.refs_23_ = bf16[4,2,64,512]{3,2,1,0:T(8,128)(2,1)S(1)} collective-permute-done((bf16[4,2,64,512]{3,2,1,0:T(8,128)(2,1)S(1)}, bf16[4,2,64,512]{3,2,1,0:T(8,128)(2,1)S(1)}, u32[]{:S(2)}, u32[]{:S(2)}) %collective-permute-start.7) | collective-permute-done | bytes 524320 | tf_op jit(solution)/shard_map/b_x3/ppermute | solution.py:30
  42.3 0.3 collective-permute-start.8
  42.6 0.0 collective-permute-done.16.refs_18_
  42.7 1.5 %collective-permute-start.17 = (bf16[4,2,32,1024]{3,2,1,0:T(8,128)(2,1)S(1)}, bf16[4,2,32,1024]{3,2,1,0:T(8,128)(2,1)S(1)}, u32[]{:S(2)}, u32[]{:S(2)}) collective-permute-start(bf16[4,2,32,1024]{3,2,1,0:T(8,128)(2,1)S(1)} %collective-permute-done.2.refs_2_), channel_id=1, source_target_pairs={{0,1},{1,0},{2,3},{3,2},{4,5},{5,4},{6,7},{7,6},{16,17},{17,16},{1... | collective-permute-start | bytes 1572872 | tf_op jit(solution)/shard_map/other_2/ppermute | solution.py:30
  44.2 0.0 collective-permute-done.12.refs_7_
  44.2 0.1 collective-permute-start.15
  44.3 3.4 %collective-permute-done.13.refs_22_ = bf16[4,2,64,512]{3,2,1,0:T(8,128)(2,1)S(1)} collective-permute-done((bf16[4,2,64,512]{3,2,1,0:T(8,128)(2,1)S(1)}, bf16[4,2,64,512]{3,2,1,0:T(8,128)(2,1)S(1)}, u32[]{:S(2)}, u32[]{:S(2)}) %collective-permute-start.13) | collective-permute-done | bytes 524320 | tf_op jit(solution)/shard_map/b_x2/ppermute | solution.py:30
  47.7 2.1 %collective-permute-start.14 = (bf16[4,2,32,1024]{3,2,1,0:T(8,128)(2,1)}, bf16[4,2,32,1024]{3,2,1,0:T(8,128)(2,1)S(1)}, u32[]{:S(2)}, u32[]{:S(2)}) collective-permute-start(bf16[4,2,32,1024]{3,2,1,0:T(8,128)(2,1)} %refs_0_.1), channel_id=1, source_target_pairs={{0,1},{1,0},{2,3},{3,2},{4,5},{5,4},{6,7},{7,6},{16,17},{17,16},{1... | collective-permute-start | bytes 1572872 | tf_op jit(solution)/shard_map/other/ppermute | solution.py:30
  49.8 0.0 collective-permute-done.10.refs_6_
  49.8 0.1 collective-permute-start.20
  49.9 0.5 collective-permute-done.8.refs_5_
  50.4 0.1 collective-permute-start.19
  50.5 0.4 collective-permute-start.21
  50.9 0.0 collective-permute-done.15.refs_9_
  50.9 0.1 collective-permute-start.18
  51.0 1.0 %collective-permute-done.20.refs_14_ = bf16[4,2,32,1024]{3,2,1,0:T(8,128)(2,1)S(1)} collective-permute-done((bf16[4,2,32,1024]{3,2,1,0:T(8,128)(2,1)S(1)}, bf16[4,2,32,1024]{3,2,1,0:T(8,128)(2,1)S(1)}, u32[]{:S(2)}, u32[]{:S(2)}) %collective-permute-start.20) | collective-permute-done | bytes 524320 | tf_op jit(solution)/shard_map/other_x2/ppermute | solution.py:30
  52.1 0.0 collective-permute-done.14.refs_8_
  52.1 1.5 %collective-permute-done.19.refs_13_ = bf16[4,2,32,1024]{3,2,1,0:T(8,128)(2,1)S(1)} collective-permute-done((bf16[4,2,32,1024]{3,2,1,0:T(8,128)(2,1)S(1)}, bf16[4,2,32,1024]{3,2,1,0:T(8,128)(2,1)S(1)}, u32[]{:S(2)}, u32[]{:S(2)}) %collective-permute-start.19) | collective-permute-done | bytes 524320 | tf_op jit(solution)/shard_map/other_x1/ppermute | solution.py:30
  53.6 0.7 %collective-permute-done.21.refs_15_ = bf16[4,2,32,1024]{3,2,1,0:T(8,128)(2,1)S(1)} collective-permute-done((bf16[4,2,32,1024]{3,2,1,0:T(8,128)(2,1)S(1)}, bf16[4,2,32,1024]{3,2,1,0:T(8,128)(2,1)S(1)}, u32[]{:S(2)}, u32[]{:S(2)}) %collective-permute-start.21) | collective-permute-done | bytes 524320 | tf_op jit(solution)/shard_map/other_x3/ppermute | solution.py:30
  54.3 0.0 copy-done.19
  54.4 0.8 %copy-done.20 = bf16[4,2,32,1024]{3,2,1,0:T(8,128)(2,1)} copy-done((bf16[4,2,32,1024]{3,2,1,0:T(8,128)(2,1)}, bf16[4,2,32,1024]{3,2,1,0:T(8,128)(2,1)S(1)}, u32[]{:S(2)}) %copy-start.20) | copy-done | bytes 524312
  55.2 0.0 collective-permute-done.18.refs_12_
  55.3 12.0 %shard_map.37 = bf16[4,2,1024,512]{3,2,1,0:T(8,128)(2,1)} custom-call(s32[12]{0:T(128)} %get-tuple-element.38.a_where, s32[12]{0:T(128)} %get-tuple-element.35.b_where, s32[12]{0:T(128)} %get-tuple-element.37.b_row, bf16[4,2,32,1024]{3,2,1,0:T(8,128)(2,1)} %refs_0_.1, bf16[4,2,32,1024]{3,2,1,0:T(8,128)(2,1)} %copy-done.4, ...), custom_call_target="tpu_custom_call" | custom-call | flops 6442450944 | bytes 20971520 | tf_op jit(solution)/shard_map/pallas_call | solution.py:114
  (41 shorter events, 0.1 us)
Async XLA Ops:
  0.0 12.5 %collective-permute-start.4 = (bf16[4,2,64,512]{3,2,1,0:T(8,128)(2,1)}, bf16[4,2,64,512]{3,2,1,0:T(8,128)(2,1)S(1)}, u32[]{:S(2)}, u32[]{:S(2)}) collective-permute-start(bf16[4,2,64,512]{3,2,1,0:T(8,128)(2,1)} %refs_16_.1), channel_id=1, source_target_pairs={{0,48},{1,17},{2,50},{3,19},{4,52},{5,21},{6,54},{7,23},{16,0},{17... | collective-permute-start | bytes 1572872 | tf_op jit(solution)/shard_map/b_3/ppermute | solution.py:30
  2.1 12.7 %collective-permute-start.6 = (bf16[4,2,64,512]{3,2,1,0:T(8,128)(2,1)}, bf16[4,2,64,512]{3,2,1,0:T(8,128)(2,1)S(1)}, u32[]{:S(2)}, u32[]{:S(2)}) collective-permute-start(bf16[4,2,64,512]{3,2,1,0:T(8,128)(2,1)} %refs_16_.1), channel_id=1, source_target_pairs={{0,64},{1,65},{2,66},{3,67},{4,68},{5,69},{6,70},{7,71},{16,80},{1... | collective-permute-start | bytes 1572872 | tf_op jit(solution)/shard_map/b_x/ppermute | solution.py:30
  4.9 10.8 %collective-permute-start.3 = (bf16[4,2,32,1024]{3,2,1,0:T(8,128)(2,1)}, bf16[4,2,32,1024]{3,2,1,0:T(8,128)(2,1)S(1)}, u32[]{:S(2)}, u32[]{:S(2)}) collective-permute-start(bf16[4,2,32,1024]{3,2,1,0:T(8,128)(2,1)} %refs_0_.1), channel_id=1, source_target_pairs={{0,6},{1,3},{2,0},{3,5},{4,2},{5,7},{6,4},{7,1},{16,22},{17,19},{1... | collective-permute-start | bytes 1572872 | tf_op jit(solution)/shard_map/a_3/ppermute | solution.py:30
  6.5 17.5 %collective-permute-start.1 = (bf16[4,2,64,512]{3,2,1,0:T(8,128)(2,1)}, bf16[4,2,64,512]{3,2,1,0:T(8,128)(2,1)S(1)}, u32[]{:S(2)}, u32[]{:S(2)}) collective-permute-start(bf16[4,2,64,512]{3,2,1,0:T(8,128)(2,1)} %refs_16_.1), channel_id=1, source_target_pairs={{0,16},{1,49},{2,18},{3,51},{4,20},{5,53},{6,22},{7,55},{16,32},{1... | collective-permute-start | bytes 1572872 | tf_op jit(solution)/shard_map/b_1/ppermute | solution.py:30
  8.0 16.1 %collective-permute-start = (bf16[4,2,32,1024]{3,2,1,0:T(8,128)(2,1)}, bf16[4,2,32,1024]{3,2,1,0:T(8,128)(2,1)S(1)}, u32[]{:S(2)}, u32[]{:S(2)}) collective-permute-start(bf16[4,2,32,1024]{3,2,1,0:T(8,128)(2,1)} %refs_0_.1), channel_id=1, source_target_pairs={{0,2},{1,7},{2,4},{3,1},{4,6},{5,3},{6,0},{7,5},{16,18},{17,23},{1... | collective-permute-start | bytes 1572872 | tf_op jit(solution)/shard_map/a_1/ppermute | solution.py:30
  12.5 42.7 %copy-start = (bf16[4,2,64,512]{3,2,1,0:T(8,128)(2,1)}, bf16[4,2,64,512]{3,2,1,0:T(8,128)(2,1)S(1)}, u32[]{:S(2)}) copy-start(bf16[4,2,64,512]{3,2,1,0:T(8,128)(2,1)S(1)} %collective-permute-done.4.refs_19_) | copy-start | bytes 1572868
  12.5 14.9 %collective-permute-start.5 = (bf16[4,2,32,1024]{3,2,1,0:T(8,128)(2,1)}, bf16[4,2,32,1024]{3,2,1,0:T(8,128)(2,1)S(1)}, u32[]{:S(2)}, u32[]{:S(2)}) collective-permute-start(bf16[4,2,32,1024]{3,2,1,0:T(8,128)(2,1)} %refs_0_.1), channel_id=1, source_target_pairs={{0,8},{1,9},{2,10},{3,11},{4,12},{5,13},{6,14},{7,15},{16,24},{17,... | collective-permute-start | bytes 1572872 | tf_op jit(solution)/shard_map/a_x/ppermute | solution.py:30
  14.9 40.3 %copy-start.1 = (bf16[4,2,64,512]{3,2,1,0:T(8,128)(2,1)}, bf16[4,2,64,512]{3,2,1,0:T(8,128)(2,1)S(1)}, u32[]{:S(2)}) copy-start(bf16[4,2,64,512]{3,2,1,0:T(8,128)(2,1)S(1)} %collective-permute-done.6.refs_20_) | copy-start | bytes 1572868
  15.7 39.5 %copy-start.2 = (bf16[4,2,32,1024]{3,2,1,0:T(8,128)(2,1)}, bf16[4,2,32,1024]{3,2,1,0:T(8,128)(2,1)S(1)}, u32[]{:S(2)}) copy-start(bf16[4,2,32,1024]{3,2,1,0:T(8,128)(2,1)S(1)} %collective-permute-done.3.refs_3_) | copy-start | bytes 1572868
  15.7 14.4 %collective-permute-start.11 = (bf16[4,2,32,1024]{3,2,1,0:T(8,128)(2,1)S(1)}, bf16[4,2,32,1024]{3,2,1,0:T(8,128)(2,1)S(1)}, u32[]{:S(2)}, u32[]{:S(2)}) collective-permute-start(bf16[4,2,32,1024]{3,2,1,0:T(8,128)(2,1)S(1)} %collective-permute-done.3.refs_3_), channel_id=1, source_target_pairs={{0,1},{1,0},{2,3},{3,2},{4,5},{5,4},{6,7},{7,6},{16,17},{17,16},{1... | collective-permute-start | bytes 1572872 | tf_op jit(solution)/shard_map/other_3/ppermute | solution.py:30
  22.5 11.4 %collective-permute-start.9 = (bf16[4,2,64,512]{3,2,1,0:T(8,128)(2,1)S(1)}, bf16[4,2,64,512]{3,2,1,0:T(8,128)(2,1)S(1)}, u32[]{:S(2)}, u32[]{:S(2)}) collective-permute-start(bf16[4,2,64,512]{3,2,1,0:T(8,128)(2,1)S(1)} %collective-permute-done.6.refs_20_), channel_id=1, source_target_pairs={{0,16},{1,49},{2,18},{3,51},{4,20},{5,53},{6,22},{7,55},{16,32},{1... | collective-permute-start | bytes 1572872 | tf_op jit(solution)/shard_map/b_x1/ppermute | solution.py:30
  24.0 31.2 %copy-start.3 = (bf16[4,2,64,512]{3,2,1,0:T(8,128)(2,1)}, bf16[4,2,64,512]{3,2,1,0:T(8,128)(2,1)S(1)}, u32[]{:S(2)}) copy-start(bf16[4,2,64,512]{3,2,1,0:T(8,128)(2,1)S(1)} %collective-permute-done.1.refs_17_) | copy-start | bytes 1572868
  24.0 31.2 %copy-start.4 = (bf16[4,2,32,1024]{3,2,1,0:T(8,128)(2,1)}, bf16[4,2,32,1024]{3,2,1,0:T(8,128)(2,1)S(1)}, u32[]{:S(2)}) copy-start(bf16[4,2,32,1024]{3,2,1,0:T(8,128)(2,1)S(1)} %collective-permute-done.refs_1_) | copy-start | bytes 1572868
  24.0 9.9 %collective-permute-start.2 = (bf16[4,2,32,1024]{3,2,1,0:T(8,128)(2,1)S(1)}, bf16[4,2,32,1024]{3,2,1,0:T(8,128)(2,1)S(1)}, u32[]{:S(2)}, u32[]{:S(2)}) collective-permute-start(bf16[4,2,32,1024]{3,2,1,0:T(8,128)(2,1)S(1)} %collective-permute-done.refs_1_), channel_id=1, source_target_pairs={{0,2},{1,7},{2,4},{3,1},{4,6},{5,3},{6,0},{7,5},{16,18},{17,23},{1... | collective-permute-start | bytes 1572872 | tf_op jit(solution)/shard_map/a_2/ppermute | solution.py:30
  27.4 15.0 %collective-permute-start.7 = (bf16[4,2,64,512]{3,2,1,0:T(8,128)(2,1)S(1)}, bf16[4,2,64,512]{3,2,1,0:T(8,128)(2,1)S(1)}, u32[]{:S(2)}, u32[]{:S(2)}) collective-permute-start(bf16[4,2,64,512]{3,2,1,0:T(8,128)(2,1)S(1)} %collective-permute-done.6.refs_20_), channel_id=1, source_target_pairs={{0,48},{1,17},{2,50},{3,19},{4,52},{5,21},{6,54},{7,23},{16,0},{17... | collective-permute-start | bytes 1572872 | tf_op jit(solution)/shard_map/b_x3/ppermute | solution.py:30
  27.4 27.8 %copy-start.5 = (bf16[4,2,32,1024]{3,2,1,0:T(8,128)(2,1)}, bf16[4,2,32,1024]{3,2,1,0:T(8,128)(2,1)S(1)}, u32[]{:S(2)}) copy-start(bf16[4,2,32,1024]{3,2,1,0:T(8,128)(2,1)S(1)} %collective-permute-done.5.refs_4_) | copy-start | bytes 1572868
  27.4 15.2 %collective-permute-start.16 = (bf16[4,2,64,512]{3,2,1,0:T(8,128)(2,1)S(1)}, bf16[4,2,64,512]{3,2,1,0:T(8,128)(2,1)S(1)}, u32[]{:S(2)}, u32[]{:S(2)}) collective-permute-start(bf16[4,2,64,512]{3,2,1,0:T(8,128)(2,1)S(1)} %collective-permute-done.1.refs_17_), channel_id=1, source_target_pairs={{0,16},{1,49},{2,18},{3,51},{4,20},{5,53},{6,22},{7,55},{16,32},{1... | collective-permute-start | bytes 1572872 | tf_op jit(solution)/shard_map/b_2/ppermute | solution.py:30
  30.1 25.2 %copy-start.6 = (bf16[4,2,32,1024]{3,2,1,0:T(8,128)(2,1)}, bf16[4,2,32,1024]{3,2,1,0:T(8,128)(2,1)S(1)}, u32[]{:S(2)}) copy-start(bf16[4,2,32,1024]{3,2,1,0:T(8,128)(2,1)S(1)} %collective-permute-done.11.refs_11_) | copy-start | bytes 1572868
  30.1 14.1 %collective-permute-start.12 = (bf16[4,2,32,1024]{3,2,1,0:T(8,128)(2,1)S(1)}, bf16[4,2,32,1024]{3,2,1,0:T(8,128)(2,1)S(1)}, u32[]{:S(2)}, u32[]{:S(2)}) collective-permute-start(bf16[4,2,32,1024]{3,2,1,0:T(8,128)(2,1)S(1)} %collective-permute-done.5.refs_4_), channel_id=1, source_target_pairs={{0,6},{1,3},{2,0},{3,5},{4,2},{5,7},{6,4},{7,1},{16,22},{17,19},{1... | collective-permute-start | bytes 1572872 | tf_op jit(solution)/shard_map/a_x3/ppermute | solution.py:30
  33.9 21.3 %copy-start.7 = (bf16[4,2,64,512]{3,2,1,0:T(8,128)(2,1)}, bf16[4,2,64,512]{3,2,1,0:T(8,128)(2,1)S(1)}, u32[]{:S(2)}) copy-start(bf16[4,2,64,512]{3,2,1,0:T(8,128)(2,1)S(1)} %collective-permute-done.9.refs_21_) | copy-start | bytes 1572868
  33.9 21.3 %copy-start.8 = (bf16[4,2,32,1024]{3,2,1,0:T(8,128)(2,1)}, bf16[4,2,32,1024]{3,2,1,0:T(8,128)(2,1)S(1)}, u32[]{:S(2)}) copy-start(bf16[4,2,32,1024]{3,2,1,0:T(8,128)(2,1)S(1)} %collective-permute-done.2.refs_2_) | copy-start | bytes 1572868
  33.9 15.8 %collective-permute-start.10 = (bf16[4,2,32,1024]{3,2,1,0:T(8,128)(2,1)S(1)}, bf16[4,2,32,1024]{3,2,1,0:T(8,128)(2,1)S(1)}, u32[]{:S(2)}, u32[]{:S(2)}) collective-permute-start(bf16[4,2,32,1024]{3,2,1,0:T(8,128)(2,1)S(1)} %collective-permute-done.2.refs_2_), channel_id=1, source_target_pairs={{0,8},{1,9},{2,10},{3,11},{4,12},{5,13},{6,14},{7,15},{16,24},{17,... | collective-permute-start | bytes 1572872 | tf_op jit(solution)/shard_map/a_x2/ppermute | solution.py:30
  34.3 13.4 %collective-permute-start.13 = (bf16[4,2,64,512]{3,2,1,0:T(8,128)(2,1)S(1)}, bf16[4,2,64,512]{3,2,1,0:T(8,128)(2,1)S(1)}, u32[]{:S(2)}, u32[]{:S(2)}) collective-permute-start(bf16[4,2,64,512]{3,2,1,0:T(8,128)(2,1)S(1)} %collective-permute-done.9.refs_21_), channel_id=1, source_target_pairs={{0,16},{1,49},{2,18},{3,51},{4,20},{5,53},{6,22},{7,55},{16,32},{1... | collective-permute-start | bytes 1572872 | tf_op jit(solution)/shard_map/b_x2/ppermute | solution.py:30
  42.3 12.9 %copy-start.9 = (bf16[4,2,64,512]{3,2,1,0:T(8,128)(2,1)}, bf16[4,2,64,512]{3,2,1,0:T(8,128)(2,1)S(1)}, u32[]{:S(2)}) copy-start(bf16[4,2,64,512]{3,2,1,0:T(8,128)(2,1)S(1)} %collective-permute-done.7.refs_23_) | copy-start | bytes 1572868
  42.3 8.0 %collective-permute-start.8 = (bf16[4,2,32,1024]{3,2,1,0:T(8,128)(2,1)S(1)}, bf16[4,2,32,1024]{3,2,1,0:T(8,128)(2,1)S(1)}, u32[]{:S(2)}, u32[]{:S(2)}) collective-permute-start(bf16[4,2,32,1024]{3,2,1,0:T(8,128)(2,1)S(1)} %collective-permute-done.5.refs_4_), channel_id=1, source_target_pairs={{0,2},{1,7},{2,4},{3,1},{4,6},{5,3},{6,0},{7,5},{16,18},{17,23},{1... | collective-permute-start | bytes 1572872 | tf_op jit(solution)/shard_map/a_x1/ppermute | solution.py:30
  42.7 12.6 %copy-start.10 = (bf16[4,2,64,512]{3,2,1,0:T(8,128)(2,1)}, bf16[4,2,64,512]{3,2,1,0:T(8,128)(2,1)S(1)}, u32[]{:S(2)}) copy-start(bf16[4,2,64,512]{3,2,1,0:T(8,128)(2,1)S(1)} %collective-permute-done.16.refs_18_) | copy-start | bytes 1572868
  42.7 7.9 %collective-permute-start.17 = (bf16[4,2,32,1024]{3,2,1,0:T(8,128)(2,1)S(1)}, bf16[4,2,32,1024]{3,2,1,0:T(8,128)(2,1)S(1)}, u32[]{:S(2)}, u32[]{:S(2)}) collective-permute-start(bf16[4,2,32,1024]{3,2,1,0:T(8,128)(2,1)S(1)} %collective-permute-done.2.refs_2_), channel_id=1, source_target_pairs={{0,1},{1,0},{2,3},{3,2},{4,5},{5,4},{6,7},{7,6},{16,17},{17,16},{1... | collective-permute-start | bytes 1572872 | tf_op jit(solution)/shard_map/other_2/ppermute | solution.py:30
  44.2 11.1 %copy-start.11 = (bf16[4,2,32,1024]{3,2,1,0:T(8,128)(2,1)}, bf16[4,2,32,1024]{3,2,1,0:T(8,128)(2,1)S(1)}, u32[]{:S(2)}) copy-start(bf16[4,2,32,1024]{3,2,1,0:T(8,128)(2,1)S(1)} %collective-permute-done.12.refs_7_) | copy-start | bytes 1572868
  44.2 6.7 %collective-permute-start.15 = (bf16[4,2,32,1024]{3,2,1,0:T(8,128)(2,1)S(1)}, bf16[4,2,32,1024]{3,2,1,0:T(8,128)(2,1)S(1)}, u32[]{:S(2)}, u32[]{:S(2)}) collective-permute-start(bf16[4,2,32,1024]{3,2,1,0:T(8,128)(2,1)S(1)} %collective-permute-done.refs_1_), channel_id=1, source_target_pairs={{0,1},{1,0},{2,3},{3,2},{4,5},{5,4},{6,7},{7,6},{16,17},{17,16},{1... | collective-permute-start | bytes 1572872 | tf_op jit(solution)/shard_map/other_1/ppermute | solution.py:30
  47.7 7.6 %copy-start.13 = (bf16[4,2,64,512]{3,2,1,0:T(8,128)(2,1)}, bf16[4,2,64,512]{3,2,1,0:T(8,128)(2,1)S(1)}, u32[]{:S(2)}) copy-start(bf16[4,2,64,512]{3,2,1,0:T(8,128)(2,1)S(1)} %collective-permute-done.13.refs_22_) | copy-start | bytes 1572868
  47.7 4.4 %collective-permute-start.14 = (bf16[4,2,32,1024]{3,2,1,0:T(8,128)(2,1)}, bf16[4,2,32,1024]{3,2,1,0:T(8,128)(2,1)S(1)}, u32[]{:S(2)}, u32[]{:S(2)}) collective-permute-start(bf16[4,2,32,1024]{3,2,1,0:T(8,128)(2,1)} %refs_0_.1), channel_id=1, source_target_pairs={{0,1},{1,0},{2,3},{3,2},{4,5},{5,4},{6,7},{7,6},{16,17},{17,16},{1... | collective-permute-start | bytes 1572872 | tf_op jit(solution)/shard_map/other/ppermute | solution.py:30
  49.8 5.5 %copy-start.12 = (bf16[4,2,32,1024]{3,2,1,0:T(8,128)(2,1)}, bf16[4,2,32,1024]{3,2,1,0:T(8,128)(2,1)S(1)}, u32[]{:S(2)}) copy-start(bf16[4,2,32,1024]{3,2,1,0:T(8,128)(2,1)S(1)} %collective-permute-done.10.refs_6_) | copy-start | bytes 1572868
  49.8 2.3 %collective-permute-start.20 = (bf16[4,2,32,1024]{3,2,1,0:T(8,128)(2,1)S(1)}, bf16[4,2,32,1024]{3,2,1,0:T(8,128)(2,1)S(1)}, u32[]{:S(2)}, u32[]{:S(2)}) collective-permute-start(bf16[4,2,32,1024]{3,2,1,0:T(8,128)(2,1)S(1)} %collective-permute-done.10.refs_6_), channel_id=1, source_target_pairs={{0,1},{1,0},{2,3},{3,2},{4,5},{5,4},{6,7},{7,6},{16,17},{17,16},{1... | collective-permute-start | bytes 1572872 | tf_op jit(solution)/shard_map/other_x2/ppermute | solution.py:30
  50.4 5.0 %copy-start.14 = (bf16[4,2,32,1024]{3,2,1,0:T(8,128)(2,1)}, bf16[4,2,32,1024]{3,2,1,0:T(8,128)(2,1)S(1)}, u32[]{:S(2)}) copy-start(bf16[4,2,32,1024]{3,2,1,0:T(8,128)(2,1)S(1)} %collective-permute-done.8.refs_5_) | copy-start | bytes 1572868
  50.4 3.2 %collective-permute-start.19 = (bf16[4,2,32,1024]{3,2,1,0:T(8,128)(2,1)S(1)}, bf16[4,2,32,1024]{3,2,1,0:T(8,128)(2,1)S(1)}, u32[]{:S(2)}, u32[]{:S(2)}) collective-permute-start(bf16[4,2,32,1024]{3,2,1,0:T(8,128)(2,1)S(1)} %collective-permute-done.8.refs_5_), channel_id=1, source_target_pairs={{0,1},{1,0},{2,3},{3,2},{4,5},{5,4},{6,7},{7,6},{16,17},{17,16},{1... | collective-permute-start | bytes 1572872 | tf_op jit(solution)/shard_map/other_x1/ppermute | solution.py:30
  50.5 3.8 %copy-start.15 = (bf16[4,2,32,1024]{3,2,1,0:T(8,128)(2,1)}, bf16[4,2,32,1024]{3,2,1,0:T(8,128)(2,1)S(1)}, u32[]{:S(2)}) copy-start(bf16[4,2,32,1024]{3,2,1,0:T(8,128)(2,1)S(1)} %collective-permute-done.17.refs_10_) | copy-start | bytes 1572868
  50.5 3.8 %collective-permute-start.21 = (bf16[4,2,32,1024]{3,2,1,0:T(8,128)(2,1)S(1)}, bf16[4,2,32,1024]{3,2,1,0:T(8,128)(2,1)S(1)}, u32[]{:S(2)}, u32[]{:S(2)}) collective-permute-start(bf16[4,2,32,1024]{3,2,1,0:T(8,128)(2,1)S(1)} %collective-permute-done.12.refs_7_), channel_id=1, source_target_pairs={{0,1},{1,0},{2,3},{3,2},{4,5},{5,4},{6,7},{7,6},{16,17},{17,16},{1... | collective-permute-start | bytes 1572872 | tf_op jit(solution)/shard_map/other_x3/ppermute | solution.py:30
  50.9 3.4 %copy-start.16 = (bf16[4,2,32,1024]{3,2,1,0:T(8,128)(2,1)}, bf16[4,2,32,1024]{3,2,1,0:T(8,128)(2,1)S(1)}, u32[]{:S(2)}) copy-start(bf16[4,2,32,1024]{3,2,1,0:T(8,128)(2,1)S(1)} %collective-permute-done.15.refs_9_) | copy-start | bytes 1572868
  50.9 4.3 %collective-permute-start.18 = (bf16[4,2,32,1024]{3,2,1,0:T(8,128)(2,1)S(1)}, bf16[4,2,32,1024]{3,2,1,0:T(8,128)(2,1)}, u32[]{:S(2)}, u32[]{:S(2)}) collective-permute-start(bf16[4,2,32,1024]{3,2,1,0:T(8,128)(2,1)S(1)} %collective-permute-done.5.refs_4_), channel_id=1, source_target_pairs={{0,1},{1,0},{2,3},{3,2},{4,5},{5,4},{6,7},{7,6},{16,17},{17,16},{1... | collective-permute-start | bytes 1572872 | tf_op jit(solution)/shard_map/other_x/ppermute | solution.py:30
  52.1 2.3 %copy-start.18 = (bf16[4,2,32,1024]{3,2,1,0:T(8,128)(2,1)}, bf16[4,2,32,1024]{3,2,1,0:T(8,128)(2,1)S(1)}, u32[]{:S(2)}) copy-start(bf16[4,2,32,1024]{3,2,1,0:T(8,128)(2,1)S(1)} %collective-permute-done.20.refs_14_) | copy-start | bytes 1572868
  52.1 2.3 %copy-start.17 = (bf16[4,2,32,1024]{3,2,1,0:T(8,128)(2,1)}, bf16[4,2,32,1024]{3,2,1,0:T(8,128)(2,1)S(1)}, u32[]{:S(2)}) copy-start(bf16[4,2,32,1024]{3,2,1,0:T(8,128)(2,1)S(1)} %collective-permute-done.14.refs_8_) | copy-start | bytes 1572868
  53.6 0.8 %copy-start.19 = (bf16[4,2,32,1024]{3,2,1,0:T(8,128)(2,1)}, bf16[4,2,32,1024]{3,2,1,0:T(8,128)(2,1)S(1)}, u32[]{:S(2)}) copy-start(bf16[4,2,32,1024]{3,2,1,0:T(8,128)(2,1)S(1)} %collective-permute-done.19.refs_13_) | copy-start | bytes 1572868
  54.4 0.8 %copy-start.20 = (bf16[4,2,32,1024]{3,2,1,0:T(8,128)(2,1)}, bf16[4,2,32,1024]{3,2,1,0:T(8,128)(2,1)S(1)}, u32[]{:S(2)}) copy-start(bf16[4,2,32,1024]{3,2,1,0:T(8,128)(2,1)S(1)} %collective-permute-done.21.refs_15_) | copy-start | bytes 1572868

commit v13 on v11

--- a/solution.py
+++ b/solution.py
@@ -8,7 +8,7 @@
 BLK = 32
 STEPS = 12
 ROWS = 256
-SURFACE_ORDER = (3, 4, 5, 6, 7, 8, 9, 10, 11, 12, 13, 14, 1, 2, 15, 0)
+SURFACE_ORDER = (1, 2, 3, 4, 5, 6, 7, 8, 9, 10, 11, 12, 13, 14, 15, 0)
 AXES = ("shot", "rcv")
 X, Y, Z, CORES = 4, 4, 4, 2
 
@@ -129,7 +129,7 @@
                 pltpu.SemaphoreType.DMA((2,)),
             ],
         ),
-        compiler_params=pltpu.CompilerParams(vmem_limit_bytes=52 * 1024 * 1024),
+        compiler_params=pltpu.CompilerParams(vmem_limit_bytes=53 * 1024 * 1024),
         cost_estimate=pl.CostEstimate(
             flops=2 * freqs * shots * 2 * rcvs * depth,
             bytes_accessed=20 * 1024 * 1024,
@@ -189,8 +189,8 @@
     other_x = swap("other_x", after(a_x, other))
     other_x3 = swap("other_x3", after(a_x3, other_2))
 
-    a_parts = [other_x3, other_x, other_x1, a, a_1, a_2, a_3, a_x]
-    a_parts += [a_x1, a_x2, a_x3, other, other_1, other_2, other_3, other_x2]
+    a_parts = [other_x3, a, a_1, a_2, a_3, a_x, a_x1, a_x2]
+    a_parts += [a_x3, other, other_1, other_2, other_3, other_x, other_x1, other_x2]
     b_parts = [b, b_1, b_2, b_3, b_x, b_x1, b_x2, b_x3]
     return multiply(a_parts, b_parts, a_where, b_where, b_row)
 

time: 66 us -> 65.7 us (level)
  local copies, waits for them, and re-layouts: 0.07 us -> 0.88 us
  waiting for transfers between devices: 14.6 us -> 13.9 us
    unnamed x38 -> x42, local copies, waits for them, and re-layouts: 0.07 us -> 0.88 us
    ppermute x22, waiting for transfers between devices: 14.6 us -> 13.9 us  [moved(): return lax.ppermute(value, AXES, pairs)]
  transfers between devices with their start and end apart: 22 -> 22, of which waited for: 9 -> 8; matrix products, arithmetic and copies ran while one was open for 2% -> 2% of each run, Pallas kernels for 0% -> 0%
where the time goes in v13:
time: 65.7 us; the launch traced here: 65.2 us
  starting transfers between devices  37.5 us (57%)
  waiting for transfers between devices  13.9 us (21%)
  Pallas kernels  11.4 us (17%)
  other arithmetic  1.36 us (2%)
  local copies, waits for them, and re-layouts  0.88 us (1%)
    ppermute x22, starting transfers between devices, moved(): return lax.ppermute(value, AXES, pairs)  37.5 us
    ppermute x22, waiting for transfers between devices, moved(): return lax.ppermute(value, AXES, pairs)  13.9 us
    pallas_call x1, Pallas kernels, multiply(): pl.pallas_call(multiply_kernel, out_shape=jax.ShapeDtypeStruct((freqs, 2,...  11.4 us
  transfers between devices with their start and end apart: 22, of which 8 were waited for; matrix products, arithmetic and copies ran while one was open for 2% of the time, Pallas kernels for 0%

profile of v13, /device:TPU:1, one launch (start us, length us, event | category | flops | bytes accessed | tf_op | source)
XLA Modules:
  0.0 65.2 jit_solution(15171461515003487055)
XLA Ops:
  0.0 2.1 %collective-permute-start = (bf16[4,2,64,512]{3,2,1,0:T(8,128)(2,1)}, bf16[4,2,64,512]{3,2,1,0:T(8,128)(2,1)S(1)}, u32[]{:S(2)}, u32[]{:S(2)}) collective-permute-start(bf16[4,2,64,512]{3,2,1,0:T(8,128)(2,1)} %refs_16_.1), channel_id=1, source_target_pairs={{0,48},{1,17},{2,50},{3,19},{4,52},{5,21},{6,54},{7,23},{16,0},{17... | collective-permute-start | bytes 1572872 | tf_op jit(solution)/shard_map/b_3/ppermute | solution.py:31
  2.1 2.7 %collective-permute-start.7 = (bf16[4,2,64,512]{3,2,1,0:T(8,128)(2,1)}, bf16[4,2,64,512]{3,2,1,0:T(8,128)(2,1)S(1)}, u32[]{:S(2)}, u32[]{:S(2)}) collective-permute-start(bf16[4,2,64,512]{3,2,1,0:T(8,128)(2,1)} %refs_16_.1), channel_id=1, source_target_pairs={{0,64},{1,65},{2,66},{3,67},{4,68},{5,69},{6,70},{7,71},{16,80},{1... | collective-permute-start | bytes 1572872 | tf_op jit(solution)/shard_map/b_x/ppermute | solution.py:31
  4.9 1.6 %collective-permute-start.6 = (bf16[4,2,32,1024]{3,2,1,0:T(8,128)(2,1)}, bf16[4,2,32,1024]{3,2,1,0:T(8,128)(2,1)S(1)}, u32[]{:S(2)}, u32[]{:S(2)}) collective-permute-start(bf16[4,2,32,1024]{3,2,1,0:T(8,128)(2,1)} %refs_1_.1), channel_id=1, source_target_pairs={{0,6},{1,3},{2,0},{3,5},{4,2},{5,7},{6,4},{7,1},{16,22},{17,19},{1... | collective-permute-start | bytes 1572872 | tf_op jit(solution)/shard_map/a_3/ppermute | solution.py:31
  6.5 1.4 %collective-permute-start.4 = (bf16[4,2,64,512]{3,2,1,0:T(8,128)(2,1)}, bf16[4,2,64,512]{3,2,1,0:T(8,128)(2,1)S(1)}, u32[]{:S(2)}, u32[]{:S(2)}) collective-permute-start(bf16[4,2,64,512]{3,2,1,0:T(8,128)(2,1)} %refs_16_.1), channel_id=1, source_target_pairs={{0,16},{1,49},{2,18},{3,51},{4,20},{5,53},{6,22},{7,55},{16,32},{1... | collective-permute-start | bytes 1572872 | tf_op jit(solution)/shard_map/b_1/ppermute | solution.py:31
  8.0 2.1 %collective-permute-start.3 = (bf16[4,2,32,1024]{3,2,1,0:T(8,128)(2,1)}, bf16[4,2,32,1024]{3,2,1,0:T(8,128)(2,1)S(1)}, u32[]{:S(2)}, u32[]{:S(2)}) collective-permute-start(bf16[4,2,32,1024]{3,2,1,0:T(8,128)(2,1)} %refs_1_.1), channel_id=1, source_target_pairs={{0,2},{1,7},{2,4},{3,1},{4,6},{5,3},{6,0},{7,5},{16,18},{17,23},{1... | collective-permute-start | bytes 1572872 | tf_op jit(solution)/shard_map/a_1/ppermute | solution.py:31
  10.1 0.7 %fusion.1 = (s32[12]{0:T(128)S(1)}, s32[12]{0:T(128)S(1)}) fusion(pred[]{:T(512)S(6)} %eq.18, s32[]{:T(128)S(6)} %select_n.83, s32[]{:T(128)S(6)} %select_n.80, s32[12]{0:T(128)} %param.5), kind=kLoop, calls=%fused_computation.25 | loop fusion | flops 612 | bytes 153 | tf_op jit(solution)/shard_map/add | solution.py:150
  10.8 0.7 %broadcast_multiply_fusion = (s32[12]{0:T(128)S(1)}, s32[12]{0:T(128)S(1)}) fusion(s32[12]{0:T(128)} %param.5, s32[12]{0:T(128)S(1)} %get-tuple-element.36, s32[]{:T(128)S(6)} %select_n.75, s32[]{:T(128)S(6)} %select_n.73, s32[]{:T(128)S(6)} %select_n.71), kind=kLoop, calls=%fused_computation.29 | loop fusion | flops 684 | bytes 204 | tf_op jit(solution)/shard_map/mul | solution.py:151
  11.4 0.0 collective-permute-done.refs_19_
  11.5 0.4 collective-permute-start.1
  11.8 3.0 %collective-permute-done.7.refs_20_ = bf16[4,2,64,512]{3,2,1,0:T(8,128)(2,1)S(1)} collective-permute-done((bf16[4,2,64,512]{3,2,1,0:T(8,128)(2,1)}, bf16[4,2,64,512]{3,2,1,0:T(8,128)(2,1)S(1)}, u32[]{:S(2)}, u32[]{:S(2)}) %collective-permute-start.7) | collective-permute-done | bytes 524320 | tf_op jit(solution)/shard_map/b_x/ppermute | solution.py:31
  14.9 0.8 %collective-permute-done.6.refs_4_ = bf16[4,2,32,1024]{3,2,1,0:T(8,128)(2,1)S(1)} collective-permute-done((bf16[4,2,32,1024]{3,2,1,0:T(8,128)(2,1)}, bf16[4,2,32,1024]{3,2,1,0:T(8,128)(2,1)S(1)}, u32[]{:S(2)}, u32[]{:S(2)}) %collective-permute-start.6) | collective-permute-done | bytes 524320 | tf_op jit(solution)/shard_map/a_3/ppermute | solution.py:31
  15.7 6.8 %collective-permute-start.8 = (bf16[4,2,32,1024]{3,2,1,0:T(8,128)(2,1)S(1)}, bf16[4,2,32,1024]{3,2,1,0:T(8,128)(2,1)S(1)}, u32[]{:S(2)}, u32[]{:S(2)}) collective-permute-start(bf16[4,2,32,1024]{3,2,1,0:T(8,128)(2,1)S(1)} %collective-permute-done.6.refs_4_), channel_id=1, source_target_pairs={{0,1},{1,0},{2,3},{3,2},{4,5},{5,4},{6,7},{7,6},{16,17},{17,16},{1... | collective-permute-start | bytes 1572872 | tf_op jit(solution)/shard_map/other_3/ppermute | solution.py:31
  22.5 1.5 %collective-permute-start.14 = (bf16[4,2,64,512]{3,2,1,0:T(8,128)(2,1)S(1)}, bf16[4,2,64,512]{3,2,1,0:T(8,128)(2,1)S(1)}, u32[]{:S(2)}, u32[]{:S(2)}) collective-permute-start(bf16[4,2,64,512]{3,2,1,0:T(8,128)(2,1)S(1)} %collective-permute-done.7.refs_20_), channel_id=1, source_target_pairs={{0,16},{1,49},{2,18},{3,51},{4,20},{5,53},{6,22},{7,55},{16,32},{1... | collective-permute-start | bytes 1572872 | tf_op jit(solution)/shard_map/b_x1/ppermute | solution.py:31
  24.0 0.0 collective-permute-done.4.refs_17_
  24.0 0.0 collective-permute-done.3.refs_2_
  24.0 3.4 %collective-permute-start.5 = (bf16[4,2,32,1024]{3,2,1,0:T(8,128)(2,1)S(1)}, bf16[4,2,32,1024]{3,2,1,0:T(8,128)(2,1)S(1)}, u32[]{:S(2)}, u32[]{:S(2)}) collective-permute-start(bf16[4,2,32,1024]{3,2,1,0:T(8,128)(2,1)S(1)} %collective-permute-done.3.refs_2_), channel_id=1, source_target_pairs={{0,2},{1,7},{2,4},{3,1},{4,6},{5,3},{6,0},{7,5},{16,18},{17,23},{1... | collective-permute-start | bytes 1572872 | tf_op jit(solution)/shard_map/a_2/ppermute | solution.py:31
  27.4 0.0 collective-permute-start.12
  27.4 0.0 collective-permute-done.1.refs_5_
  27.4 0.4 collective-permute-start.2
  27.8 0.0 collective-permute-done.8.refs_12_
  27.8 2.4 %collective-permute-start.9 = (bf16[4,2,64,512]{3,2,1,0:T(8,128)(2,1)S(1)}, bf16[4,2,64,512]{3,2,1,0:T(8,128)(2,1)S(1)}, u32[]{:S(2)}, u32[]{:S(2)}) collective-permute-start(bf16[4,2,64,512]{3,2,1,0:T(8,128)(2,1)S(1)} %collective-permute-done.4.refs_17_), channel_id=1, source_target_pairs={{0,16},{1,49},{2,18},{3,51},{4,20},{5,53},{6,22},{7,55},{16,32},{1... | collective-permute-start | bytes 1572872 | tf_op jit(solution)/shard_map/b_2/ppermute | solution.py:31
  30.3 3.7 %collective-permute-done.14.refs_21_ = bf16[4,2,64,512]{3,2,1,0:T(8,128)(2,1)S(1)} collective-permute-done((bf16[4,2,64,512]{3,2,1,0:T(8,128)(2,1)S(1)}, bf16[4,2,64,512]{3,2,1,0:T(8,128)(2,1)S(1)}, u32[]{:S(2)}, u32[]{:S(2)}) %collective-permute-start.14) | collective-permute-done | bytes 524320 | tf_op jit(solution)/shard_map/b_x1/ppermute | solution.py:31
  33.9 0.0 collective-permute-done.5.refs_3_
  33.9 0.4 collective-permute-start.15
  34.3 1.2 %collective-permute-start.20 = (bf16[4,2,64,512]{3,2,1,0:T(8,128)(2,1)S(1)}, bf16[4,2,64,512]{3,2,1,0:T(8,128)(2,1)S(1)}, u32[]{:S(2)}, u32[]{:S(2)}) collective-permute-start(bf16[4,2,64,512]{3,2,1,0:T(8,128)(2,1)S(1)} %collective-permute-done.14.refs_21_), channel_id=1, source_target_pairs={{0,16},{1,49},{2,18},{3,51},{4,20},{5,53},{6,22},{7,55},{16,32},{1... | collective-permute-start | bytes 1572872 | tf_op jit(solution)/shard_map/b_x2/ppermute | solution.py:31
  35.5 2.8 %collective-permute-done.12.refs_23_ = bf16[4,2,64,512]{3,2,1,0:T(8,128)(2,1)S(1)} collective-permute-done((bf16[4,2,64,512]{3,2,1,0:T(8,128)(2,1)S(1)}, bf16[4,2,64,512]{3,2,1,0:T(8,128)(2,1)S(1)}, u32[]{:S(2)}, u32[]{:S(2)}) %collective-permute-start.12) | collective-permute-done | bytes 524320 | tf_op jit(solution)/shard_map/b_x3/ppermute | solution.py:31
  38.3 4.3 %collective-permute-start.13 = (bf16[4,2,32,1024]{3,2,1,0:T(8,128)(2,1)S(1)}, bf16[4,2,32,1024]{3,2,1,0:T(8,128)(2,1)S(1)}, u32[]{:S(2)}, u32[]{:S(2)}) collective-permute-start(bf16[4,2,32,1024]{3,2,1,0:T(8,128)(2,1)S(1)} %collective-permute-done.1.refs_5_), channel_id=1, source_target_pairs={{0,2},{1,7},{2,4},{3,1},{4,6},{5,3},{6,0},{7,5},{16,18},{17,23},{1... | collective-permute-start | bytes 1572872 | tf_op jit(solution)/shard_map/a_x1/ppermute | solution.py:31
  42.6 0.0 collective-permute-done.2.refs_8_
  42.7 0.0 collective-permute-start.16
  42.7 0.0 collective-permute-done.9.refs_18_
  42.7 1.5 %collective-permute-start.10 = (bf16[4,2,32,1024]{3,2,1,0:T(8,128)(2,1)S(1)}, bf16[4,2,32,1024]{3,2,1,0:T(8,128)(2,1)S(1)}, u32[]{:S(2)}, u32[]{:S(2)}) collective-permute-start(bf16[4,2,32,1024]{3,2,1,0:T(8,128)(2,1)S(1)} %collective-permute-done.5.refs_3_), channel_id=1, source_target_pairs={{0,1},{1,0},{2,3},{3,2},{4,5},{5,4},{6,7},{7,6},{16,17},{17,16},{1... | collective-permute-start | bytes 1572872 | tf_op jit(solution)/shard_map/other_2/ppermute | solution.py:31
  44.2 1.8 %collective-permute-done.15.refs_7_ = bf16[4,2,32,1024]{3,2,1,0:T(8,128)(2,1)S(1)} collective-permute-done((bf16[4,2,32,1024]{3,2,1,0:T(8,128)(2,1)S(1)}, bf16[4,2,32,1024]{3,2,1,0:T(8,128)(2,1)S(1)}, u32[]{:S(2)}, u32[]{:S(2)}) %collective-permute-start.15) | collective-permute-done | bytes 524320 | tf_op jit(solution)/shard_map/a_x2/ppermute | solution.py:31
  45.9 2.4 %collective-permute-start.17 = (bf16[4,2,32,1024]{3,2,1,0:T(8,128)(2,1)S(1)}, bf16[4,2,32,1024]{3,2,1,0:T(8,128)(2,1)S(1)}, u32[]{:S(2)}, u32[]{:S(2)}) collective-permute-start(bf16[4,2,32,1024]{3,2,1,0:T(8,128)(2,1)S(1)} %collective-permute-done.3.refs_2_), channel_id=1, source_target_pairs={{0,1},{1,0},{2,3},{3,2},{4,5},{5,4},{6,7},{7,6},{16,17},{17,16},{1... | collective-permute-start | bytes 1572872 | tf_op jit(solution)/shard_map/other_1/ppermute | solution.py:31
  48.4 0.0 collective-permute-done.20.refs_22_
  48.4 1.4 %collective-permute-start.21 = (bf16[4,2,32,1024]{3,2,1,0:T(8,128)(2,1)S(1)}, bf16[4,2,32,1024]{3,2,1,0:T(8,128)(2,1)S(1)}, u32[]{:S(2)}, u32[]{:S(2)}) collective-permute-start(bf16[4,2,32,1024]{3,2,1,0:T(8,128)(2,1)S(1)} %collective-permute-done.15.refs_7_), channel_id=1, source_target_pairs={{0,1},{1,0},{2,3},{3,2},{4,5},{5,4},{6,7},{7,6},{16,17},{17,16},{1... | collective-permute-start | bytes 1572872 | tf_op jit(solution)/shard_map/other_x2/ppermute | solution.py:31
  49.8 0.0 collective-permute-done.13.refs_6_
  49.8 0.7 %collective-permute-start.19 = (bf16[4,2,32,1024]{3,2,1,0:T(8,128)(2,1)S(1)}, bf16[4,2,32,1024]{3,2,1,0:T(8,128)(2,1)S(1)}, u32[]{:S(2)}, u32[]{:S(2)}) collective-permute-start(bf16[4,2,32,1024]{3,2,1,0:T(8,128)(2,1)S(1)} %collective-permute-done.13.refs_6_), channel_id=1, source_target_pairs={{0,1},{1,0},{2,3},{3,2},{4,5},{5,4},{6,7},{7,6},{16,17},{17,16},{1... | collective-permute-start | bytes 1572872 | tf_op jit(solution)/shard_map/other_x1/ppermute | solution.py:31
  50.5 0.0 collective-permute-done.16.refs_9_
  50.5 0.1 collective-permute-start.18
  50.6 0.0 collective-permute-done.10.refs_11_
  50.6 0.4 collective-permute-start.11
  51.0 0.0 collective-permute-done.17.refs_10_
  51.1 0.3 collective-permute-done.21.refs_15_
  51.3 0.7 %collective-permute-done.19.refs_14_ = bf16[4,2,32,1024]{3,2,1,0:T(8,128)(2,1)S(1)} collective-permute-done((bf16[4,2,32,1024]{3,2,1,0:T(8,128)(2,1)S(1)}, bf16[4,2,32,1024]{3,2,1,0:T(8,128)(2,1)S(1)}, u32[]{:S(2)}, u32[]{:S(2)}) %collective-permute-start.19) | collective-permute-done | bytes 524320 | tf_op jit(solution)/shard_map/other_x1/ppermute | solution.py:31
  52.1 0.7 %collective-permute-done.18.refs_13_ = bf16[4,2,32,1024]{3,2,1,0:T(8,128)(2,1)S(1)} collective-permute-done((bf16[4,2,32,1024]{3,2,1,0:T(8,128)(2,1)S(1)}, bf16[4,2,32,1024]{3,2,1,0:T(8,128)(2,1)S(1)}, u32[]{:S(2)}, u32[]{:S(2)}) %collective-permute-start.18) | collective-permute-done | bytes 524320 | tf_op jit(solution)/shard_map/other_x/ppermute | solution.py:31
  52.8 0.8 %copy-done.20 = bf16[4,2,32,1024]{3,2,1,0:T(8,128)(2,1)} copy-done((bf16[4,2,32,1024]{3,2,1,0:T(8,128)(2,1)}, bf16[4,2,32,1024]{3,2,1,0:T(8,128)(2,1)S(1)}, u32[]{:S(2)}) %copy-start.20) | copy-done | bytes 524312
  53.6 0.0 collective-permute-done.11.refs_0_
  53.8 11.4 %shard_map.37 = bf16[4,2,1024,512]{3,2,1,0:T(8,128)(2,1)} custom-call(s32[12]{0:T(128)S(1)} %get-tuple-element.38.a_where, s32[12]{0:T(128)S(1)} %get-tuple-element.35.b_where, s32[12]{0:T(128)S(1)} %get-tuple-element.37.b_row, bf16[4,2,32,1024]{3,2,1,0:T(8,128)(2,1)S(1)} %collective-permute-done.11.refs_0_, bf16[4,2,32,1024]{3,2,1,0:T(8,128)(2,1)} %refs_1_.1, ...), custom_call_target="tpu_custom_call" | custom-call | flops 6442450944 | bytes 20971520 | tf_op jit(solution)/shard_map/pallas_call | solution.py:115
  (41 shorter events, 0.1 us)
Async XLA Ops:
  0.0 11.4 %collective-permute-start = (bf16[4,2,64,512]{3,2,1,0:T(8,128)(2,1)}, bf16[4,2,64,512]{3,2,1,0:T(8,128)(2,1)S(1)}, u32[]{:S(2)}, u32[]{:S(2)}) collective-permute-start(bf16[4,2,64,512]{3,2,1,0:T(8,128)(2,1)} %refs_16_.1), channel_id=1, source_target_pairs={{0,48},{1,17},{2,50},{3,19},{4,52},{5,21},{6,54},{7,23},{16,0},{17... | collective-permute-start | bytes 1572872 | tf_op jit(solution)/shard_map/b_3/ppermute | solution.py:31
  2.1 12.7 %collective-permute-start.7 = (bf16[4,2,64,512]{3,2,1,0:T(8,128)(2,1)}, bf16[4,2,64,512]{3,2,1,0:T(8,128)(2,1)S(1)}, u32[]{:S(2)}, u32[]{:S(2)}) collective-permute-start(bf16[4,2,64,512]{3,2,1,0:T(8,128)(2,1)} %refs_16_.1), channel_id=1, source_target_pairs={{0,64},{1,65},{2,66},{3,67},{4,68},{5,69},{6,70},{7,71},{16,80},{1... | collective-permute-start | bytes 1572872 | tf_op jit(solution)/shard_map/b_x/ppermute | solution.py:31
  4.9 10.8 %collective-permute-start.6 = (bf16[4,2,32,1024]{3,2,1,0:T(8,128)(2,1)}, bf16[4,2,32,1024]{3,2,1,0:T(8,128)(2,1)S(1)}, u32[]{:S(2)}, u32[]{:S(2)}) collective-permute-start(bf16[4,2,32,1024]{3,2,1,0:T(8,128)(2,1)} %refs_1_.1), channel_id=1, source_target_pairs={{0,6},{1,3},{2,0},{3,5},{4,2},{5,7},{6,4},{7,1},{16,22},{17,19},{1... | collective-permute-start | bytes 1572872 | tf_op jit(solution)/shard_map/a_3/ppermute | solution.py:31
  6.5 17.5 %collective-permute-start.4 = (bf16[4,2,64,512]{3,2,1,0:T(8,128)(2,1)}, bf16[4,2,64,512]{3,2,1,0:T(8,128)(2,1)S(1)}, u32[]{:S(2)}, u32[]{:S(2)}) collective-permute-start(bf16[4,2,64,512]{3,2,1,0:T(8,128)(2,1)} %refs_16_.1), channel_id=1, source_target_pairs={{0,16},{1,49},{2,18},{3,51},{4,20},{5,53},{6,22},{7,55},{16,32},{1... | collective-permute-start | bytes 1572872 | tf_op jit(solution)/shard_map/b_1/ppermute | solution.py:31
  8.0 16.1 %collective-permute-start.3 = (bf16[4,2,32,1024]{3,2,1,0:T(8,128)(2,1)}, bf16[4,2,32,1024]{3,2,1,0:T(8,128)(2,1)S(1)}, u32[]{:S(2)}, u32[]{:S(2)}) collective-permute-start(bf16[4,2,32,1024]{3,2,1,0:T(8,128)(2,1)} %refs_1_.1), channel_id=1, source_target_pairs={{0,2},{1,7},{2,4},{3,1},{4,6},{5,3},{6,0},{7,5},{16,18},{17,23},{1... | collective-permute-start | bytes 1572872 | tf_op jit(solution)/shard_map/a_1/ppermute | solution.py:31
  11.4 42.2 %copy-start = (bf16[4,2,64,512]{3,2,1,0:T(8,128)(2,1)}, bf16[4,2,64,512]{3,2,1,0:T(8,128)(2,1)S(1)}, u32[]{:S(2)}) copy-start(bf16[4,2,64,512]{3,2,1,0:T(8,128)(2,1)S(1)} %collective-permute-done.refs_19_) | copy-start | bytes 1572868
  11.5 15.9 %collective-permute-start.1 = (bf16[4,2,32,1024]{3,2,1,0:T(8,128)(2,1)}, bf16[4,2,32,1024]{3,2,1,0:T(8,128)(2,1)S(1)}, u32[]{:S(2)}, u32[]{:S(2)}) collective-permute-start(bf16[4,2,32,1024]{3,2,1,0:T(8,128)(2,1)} %refs_1_.1), channel_id=1, source_target_pairs={{0,8},{1,9},{2,10},{3,11},{4,12},{5,13},{6,14},{7,15},{16,24},{17,... | collective-permute-start | bytes 1572872 | tf_op jit(solution)/shard_map/a_x/ppermute | solution.py:31
  14.9 38.8 %copy-start.1 = (bf16[4,2,64,512]{3,2,1,0:T(8,128)(2,1)}, bf16[4,2,64,512]{3,2,1,0:T(8,128)(2,1)S(1)}, u32[]{:S(2)}) copy-start(bf16[4,2,64,512]{3,2,1,0:T(8,128)(2,1)S(1)} %collective-permute-done.7.refs_20_) | copy-start | bytes 1572868
  15.7 37.9 %copy-start.2 = (bf16[4,2,32,1024]{3,2,1,0:T(8,128)(2,1)}, bf16[4,2,32,1024]{3,2,1,0:T(8,128)(2,1)S(1)}, u32[]{:S(2)}) copy-start(bf16[4,2,32,1024]{3,2,1,0:T(8,128)(2,1)S(1)} %collective-permute-done.6.refs_4_) | copy-start | bytes 1572868
  15.7 12.1 %collective-permute-start.8 = (bf16[4,2,32,1024]{3,2,1,0:T(8,128)(2,1)S(1)}, bf16[4,2,32,1024]{3,2,1,0:T(8,128)(2,1)S(1)}, u32[]{:S(2)}, u32[]{:S(2)}) collective-permute-start(bf16[4,2,32,1024]{3,2,1,0:T(8,128)(2,1)S(1)} %collective-permute-done.6.refs_4_), channel_id=1, source_target_pairs={{0,1},{1,0},{2,3},{3,2},{4,5},{5,4},{6,7},{7,6},{16,17},{17,16},{1... | collective-permute-start | bytes 1572872 | tf_op jit(solution)/shard_map/other_3/ppermute | solution.py:31
  22.5 11.4 %collective-permute-start.14 = (bf16[4,2,64,512]{3,2,1,0:T(8,128)(2,1)S(1)}, bf16[4,2,64,512]{3,2,1,0:T(8,128)(2,1)S(1)}, u32[]{:S(2)}, u32[]{:S(2)}) collective-permute-start(bf16[4,2,64,512]{3,2,1,0:T(8,128)(2,1)S(1)} %collective-permute-done.7.refs_20_), channel_id=1, source_target_pairs={{0,16},{1,49},{2,18},{3,51},{4,20},{5,53},{6,22},{7,55},{16,32},{1... | collective-permute-start | bytes 1572872 | tf_op jit(solution)/shard_map/b_x1/ppermute | solution.py:31
  24.0 29.6 %copy-start.3 = (bf16[4,2,64,512]{3,2,1,0:T(8,128)(2,1)}, bf16[4,2,64,512]{3,2,1,0:T(8,128)(2,1)S(1)}, u32[]{:S(2)}) copy-start(bf16[4,2,64,512]{3,2,1,0:T(8,128)(2,1)S(1)} %collective-permute-done.4.refs_17_) | copy-start | bytes 1572868
  24.0 29.6 %copy-start.4 = (bf16[4,2,32,1024]{3,2,1,0:T(8,128)(2,1)}, bf16[4,2,32,1024]{3,2,1,0:T(8,128)(2,1)S(1)}, u32[]{:S(2)}) copy-start(bf16[4,2,32,1024]{3,2,1,0:T(8,128)(2,1)S(1)} %collective-permute-done.3.refs_2_) | copy-start | bytes 1572868
  24.0 9.9 %collective-permute-start.5 = (bf16[4,2,32,1024]{3,2,1,0:T(8,128)(2,1)S(1)}, bf16[4,2,32,1024]{3,2,1,0:T(8,128)(2,1)S(1)}, u32[]{:S(2)}, u32[]{:S(2)}) collective-permute-start(bf16[4,2,32,1024]{3,2,1,0:T(8,128)(2,1)S(1)} %collective-permute-done.3.refs_2_), channel_id=1, source_target_pairs={{0,2},{1,7},{2,4},{3,1},{4,6},{5,3},{6,0},{7,5},{16,18},{17,23},{1... | collective-permute-start | bytes 1572872 | tf_op jit(solution)/shard_map/a_2/ppermute | solution.py:31
  27.4 10.9 %collective-permute-start.12 = (bf16[4,2,64,512]{3,2,1,0:T(8,128)(2,1)S(1)}, bf16[4,2,64,512]{3,2,1,0:T(8,128)(2,1)S(1)}, u32[]{:S(2)}, u32[]{:S(2)}) collective-permute-start(bf16[4,2,64,512]{3,2,1,0:T(8,128)(2,1)S(1)} %collective-permute-done.7.refs_20_), channel_id=1, source_target_pairs={{0,48},{1,17},{2,50},{3,19},{4,52},{5,21},{6,54},{7,23},{16,0},{17... | collective-permute-start | bytes 1572872 | tf_op jit(solution)/shard_map/b_x3/ppermute | solution.py:31
  27.4 26.3 %copy-start.5 = (bf16[4,2,32,1024]{3,2,1,0:T(8,128)(2,1)}, bf16[4,2,32,1024]{3,2,1,0:T(8,128)(2,1)S(1)}, u32[]{:S(2)}) copy-start(bf16[4,2,32,1024]{3,2,1,0:T(8,128)(2,1)S(1)} %collective-permute-done.1.refs_5_) | copy-start | bytes 1572868
  27.4 15.2 %collective-permute-start.2 = (bf16[4,2,32,1024]{3,2,1,0:T(8,128)(2,1)S(1)}, bf16[4,2,32,1024]{3,2,1,0:T(8,128)(2,1)S(1)}, u32[]{:S(2)}, u32[]{:S(2)}) collective-permute-start(bf16[4,2,32,1024]{3,2,1,0:T(8,128)(2,1)S(1)} %collective-permute-done.1.refs_5_), channel_id=1, source_target_pairs={{0,6},{1,3},{2,0},{3,5},{4,2},{5,7},{6,4},{7,1},{16,22},{17,19},{1... | collective-permute-start | bytes 1572872 | tf_op jit(solution)/shard_map/a_x3/ppermute | solution.py:31
  27.8 25.8 %copy-start.6 = (bf16[4,2,32,1024]{3,2,1,0:T(8,128)(2,1)}, bf16[4,2,32,1024]{3,2,1,0:T(8,128)(2,1)S(1)}, u32[]{:S(2)}) copy-start(bf16[4,2,32,1024]{3,2,1,0:T(8,128)(2,1)S(1)} %collective-permute-done.8.refs_12_) | copy-start | bytes 1572868
  27.8 14.8 %collective-permute-start.9 = (bf16[4,2,64,512]{3,2,1,0:T(8,128)(2,1)S(1)}, bf16[4,2,64,512]{3,2,1,0:T(8,128)(2,1)S(1)}, u32[]{:S(2)}, u32[]{:S(2)}) collective-permute-start(bf16[4,2,64,512]{3,2,1,0:T(8,128)(2,1)S(1)} %collective-permute-done.4.refs_17_), channel_id=1, source_target_pairs={{0,16},{1,49},{2,18},{3,51},{4,20},{5,53},{6,22},{7,55},{16,32},{1... | collective-permute-start | bytes 1572872 | tf_op jit(solution)/shard_map/b_2/ppermute | solution.py:31
  33.9 19.7 %copy-start.7 = (bf16[4,2,64,512]{3,2,1,0:T(8,128)(2,1)}, bf16[4,2,64,512]{3,2,1,0:T(8,128)(2,1)S(1)}, u32[]{:S(2)}) copy-start(bf16[4,2,64,512]{3,2,1,0:T(8,128)(2,1)S(1)} %collective-permute-done.14.refs_21_) | copy-start | bytes 1572868
  33.9 19.8 %copy-start.8 = (bf16[4,2,32,1024]{3,2,1,0:T(8,128)(2,1)}, bf16[4,2,32,1024]{3,2,1,0:T(8,128)(2,1)S(1)}, u32[]{:S(2)}) copy-start(bf16[4,2,32,1024]{3,2,1,0:T(8,128)(2,1)S(1)} %collective-permute-done.5.refs_3_) | copy-start | bytes 1572868
  33.9 12.0 %collective-permute-start.15 = (bf16[4,2,32,1024]{3,2,1,0:T(8,128)(2,1)S(1)}, bf16[4,2,32,1024]{3,2,1,0:T(8,128)(2,1)S(1)}, u32[]{:S(2)}, u32[]{:S(2)}) collective-permute-start(bf16[4,2,32,1024]{3,2,1,0:T(8,128)(2,1)S(1)} %collective-permute-done.5.refs_3_), channel_id=1, source_target_pairs={{0,8},{1,9},{2,10},{3,11},{4,12},{5,13},{6,14},{7,15},{16,24},{17,... | collective-permute-start | bytes 1572872 | tf_op jit(solution)/shard_map/a_x2/ppermute | solution.py:31
  34.3 14.0 %collective-permute-start.20 = (bf16[4,2,64,512]{3,2,1,0:T(8,128)(2,1)S(1)}, bf16[4,2,64,512]{3,2,1,0:T(8,128)(2,1)S(1)}, u32[]{:S(2)}, u32[]{:S(2)}) collective-permute-start(bf16[4,2,64,512]{3,2,1,0:T(8,128)(2,1)S(1)} %collective-permute-done.14.refs_21_), channel_id=1, source_target_pairs={{0,16},{1,49},{2,18},{3,51},{4,20},{5,53},{6,22},{7,55},{16,32},{1... | collective-permute-start | bytes 1572872 | tf_op jit(solution)/shard_map/b_x2/ppermute | solution.py:31
  38.3 15.4 %copy-start.9 = (bf16[4,2,64,512]{3,2,1,0:T(8,128)(2,1)}, bf16[4,2,64,512]{3,2,1,0:T(8,128)(2,1)S(1)}, u32[]{:S(2)}) copy-start(bf16[4,2,64,512]{3,2,1,0:T(8,128)(2,1)S(1)} %collective-permute-done.12.refs_23_) | copy-start | bytes 1572868
  38.3 11.5 %collective-permute-start.13 = (bf16[4,2,32,1024]{3,2,1,0:T(8,128)(2,1)S(1)}, bf16[4,2,32,1024]{3,2,1,0:T(8,128)(2,1)S(1)}, u32[]{:S(2)}, u32[]{:S(2)}) collective-permute-start(bf16[4,2,32,1024]{3,2,1,0:T(8,128)(2,1)S(1)} %collective-permute-done.1.refs_5_), channel_id=1, source_target_pairs={{0,2},{1,7},{2,4},{3,1},{4,6},{5,3},{6,0},{7,5},{16,18},{17,23},{1... | collective-permute-start | bytes 1572872 | tf_op jit(solution)/shard_map/a_x1/ppermute | solution.py:31
  42.7 11.1 %copy-start.10 = (bf16[4,2,32,1024]{3,2,1,0:T(8,128)(2,1)}, bf16[4,2,32,1024]{3,2,1,0:T(8,128)(2,1)S(1)}, u32[]{:S(2)}) copy-start(bf16[4,2,32,1024]{3,2,1,0:T(8,128)(2,1)S(1)} %collective-permute-done.2.refs_8_) | copy-start | bytes 1572868
  42.7 7.9 %collective-permute-start.16 = (bf16[4,2,32,1024]{3,2,1,0:T(8,128)(2,1)}, bf16[4,2,32,1024]{3,2,1,0:T(8,128)(2,1)S(1)}, u32[]{:S(2)}, u32[]{:S(2)}) collective-permute-start(bf16[4,2,32,1024]{3,2,1,0:T(8,128)(2,1)} %refs_1_.1), channel_id=1, source_target_pairs={{0,1},{1,0},{2,3},{3,2},{4,5},{5,4},{6,7},{7,6},{16,17},{17,16},{1... | collective-permute-start | bytes 1572872 | tf_op jit(solution)/shard_map/other/ppermute | solution.py:31
  42.7 11.1 %copy-start.11 = (bf16[4,2,64,512]{3,2,1,0:T(8,128)(2,1)}, bf16[4,2,64,512]{3,2,1,0:T(8,128)(2,1)S(1)}, u32[]{:S(2)}) copy-start(bf16[4,2,64,512]{3,2,1,0:T(8,128)(2,1)S(1)} %collective-permute-done.9.refs_18_) | copy-start | bytes 1572868
  42.7 7.9 %collective-permute-start.10 = (bf16[4,2,32,1024]{3,2,1,0:T(8,128)(2,1)S(1)}, bf16[4,2,32,1024]{3,2,1,0:T(8,128)(2,1)S(1)}, u32[]{:S(2)}, u32[]{:S(2)}) collective-permute-start(bf16[4,2,32,1024]{3,2,1,0:T(8,128)(2,1)S(1)} %collective-permute-done.5.refs_3_), channel_id=1, source_target_pairs={{0,1},{1,0},{2,3},{3,2},{4,5},{5,4},{6,7},{7,6},{16,17},{17,16},{1... | collective-permute-start | bytes 1572872 | tf_op jit(solution)/shard_map/other_2/ppermute | solution.py:31
  45.9 7.8 %copy-start.12 = (bf16[4,2,32,1024]{3,2,1,0:T(8,128)(2,1)}, bf16[4,2,32,1024]{3,2,1,0:T(8,128)(2,1)S(1)}, u32[]{:S(2)}) copy-start(bf16[4,2,32,1024]{3,2,1,0:T(8,128)(2,1)S(1)} %collective-permute-done.15.refs_7_) | copy-start | bytes 1572868
  45.9 5.1 %collective-permute-start.17 = (bf16[4,2,32,1024]{3,2,1,0:T(8,128)(2,1)S(1)}, bf16[4,2,32,1024]{3,2,1,0:T(8,128)(2,1)S(1)}, u32[]{:S(2)}, u32[]{:S(2)}) collective-permute-start(bf16[4,2,32,1024]{3,2,1,0:T(8,128)(2,1)S(1)} %collective-permute-done.3.refs_2_), channel_id=1, source_target_pairs={{0,1},{1,0},{2,3},{3,2},{4,5},{5,4},{6,7},{7,6},{16,17},{17,16},{1... | collective-permute-start | bytes 1572872 | tf_op jit(solution)/shard_map/other_1/ppermute | solution.py:31
  48.4 5.4 %copy-start.13 = (bf16[4,2,64,512]{3,2,1,0:T(8,128)(2,1)}, bf16[4,2,64,512]{3,2,1,0:T(8,128)(2,1)S(1)}, u32[]{:S(2)}) copy-start(bf16[4,2,64,512]{3,2,1,0:T(8,128)(2,1)S(1)} %collective-permute-done.20.refs_22_) | copy-start | bytes 1572868
  48.4 3.0 %collective-permute-start.21 = (bf16[4,2,32,1024]{3,2,1,0:T(8,128)(2,1)S(1)}, bf16[4,2,32,1024]{3,2,1,0:T(8,128)(2,1)S(1)}, u32[]{:S(2)}, u32[]{:S(2)}) collective-permute-start(bf16[4,2,32,1024]{3,2,1,0:T(8,128)(2,1)S(1)} %collective-permute-done.15.refs_7_), channel_id=1, source_target_pairs={{0,1},{1,0},{2,3},{3,2},{4,5},{5,4},{6,7},{7,6},{16,17},{17,16},{1... | collective-permute-start | bytes 1572872 | tf_op jit(solution)/shard_map/other_x2/ppermute | solution.py:31
  49.8 4.0 %copy-start.14 = (bf16[4,2,32,1024]{3,2,1,0:T(8,128)(2,1)}, bf16[4,2,32,1024]{3,2,1,0:T(8,128)(2,1)S(1)}, u32[]{:S(2)}) copy-start(bf16[4,2,32,1024]{3,2,1,0:T(8,128)(2,1)S(1)} %collective-permute-done.13.refs_6_) | copy-start | bytes 1572868
  49.8 2.3 %collective-permute-start.19 = (bf16[4,2,32,1024]{3,2,1,0:T(8,128)(2,1)S(1)}, bf16[4,2,32,1024]{3,2,1,0:T(8,128)(2,1)S(1)}, u32[]{:S(2)}, u32[]{:S(2)}) collective-permute-start(bf16[4,2,32,1024]{3,2,1,0:T(8,128)(2,1)S(1)} %collective-permute-done.13.refs_6_), channel_id=1, source_target_pairs={{0,1},{1,0},{2,3},{3,2},{4,5},{5,4},{6,7},{7,6},{16,17},{17,16},{1... | collective-permute-start | bytes 1572872 | tf_op jit(solution)/shard_map/other_x1/ppermute | solution.py:31
  50.5 3.2 %copy-start.15 = (bf16[4,2,32,1024]{3,2,1,0:T(8,128)(2,1)}, bf16[4,2,32,1024]{3,2,1,0:T(8,128)(2,1)S(1)}, u32[]{:S(2)}) copy-start(bf16[4,2,32,1024]{3,2,1,0:T(8,128)(2,1)S(1)} %collective-permute-done.16.refs_9_) | copy-start | bytes 1572868
  50.5 2.3 %collective-permute-start.18 = (bf16[4,2,32,1024]{3,2,1,0:T(8,128)(2,1)S(1)}, bf16[4,2,32,1024]{3,2,1,0:T(8,128)(2,1)S(1)}, u32[]{:S(2)}, u32[]{:S(2)}) collective-permute-start(bf16[4,2,32,1024]{3,2,1,0:T(8,128)(2,1)S(1)} %collective-permute-done.1.refs_5_), channel_id=1, source_target_pairs={{0,1},{1,0},{2,3},{3,2},{4,5},{5,4},{6,7},{7,6},{16,17},{17,16},{1... | collective-permute-start | bytes 1572872 | tf_op jit(solution)/shard_map/other_x/ppermute | solution.py:31
  50.6 3.1 %copy-start.16 = (bf16[4,2,32,1024]{3,2,1,0:T(8,128)(2,1)}, bf16[4,2,32,1024]{3,2,1,0:T(8,128)(2,1)S(1)}, u32[]{:S(2)}) copy-start(bf16[4,2,32,1024]{3,2,1,0:T(8,128)(2,1)S(1)} %collective-permute-done.10.refs_11_) | copy-start | bytes 1572868
  50.6 3.0 %collective-permute-start.11 = (bf16[4,2,32,1024]{3,2,1,0:T(8,128)(2,1)S(1)}, bf16[4,2,32,1024]{3,2,1,0:T(8,128)(2,1)S(1)}, u32[]{:S(2)}, u32[]{:S(2)}) collective-permute-start(bf16[4,2,32,1024]{3,2,1,0:T(8,128)(2,1)S(1)} %collective-permute-done.2.refs_8_), channel_id=1, source_target_pairs={{0,1},{1,0},{2,3},{3,2},{4,5},{5,4},{6,7},{7,6},{16,17},{17,16},{1... | collective-permute-start | bytes 1572872 | tf_op jit(solution)/shard_map/other_x3/ppermute | solution.py:31
  51.1 2.7 %copy-start.17 = (bf16[4,2,32,1024]{3,2,1,0:T(8,128)(2,1)}, bf16[4,2,32,1024]{3,2,1,0:T(8,128)(2,1)S(1)}, u32[]{:S(2)}) copy-start(bf16[4,2,32,1024]{3,2,1,0:T(8,128)(2,1)S(1)} %collective-permute-done.17.refs_10_) | copy-start | bytes 1572868
  51.3 2.5 %copy-start.18 = (bf16[4,2,32,1024]{3,2,1,0:T(8,128)(2,1)}, bf16[4,2,32,1024]{3,2,1,0:T(8,128)(2,1)S(1)}, u32[]{:S(2)}) copy-start(bf16[4,2,32,1024]{3,2,1,0:T(8,128)(2,1)S(1)} %collective-permute-done.21.refs_15_) | copy-start | bytes 1572868
  52.1 1.7 %copy-start.19 = (bf16[4,2,32,1024]{3,2,1,0:T(8,128)(2,1)}, bf16[4,2,32,1024]{3,2,1,0:T(8,128)(2,1)S(1)}, u32[]{:S(2)}) copy-start(bf16[4,2,32,1024]{3,2,1,0:T(8,128)(2,1)S(1)} %collective-permute-done.19.refs_14_) | copy-start | bytes 1572868
  52.8 0.8 %copy-start.20 = (bf16[4,2,32,1024]{3,2,1,0:T(8,128)(2,1)}, bf16[4,2,32,1024]{3,2,1,0:T(8,128)(2,1)S(1)}, u32[]{:S(2)}) copy-start(bf16[4,2,32,1024]{3,2,1,0:T(8,128)(2,1)S(1)} %collective-permute-done.18.refs_13_) | copy-start | bytes 1572868

commit v14 on v13

--- a/solution.py
+++ b/solution.py
@@ -8,7 +8,7 @@
 BLK = 32
 STEPS = 12
 ROWS = 256
-SURFACE_ORDER = (1, 2, 3, 4, 5, 6, 7, 8, 9, 10, 11, 12, 13, 14, 15, 0)
+SURFACE_ORDER = (2, 3, 4, 5, 6, 7, 8, 9, 10, 11, 12, 13, 1, 14, 15, 0)
 AXES = ("shot", "rcv")
 X, Y, Z, CORES = 4, 4, 4, 2
 
@@ -129,7 +129,7 @@
                 pltpu.SemaphoreType.DMA((2,)),
             ],
         ),
-        compiler_params=pltpu.CompilerParams(vmem_limit_bytes=53 * 1024 * 1024),
+        compiler_params=pltpu.CompilerParams(vmem_limit_bytes=105 * 512 * 1024),
         cost_estimate=pl.CostEstimate(
             flops=2 * freqs * shots * 2 * rcvs * depth,
             bytes_accessed=20 * 1024 * 1024,
@@ -189,8 +189,8 @@
     other_x = swap("other_x", after(a_x, other))
     other_x3 = swap("other_x3", after(a_x3, other_2))
 
-    a_parts = [other_x3, a, a_1, a_2, a_3, a_x, a_x1, a_x2]
-    a_parts += [a_x3, other, other_1, other_2, other_3, other_x, other_x1, other_x2]
+    a_parts = [other_x3, other_x, a, a_1, a_2, a_3, a_x, a_x1]
+    a_parts += [a_x2, a_x3, other, other_1, other_2, other_3, other_x1, other_x2]
     b_parts = [b, b_1, b_2, b_3, b_x, b_x1, b_x2, b_x3]
     return multiply(a_parts, b_parts, a_where, b_where, b_row)
 

time: 65.7 us -> 65.6 us (level)
  local copies, waits for them, and re-layouts: 0.88 us -> 0.08 us
  waiting for transfers between devices: 13.9 us -> 14.6 us
    unnamed x42 -> x40, local copies, waits for them, and re-layouts: 0.88 us -> 0.08 us
    ppermute x22, waiting for transfers between devices: 13.9 us -> 14.6 us  [moved(): return lax.ppermute(value, AXES, pairs)]
  transfers between devices with their start and end apart: 22 -> 22, of which waited for: 8 -> 9; matrix products, arithmetic and copies ran while one was open for 2% -> 2% of each run, Pallas kernels for 0% -> 0%
where the time goes in v14:
time: 65.6 us; the launch traced here: 65.7 us
  starting transfers between devices  37.5 us (57%)
  waiting for transfers between devices  14.6 us (22%)
  Pallas kernels  11.9 us (18%)
  other arithmetic  1.36 us (2%)
    ppermute x22, starting transfers between devices, moved(): return lax.ppermute(value, AXES, pairs)  37.5 us
    ppermute x22, waiting for transfers between devices, moved(): return lax.ppermute(value, AXES, pairs)  14.6 us
    pallas_call x1, Pallas kernels, multiply(): pl.pallas_call(multiply_kernel, out_shape=jax.ShapeDtypeStruct((freqs, 2,...  11.9 us
  transfers between devices with their start and end apart: 22, of which 9 were waited for; matrix products, arithmetic and copies ran while one was open for 2% of the time, Pallas kernels for 0%

profile of v14, /device:TPU:1, one launch (start us, length us, event | category | flops | bytes accessed | tf_op | source)
XLA Modules:
  0.0 65.7 jit_solution(17302578852485598901)
XLA Ops:
  0.0 2.1 %collective-permute-start = (bf16[4,2,64,512]{3,2,1,0:T(8,128)(2,1)}, bf16[4,2,64,512]{3,2,1,0:T(8,128)(2,1)S(1)}, u32[]{:S(2)}, u32[]{:S(2)}) collective-permute-start(bf16[4,2,64,512]{3,2,1,0:T(8,128)(2,1)} %refs_16_.1), channel_id=1, source_target_pairs={{0,48},{1,17},{2,50},{3,19},{4,52},{5,21},{6,54},{7,23},{16,0},{17... | collective-permute-start | bytes 1572872 | tf_op jit(solution)/shard_map/b_3/ppermute | solution.py:31
  2.1 2.7 %collective-permute-start.7 = (bf16[4,2,64,512]{3,2,1,0:T(8,128)(2,1)}, bf16[4,2,64,512]{3,2,1,0:T(8,128)(2,1)S(1)}, u32[]{:S(2)}, u32[]{:S(2)}) collective-permute-start(bf16[4,2,64,512]{3,2,1,0:T(8,128)(2,1)} %refs_16_.1), channel_id=1, source_target_pairs={{0,64},{1,65},{2,66},{3,67},{4,68},{5,69},{6,70},{7,71},{16,80},{1... | collective-permute-start | bytes 1572872 | tf_op jit(solution)/shard_map/b_x/ppermute | solution.py:31
  4.9 1.6 %collective-permute-start.6 = (bf16[4,2,32,1024]{3,2,1,0:T(8,128)(2,1)}, bf16[4,2,32,1024]{3,2,1,0:T(8,128)(2,1)S(1)}, u32[]{:S(2)}, u32[]{:S(2)}) collective-permute-start(bf16[4,2,32,1024]{3,2,1,0:T(8,128)(2,1)} %refs_2_.1), channel_id=1, source_target_pairs={{0,6},{1,3},{2,0},{3,5},{4,2},{5,7},{6,4},{7,1},{16,22},{17,19},{1... | collective-permute-start | bytes 1572872 | tf_op jit(solution)/shard_map/a_3/ppermute | solution.py:31
  6.5 1.4 %collective-permute-start.4 = (bf16[4,2,64,512]{3,2,1,0:T(8,128)(2,1)}, bf16[4,2,64,512]{3,2,1,0:T(8,128)(2,1)S(1)}, u32[]{:S(2)}, u32[]{:S(2)}) collective-permute-start(bf16[4,2,64,512]{3,2,1,0:T(8,128)(2,1)} %refs_16_.1), channel_id=1, source_target_pairs={{0,16},{1,49},{2,18},{3,51},{4,20},{5,53},{6,22},{7,55},{16,32},{1... | collective-permute-start | bytes 1572872 | tf_op jit(solution)/shard_map/b_1/ppermute | solution.py:31
  8.0 2.1 %collective-permute-start.3 = (bf16[4,2,32,1024]{3,2,1,0:T(8,128)(2,1)}, bf16[4,2,32,1024]{3,2,1,0:T(8,128)(2,1)S(1)}, u32[]{:S(2)}, u32[]{:S(2)}) collective-permute-start(bf16[4,2,32,1024]{3,2,1,0:T(8,128)(2,1)} %refs_2_.1), channel_id=1, source_target_pairs={{0,2},{1,7},{2,4},{3,1},{4,6},{5,3},{6,0},{7,5},{16,18},{17,23},{1... | collective-permute-start | bytes 1572872 | tf_op jit(solution)/shard_map/a_1/ppermute | solution.py:31
  10.1 0.7 %fusion.1 = (s32[12]{0:T(128)S(1)}, s32[12]{0:T(128)S(1)}) fusion(pred[]{:T(512)S(6)} %eq.18, s32[]{:T(128)S(6)} %select_n.83, s32[]{:T(128)S(6)} %select_n.80, s32[12]{0:T(128)} %param.5), kind=kLoop, calls=%fused_computation.25 | loop fusion | flops 612 | bytes 153 | tf_op jit(solution)/shard_map/add | solution.py:150
  10.8 0.7 %broadcast_multiply_fusion = (s32[12]{0:T(128)S(1)}, s32[12]{0:T(128)S(1)}) fusion(s32[12]{0:T(128)} %param.5, s32[12]{0:T(128)S(1)} %get-tuple-element.36, s32[]{:T(128)S(6)} %select_n.75, s32[]{:T(128)S(6)} %select_n.73, s32[]{:T(128)S(6)} %select_n.71), kind=kLoop, calls=%fused_computation.29 | loop fusion | flops 684 | bytes 204 | tf_op jit(solution)/shard_map/mul | solution.py:151
  11.4 0.0 collective-permute-done.refs_19_
  11.5 0.4 collective-permute-start.1
  11.8 3.0 %collective-permute-done.7.refs_20_ = bf16[4,2,64,512]{3,2,1,0:T(8,128)(2,1)S(1)} collective-permute-done((bf16[4,2,64,512]{3,2,1,0:T(8,128)(2,1)}, bf16[4,2,64,512]{3,2,1,0:T(8,128)(2,1)S(1)}, u32[]{:S(2)}, u32[]{:S(2)}) %collective-permute-start.7) | collective-permute-done | bytes 524320 | tf_op jit(solution)/shard_map/b_x/ppermute | solution.py:31
  14.9 0.8 %collective-permute-done.6.refs_5_ = bf16[4,2,32,1024]{3,2,1,0:T(8,128)(2,1)S(1)} collective-permute-done((bf16[4,2,32,1024]{3,2,1,0:T(8,128)(2,1)}, bf16[4,2,32,1024]{3,2,1,0:T(8,128)(2,1)S(1)}, u32[]{:S(2)}, u32[]{:S(2)}) %collective-permute-start.6) | collective-permute-done | bytes 524320 | tf_op jit(solution)/shard_map/a_3/ppermute | solution.py:31
  15.7 6.8 %collective-permute-start.8 = (bf16[4,2,32,1024]{3,2,1,0:T(8,128)(2,1)S(1)}, bf16[4,2,32,1024]{3,2,1,0:T(8,128)(2,1)S(1)}, u32[]{:S(2)}, u32[]{:S(2)}) collective-permute-start(bf16[4,2,32,1024]{3,2,1,0:T(8,128)(2,1)S(1)} %collective-permute-done.6.refs_5_), channel_id=1, source_target_pairs={{0,1},{1,0},{2,3},{3,2},{4,5},{5,4},{6,7},{7,6},{16,17},{17,16},{1... | collective-permute-start | bytes 1572872 | tf_op jit(solution)/shard_map/other_3/ppermute | solution.py:31
  22.5 1.5 %collective-permute-start.16 = (bf16[4,2,64,512]{3,2,1,0:T(8,128)(2,1)S(1)}, bf16[4,2,64,512]{3,2,1,0:T(8,128)(2,1)S(1)}, u32[]{:S(2)}, u32[]{:S(2)}) collective-permute-start(bf16[4,2,64,512]{3,2,1,0:T(8,128)(2,1)S(1)} %collective-permute-done.7.refs_20_), channel_id=1, source_target_pairs={{0,16},{1,49},{2,18},{3,51},{4,20},{5,53},{6,22},{7,55},{16,32},{1... | collective-permute-start | bytes 1572872 | tf_op jit(solution)/shard_map/b_x1/ppermute | solution.py:31
  24.0 0.0 collective-permute-done.4.refs_17_
  24.0 0.0 collective-permute-done.3.refs_3_
  24.0 3.4 %collective-permute-start.5 = (bf16[4,2,32,1024]{3,2,1,0:T(8,128)(2,1)S(1)}, bf16[4,2,32,1024]{3,2,1,0:T(8,128)(2,1)S(1)}, u32[]{:S(2)}, u32[]{:S(2)}) collective-permute-start(bf16[4,2,32,1024]{3,2,1,0:T(8,128)(2,1)S(1)} %collective-permute-done.3.refs_3_), channel_id=1, source_target_pairs={{0,2},{1,7},{2,4},{3,1},{4,6},{5,3},{6,0},{7,5},{16,18},{17,23},{1... | collective-permute-start | bytes 1572872 | tf_op jit(solution)/shard_map/a_2/ppermute | solution.py:31
  27.4 0.0 collective-permute-start.14
  27.4 0.0 collective-permute-done.1.refs_6_
  27.4 0.4 collective-permute-start.2
  27.8 0.0 collective-permute-done.8.refs_13_
  27.8 2.4 %collective-permute-start.9 = (bf16[4,2,64,512]{3,2,1,0:T(8,128)(2,1)S(1)}, bf16[4,2,64,512]{3,2,1,0:T(8,128)(2,1)S(1)}, u32[]{:S(2)}, u32[]{:S(2)}) collective-permute-start(bf16[4,2,64,512]{3,2,1,0:T(8,128)(2,1)S(1)} %collective-permute-done.4.refs_17_), channel_id=1, source_target_pairs={{0,16},{1,49},{2,18},{3,51},{4,20},{5,53},{6,22},{7,55},{16,32},{1... | collective-permute-start | bytes 1572872 | tf_op jit(solution)/shard_map/b_2/ppermute | solution.py:31
  30.3 3.7 %collective-permute-done.16.refs_21_ = bf16[4,2,64,512]{3,2,1,0:T(8,128)(2,1)S(1)} collective-permute-done((bf16[4,2,64,512]{3,2,1,0:T(8,128)(2,1)S(1)}, bf16[4,2,64,512]{3,2,1,0:T(8,128)(2,1)S(1)}, u32[]{:S(2)}, u32[]{:S(2)}) %collective-permute-start.16) | collective-permute-done | bytes 524320 | tf_op jit(solution)/shard_map/b_x1/ppermute | solution.py:31
  33.9 0.0 collective-permute-done.5.refs_4_
  33.9 0.4 collective-permute-start.17
  34.3 1.2 %collective-permute-start.20 = (bf16[4,2,64,512]{3,2,1,0:T(8,128)(2,1)S(1)}, bf16[4,2,64,512]{3,2,1,0:T(8,128)(2,1)S(1)}, u32[]{:S(2)}, u32[]{:S(2)}) collective-permute-start(bf16[4,2,64,512]{3,2,1,0:T(8,128)(2,1)S(1)} %collective-permute-done.16.refs_21_), channel_id=1, source_target_pairs={{0,16},{1,49},{2,18},{3,51},{4,20},{5,53},{6,22},{7,55},{16,32},{1... | collective-permute-start | bytes 1572872 | tf_op jit(solution)/shard_map/b_x2/ppermute | solution.py:31
  35.5 2.8 %collective-permute-done.14.refs_23_ = bf16[4,2,64,512]{3,2,1,0:T(8,128)(2,1)S(1)} collective-permute-done((bf16[4,2,64,512]{3,2,1,0:T(8,128)(2,1)S(1)}, bf16[4,2,64,512]{3,2,1,0:T(8,128)(2,1)S(1)}, u32[]{:S(2)}, u32[]{:S(2)}) %collective-permute-start.14) | collective-permute-done | bytes 524320 | tf_op jit(solution)/shard_map/b_x3/ppermute | solution.py:31
  38.3 4.3 %collective-permute-start.15 = (bf16[4,2,32,1024]{3,2,1,0:T(8,128)(2,1)S(1)}, bf16[4,2,32,1024]{3,2,1,0:T(8,128)(2,1)S(1)}, u32[]{:S(2)}, u32[]{:S(2)}) collective-permute-start(bf16[4,2,32,1024]{3,2,1,0:T(8,128)(2,1)S(1)} %collective-permute-done.1.refs_6_), channel_id=1, source_target_pairs={{0,2},{1,7},{2,4},{3,1},{4,6},{5,3},{6,0},{7,5},{16,18},{17,23},{1... | collective-permute-start | bytes 1572872 | tf_op jit(solution)/shard_map/a_x1/ppermute | solution.py:31
  42.6 0.0 collective-permute-done.2.refs_9_
  42.7 0.0 collective-permute-start.12
  42.7 0.0 collective-permute-done.9.refs_18_
  42.7 1.5 %collective-permute-start.10 = (bf16[4,2,32,1024]{3,2,1,0:T(8,128)(2,1)S(1)}, bf16[4,2,32,1024]{3,2,1,0:T(8,128)(2,1)S(1)}, u32[]{:S(2)}, u32[]{:S(2)}) collective-permute-start(bf16[4,2,32,1024]{3,2,1,0:T(8,128)(2,1)S(1)} %collective-permute-done.5.refs_4_), channel_id=1, source_target_pairs={{0,1},{1,0},{2,3},{3,2},{4,5},{5,4},{6,7},{7,6},{16,17},{17,16},{1... | collective-permute-start | bytes 1572872 | tf_op jit(solution)/shard_map/other_2/ppermute | solution.py:31
  44.2 1.8 %collective-permute-done.17.refs_8_ = bf16[4,2,32,1024]{3,2,1,0:T(8,128)(2,1)S(1)} collective-permute-done((bf16[4,2,32,1024]{3,2,1,0:T(8,128)(2,1)S(1)}, bf16[4,2,32,1024]{3,2,1,0:T(8,128)(2,1)S(1)}, u32[]{:S(2)}, u32[]{:S(2)}) %collective-permute-start.17) | collective-permute-done | bytes 524320 | tf_op jit(solution)/shard_map/a_x2/ppermute | solution.py:31
  45.9 2.4 %collective-permute-start.18 = (bf16[4,2,32,1024]{3,2,1,0:T(8,128)(2,1)S(1)}, bf16[4,2,32,1024]{3,2,1,0:T(8,128)(2,1)S(1)}, u32[]{:S(2)}, u32[]{:S(2)}) collective-permute-start(bf16[4,2,32,1024]{3,2,1,0:T(8,128)(2,1)S(1)} %collective-permute-done.3.refs_3_), channel_id=1, source_target_pairs={{0,1},{1,0},{2,3},{3,2},{4,5},{5,4},{6,7},{7,6},{16,17},{17,16},{1... | collective-permute-start | bytes 1572872 | tf_op jit(solution)/shard_map/other_1/ppermute | solution.py:31
  48.4 0.0 collective-permute-done.20.refs_22_
  48.4 1.4 %collective-permute-start.21 = (bf16[4,2,32,1024]{3,2,1,0:T(8,128)(2,1)S(1)}, bf16[4,2,32,1024]{3,2,1,0:T(8,128)(2,1)S(1)}, u32[]{:S(2)}, u32[]{:S(2)}) collective-permute-start(bf16[4,2,32,1024]{3,2,1,0:T(8,128)(2,1)S(1)} %collective-permute-done.17.refs_8_), channel_id=1, source_target_pairs={{0,1},{1,0},{2,3},{3,2},{4,5},{5,4},{6,7},{7,6},{16,17},{17,16},{1... | collective-permute-start | bytes 1572872 | tf_op jit(solution)/shard_map/other_x2/ppermute | solution.py:31
  49.8 0.0 collective-permute-done.15.refs_7_
  49.8 0.7 %collective-permute-start.19 = (bf16[4,2,32,1024]{3,2,1,0:T(8,128)(2,1)S(1)}, bf16[4,2,32,1024]{3,2,1,0:T(8,128)(2,1)S(1)}, u32[]{:S(2)}, u32[]{:S(2)}) collective-permute-start(bf16[4,2,32,1024]{3,2,1,0:T(8,128)(2,1)S(1)} %collective-permute-done.15.refs_7_), channel_id=1, source_target_pairs={{0,1},{1,0},{2,3},{3,2},{4,5},{5,4},{6,7},{7,6},{16,17},{17,16},{1... | collective-permute-start | bytes 1572872 | tf_op jit(solution)/shard_map/other_x1/ppermute | solution.py:31
  50.5 0.0 collective-permute-done.12.refs_10_
  50.5 0.1 collective-permute-start.13
  50.6 0.0 collective-permute-done.10.refs_12_
  50.6 0.4 collective-permute-start.11
  51.0 0.0 collective-permute-done.18.refs_11_
  51.1 0.3 collective-permute-done.21.refs_15_
  51.3 0.7 %collective-permute-done.19.refs_14_ = bf16[4,2,32,1024]{3,2,1,0:T(8,128)(2,1)S(1)} collective-permute-done((bf16[4,2,32,1024]{3,2,1,0:T(8,128)(2,1)S(1)}, bf16[4,2,32,1024]{3,2,1,0:T(8,128)(2,1)S(1)}, u32[]{:S(2)}, u32[]{:S(2)}) %collective-permute-start.19) | collective-permute-done | bytes 524320 | tf_op jit(solution)/shard_map/other_x1/ppermute | solution.py:31
  52.1 0.7 %collective-permute-done.13.refs_1_ = bf16[4,2,32,1024]{3,2,1,0:T(8,128)(2,1)S(1)} collective-permute-done((bf16[4,2,32,1024]{3,2,1,0:T(8,128)(2,1)S(1)}, bf16[4,2,32,1024]{3,2,1,0:T(8,128)(2,1)S(1)}, u32[]{:S(2)}, u32[]{:S(2)}) %collective-permute-start.13) | collective-permute-done | bytes 524320 | tf_op jit(solution)/shard_map/other_x/ppermute | solution.py:31
  52.8 0.7 %collective-permute-done.11.refs_0_ = bf16[4,2,32,1024]{3,2,1,0:T(8,128)(2,1)S(1)} collective-permute-done((bf16[4,2,32,1024]{3,2,1,0:T(8,128)(2,1)S(1)}, bf16[4,2,32,1024]{3,2,1,0:T(8,128)(2,1)S(1)}, u32[]{:S(2)}, u32[]{:S(2)}) %collective-permute-start.11) | collective-permute-done | bytes 524320 | tf_op jit(solution)/shard_map/other_x3/ppermute | solution.py:31
  53.6 0.0 copy-done.3
  53.7 11.9 %shard_map.37 = bf16[4,2,1024,512]{3,2,1,0:T(8,128)(2,1)} custom-call(s32[12]{0:T(128)S(1)} %get-tuple-element.38.a_where, s32[12]{0:T(128)S(1)} %get-tuple-element.35.b_where, s32[12]{0:T(128)S(1)} %get-tuple-element.37.b_row, bf16[4,2,32,1024]{3,2,1,0:T(8,128)(2,1)S(1)} %collective-permute-done.11.refs_0_, ...), custom_call_target="tpu_custom_call" | custom-call | flops 6442450944 | bytes 20971520 | tf_op jit(solution)/shard_map/pallas_call | solution.py:115
  (39 shorter events, 0.1 us)
Async XLA Ops:
  0.0 11.4 %collective-permute-start = (bf16[4,2,64,512]{3,2,1,0:T(8,128)(2,1)}, bf16[4,2,64,512]{3,2,1,0:T(8,128)(2,1)S(1)}, u32[]{:S(2)}, u32[]{:S(2)}) collective-permute-start(bf16[4,2,64,512]{3,2,1,0:T(8,128)(2,1)} %refs_16_.1), channel_id=1, source_target_pairs={{0,48},{1,17},{2,50},{3,19},{4,52},{5,21},{6,54},{7,23},{16,0},{17... | collective-permute-start | bytes 1572872 | tf_op jit(solution)/shard_map/b_3/ppermute | solution.py:31
  2.1 12.7 %collective-permute-start.7 = (bf16[4,2,64,512]{3,2,1,0:T(8,128)(2,1)}, bf16[4,2,64,512]{3,2,1,0:T(8,128)(2,1)S(1)}, u32[]{:S(2)}, u32[]{:S(2)}) collective-permute-start(bf16[4,2,64,512]{3,2,1,0:T(8,128)(2,1)} %refs_16_.1), channel_id=1, source_target_pairs={{0,64},{1,65},{2,66},{3,67},{4,68},{5,69},{6,70},{7,71},{16,80},{1... | collective-permute-start | bytes 1572872 | tf_op jit(solution)/shard_map/b_x/ppermute | solution.py:31
  4.9 10.8 %collective-permute-start.6 = (bf16[4,2,32,1024]{3,2,1,0:T(8,128)(2,1)}, bf16[4,2,32,1024]{3,2,1,0:T(8,128)(2,1)S(1)}, u32[]{:S(2)}, u32[]{:S(2)}) collective-permute-start(bf16[4,2,32,1024]{3,2,1,0:T(8,128)(2,1)} %refs_2_.1), channel_id=1, source_target_pairs={{0,6},{1,3},{2,0},{3,5},{4,2},{5,7},{6,4},{7,1},{16,22},{17,19},{1... | collective-permute-start | bytes 1572872 | tf_op jit(solution)/shard_map/a_3/ppermute | solution.py:31
  6.5 17.5 %collective-permute-start.4 = (bf16[4,2,64,512]{3,2,1,0:T(8,128)(2,1)}, bf16[4,2,64,512]{3,2,1,0:T(8,128)(2,1)S(1)}, u32[]{:S(2)}, u32[]{:S(2)}) collective-permute-start(bf16[4,2,64,512]{3,2,1,0:T(8,128)(2,1)} %refs_16_.1), channel_id=1, source_target_pairs={{0,16},{1,49},{2,18},{3,51},{4,20},{5,53},{6,22},{7,55},{16,32},{1... | collective-permute-start | bytes 1572872 | tf_op jit(solution)/shard_map/b_1/ppermute | solution.py:31
  8.0 16.1 %collective-permute-start.3 = (bf16[4,2,32,1024]{3,2,1,0:T(8,128)(2,1)}, bf16[4,2,32,1024]{3,2,1,0:T(8,128)(2,1)S(1)}, u32[]{:S(2)}, u32[]{:S(2)}) collective-permute-start(bf16[4,2,32,1024]{3,2,1,0:T(8,128)(2,1)} %refs_2_.1), channel_id=1, source_target_pairs={{0,2},{1,7},{2,4},{3,1},{4,6},{5,3},{6,0},{7,5},{16,18},{17,23},{1... | collective-permute-start | bytes 1572872 | tf_op jit(solution)/shard_map/a_1/ppermute | solution.py:31
  11.4 42.1 %copy-start = (bf16[4,2,64,512]{3,2,1,0:T(8,128)(2,1)}, bf16[4,2,64,512]{3,2,1,0:T(8,128)(2,1)S(1)}, u32[]{:S(2)}) copy-start(bf16[4,2,64,512]{3,2,1,0:T(8,128)(2,1)S(1)} %collective-permute-done.refs_19_) | copy-start | bytes 1572868
  11.5 15.9 %collective-permute-start.1 = (bf16[4,2,32,1024]{3,2,1,0:T(8,128)(2,1)}, bf16[4,2,32,1024]{3,2,1,0:T(8,128)(2,1)S(1)}, u32[]{:S(2)}, u32[]{:S(2)}) collective-permute-start(bf16[4,2,32,1024]{3,2,1,0:T(8,128)(2,1)} %refs_2_.1), channel_id=1, source_target_pairs={{0,8},{1,9},{2,10},{3,11},{4,12},{5,13},{6,14},{7,15},{16,24},{17,... | collective-permute-start | bytes 1572872 | tf_op jit(solution)/shard_map/a_x/ppermute | solution.py:31
  14.9 38.7 %copy-start.1 = (bf16[4,2,64,512]{3,2,1,0:T(8,128)(2,1)}, bf16[4,2,64,512]{3,2,1,0:T(8,128)(2,1)S(1)}, u32[]{:S(2)}) copy-start(bf16[4,2,64,512]{3,2,1,0:T(8,128)(2,1)S(1)} %collective-permute-done.7.refs_20_) | copy-start | bytes 1572868
  15.7 37.9 %copy-start.2 = (bf16[4,2,32,1024]{3,2,1,0:T(8,128)(2,1)}, bf16[4,2,32,1024]{3,2,1,0:T(8,128)(2,1)S(1)}, u32[]{:S(2)}) copy-start(bf16[4,2,32,1024]{3,2,1,0:T(8,128)(2,1)S(1)} %collective-permute-done.6.refs_5_) | copy-start | bytes 1572868
  15.7 12.1 %collective-permute-start.8 = (bf16[4,2,32,1024]{3,2,1,0:T(8,128)(2,1)S(1)}, bf16[4,2,32,1024]{3,2,1,0:T(8,128)(2,1)S(1)}, u32[]{:S(2)}, u32[]{:S(2)}) collective-permute-start(bf16[4,2,32,1024]{3,2,1,0:T(8,128)(2,1)S(1)} %collective-permute-done.6.refs_5_), channel_id=1, source_target_pairs={{0,1},{1,0},{2,3},{3,2},{4,5},{5,4},{6,7},{7,6},{16,17},{17,16},{1... | collective-permute-start | bytes 1572872 | tf_op jit(solution)/shard_map/other_3/ppermute | solution.py:31
  22.5 11.4 %collective-permute-start.16 = (bf16[4,2,64,512]{3,2,1,0:T(8,128)(2,1)S(1)}, bf16[4,2,64,512]{3,2,1,0:T(8,128)(2,1)S(1)}, u32[]{:S(2)}, u32[]{:S(2)}) collective-permute-start(bf16[4,2,64,512]{3,2,1,0:T(8,128)(2,1)S(1)} %collective-permute-done.7.refs_20_), channel_id=1, source_target_pairs={{0,16},{1,49},{2,18},{3,51},{4,20},{5,53},{6,22},{7,55},{16,32},{1... | collective-permute-start | bytes 1572872 | tf_op jit(solution)/shard_map/b_x1/ppermute | solution.py:31
  24.0 29.6 %copy-start.3 = (bf16[4,2,64,512]{3,2,1,0:T(8,128)(2,1)}, bf16[4,2,64,512]{3,2,1,0:T(8,128)(2,1)S(1)}, u32[]{:S(2)}) copy-start(bf16[4,2,64,512]{3,2,1,0:T(8,128)(2,1)S(1)} %collective-permute-done.4.refs_17_) | copy-start | bytes 1572868
  24.0 29.6 %copy-start.4 = (bf16[4,2,32,1024]{3,2,1,0:T(8,128)(2,1)}, bf16[4,2,32,1024]{3,2,1,0:T(8,128)(2,1)S(1)}, u32[]{:S(2)}) copy-start(bf16[4,2,32,1024]{3,2,1,0:T(8,128)(2,1)S(1)} %collective-permute-done.3.refs_3_) | copy-start | bytes 1572868
  24.0 9.9 %collective-permute-start.5 = (bf16[4,2,32,1024]{3,2,1,0:T(8,128)(2,1)S(1)}, bf16[4,2,32,1024]{3,2,1,0:T(8,128)(2,1)S(1)}, u32[]{:S(2)}, u32[]{:S(2)}) collective-permute-start(bf16[4,2,32,1024]{3,2,1,0:T(8,128)(2,1)S(1)} %collective-permute-done.3.refs_3_), channel_id=1, source_target_pairs={{0,2},{1,7},{2,4},{3,1},{4,6},{5,3},{6,0},{7,5},{16,18},{17,23},{1... | collective-permute-start | bytes 1572872 | tf_op jit(solution)/shard_map/a_2/ppermute | solution.py:31
  27.4 10.9 %collective-permute-start.14 = (bf16[4,2,64,512]{3,2,1,0:T(8,128)(2,1)S(1)}, bf16[4,2,64,512]{3,2,1,0:T(8,128)(2,1)S(1)}, u32[]{:S(2)}, u32[]{:S(2)}) collective-permute-start(bf16[4,2,64,512]{3,2,1,0:T(8,128)(2,1)S(1)} %collective-permute-done.7.refs_20_), channel_id=1, source_target_pairs={{0,48},{1,17},{2,50},{3,19},{4,52},{5,21},{6,54},{7,23},{16,0},{17... | collective-permute-start | bytes 1572872 | tf_op jit(solution)/shard_map/b_x3/ppermute | solution.py:31
  27.4 26.2 %copy-start.5 = (bf16[4,2,32,1024]{3,2,1,0:T(8,128)(2,1)}, bf16[4,2,32,1024]{3,2,1,0:T(8,128)(2,1)S(1)}, u32[]{:S(2)}) copy-start(bf16[4,2,32,1024]{3,2,1,0:T(8,128)(2,1)S(1)} %collective-permute-done.1.refs_6_) | copy-start | bytes 1572868
  27.4 15.2 %collective-permute-start.2 = (bf16[4,2,32,1024]{3,2,1,0:T(8,128)(2,1)S(1)}, bf16[4,2,32,1024]{3,2,1,0:T(8,128)(2,1)S(1)}, u32[]{:S(2)}, u32[]{:S(2)}) collective-permute-start(bf16[4,2,32,1024]{3,2,1,0:T(8,128)(2,1)S(1)} %collective-permute-done.1.refs_6_), channel_id=1, source_target_pairs={{0,6},{1,3},{2,0},{3,5},{4,2},{5,7},{6,4},{7,1},{16,22},{17,19},{1... | collective-permute-start | bytes 1572872 | tf_op jit(solution)/shard_map/a_x3/ppermute | solution.py:31
  27.8 25.8 %copy-start.6 = (bf16[4,2,32,1024]{3,2,1,0:T(8,128)(2,1)}, bf16[4,2,32,1024]{3,2,1,0:T(8,128)(2,1)S(1)}, u32[]{:S(2)}) copy-start(bf16[4,2,32,1024]{3,2,1,0:T(8,128)(2,1)S(1)} %collective-permute-done.8.refs_13_) | copy-start | bytes 1572868
  27.8 14.8 %collective-permute-start.9 = (bf16[4,2,64,512]{3,2,1,0:T(8,128)(2,1)S(1)}, bf16[4,2,64,512]{3,2,1,0:T(8,128)(2,1)S(1)}, u32[]{:S(2)}, u32[]{:S(2)}) collective-permute-start(bf16[4,2,64,512]{3,2,1,0:T(8,128)(2,1)S(1)} %collective-permute-done.4.refs_17_), channel_id=1, source_target_pairs={{0,16},{1,49},{2,18},{3,51},{4,20},{5,53},{6,22},{7,55},{16,32},{1... | collective-permute-start | bytes 1572872 | tf_op jit(solution)/shard_map/b_2/ppermute | solution.py:31
  33.9 19.7 %copy-start.7 = (bf16[4,2,64,512]{3,2,1,0:T(8,128)(2,1)}, bf16[4,2,64,512]{3,2,1,0:T(8,128)(2,1)S(1)}, u32[]{:S(2)}) copy-start(bf16[4,2,64,512]{3,2,1,0:T(8,128)(2,1)S(1)} %collective-permute-done.16.refs_21_) | copy-start | bytes 1572868
  33.9 19.7 %copy-start.8 = (bf16[4,2,32,1024]{3,2,1,0:T(8,128)(2,1)}, bf16[4,2,32,1024]{3,2,1,0:T(8,128)(2,1)S(1)}, u32[]{:S(2)}) copy-start(bf16[4,2,32,1024]{3,2,1,0:T(8,128)(2,1)S(1)} %collective-permute-done.5.refs_4_) | copy-start | bytes 1572868
  33.9 12.0 %collective-permute-start.17 = (bf16[4,2,32,1024]{3,2,1,0:T(8,128)(2,1)S(1)}, bf16[4,2,32,1024]{3,2,1,0:T(8,128)(2,1)S(1)}, u32[]{:S(2)}, u32[]{:S(2)}) collective-permute-start(bf16[4,2,32,1024]{3,2,1,0:T(8,128)(2,1)S(1)} %collective-permute-done.5.refs_4_), channel_id=1, source_target_pairs={{0,8},{1,9},{2,10},{3,11},{4,12},{5,13},{6,14},{7,15},{16,24},{17,... | collective-permute-start | bytes 1572872 | tf_op jit(solution)/shard_map/a_x2/ppermute | solution.py:31
  34.3 14.0 %collective-permute-start.20 = (bf16[4,2,64,512]{3,2,1,0:T(8,128)(2,1)S(1)}, bf16[4,2,64,512]{3,2,1,0:T(8,128)(2,1)S(1)}, u32[]{:S(2)}, u32[]{:S(2)}) collective-permute-start(bf16[4,2,64,512]{3,2,1,0:T(8,128)(2,1)S(1)} %collective-permute-done.16.refs_21_), channel_id=1, source_target_pairs={{0,16},{1,49},{2,18},{3,51},{4,20},{5,53},{6,22},{7,55},{16,32},{1... | collective-permute-start | bytes 1572872 | tf_op jit(solution)/shard_map/b_x2/ppermute | solution.py:31
  38.3 15.3 %copy-start.9 = (bf16[4,2,64,512]{3,2,1,0:T(8,128)(2,1)}, bf16[4,2,64,512]{3,2,1,0:T(8,128)(2,1)S(1)}, u32[]{:S(2)}) copy-start(bf16[4,2,64,512]{3,2,1,0:T(8,128)(2,1)S(1)} %collective-permute-done.14.refs_23_) | copy-start | bytes 1572868
  38.3 11.5 %collective-permute-start.15 = (bf16[4,2,32,1024]{3,2,1,0:T(8,128)(2,1)S(1)}, bf16[4,2,32,1024]{3,2,1,0:T(8,128)(2,1)S(1)}, u32[]{:S(2)}, u32[]{:S(2)}) collective-permute-start(bf16[4,2,32,1024]{3,2,1,0:T(8,128)(2,1)S(1)} %collective-permute-done.1.refs_6_), channel_id=1, source_target_pairs={{0,2},{1,7},{2,4},{3,1},{4,6},{5,3},{6,0},{7,5},{16,18},{17,23},{1... | collective-permute-start | bytes 1572872 | tf_op jit(solution)/shard_map/a_x1/ppermute | solution.py:31
  42.7 11.0 %copy-start.10 = (bf16[4,2,32,1024]{3,2,1,0:T(8,128)(2,1)}, bf16[4,2,32,1024]{3,2,1,0:T(8,128)(2,1)S(1)}, u32[]{:S(2)}) copy-start(bf16[4,2,32,1024]{3,2,1,0:T(8,128)(2,1)S(1)} %collective-permute-done.2.refs_9_) | copy-start | bytes 1572868
  42.7 7.9 %collective-permute-start.12 = (bf16[4,2,32,1024]{3,2,1,0:T(8,128)(2,1)}, bf16[4,2,32,1024]{3,2,1,0:T(8,128)(2,1)S(1)}, u32[]{:S(2)}, u32[]{:S(2)}) collective-permute-start(bf16[4,2,32,1024]{3,2,1,0:T(8,128)(2,1)} %refs_2_.1), channel_id=1, source_target_pairs={{0,1},{1,0},{2,3},{3,2},{4,5},{5,4},{6,7},{7,6},{16,17},{17,16},{1... | collective-permute-start | bytes 1572872 | tf_op jit(solution)/shard_map/other/ppermute | solution.py:31
  42.7 11.0 %copy-start.11 = (bf16[4,2,64,512]{3,2,1,0:T(8,128)(2,1)}, bf16[4,2,64,512]{3,2,1,0:T(8,128)(2,1)S(1)}, u32[]{:S(2)}) copy-start(bf16[4,2,64,512]{3,2,1,0:T(8,128)(2,1)S(1)} %collective-permute-done.9.refs_18_) | copy-start | bytes 1572868
  42.7 7.9 %collective-permute-start.10 = (bf16[4,2,32,1024]{3,2,1,0:T(8,128)(2,1)S(1)}, bf16[4,2,32,1024]{3,2,1,0:T(8,128)(2,1)S(1)}, u32[]{:S(2)}, u32[]{:S(2)}) collective-permute-start(bf16[4,2,32,1024]{3,2,1,0:T(8,128)(2,1)S(1)} %collective-permute-done.5.refs_4_), channel_id=1, source_target_pairs={{0,1},{1,0},{2,3},{3,2},{4,5},{5,4},{6,7},{7,6},{16,17},{17,16},{1... | collective-permute-start | bytes 1572872 | tf_op jit(solution)/shard_map/other_2/ppermute | solution.py:31
  45.9 7.7 %copy-start.12 = (bf16[4,2,32,1024]{3,2,1,0:T(8,128)(2,1)}, bf16[4,2,32,1024]{3,2,1,0:T(8,128)(2,1)S(1)}, u32[]{:S(2)}) copy-start(bf16[4,2,32,1024]{3,2,1,0:T(8,128)(2,1)S(1)} %collective-permute-done.17.refs_8_) | copy-start | bytes 1572868
  45.9 5.1 %collective-permute-start.18 = (bf16[4,2,32,1024]{3,2,1,0:T(8,128)(2,1)S(1)}, bf16[4,2,32,1024]{3,2,1,0:T(8,128)(2,1)S(1)}, u32[]{:S(2)}, u32[]{:S(2)}) collective-permute-start(bf16[4,2,32,1024]{3,2,1,0:T(8,128)(2,1)S(1)} %collective-permute-done.3.refs_3_), channel_id=1, source_target_pairs={{0,1},{1,0},{2,3},{3,2},{4,5},{5,4},{6,7},{7,6},{16,17},{17,16},{1... | collective-permute-start | bytes 1572872 | tf_op jit(solution)/shard_map/other_1/ppermute | solution.py:31
  48.4 5.3 %copy-start.13 = (bf16[4,2,64,512]{3,2,1,0:T(8,128)(2,1)}, bf16[4,2,64,512]{3,2,1,0:T(8,128)(2,1)S(1)}, u32[]{:S(2)}) copy-start(bf16[4,2,64,512]{3,2,1,0:T(8,128)(2,1)S(1)} %collective-permute-done.20.refs_22_) | copy-start | bytes 1572868
  48.4 3.0 %collective-permute-start.21 = (bf16[4,2,32,1024]{3,2,1,0:T(8,128)(2,1)S(1)}, bf16[4,2,32,1024]{3,2,1,0:T(8,128)(2,1)S(1)}, u32[]{:S(2)}, u32[]{:S(2)}) collective-permute-start(bf16[4,2,32,1024]{3,2,1,0:T(8,128)(2,1)S(1)} %collective-permute-done.17.refs_8_), channel_id=1, source_target_pairs={{0,1},{1,0},{2,3},{3,2},{4,5},{5,4},{6,7},{7,6},{16,17},{17,16},{1... | collective-permute-start | bytes 1572872 | tf_op jit(solution)/shard_map/other_x2/ppermute | solution.py:31
  49.8 3.9 %copy-start.14 = (bf16[4,2,32,1024]{3,2,1,0:T(8,128)(2,1)}, bf16[4,2,32,1024]{3,2,1,0:T(8,128)(2,1)S(1)}, u32[]{:S(2)}) copy-start(bf16[4,2,32,1024]{3,2,1,0:T(8,128)(2,1)S(1)} %collective-permute-done.15.refs_7_) | copy-start | bytes 1572868
  49.8 2.3 %collective-permute-start.19 = (bf16[4,2,32,1024]{3,2,1,0:T(8,128)(2,1)S(1)}, bf16[4,2,32,1024]{3,2,1,0:T(8,128)(2,1)S(1)}, u32[]{:S(2)}, u32[]{:S(2)}) collective-permute-start(bf16[4,2,32,1024]{3,2,1,0:T(8,128)(2,1)S(1)} %collective-permute-done.15.refs_7_), channel_id=1, source_target_pairs={{0,1},{1,0},{2,3},{3,2},{4,5},{5,4},{6,7},{7,6},{16,17},{17,16},{1... | collective-permute-start | bytes 1572872 | tf_op jit(solution)/shard_map/other_x1/ppermute | solution.py:31
  50.5 3.2 %copy-start.15 = (bf16[4,2,32,1024]{3,2,1,0:T(8,128)(2,1)}, bf16[4,2,32,1024]{3,2,1,0:T(8,128)(2,1)S(1)}, u32[]{:S(2)}) copy-start(bf16[4,2,32,1024]{3,2,1,0:T(8,128)(2,1)S(1)} %collective-permute-done.12.refs_10_) | copy-start | bytes 1572868
  50.5 2.3 %collective-permute-start.13 = (bf16[4,2,32,1024]{3,2,1,0:T(8,128)(2,1)S(1)}, bf16[4,2,32,1024]{3,2,1,0:T(8,128)(2,1)S(1)}, u32[]{:S(2)}, u32[]{:S(2)}) collective-permute-start(bf16[4,2,32,1024]{3,2,1,0:T(8,128)(2,1)S(1)} %collective-permute-done.1.refs_6_), channel_id=1, source_target_pairs={{0,1},{1,0},{2,3},{3,2},{4,5},{5,4},{6,7},{7,6},{16,17},{17,16},{1... | collective-permute-start | bytes 1572872 | tf_op jit(solution)/shard_map/other_x/ppermute | solution.py:31
  50.6 3.1 %copy-start.16 = (bf16[4,2,32,1024]{3,2,1,0:T(8,128)(2,1)}, bf16[4,2,32,1024]{3,2,1,0:T(8,128)(2,1)S(1)}, u32[]{:S(2)}) copy-start(bf16[4,2,32,1024]{3,2,1,0:T(8,128)(2,1)S(1)} %collective-permute-done.10.refs_12_) | copy-start | bytes 1572868
  50.6 2.9 %collective-permute-start.11 = (bf16[4,2,32,1024]{3,2,1,0:T(8,128)(2,1)S(1)}, bf16[4,2,32,1024]{3,2,1,0:T(8,128)(2,1)S(1)}, u32[]{:S(2)}, u32[]{:S(2)}) collective-permute-start(bf16[4,2,32,1024]{3,2,1,0:T(8,128)(2,1)S(1)} %collective-permute-done.2.refs_9_), channel_id=1, source_target_pairs={{0,1},{1,0},{2,3},{3,2},{4,5},{5,4},{6,7},{7,6},{16,17},{17,16},{1... | collective-permute-start | bytes 1572872 | tf_op jit(solution)/shard_map/other_x3/ppermute | solution.py:31
  51.1 2.7 %copy-start.17 = (bf16[4,2,32,1024]{3,2,1,0:T(8,128)(2,1)}, bf16[4,2,32,1024]{3,2,1,0:T(8,128)(2,1)S(1)}, u32[]{:S(2)}) copy-start(bf16[4,2,32,1024]{3,2,1,0:T(8,128)(2,1)S(1)} %collective-permute-done.18.refs_11_) | copy-start | bytes 1572868
  51.3 2.4 %copy-start.18 = (bf16[4,2,32,1024]{3,2,1,0:T(8,128)(2,1)}, bf16[4,2,32,1024]{3,2,1,0:T(8,128)(2,1)S(1)}, u32[]{:S(2)}) copy-start(bf16[4,2,32,1024]{3,2,1,0:T(8,128)(2,1)S(1)} %collective-permute-done.21.refs_15_) | copy-start | bytes 1572868
  52.1 1.7 %copy-start.19 = (bf16[4,2,32,1024]{3,2,1,0:T(8,128)(2,1)}, bf16[4,2,32,1024]{3,2,1,0:T(8,128)(2,1)S(1)}, u32[]{:S(2)}) copy-start(bf16[4,2,32,1024]{3,2,1,0:T(8,128)(2,1)S(1)} %collective-permute-done.19.refs_14_) | copy-start | bytes 1572868
